TPU v7x, 32 devices: a whole 2x2x4 slice. The times are simulated.
32 devices in a mesh: ctx: 8 (over y, x, core), head: 4 (over z).
Axes of the slice: x: 2, y: 2, z: 4, core: 2. Of those that a mesh axis runs over, the one named last changes fastest.
Arguments:
- hidden_in: bfloat16 [2, 4096, 2048], P(None, 'ctx', 'head'), may hold values from -6 to 6
- projected: bfloat16 [3, 2, 4096, 2048], P(None, None, 'ctx', 'head'), may hold values from -4.5 to 4.5
- w_out: bfloat16 [2048, 2048], P(None, 'head'), may hold values from -0.125 to 0.125
- fast_up: bfloat16 [2, 4, 512, 512], P(None, 'head'), may hold values from -0.25 to 0.25
- fast_down: bfloat16 [4, 512, 512], P('head'), may hold values from -0.25 to 0.25
- learn_rates: float32 [4, 2, 4096], P('head', None, 'ctx'), may hold values from 0.02 to 0.2
Outputs:
- layer_out: bfloat16 [2, 4096, 2048], P(None, 'ctx', 'head')
- fast_up_final: float32 [2, 4, 512, 512], P(None, 'head')
- fast_down_final: float32 [4, 512, 512], P('head')
All inputs are finite; a program needn't handle non-finite values.
Results may differ from a plain program's by a relative error of at most 0.0087.
Values may be sent and summed in bfloat16 or wider, within the bound.
No kernel may reach another device: no remote copies, remote signals or barrier semaphores. Data moves between devices by JAX's collectives and lax.ppermute only.
A program may use at most 128 MiB of HBM per device.

v0:
```python
import math

import jax
import jax.numpy as jnp
from jax import lax
from jax.sharding import PartitionSpec as P

HD = 128
WIN = 512


def shifted(shard, axis, by):
    peers = lax.axis_size(axis)
    return lax.ppermute(shard, axis, [(i, (i + by) % peers) for i in range(peers)])


def fast_apply(rows_in, w_one, w_three, w_two):
    pre_gate = jnp.dot(rows_in, w_one, preferred_element_type=jnp.float32)
    pre_up = jnp.dot(rows_in, w_three, preferred_element_type=jnp.float32)
    hidden = (pre_gate * jax.nn.sigmoid(pre_gate) * pre_up).astype(jnp.bfloat16)
    result = jnp.dot(hidden, w_two, preferred_element_type=jnp.float32)
    return result * lax.rsqrt(jnp.mean(result * result, axis=-1, keepdims=True) + 1e-05)


def fast_grads(key_rows, value_rows, step_size, w_one, w_three, w_two):
    pre_gate = jnp.dot(key_rows, w_one, preferred_element_type=jnp.float32)
    pre_up = jnp.dot(key_rows, w_three, preferred_element_type=jnp.float32)
    gate_sig = jax.nn.sigmoid(pre_gate)
    hidden = (pre_gate * gate_sig * pre_up).astype(jnp.bfloat16)
    out_grad = (-step_size[:, None] * value_rows.astype(jnp.float32)).astype(jnp.bfloat16)
    grad_two = jnp.einsum("tf,tg->fg", hidden, out_grad, preferred_element_type=jnp.float32)
    hidden_grad = jnp.einsum("tg,fg->tf", out_grad, w_two, preferred_element_type=jnp.float32)
    gate_grad = (hidden_grad * pre_up * gate_sig * (1.0 + pre_gate * (1.0 - gate_sig))).astype(
        jnp.bfloat16
    )
    up_grad = (hidden_grad * pre_gate * gate_sig).astype(jnp.bfloat16)
    grad_one = jnp.einsum("tf,tg->fg", key_rows, gate_grad, preferred_element_type=jnp.float32)
    grad_three = jnp.einsum("tf,tg->fg", key_rows, up_grad, preferred_element_type=jnp.float32)
    return (grad_one, grad_three, grad_two)


def renorm(old_weight, gradient):
    moved_weight = old_weight - gradient
    return moved_weight * (
        jnp.sqrt(jnp.sum(old_weight * old_weight))
        / jnp.sqrt(jnp.sum(moved_weight * moved_weight) + 1e-06)
    )


def update_weights(weights_now, gradients):
    summed = lax.psum((gradients[0], gradients[1], gradients[2]), "ctx")
    return (
        renorm(weights_now[0], summed[0]),
        renorm(weights_now[1], summed[1]),
        renorm(weights_now[2], summed[2]),
    )


def body(hidden_in, projected, w_out, fast_up, fast_down, learn_rates):
    block_count, tok_rows, feat_dim = hidden_in.shape
    ctx_index = lax.axis_index("ctx")
    block_len = tok_rows * lax.axis_size("ctx")
    queries = projected[0]
    key_own = projected[1]
    value_own = projected[2]
    key_prev, value_prev = shifted((key_own, value_own), "ctx", 1)
    at_start = ctx_index == 0
    key_lower = jnp.concatenate([key_prev[:1], key_prev[:-1]], axis=0)
    value_lower = jnp.concatenate([value_prev[:1], value_prev[:-1]], axis=0)
    key_before = jnp.where(at_start, key_lower, key_prev)
    value_before = jnp.where(at_start, value_lower, value_prev)
    head_count = feat_dim // HD
    key_all = jnp.concatenate([key_before, key_own], axis=1).reshape(
        block_count, 2 * tok_rows, head_count, HD
    )
    value_all = jnp.concatenate([value_before, value_own], axis=1).reshape(
        block_count, 2 * tok_rows, head_count, HD
    )
    query_heads = queries.reshape(block_count, tok_rows, head_count, HD)
    scores = jnp.einsum(
        "cqhd,ckhd->chqk", query_heads, key_all, preferred_element_type=jnp.float32
    ) * (1.0 / math.sqrt(HD))
    row_ids = jnp.arange(tok_rows, dtype=jnp.int32)[:, None]
    col_ids = jnp.arange(2 * tok_rows, dtype=jnp.int32)[None, :]
    distance = row_ids + tok_rows - col_ids
    prev_usable = (ctx_index > 0) | (jnp.arange(block_count, dtype=jnp.int32) > 0)
    allowed = ((distance >= 0) & (distance < WIN))[None] & (
        (col_ids >= tok_rows)[None] | prev_usable[:, None, None]
    )
    scores = jnp.where(allowed[:, None], scores, -1e30)
    row_peak = jnp.max(scores, axis=-1, keepdims=True)
    lifted = jnp.exp(scores - row_peak)
    weights = (lifted / jnp.sum(lifted, axis=-1, keepdims=True)).astype(jnp.bfloat16)
    attended = jnp.einsum("chqk,ckhd->cqhd", weights, value_all, preferred_element_type=jnp.float32)
    attended = attended.astype(jnp.bfloat16).reshape(block_count, tok_rows, feat_dim)
    weights_now = (
        fast_up[0, 0].astype(jnp.float32),
        fast_up[1, 0].astype(jnp.float32),
        fast_down[0].astype(jnp.float32),
    )
    step_scale = 1.0 / math.sqrt(block_len)
    mixed_rows = []
    for block_idx in range(block_count):
        w_one = weights_now[0].astype(jnp.bfloat16)
        w_three = weights_now[1].astype(jnp.bfloat16)
        w_two = weights_now[2].astype(jnp.bfloat16)
        fast_out = fast_apply(queries[block_idx], w_one, w_three, w_two)
        mixed_rows.append((attended[block_idx].astype(jnp.float32) + fast_out).astype(jnp.bfloat16))
        gradients = fast_grads(
            key_own[block_idx],
            value_own[block_idx],
            learn_rates[0, block_idx] * step_scale,
            w_one,
            w_three,
            w_two,
        )
        weights_now = update_weights(weights_now, gradients)
    mixed = jnp.stack(mixed_rows)
    projected_out = jnp.einsum(
        "ctf,fg->ctg",
        lax.all_gather(mixed, "head", axis=2, tiled=True),
        w_out,
        preferred_element_type=jnp.float32,
    )
    layer_out = (hidden_in.astype(jnp.float32) + projected_out).astype(jnp.bfloat16)
    fast_up_final = jnp.stack([weights_now[0], weights_now[1]])[:, None]
    fast_down_final = weights_now[2][None]
    return (layer_out, fast_up_final, fast_down_final)


def solution(mesh):
    in_specs = (
        P(None, "ctx", "head"),
        P(None, None, "ctx", "head"),
        P(None, "head"),
        P(None, "head", None, None),
        P("head", None, None),
        P("head", None, "ctx"),
    )
    out_specs = (P(None, "ctx", "head"), P(None, "head", None, None), P("head", None, None))
    return jax.shard_map(body, mesh=mesh, in_specs=in_specs, out_specs=out_specs, check_vma=False)
```

profile of v0, /device:TPU:0, one launch (start us, length us, event | category | flops | bytes accessed | tf_op | source)
XLA Modules:
  0.0 296.3 jit_solution(5415664548398649168)
XLA Ops:
  7.2 3.7 %fusion.124 = (bf16[1,2,512,512]{3,2,1,0:T(8,128)(2,1)}, bf16[1,2,512,512]{3,2,1,0:T(8,128)(2,1)}, bf16[1,2,512,512]{3,2,1,0:T(8,128)(2,1)}) fusion(bf16[3,2,512,512]{3,2,1,0:T(8,128)(2,1)} %param.7), kind=kLoop, calls=%fused_computation.174 | loop fusion | bytes 6291456 | tf_op jit(solution)/shard_map/slice | solution.py:65
  11.0 2.4 copy.39
  13.8 2.3 copy.40
  16.1 2.6 collective-permute-start.1
  28.3 2.5 fusion.63
  30.7 3.4 %multiply_reduce_fusion.10 = (f32[512]{0:T(512)S(1)}, f32[512,512]{0,1:T(8,128)}) fusion(bf16[1,512,512]{2,1,0:T(8,128)(2,1)} %param.10, f32[512,512]{1,0:T(8,128)} %fusion.63, bf16[3,2,512,512]{3,2,1,0:T(8,128)(2,1)} %param.7, bf16[2,1,512,512]{3,2,1,0:T(8,128)(2,1)S(1)} %copy-done.4), kind=kOutput, calls=%fused_computation.90 | convolution fusion | flops 538967552 | bytes 3672064 | tf_op jit(solution)/shard_map/dot_general | solution.py:21
  39.9 2.3 copy.41
  45.4 4.2 %collective-permute-done.1 = bf16[2,512,512]{1,2,0:T(8,128)(2,1)} collective-permute-done((bf16[2,512,512]{1,2,0:T(8,128)(2,1)}, bf16[2,512,512]{1,2,0:T(8,128)(2,1)}, u32[]{:S(2)}, u32[]{:S(2)}) %collective-permute-start.1) | collective-permute-done | bytes 1048608 | tf_op jit(solution)/shard_map/ppermute | solution.py:14
  52.3 2.3 copy.21
  54.6 9.7 %fusion.9 = f32[2,4,1024,512]{3,2,1,0:T(8,128)} fusion(bf16[2,512,4,128]{1,3,2,0:T(8,128)(2,1)} %bitcast.153, bf16[2,512,4,128]{3,1,2,0:T(8,128)(2,1)S(1)} %copy.22, bf16[2,512,4,128]{3,1,2,0:T(8,128)(2,1)} %copy.21), kind=kOutput, calls=%fused_computation.12 | convolution fusion | flops 1077936128 | bytes 19922944 | tf_op jit(solution)/shard_map/cqhd,ckhd->chqk/dot_general | solution.py:80
  64.4 19.3 %fusion.127 = (f32[2,4,512]{2,1,0:T(4,128)S(1)}, f32[2,4,512,1024]{2,3,1,0:T(8,128)}) fusion(f32[2,4,1024,512]{3,2,1,0:T(8,128)} %fusion.9, pred[2,512,1024]{1,2,0:T(8,128)(4,1)} %broadcast_and_fusion), kind=kOutput, calls=%fused_computation.177 | output fusion | flops 25166848 | bytes 34619392 | tf_op jit(solution)/shard_map/sub | solution.py:92
  83.7 8.0 %fusion.23 = bf16[2,512,4,128]{1,3,2,0:T(8,128)(2,1)S(1)} fusion(f32[2,4,512,1024]{2,3,1,0:T(8,128)} %get-tuple-element.40, f32[2,4,512]{2,1,0:T(4,128)S(1)} %get-tuple-element.39, bf16[2,512,4,128]{1,3,2,0:T(8,128)(2,1)S(1)} %bitcast.158, bf16[2,512,4,128]{1,3,2,0:T(8,128)(2,1)} %bitcast.159), kind=kOutput, calls=%fused_computation.26 | convolution fusion | flops 1086849024 | bytes 19939328 | tf_op jit(solution)/shard_map/chqk,ckhd->cqhd/dot_general | solution.py:94
  92.8 11.2 %all-reduce.7.cloned.1.call-done = (f32[512,512]{0,1:T(8,128)}, f32[512,512]{0,1:T(8,128)}, f32[512,512]{1,0:T(8,128)}) async-done(((f32[512,512]{0,1:T(8,128)}, f32[512,512]{0,1:T(8,128)}, f32[512,512]{1,0:T(8,128)}), (f32[512,512]{0,1:T(8,128)}, f32[512,512]{0,1:T(8,128)}, f32[512,512]{1,0:T(8,128)})) %all-reduce.7.cloned.1.call-update) | async-done | bytes 3145744 | tf_op jit(solution)/shard_map/psum | solution.py:51
  104.0 3.9 %multiply_reduce_fusion.8 = (f32[]{:T(128)}, f32[512,512]{0,1:T(8,128)}, f32[]{:T(128)}, f32[]{:T(128)}, f32[]{:T(128)}, /*index=5*/f32[512,512]{0,1:T(8,128)S(1)}) fusion(f32[512,512]{0,1:T(8,128)} %get-tuple-element.19, bf16[1,1,512,512]{2,3,1,0:T(8,128)(2,1)} %copy.43, bf16[1,1,512,512]{2,3,1,0:T(8,128)(2,1)} %copy.42, f32[512,512]{0,1:T(8,128)} %get-tuple-element.18), kind=kLoop, calls=%fused_computation.80 | loop fusion | flops 3145724 | bytes 5242896 | tf_op jit(solution)/shard_map/reduce_sum | solution.py:46
  110.6 3.2 %multiply_reduce_fusion.7 = (f32[]{:T(128)}, f32[512,512]{1,0:T(8,128)}, f32[]{:T(128)}) fusion(f32[512,512]{1,0:T(8,128)} %get-tuple-element.20, bf16[1,512,512]{2,1,0:T(8,128)(2,1)} %param.10), kind=kLoop, calls=%fused_computation.78 | loop fusion | flops 1572862 | bytes 2621448 | tf_op jit(solution)/shard_map/reduce_sum | solution.py:46
  115.3 2.5 convolution_bitcast_fusion.2
  117.8 2.8 convolution_bitcast_fusion.3
  122.5 3.5 %fusion.87 = f32[512,512]{1,0:T(8,128)} fusion(f32[512,512]{1,0:T(8,128)} %convolution_bitcast_fusion.3, f32[512,512]{1,0:T(8,128)} %convolution_bitcast_fusion.2, bf16[3,2,512,512]{3,2,1,0:T(8,128)(2,1)} %param.7, f32[512]{0:T(512)S(1)} %bitcast.161), kind=kOutput, calls=%fused_computation.134 | convolution fusion | flops 270794752 | bytes 3672064 | tf_op jit(solution)/shard_map/tf,tg->fg/dot_general | solution.py:31
  126.0 2.8 convolution_bitcast_fusion.1
  128.8 2.5 convolution_bitcast_fusion
  131.4 2.3 fusion.50
  133.7 2.5 convolution_bitcast_fusion.6
  136.2 4.5 %multiply_reduce_fusion.6 = (f32[512]{0:T(512)S(1)}, f32[512,512]{0,1:T(8,128)}) fusion(f32[512,512]{1,0:T(8,128)} %get-tuple-element.22, f32[]{:T(128)S(6)} %div.52, f32[512,512]{1,0:T(8,128)} %convolution_bitcast_fusion.6, bf16[3,2,512,512]{3,2,1,0:T(8,128)(2,1)} %param.7, f32[512,512]{0,1:T(8,128)} %get-tuple-element.24, f32[]{:T(128)S(6)} %div.51), kind=kOutput, calls=%fused_computation.77 | convolution fusion | flops 540016128 | bytes 4720648 | tf_op jit(solution)/shard_map/dot_general | solution.py:21
  142.2 2.1 pad_maximum_fusion
  144.4 57.1 %all-reduce.5.cloned.1.call-done = (f32[512,512]{0,1:T(8,128)}, f32[512,512]{0,1:T(8,128)}, f32[512,512]{1,0:T(8,128)}) async-done(((f32[512,512]{0,1:T(8,128)}, f32[512,512]{0,1:T(8,128)}, f32[512,512]{1,0:T(8,128)}), (f32[512,512]{0,1:T(8,128)}, f32[512,512]{0,1:T(8,128)}, f32[512,512]{1,0:T(8,128)})) %all-reduce.5.cloned.1.call-update) | async-done | bytes 3145744 | tf_op jit(solution)/shard_map/psum | solution.py:51
  201.5 2.4 multiply_reduce_fusion
  205.2 2.1 multiply_reduce_fusion.4
  208.6 2.6 multiply_reduce_fusion.2
  216.3 3.0 %copy.32 = f32[2,1,512,512]{3,2,1,0:T(8,128)} copy(f32[2,1,512,512]{2,3,0,1:T(8,128)} %maximum_bitcast_fusion) | data formatting | bytes 4194304
  219.3 2.4 multiply_bitcast_fusion
  221.7 62.2 %all-gather.2.cloned.1.call-done = bf16[2,512,2048]{1,2,0:T(8,128)(2,1)} async-done(((bf16[2,512,512]{1,2,0:T(8,128)(2,1)}), bf16[2,512,2048]{1,2,0:T(8,128)(2,1)}) %all-gather.2.cloned.1.call-update) | async-done | bytes 4194320 | tf_op jit(solution)/shard_map/all_gather | solution.py:121
  283.9 5.8 %add_convert_fusion = bf16[2,512,512]{2,1,0:T(8,128)(2,1)} fusion(bf16[2,512,512]{2,1,0:T(8,128)(2,1)} %param.6, bf16[2,512,2048]{1,2,0:T(8,128)(2,1)} %all-gather.2.cloned.1.call-done, bf16[2048,512]{1,0:T(8,128)(2,1)S(1)} %copy-done), kind=kOutput, calls=%fused_computation.19 | convolution fusion | flops 2149056512 | bytes 8388608 | tf_op jit(solution)/shard_map/ctf,fg->ctg/dot_general | solution.py:119
  (58 shorter events, 30.0 us)
Async XLA Ops:
  7.2 276.8 %copy-start = (bf16[2048,512]{1,0:T(8,128)(2,1)S(1)}, bf16[2048,512]{1,0:T(8,128)(2,1)}, u32[]{:S(2)}) copy-start(bf16[2048,512]{1,0:T(8,128)(2,1)} %param.8) | copy-start | bytes 6291460
  7.2 96.8 %all-reduce.7.cloned.1.call-start = ((), (), s32[]{:S(2)}) async-start(), calls=%async_computation.2 | async-start | bytes 6291456 | tf_op jit(solution)/shard_map/psum | solution.py:51
  11.0 7.7 %copy-start.4 = (bf16[2,1,512,512]{3,2,1,0:T(8,128)(2,1)S(1)}, bf16[2,1,512,512]{3,2,1,0:T(8,128)(2,1)}, u32[]{:S(2)}) copy-start(bf16[2,1,512,512]{3,2,1,0:T(8,128)(2,1)} %param.9) | copy-start | bytes 3145732
  13.3 31.0 %collective-permute-start = (bf16[2,512,512]{1,2,0:T(8,128)(2,1)}, bf16[2,512,512]{1,2,0:T(8,128)(2,1)}, u32[]{:S(2)}, u32[]{:S(2)}) collective-permute-start(bf16[2,512,512]{1,2,0:T(8,128)(2,1)} %bitcast.157), channel_id=1, source_target_pairs={{0,4},{4,8},{8,12},{12,16},{16,20},{20,24},{24,28},{28,0},{1,5},{5... | collective-permute-start | bytes 3145736 | tf_op jit(solution)/shard_map/ppermute | solution.py:14
  13.8 7.9 %copy-start.10 = (f32[1,2,512]{2,1,0:T(2,128)S(1)}, f32[1,2,512]{2,1,0:T(2,128)}, u32[]{:S(2)}) copy-start(f32[1,2,512]{2,1,0:T(2,128)} %param.11) | copy-start | bytes 12292
  16.1 5.6 %copy-start.1 = (bf16[3,2,512,512]{3,2,1,0:T(8,128)(2,1)S(1)}, bf16[3,2,512,512]{3,2,1,0:T(8,128)(2,1)}, u32[]{:S(2)}) copy-start(bf16[3,2,512,512]{3,2,1,0:T(8,128)(2,1)} %param.7) | copy-start | bytes 9437188
  16.1 5.6 %copy-start.6 = (bf16[1,512,512]{2,1,0:T(8,128)(2,1)S(1)}, bf16[1,512,512]{2,1,0:T(8,128)(2,1)}, u32[]{:S(2)}) copy-start(bf16[1,512,512]{2,1,0:T(8,128)(2,1)} %param.10) | copy-start | bytes 1572868
  16.1 33.6 %collective-permute-start.1 = (bf16[2,512,512]{1,2,0:T(8,128)(2,1)}, bf16[2,512,512]{1,2,0:T(8,128)(2,1)}, u32[]{:S(2)}, u32[]{:S(2)}) collective-permute-start(bf16[2,512,512]{1,2,0:T(8,128)(2,1)} %bitcast.154), channel_id=1, source_target_pairs={{0,4},{4,8},{8,12},{12,16},{16,20},{20,24},{24,28},{28,0},{1,5},{5... | collective-permute-start | bytes 3145736 | tf_op jit(solution)/shard_map/ppermute | solution.py:14
  27.0 174.4 %all-reduce.5.cloned.1.call-start = ((), (), s32[]{:S(2)}) async-start(), calls=%async_computation.1 | async-start | bytes 6291456 | tf_op jit(solution)/shard_map/psum | solution.py:51
  64.4 19.3 %copy-start.7 = (bf16[1,2,512,512]{2,3,1,0:T(8,128)(2,1)S(1)}, bf16[1,2,512,512]{2,3,1,0:T(8,128)(2,1)}, u32[]{:S(2)}) copy-start(bf16[1,2,512,512]{2,3,1,0:T(8,128)(2,1)} %copy.39) | copy-start | bytes 3145732
  122.5 3.5 %copy-start.8 = (f32[512,512]{1,0:T(8,128)S(1)}, f32[512,512]{1,0:T(8,128)}, u32[]{:S(2)}) copy-start(f32[512,512]{1,0:T(8,128)} %convolution_bitcast_fusion.2) | copy-start | bytes 3145732
  122.5 3.5 %copy-start.9 = (f32[512,512]{1,0:T(8,128)S(1)}, f32[512,512]{1,0:T(8,128)}, u32[]{:S(2)}) copy-start(f32[512,512]{1,0:T(8,128)} %convolution_bitcast_fusion.3) | copy-start | bytes 3145732
  131.3 152.6 %all-gather.2.cloned.1.call-start = ((), (), s32[]{:S(2)}) async-start(), calls=%async_computation | async-start | bytes 5242880 | tf_op jit(solution)/shard_map/all_gather | solution.py:121
  212.5 1.7 copy-start.2
  212.5 2.0 copy-start.5
  216.3 3.0 %copy-start.3 = (f32[512,512]{1,0:T(8,128)S(1)}, f32[512,512]{1,0:T(8,128)}, u32[]{:S(2)}) copy-start(f32[512,512]{1,0:T(8,128)} %get-tuple-element.22) | copy-start | bytes 3145732
Sparse Core Ops, SparseCore 0:
  27.2 76.7 all-reduce.6
  131.4 69.9 all-reduce.4
  203.1 80.8 all-gather.1
where the time goes:
time: 298 us; the launch traced here: 296 us
  waiting for transfers between devices  135 us (45%)
  matrix products  60.6 us (20%)
  other arithmetic  49.2 us (17%)
  local copies, waits for them, and re-layouts  26.3 us (9%)
  between operations  22 us (7%)
  starting transfers between devices  3.36 us (1%)
    psum x2, waiting for transfers between devices, update_weights(): summed = lax.psum((gradients[0], gradients[1], gradients[2]), 'ctx')  68.3 us
    all_gather x1, waiting for transfers between devices, body(): lax.all_gather(mixed, 'head', axis=2, tiled=True)  62.2 us
    sub x1, other arithmetic, body(): lifted = jnp.exp(scores - row_peak)  19.3 us
    unnamed x28, local copies, waits for them, and re-layouts  14.4 us
    reduce_sum x5, other arithmetic, renorm(): jnp.sum(moved_weight * moved_weight) + 1e-06  14.3 us
    dot_general x1, matrix products, body(): jnp.einsum('cqhd,ckhd->chqk', query_heads, key_all, preferred_element_typ...  9.73 us
    dot_general x1, matrix products, body(): jnp.einsum('chqk,ckhd->cqhd', weights, value_all, preferred_element_type=...  8 us
    dot_general x2, matrix products, fast_apply(): result = jnp.dot(hidden, w_two, preferred_element_type=jnp.float32)  7.88 us
  transfers between devices with their start and end apart: 5, of which 4 were waited for; matrix products, arithmetic and copies ran while one was open for 34% of the time, Pallas kernels for 0%

commit v1 on v0

v1 whole, which is shorter than its diff:
```python
import functools
import math

import jax
import jax.numpy as jnp
from jax import lax
from jax.experimental import pallas as pl
from jax.experimental.pallas import tpu as pltpu
from jax.sharding import PartitionSpec as P

HD = 128
WIN = 512
TILE = 256
MASKED = -1e30
BF = jnp.bfloat16
F32 = jnp.float32
LIMIT = 48 * 1024 * 1024


def mm(a, b):
    return jnp.dot(a, b, preferred_element_type=F32)


def mm_nt(a, b):
    return lax.dot_general(a, b, (((1,), (1,)), ((), ())), preferred_element_type=F32)


def mm_tn(a, b):
    return lax.dot_general(a, b, (((0,), (0,)), ((), ())), preferred_element_type=F32)


def sigmoid(x):
    return 0.5 + 0.5 * jnp.tanh(0.5 * x)


def whole(array):
    zeros = (0,) * array.ndim
    return pl.BlockSpec(array.shape, lambda *_: zeros)


def whole_out(shape):
    zeros = (0,) * len(shape)
    return pl.BlockSpec(shape, lambda *_: zeros)


def call(kernel, name, scalars, inputs, specs, outs, scratch=(), grid=(1,), flops=0, nbytes=0):
    single = not isinstance(outs, (list, tuple))
    outs_list = [outs] if single else list(outs)
    got = pl.pallas_call(
        kernel,
        out_shape=outs_list,
        grid_spec=pltpu.PrefetchScalarGridSpec(
            num_scalar_prefetch=1,
            grid=grid,
            in_specs=specs,
            out_specs=[whole_out(o.shape) for o in outs_list],
            scratch_shapes=list(scratch),
        ),
        compiler_params=pltpu.CompilerParams(vmem_limit_bytes=LIMIT),
        cost_estimate=pl.CostEstimate(flops=flops, bytes_accessed=nbytes, transcendentals=0),
        name=name,
    )(scalars, *inputs)
    return got[0] if single else got


def grads_kernel(block, step_scale, sc, k_ref, v_ref, lr_ref, w1_ref, w3_ref, w2_ref, keep_ref, send_ref, acc):
    step = pl.program_id(0)
    k = k_ref[...]
    w_two = w2_ref[...]
    rates = lr_ref[0, block : block + 1, :] * step_scale
    rates = jnp.broadcast_to(rates, (HD, rates.shape[1])).T[:, :1]
    out_grad = (-rates * v_ref[...].astype(F32)).astype(BF)
    gate = mm(k, w1_ref[...])
    up = mm(k, w3_ref[...])
    hidden_grad = mm_nt(out_grad, w_two)
    sig = sigmoid(gate)
    gate_sig = gate * sig
    hidden = (gate_sig * up).astype(BF)
    up_grad = (hidden_grad * gate_sig).astype(BF)
    gate_grad = (hidden_grad * up * sig * (1.0 + gate - gate_sig)).astype(BF)
    parts = (mm_tn(k, gate_grad), mm_tn(k, up_grad), mm_tn(hidden, out_grad))

    @pl.when(step == 0)
    def _():
        for i, part in enumerate(parts):
            acc[i] = part

    @pl.when(step > 0)
    def _():
        for i, part in enumerate(parts):
            acc[i] = acc[i] + part

    @pl.when(step == pl.num_programs(0) - 1)
    def _():
        half = keep_ref.shape[1]
        own = pl.multiple_of(sc[0] * half, half)
        other = pl.multiple_of((1 - sc[0]) * half, half)
        keep_ref[...] = acc[:, pl.ds(own, half), :].astype(BF)
        send_ref[...] = acc[:, pl.ds(other, half), :].astype(BF)


def block_grads(block, scalars, projected, learn_rates, weights, step_scale, weight_specs):
    _, _, rows, feats = projected.shape
    half = feats // 2
    shape = jax.ShapeDtypeStruct((3, half, feats), BF)
    tile = min(TILE, rows)
    return call(
        functools.partial(grads_kernel, block, step_scale),
        f"grads_{block}",
        scalars,
        (projected, projected, learn_rates, *weights),
        [
            pl.BlockSpec((None, None, tile, feats), lambda i, s: (1, block, i, 0)),
            pl.BlockSpec((None, None, tile, feats), lambda i, s: (2, block, i, 0)),
            pl.BlockSpec((1, learn_rates.shape[1], tile), lambda i, s: (0, 0, i)),
            *weight_specs,
        ],
        [shape, shape],
        scratch=[pltpu.VMEM((3, feats, feats), F32)],
        grid=(rows // tile,),
        flops=12 * rows * feats * feats,
        nbytes=4 * feats * feats * 2,
    )


def attend_rows(q, keys, values, usable):
    rows = q.shape[0]
    row_ids = lax.broadcasted_iota(jnp.int32, (rows, rows), 0)
    col_ids = lax.broadcasted_iota(jnp.int32, (rows, rows), 1)
    scale = math.log2(math.e) / math.sqrt(HD)
    scores = []
    last = len(keys) - 1
    for i, (key, before) in enumerate(keys):
        s = mm_nt(q, key)
        if before:
            s = s + usable
        if i == 0:
            s = jnp.where(col_ids > row_ids, s, MASKED)
        if i == last:
            s = jnp.where(col_ids <= row_ids, s, MASKED)
        scores.append(s)
    top = functools.reduce(jnp.maximum, scores)
    peak = jnp.max(top, axis=-1, keepdims=True) * scale
    total = None
    result = None
    for s, value in zip(scores, values):
        lifted = jnp.exp2(s * scale - peak)
        total = lifted if total is None else total + lifted
        part = mm(lifted.astype(BF), value)
        result = part if result is None else result + part
    return (result / jnp.sum(total, axis=-1, keepdims=True)).astype(BF)


def attend(q_ref, k_ref, v_ref, halo_ref, usable, store):
    rows, feats = q_ref.shape
    tile = min(TILE, rows)
    for start in range(0, rows, tile):
        for head in range(feats // HD):
            cols = slice(head * HD, (head + 1) * HD)
            keys, values = [], []
            for at in range(start - WIN, start + tile, tile):
                before = at < 0
                where = slice(at + WIN, at + WIN + tile) if before else slice(at, at + tile)
                keys.append(((halo_ref[0, where, cols] if before else k_ref[where, cols]), before))
                values.append(halo_ref[1, where, cols] if before else v_ref[where, cols])
            store(slice(start, start + tile), cols, attend_rows(q_ref[start : start + tile, cols], keys, values, usable))


def fast_rows(q, w_one, w_three, w_two):
    gate = mm(q, w_one)
    up = mm(q, w_three)
    hidden = (gate * sigmoid(gate) * up).astype(BF)
    result = mm(hidden, w_two)
    return result * lax.rsqrt(jnp.mean(result * result, axis=-1, keepdims=True) + 1e-05)


def usable_bias(block, sc):
    return jnp.where((sc[1] > 0) | (block > 0), 0.0, MASKED).astype(F32)


def mixed_kernel(block, sc, q_ref, k_ref, v_ref, halo_ref, w1_ref, w3_ref, w2_ref, out_ref, att):
    def store(rows, cols, value):
        att[rows, cols] = value

    attend(q_ref, k_ref, v_ref, halo_ref, usable_bias(block, sc), store)
    rows = q_ref.shape[0]
    tile = min(TILE, rows)
    for start in range(0, rows, tile):
        at = slice(start, start + tile)
        fast = fast_rows(q_ref[at, :], w1_ref[...], w3_ref[...], w2_ref[...])
        out_ref[at, :] = (att[at, :].astype(F32) + fast).astype(BF)


def attend_kernel(block, sc, q_ref, k_ref, v_ref, halo_ref, out_ref):
    def store(rows, cols, value):
        out_ref[rows, cols] = value

    attend(q_ref, k_ref, v_ref, halo_ref, usable_bias(block, sc), store)


def qkv_specs(block, projected):
    _, _, rows, feats = projected.shape
    return [
        pl.BlockSpec((None, None, rows, feats), functools.partial(lambda kind, i, s: (kind, block, 0, 0), kind))
        for kind in range(3)
    ]


def attention_only(block, scalars, projected, halo):
    _, _, rows, feats = projected.shape
    return call(
        functools.partial(attend_kernel, block),
        f"attend_{block}",
        scalars,
        (projected, projected, projected, halo),
        [*qkv_specs(block, projected), whole(halo)],
        jax.ShapeDtypeStruct((rows, feats), BF),
        flops=8 * rows * WIN * feats,
        nbytes=6 * rows * feats * 2,
    )


def mixed_first(block, scalars, projected, halo, weights, weight_specs):
    _, _, rows, feats = projected.shape
    return call(
        functools.partial(mixed_kernel, block),
        f"mixed_{block}",
        scalars,
        (projected, projected, projected, halo, *weights),
        [*qkv_specs(block, projected), whole(halo), *weight_specs],
        jax.ShapeDtypeStruct((rows, feats), BF),
        scratch=[pltpu.VMEM((rows, feats), BF)],
        flops=8 * rows * WIN * feats + 6 * rows * feats * feats,
        nbytes=8 * rows * feats * 2,
    )


def renorm_into(sc, old, mine_ref, theirs_ref, moved):
    half = mine_ref.shape[1]
    own = pl.multiple_of(sc[0] * half, half)
    other = pl.multiple_of((1 - sc[0]) * half, half)
    for i in range(3):
        before = jnp.zeros((), F32)
        after = jnp.zeros((), F32)
        for start, part in ((own, mine_ref), (other, theirs_ref)):
            w = old(i, pl.ds(start, half)).astype(F32)
            new = w - part[i].astype(F32)
            moved[i, pl.ds(start, half), :] = new
            before += jnp.sum(w * w)
            after += jnp.sum(new * new)
        ratio = jnp.sqrt(before) / jnp.sqrt(after + 1e-06)
        moved[i] = moved[i] * ratio


def update_kernel(first, sc, mine_ref, theirs_ref, up_ref, down_ref, q_ref, att_ref, mix_ref, new_ref, new_bf_ref):
    if first:
        old = lambda i, rows: up_ref[i, 0, rows, :] if i < 2 else down_ref[0, rows, :]
    else:
        old = lambda i, rows: up_ref[i, rows, :]
    renorm_into(sc, old, mine_ref, theirs_ref, new_ref)
    new_bf_ref[...] = new_ref[...].astype(BF)
    rows = q_ref.shape[0]
    tile = min(TILE, rows)
    for start in range(0, rows, tile):
        at = slice(start, start + tile)
        fast = fast_rows(q_ref[at, :], new_bf_ref[0], new_bf_ref[1], new_bf_ref[2])
        mix_ref[at, :] = (att_ref[at, :].astype(F32) + fast).astype(BF)


def update_and_mix(block, scalars, mine, theirs, state, projected, attended):
    _, _, rows, feats = projected.shape
    first = block == 1
    return call(
        functools.partial(update_kernel, first),
        f"update_{block}",
        scalars,
        (mine, theirs, state[0], state[1], projected, attended),
        [
            whole(mine),
            whole(theirs),
            whole(state[0]),
            whole(state[1]),
            pl.BlockSpec((None, None, rows, feats), lambda i, s: (0, block, 0, 0)),
            whole(attended),
        ],
        [
            jax.ShapeDtypeStruct((rows, feats), BF),
            jax.ShapeDtypeStruct((3, feats, feats), F32),
            jax.ShapeDtypeStruct((3, feats, feats), BF),
        ],
        flops=6 * rows * feats * feats,
        nbytes=9 * feats * feats * 2,
    )


def final_kernel(first, sc, mine_ref, theirs_ref, up_ref, down_ref, up_out, down_out, moved):
    if first:
        old = lambda i, rows: up_ref[i, 0, rows, :] if i < 2 else down_ref[0, rows, :]
    else:
        old = lambda i, rows: up_ref[i, rows, :]
    renorm_into(sc, old, mine_ref, theirs_ref, moved)
    up_out[0, 0] = moved[0]
    up_out[1, 0] = moved[1]
    down_out[0] = moved[2]


def final_update(first, scalars, mine, theirs, state):
    feats = mine.shape[2]
    return call(
        functools.partial(final_kernel, first),
        "final_update",
        scalars,
        (mine, theirs, *state),
        [whole(mine), whole(theirs), whole(state[0]), whole(state[1])],
        [jax.ShapeDtypeStruct((2, 1, feats, feats), F32), jax.ShapeDtypeStruct((1, feats, feats), F32)],
        scratch=[pltpu.VMEM((3, feats, feats), F32)],
        flops=10 * feats * feats,
        nbytes=9 * feats * feats * 2,
    )


def edge_kernel(sc, m_ref, ya_ref, yb_ref, v_ref, out_ref):
    out_ref[...] = (mm(m_ref[...], v_ref[0]) + mm(ya_ref[...], v_ref[1]) + mm(yb_ref[...], v_ref[2])).astype(BF)


def edge_part(block, scalars, m, ya, yb, v):
    rows, feats = m.shape
    return call(
        edge_kernel,
        f"edge_{block}",
        scalars,
        (m, ya, yb, v),
        [whole(m), whole(ya), whole(yb), whole(v)],
        jax.ShapeDtypeStruct((rows, feats), BF),
        flops=6 * rows * feats * feats,
        nbytes=7 * rows * feats * 2,
    )


def own_kernel(sc, m_ref, x_ref, ya_ref, yb_ref, w_ref, hid_ref, out_ref):
    feats = m_ref.shape[1]
    head = sc[2]

    def weight(which):
        return w_ref[pl.ds(pl.multiple_of(which * feats, feats), feats), :]

    out_ref[...] = hid_ref[...].astype(F32) + mm(m_ref[...], weight(head))

    @pl.when(sc[3] == 1)
    def _():
        out_ref[...] = (
            out_ref[...]
            + mm(x_ref[...], weight(head ^ 1))
            + mm(ya_ref[...], weight(head ^ 3))
            + mm(yb_ref[...], weight(head ^ 2))
        )


def own_part(block, scalars, m, x, ya, yb, w_out, hidden_in):
    rows, feats = m.shape
    return call(
        own_kernel,
        f"own_{block}",
        scalars,
        (m, x, ya, yb, w_out, hidden_in),
        [
            whole(m),
            whole(x),
            whole(ya),
            whole(yb),
            whole(w_out),
            pl.BlockSpec((None, rows, feats), lambda i, s: (block, 0, 0)),
        ],
        jax.ShapeDtypeStruct((rows, feats), F32),
        flops=8 * rows * feats * feats,
        nbytes=10 * rows * feats * 2,
    )


def move(x, axis, pairs):
    return lax.ppermute(x, axis, pairs)


def flip(x, bit):
    count = lax.axis_size("ctx")
    return move(x, "ctx", [(i, i ^ (1 << bit)) for i in range(count)])


def add(a, b):
    return (a.astype(F32) + b.astype(F32)).astype(BF)


def sum_over_ctx(keep, send):
    count = lax.axis_size("ctx")
    bits = list(range(1, count.bit_length() - 1))
    total = add(keep, flip(send, 0))
    for step in range(len(bits)):
        pairs = []
        for i in range(count):
            order = bits if i % 2 == 0 else bits[::-1]
            pairs.append((i, i ^ (1 << order[step])))
        total = add(total, move(total, "ctx", pairs))
    return total, flip(total, 0)


def body(hidden_in, projected, w_out, fast_up, fast_down, learn_rates):
    blocks, rows, feats = hidden_in.shape
    ctx = lax.axis_index("ctx")
    head = lax.axis_index("head")
    ctx_count = lax.axis_size("ctx")
    parity = ctx % 2
    inner = ((head == 1) | (head == 2)).astype(jnp.int32)
    scalars = jnp.stack([parity, ctx, head, inner]).astype(jnp.int32)
    step_scale = 1.0 / math.sqrt(rows * ctx_count)

    kv = projected[1:3, :, rows - WIN :, :]
    forward = [(i, i + 1) for i in range(ctx_count - 1)]
    halos = []
    for block in range(blocks):
        if block == 0:
            halos.append(move(kv[:, 0], "ctx", forward))
        else:
            source = jnp.where(ctx == ctx_count - 1, kv[:, block - 1], kv[:, block])
            halos.append(move(source, "ctx", forward + [(ctx_count - 1, 0)]))

    edge_in = [(0, 1), (3, 2)]
    middle = [(1, 2), (2, 1)]
    w_parts = w_out.reshape(4, feats, w_out.shape[1])
    half = feats // 2
    v_send = jnp.stack(
        [
            lax.dynamic_slice(w_parts, (head ^ k, parity * half, 0), (1, half, w_out.shape[1]))[0]
            for k in (1, 2, 3)
        ]
    )
    v_mine = move(v_send, "head", edge_in)
    v_other = flip(v_mine, 0)
    v = jnp.where(
        parity == 0,
        jnp.concatenate([v_mine, v_other], axis=1),
        jnp.concatenate([v_other, v_mine], axis=1),
    )

    up_spec = [
        pl.BlockSpec((None, None, feats, feats), lambda *_: (0, 0, 0, 0)),
        pl.BlockSpec((None, None, feats, feats), lambda *_: (1, 0, 0, 0)),
        pl.BlockSpec((None, feats, feats), lambda *_: (0, 0, 0)),
    ]
    bf_spec = [
        pl.BlockSpec((None, feats, feats), functools.partial(lambda k, *_: (k, 0, 0), k)) for k in range(3)
    ]
    weights, specs = (fast_up, fast_up, fast_down), up_spec
    state = (fast_up, fast_down)
    mine = theirs = None
    c_before = None
    accs, edges = [], []
    for block in range(blocks):
        if block == 0:
            mixed = mixed_first(block, scalars, projected, halos[block], weights, specs)
        else:
            attended = attention_only(block, scalars, projected, halos[block])
            mixed, new, new_bf = update_and_mix(block, scalars, mine, theirs, state, projected, attended)
            weights, specs = (new_bf, new_bf, new_bf), bf_spec
            state = (new, new_bf)
        keep, send = block_grads(block, scalars, projected, learn_rates, weights, step_scale, specs)
        mine, theirs = sum_over_ctx(keep, send)
        if block == 0:
            x = move(mixed, "head", edge_in)
        else:
            x = move(
                jnp.where(inner == 1, c_before, mixed), "head", [(0, 1), (1, 0), (2, 3), (3, 2)]
            )
            edges.append(x)
        ya = move(mixed, "head", middle)
        yb = move(x, "head", middle)
        c_before = edge_part(block, scalars, mixed, ya, yb, v)
        accs.append(own_part(block, scalars, mixed, x, ya, yb, w_out, hidden_in))
    edges.append(move(c_before, "head", [(1, 0), (2, 3)]))
    up_final, down_final = final_update(blocks == 1, scalars, mine, theirs, state)
    is_edge = (inner == 0).astype(F32)
    layer_out = jnp.stack(
        [(acc + is_edge * edge.astype(F32)).astype(BF) for acc, edge in zip(accs, edges)]
    )
    return layer_out, up_final, down_final


def solution(mesh):
    in_specs = (
        P(None, "ctx", "head"),
        P(None, None, "ctx", "head"),
        P(None, "head"),
        P(None, "head", None, None),
        P("head", None, None),
        P("head", None, "ctx"),
    )
    out_specs = (P(None, "ctx", "head"), P(None, "head", None, None), P("head", None, None))
    return jax.shard_map(body, mesh=mesh, in_specs=in_specs, out_specs=out_specs, check_vma=False)
```

time: 298 us -> 172 us (0.58)
  waiting for transfers between devices: 135 us -> 64.7 us
  matrix products: 60.6 us -> 0 us
  Pallas kernels: 0 us -> 45.7 us
  starting transfers between devices: 3.36 us -> 36.8 us
  other arithmetic: 49.2 us -> 16.3 us
  between operations: 22 us -> 0.9 us
  local copies, waits for them, and re-layouts: 26.3 us -> 6.4 us
    psum x2 -> x0, waiting for transfers between devices: 68.3 us -> none  [update_weights(): summed = lax.psum((gradients[0], gradients[1], gradients[2]), 'ctx')]
    all_gather x1 -> x0, waiting for transfers between devices: 62.2 us -> none  [body(): lax.all_gather(mixed, 'head', axis=2, tiled=True)]
    dot_general x19 -> x0, matrix products: 60.6 us -> none  [the longest x1 9.73 us: body(): jnp.einsum('cqhd,ckhd->chqk', query_heads, key_all, preferred_element_typ...]
    ppermute x2 -> x19, waiting for transfers between devices: 4.24 us -> 64.7 us  [move(): return lax.ppermute(x, axis, pairs)]
    pallas_call x0 -> x10, Pallas kernels: none -> 45.7 us  [call(): pl.pallas_call(kernel, out_shape=outs_list, grid_spec=pltpu.PrefetchScala...]
    ppermute x2 -> x19, starting transfers between devices: 3.05 us -> 36.8 us  [move(): return lax.ppermute(x, axis, pairs)]
    sub x1 -> x0, other arithmetic: 19.3 us -> none  [body(): lifted = jnp.exp(scores - row_peak)]
    reduce_sum x5 -> x0, other arithmetic: 14.3 us -> none  [renorm(): jnp.sum(moved_weight * moved_weight) + 1e-06]
  transfers between devices with their start and end apart: 5 -> 19, of which waited for: 4 -> 6; matrix products, arithmetic and copies ran while one was open for 34% -> 10% of each run, Pallas kernels for 0% -> 21%
where the time goes in v1:
time: 172 us; the launch traced here: 171 us
  waiting for transfers between devices  64.7 us (38%)
  Pallas kernels  45.7 us (27%)
  starting transfers between devices  36.8 us (21%)
  other arithmetic  16.3 us (9%)
  local copies, waits for them, and re-layouts  6.4 us (4%)
    ppermute x19, waiting for transfers between devices, move(): return lax.ppermute(x, axis, pairs)  64.7 us
    pallas_call x10, Pallas kernels, call(): pl.pallas_call(kernel, out_shape=outs_list, grid_spec=pltpu.PrefetchScala...  45.7 us
    ppermute x19, starting transfers between devices, move(): return lax.ppermute(x, axis, pairs)  36.8 us
    convert_element_type x6, other arithmetic, add(): return (a.astype(F32) + b.astype(F32)).astype(BF)  8.98 us
    unnamed x18, local copies, waits for them, and re-layouts  4.21 us
  transfers between devices with their start and end apart: 19, of which 6 were waited for; matrix products, arithmetic and copies ran while one was open for 10% of the time, Pallas kernels for 21%

profile of v1, /device:TPU:0, one launch (start us, length us, event | category | flops | bytes accessed | tf_op | source)
XLA Modules:
  0.0 170.7 jit_solution(17514271289979116508)
XLA Ops:
  3.7 4.8 %grads_0.1 = (bf16[3,256,512]{2,1,0:T(8,128)(2,1)S(1)}, bf16[3,256,512]{2,1,0:T(8,128)(2,1)S(1)}) custom-call(s32[4]{0:T(128)S(1)} %pad_add_fusion.sc, bf16[3,2,512,512]{3,2,1,0:T(8,128)(2,1)} %v_ref.7, bf16[3,2,512,512]{3,2,1,0:T(8,128)(2,1)} %v_ref.7, f32[1,2,512]{2,1,0:T(2,128)S(1)} %copy-done.7, bf16[2,1,512,512]{3,2,1,0:T(8,128)(2,1)S(1)} %copy-done.1, ...), custom_call_target="tpu_custom_call" | custom-call | flops 1610612736 | bytes 2097152 | tf_op jit(solution)/shard_map/grads_0/pallas_call | solution.py:49
  9.0 1.9 %collective-permute-done.6 = bf16[3,256,512]{2,1,0:T(8,128)(2,1)S(1)} collective-permute-done((bf16[3,256,512]{2,1,0:T(8,128)(2,1)S(1)}, bf16[3,256,512]{2,1,0:T(8,128)(2,1)S(1)}, u32[]{:S(2)}, u32[]{:S(2)}) %collective-permute-start.6) | collective-permute-done | bytes 786464 | tf_op jit(solution)/shard_map/ppermute | solution.py:381
  11.1 2.9 %collective-permute-start.7 = (bf16[3,256,512]{2,1,0:T(8,128)(2,1)S(1)}, bf16[3,256,512]{2,1,0:T(8,128)(2,1)S(1)}, u32[]{:S(2)}, u32[]{:S(2)}) collective-permute-start(bf16[3,256,512]{2,1,0:T(8,128)(2,1)S(1)} %add_convert_fusion.5), channel_id=1, source_target_pairs={{0,8},{4,20},{8,0},{12,28},{16,24},{20,4},{24,16},{28,12},{1,9},{5... | collective-permute-start | bytes 2359304 | tf_op jit(solution)/shard_map/ppermute | solution.py:381
  14.0 10.0 %collective-permute-done.7 = bf16[3,256,512]{2,1,0:T(8,128)(2,1)S(1)} collective-permute-done((bf16[3,256,512]{2,1,0:T(8,128)(2,1)S(1)}, bf16[3,256,512]{2,1,0:T(8,128)(2,1)S(1)}, u32[]{:S(2)}, u32[]{:S(2)}) %collective-permute-start.7) | collective-permute-done | bytes 786464 | tf_op jit(solution)/shard_map/ppermute | solution.py:381
  25.1 2.0 %collective-permute-start.8 = (bf16[3,256,512]{2,1,0:T(8,128)(2,1)}, bf16[3,256,512]{2,1,0:T(8,128)(2,1)}, u32[]{:S(2)}, u32[]{:S(2)}) collective-permute-start(bf16[3,256,512]{2,1,0:T(8,128)(2,1)} %add_convert_fusion.4), channel_id=1, source_target_pairs={{0,16},{4,12},{8,24},{12,4},{16,0},{20,28},{24,8},{28,20},{1,17},{... | collective-permute-start | bytes 2359304 | tf_op jit(solution)/shard_map/ppermute | solution.py:381
  28.3 20.4 %collective-permute-done.8 = bf16[3,256,512]{2,1,0:T(8,128)(2,1)} collective-permute-done((bf16[3,256,512]{2,1,0:T(8,128)(2,1)}, bf16[3,256,512]{2,1,0:T(8,128)(2,1)}, u32[]{:S(2)}, u32[]{:S(2)}) %collective-permute-start.8) | collective-permute-done | bytes 786464 | tf_op jit(solution)/shard_map/ppermute | solution.py:381
  48.7 2.5 %add_convert_fusion.3.mine_ref = bf16[3,256,512]{2,1,0:T(8,128)(2,1)} fusion(bf16[3,256,512]{2,1,0:T(8,128)(2,1)} %collective-permute-done.8, bf16[3,256,512]{2,1,0:T(8,128)(2,1)} %add_convert_fusion.4), kind=kLoop, calls=%fused_computation.4 | loop fusion | flops 1572864 | bytes 2359296 | tf_op jit(solution)/shard_map/convert_element_type | solution.py:390
  52.2 3.4 %collective-permute-start = (bf16[2,512,512]{2,1,0:T(8,128)(2,1)}, bf16[2,512,512]{2,1,0:T(8,128)(2,1)}, u32[]{:S(2)}, u32[]{:S(2)}) collective-permute-start(bf16[2,512,512]{2,1,0:T(8,128)(2,1)} %slice_bitcast_fusion), channel_id=1, source_target_pairs={{0,4},{4,8},{8,12},{12,16},{16,20},{20,24},{24,28},{1,5},{5,9},{9,... | collective-permute-start | bytes 3145736 | tf_op jit(solution)/shard_map/ppermute | solution.py:381
  56.9 5.0 %collective-permute-start.4 = (bf16[3,256,512]{2,1,0:T(8,128)(2,1)S(1)}, bf16[3,256,512]{2,1,0:T(8,128)(2,1)}, u32[]{:S(2)}, u32[]{:S(2)}) collective-permute-start(bf16[3,256,512]{2,1,0:T(8,128)(2,1)S(1)} %pad_maximum_fusion.1), channel_id=1, source_target_pairs={{0,1},{3,2},{4,5},{7,6},{8,9},{11,10},{12,13},{15,14},{16,17},{19,... | collective-permute-start | bytes 2359304 | tf_op jit(solution)/shard_map/ppermute | solution.py:381
  61.9 5.2 %attend_1.1.att_ref = bf16[512,512]{1,0:T(8,128)(2,1)S(1)} custom-call(s32[4]{0:T(128)S(1)} %pad_add_fusion.sc, bf16[3,2,512,512]{3,2,1,0:T(8,128)(2,1)S(1)} %copy-done, bf16[3,2,512,512]{3,2,1,0:T(8,128)(2,1)S(1)} %copy-done, bf16[3,2,512,512]{3,2,1,0:T(8,128)(2,1)S(1)} %copy-done, bf16[2,512,512]{2,1,0:T(8,128)(2,1)} %collective-permute-done.10.halo_ref), custom_call_target="tpu_custom_call" | custom-call | flops 1073741824 | bytes 3145728 | tf_op jit(solution)/shard_map/attend_1/pallas_call | solution.py:49
  67.2 5.7 %update_1.1 = (bf16[512,512]{1,0:T(8,128)(2,1)}, f32[3,512,512]{2,1,0:T(8,128)}, bf16[3,512,512]{2,1,0:T(8,128)(2,1)S(1)}) custom-call(s32[4]{0:T(128)S(1)} %pad_add_fusion.sc, bf16[3,256,512]{2,1,0:T(8,128)(2,1)} %add_convert_fusion.3.mine_ref, bf16[3,256,512]{2,1,0:T(8,128)(2,1)} %collective-permute-done.9.theirs_ref, ...), custom_call_target="tpu_custom_call" | custom-call | flops 805306368 | bytes 4718592 | tf_op jit(solution)/shard_map/update_1/pallas_call | solution.py:49
  72.9 4.7 %grads_1.1 = (bf16[3,256,512]{2,1,0:T(8,128)(2,1)S(1)}, bf16[3,256,512]{2,1,0:T(8,128)(2,1)S(1)}) custom-call(s32[4]{0:T(128)S(1)} %pad_add_fusion.sc, bf16[3,2,512,512]{3,2,1,0:T(8,128)(2,1)} %v_ref.7, bf16[3,2,512,512]{3,2,1,0:T(8,128)(2,1)} %v_ref.7, f32[1,2,512]{2,1,0:T(2,128)S(1)} %copy-done.8, ...), custom_call_target="tpu_custom_call" | custom-call | flops 1610612736 | bytes 2097152 | tf_op jit(solution)/shard_map/grads_1/pallas_call | solution.py:49
  77.7 7.6 %mixed_0.1.m_ref = bf16[512,512]{1,0:T(8,128)(2,1)} custom-call(s32[4]{0:T(128)S(1)} %pad_add_fusion.sc, bf16[3,2,512,512]{3,2,1,0:T(8,128)(2,1)} %v_ref.7, bf16[3,2,512,512]{3,2,1,0:T(8,128)(2,1)} %v_ref.7, bf16[3,2,512,512]{3,2,1,0:T(8,128)(2,1)} %v_ref.7, bf16[2,512,512]{2,1,0:T(8,128)(2,1)} %collective-permute-done.halo_ref, ...), custom_call_target="tpu_custom_call" | custom-call | flops 1879048192 | bytes 4194304 | tf_op jit(solution)/shard_map/mixed_0/pallas_call | solution.py:49
  85.3 2.1 %collective-permute-start.1 = (bf16[512,512]{1,0:T(8,128)(2,1)}, bf16[512,512]{1,0:T(8,128)(2,1)}, u32[]{:S(2)}, u32[]{:S(2)}) collective-permute-start(bf16[512,512]{1,0:T(8,128)(2,1)} %mixed_0.1.m_ref), channel_id=1, source_target_pairs={{0,1},{3,2},{4,5},{7,6},{8,9},{11,10},{12,13},{15,14},{16,17},{19,... | collective-permute-start | bytes 1572872 | tf_op jit(solution)/shard_map/ppermute | solution.py:381
  87.9 1.5 collective-permute-start.2
  89.3 9.7 %collective-permute-done.1.x_ref = bf16[512,512]{1,0:T(8,128)(2,1)} collective-permute-done((bf16[512,512]{1,0:T(8,128)(2,1)}, bf16[512,512]{1,0:T(8,128)(2,1)}, u32[]{:S(2)}, u32[]{:S(2)}) %collective-permute-start.1) | collective-permute-done | bytes 524320 | tf_op jit(solution)/shard_map/ppermute | solution.py:381
  99.0 1.5 collective-permute-start.3
  102.5 2.4 %maximum_select_fusion.v_ref = bf16[3,512,512]{2,1,0:T(8,128)(2,1)S(1)} fusion(bf16[3,256,512]{2,1,0:T(8,128)(2,1)} %collective-permute-done.5, bf16[3,256,512]{2,1,0:T(8,128)(2,1)} %collective-permute-done.4, pred[]{:T(512)S(6)} %eq.24), kind=kLoop, calls=%fused_computation | loop fusion | flops 7077888 | bytes 3145729 | tf_op jit(solution)/shard_map/jit(_where)/select_n | solution.py:438
  104.9 2.9 %edge_0.1 = bf16[512,512]{1,0:T(8,128)(2,1)S(1)} custom-call(s32[4]{0:T(128)S(1)} %pad_add_fusion.sc, bf16[512,512]{1,0:T(8,128)(2,1)} %mixed_0.1.m_ref, bf16[512,512]{1,0:T(8,128)(2,1)} %collective-permute-done.2.ya_ref, bf16[512,512]{1,0:T(8,128)(2,1)} %collective-permute-done.3.yb_ref, bf16[3,512,512]{2,1,0:T(8,128)(2,1)S(1)} %maximum_select_fusion.v_ref), custom_call_target="tpu_custom_call" | custom-call | flops 805306368 | bytes 3670016 | tf_op jit(solution)/shard_map/edge_0/pallas_call | solution.py:49
  108.9 11.5 %collective-permute-start.11 = (bf16[512,512]{1,0:T(8,128)(2,1)S(1)}, bf16[512,512]{1,0:T(8,128)(2,1)}, u32[]{:S(2)}, u32[]{:S(2)}) collective-permute-start(bf16[512,512]{1,0:T(8,128)(2,1)S(1)} %broadcast_select_fusion), channel_id=1, source_target_pairs={{0,1},{1,0},{2,3},{3,2},{4,5},{5,4},{6,7},{7,6},{8,9},{9,8},{10,11... | collective-permute-start | bytes 1572872 | tf_op jit(solution)/shard_map/ppermute | solution.py:381
  120.4 2.5 %add_convert_fusion.1 = bf16[3,256,512]{2,1,0:T(8,128)(2,1)} fusion(bf16[3,256,512]{2,1,0:T(8,128)(2,1)} %collective-permute-done.16, bf16[3,256,512]{2,1,0:T(8,128)(2,1)} %add_convert_fusion.2), kind=kLoop, calls=%fused_computation.2 | loop fusion | flops 1572864 | bytes 2359296 | tf_op jit(solution)/shard_map/convert_element_type | solution.py:390
  123.5 1.5 collective-permute-start.12
  124.9 6.7 %collective-permute-done.11.x_ref = bf16[512,512]{1,0:T(8,128)(2,1)} collective-permute-done((bf16[512,512]{1,0:T(8,128)(2,1)S(1)}, bf16[512,512]{1,0:T(8,128)(2,1)}, u32[]{:S(2)}, u32[]{:S(2)}) %collective-permute-start.11) | collective-permute-done | bytes 524320 | tf_op jit(solution)/shard_map/ppermute | solution.py:381
  131.7 1.5 collective-permute-start.13
  134.4 3.2 %own_0.1 = f32[512,512]{1,0:T(8,128)S(1)} custom-call(s32[4]{0:T(128)S(1)} %pad_add_fusion.sc, bf16[512,512]{1,0:T(8,128)(2,1)} %mixed_0.1.m_ref, bf16[512,512]{1,0:T(8,128)(2,1)} %collective-permute-done.1.x_ref, bf16[512,512]{1,0:T(8,128)(2,1)} %collective-permute-done.2.ya_ref, bf16[512,512]{1,0:T(8,128)(2,1)} %collective-permute-done.3.yb_ref, ...), custom_call_target="tpu_custom_call" | custom-call | flops 1073741824 | bytes 5242880 | tf_op jit(solution)/shard_map/own_0/pallas_call | solution.py:49
  137.6 2.9 %edge_1.1 = bf16[512,512]{1,0:T(8,128)(2,1)S(1)} custom-call(s32[4]{0:T(128)S(1)} %pad_add_fusion.sc, bf16[512,512]{1,0:T(8,128)(2,1)} %get-tuple-element.14.m_ref, bf16[512,512]{1,0:T(8,128)(2,1)} %collective-permute-done.12.ya_ref, bf16[512,512]{1,0:T(8,128)(2,1)} %collective-permute-done.13.yb_ref, bf16[3,512,512]{2,1,0:T(8,128)(2,1)S(1)} %maximum_select_fusion.v_ref), custom_call_target="tpu_custom_call" | custom-call | flops 805306368 | bytes 3670016 | tf_op jit(solution)/shard_map/edge_1/pallas_call | solution.py:49
  140.5 1.3 collective-permute-start.14
  141.8 1.6 add_convert_fusion.mine_ref
  143.5 1.3 fusion
  144.8 3.2 %own_1.1 = f32[512,512]{1,0:T(8,128)S(1)} custom-call(s32[4]{0:T(128)S(1)} %pad_add_fusion.sc, bf16[512,512]{1,0:T(8,128)(2,1)} %get-tuple-element.14.m_ref, bf16[512,512]{1,0:T(8,128)(2,1)} %collective-permute-done.11.x_ref, bf16[512,512]{1,0:T(8,128)(2,1)} %collective-permute-done.12.ya_ref, bf16[512,512]{1,0:T(8,128)(2,1)} %collective-permute-done.13.yb_ref, ...), custom_call_target="tpu_custom_call" | custom-call | flops 1073741824 | bytes 5242880 | tf_op jit(solution)/shard_map/own_1/pallas_call | solution.py:49
  148.0 15.9 %collective-permute-done.14 = bf16[512,512]{1,0:T(8,128)(2,1)S(1)} collective-permute-done((bf16[512,512]{1,0:T(8,128)(2,1)S(1)}, bf16[512,512]{1,0:T(8,128)(2,1)S(1)}, u32[]{:S(2)}, u32[]{:S(2)}) %collective-permute-start.14) | collective-permute-done | bytes 524320 | tf_op jit(solution)/shard_map/ppermute | solution.py:381
  165.2 5.5 %final_update.1 = (f32[2,1,512,512]{3,2,1,0:T(8,128)}, f32[1,512,512]{2,1,0:T(8,128)}) custom-call(s32[4]{0:T(128)S(1)} %pad_add_fusion.sc, bf16[3,256,512]{2,1,0:T(8,128)(2,1)S(1)} %add_convert_fusion.mine_ref, bf16[3,256,512]{2,1,0:T(8,128)(2,1)S(1)} %collective-permute-done.18.theirs_ref, f32[3,512,512]{2,1,0:T(8,128)} %get-tuple-element.18.up_ref, ...), custom_call_target="tpu_custom_call" | custom-call | flops 2621440 | bytes 4718592 | tf_op jit(solution)/shard_map/final_update/pallas_call | solution.py:49
  (50 shorter events, 15.1 us)
Async XLA Ops:
  0.7 1.2 copy-start.1
  2.0 1.0 copy-start.3
  3.0 0.7 copy-start.7
  8.4 2.4 %collective-permute-start.6 = (bf16[3,256,512]{2,1,0:T(8,128)(2,1)S(1)}, bf16[3,256,512]{2,1,0:T(8,128)(2,1)S(1)}, u32[]{:S(2)}, u32[]{:S(2)}) collective-permute-start(bf16[3,256,512]{2,1,0:T(8,128)(2,1)S(1)} %get-tuple-element.13), channel_id=1, source_target_pairs={{0,4},{4,0},{8,12},{12,8},{16,20},{20,16},{24,28},{28,24},{1,5},{5... | collective-permute-start | bytes 2359304 | tf_op jit(solution)/shard_map/ppermute | solution.py:381
  10.9 16.3 %copy-start = (bf16[3,2,512,512]{3,2,1,0:T(8,128)(2,1)S(1)}, bf16[3,2,512,512]{3,2,1,0:T(8,128)(2,1)}, u32[]{:S(2)}) copy-start(bf16[3,2,512,512]{3,2,1,0:T(8,128)(2,1)} %v_ref.7) | copy-start | bytes 9437188
  11.1 12.9 %collective-permute-start.7 = (bf16[3,256,512]{2,1,0:T(8,128)(2,1)S(1)}, bf16[3,256,512]{2,1,0:T(8,128)(2,1)S(1)}, u32[]{:S(2)}, u32[]{:S(2)}) collective-permute-start(bf16[3,256,512]{2,1,0:T(8,128)(2,1)S(1)} %add_convert_fusion.5), channel_id=1, source_target_pairs={{0,8},{4,20},{8,0},{12,28},{16,24},{20,4},{24,16},{28,12},{1,9},{5... | collective-permute-start | bytes 2359304 | tf_op jit(solution)/shard_map/ppermute | solution.py:381
  25.1 23.6 %collective-permute-start.8 = (bf16[3,256,512]{2,1,0:T(8,128)(2,1)}, bf16[3,256,512]{2,1,0:T(8,128)(2,1)}, u32[]{:S(2)}, u32[]{:S(2)}) collective-permute-start(bf16[3,256,512]{2,1,0:T(8,128)(2,1)} %add_convert_fusion.4), channel_id=1, source_target_pairs={{0,16},{4,12},{8,24},{12,4},{16,0},{20,28},{24,8},{28,20},{1,17},{... | collective-permute-start | bytes 2359304 | tf_op jit(solution)/shard_map/ppermute | solution.py:381
  28.3 33.6 %collective-permute-start.10 = (bf16[2,512,512]{2,1,0:T(8,128)(2,1)}, bf16[2,512,512]{2,1,0:T(8,128)(2,1)}, u32[]{:S(2)}, u32[]{:S(2)}) collective-permute-start(bf16[2,512,512]{2,1,0:T(8,128)(2,1)} %bitcast_select_fusion), channel_id=1, source_target_pairs={{0,4},{4,8},{8,12},{12,16},{16,20},{20,24},{24,28},{28,0},{1,5},{5... | collective-permute-start | bytes 3145736 | tf_op jit(solution)/shard_map/ppermute | solution.py:381
  51.2 16.0 %collective-permute-start.9 = (bf16[3,256,512]{2,1,0:T(8,128)(2,1)}, bf16[3,256,512]{2,1,0:T(8,128)(2,1)}, u32[]{:S(2)}, u32[]{:S(2)}) collective-permute-start(bf16[3,256,512]{2,1,0:T(8,128)(2,1)} %add_convert_fusion.3.mine_ref), channel_id=1, source_target_pairs={{0,4},{4,0},{8,12},{12,8},{16,20},{20,16},{24,28},{28,24},{1,5},{5... | collective-permute-start | bytes 2359304 | tf_op jit(solution)/shard_map/ppermute | solution.py:381
  52.2 25.5 %collective-permute-start = (bf16[2,512,512]{2,1,0:T(8,128)(2,1)}, bf16[2,512,512]{2,1,0:T(8,128)(2,1)}, u32[]{:S(2)}, u32[]{:S(2)}) collective-permute-start(bf16[2,512,512]{2,1,0:T(8,128)(2,1)} %slice_bitcast_fusion), channel_id=1, source_target_pairs={{0,4},{4,8},{8,12},{12,16},{16,20},{20,24},{24,28},{1,5},{5,9},{9,... | collective-permute-start | bytes 3145736 | tf_op jit(solution)/shard_map/ppermute | solution.py:381
  56.8 10.3 %copy-start.2 = (bf16[2,1,512,512]{3,2,1,0:T(8,128)(2,1)S(1)}, bf16[2,1,512,512]{3,2,1,0:T(8,128)(2,1)}, u32[]{:S(2)}) copy-start(bf16[2,1,512,512]{3,2,1,0:T(8,128)(2,1)} %up_ref.1) | copy-start | bytes 3145732
  56.9 10.3 %copy-start.4 = (bf16[1,512,512]{2,1,0:T(8,128)(2,1)S(1)}, bf16[1,512,512]{2,1,0:T(8,128)(2,1)}, u32[]{:S(2)}) copy-start(bf16[1,512,512]{2,1,0:T(8,128)(2,1)} %down_ref.1) | copy-start | bytes 1572868
  56.9 30.5 %collective-permute-start.4 = (bf16[3,256,512]{2,1,0:T(8,128)(2,1)S(1)}, bf16[3,256,512]{2,1,0:T(8,128)(2,1)}, u32[]{:S(2)}, u32[]{:S(2)}) collective-permute-start(bf16[3,256,512]{2,1,0:T(8,128)(2,1)S(1)} %pad_maximum_fusion.1), channel_id=1, source_target_pairs={{0,1},{3,2},{4,5},{7,6},{8,9},{11,10},{12,13},{15,14},{16,17},{19,... | collective-permute-start | bytes 2359304 | tf_op jit(solution)/shard_map/ppermute | solution.py:381
  67.1 5.8 %copy-start.8 = (f32[1,2,512]{2,1,0:T(2,128)S(1)}, f32[1,2,512]{2,1,0:T(2,128)}, u32[]{:S(2)}) copy-start(f32[1,2,512]{2,1,0:T(2,128)} %lr_ref.3) | copy-start | bytes 12292
  77.6 22.8 %collective-permute-start.15 = (bf16[3,256,512]{2,1,0:T(8,128)(2,1)S(1)}, bf16[3,256,512]{2,1,0:T(8,128)(2,1)S(1)}, u32[]{:S(2)}, u32[]{:S(2)}) collective-permute-start(bf16[3,256,512]{2,1,0:T(8,128)(2,1)S(1)} %get-tuple-element.17), channel_id=1, source_target_pairs={{0,4},{4,0},{8,12},{12,8},{16,20},{20,16},{24,28},{28,24},{1,5},{5... | collective-permute-start | bytes 2359304 | tf_op jit(solution)/shard_map/ppermute | solution.py:381
  85.3 13.7 %collective-permute-start.1 = (bf16[512,512]{1,0:T(8,128)(2,1)}, bf16[512,512]{1,0:T(8,128)(2,1)}, u32[]{:S(2)}, u32[]{:S(2)}) collective-permute-start(bf16[512,512]{1,0:T(8,128)(2,1)} %mixed_0.1.m_ref), channel_id=1, source_target_pairs={{0,1},{3,2},{4,5},{7,6},{8,9},{11,10},{12,13},{15,14},{16,17},{19,... | collective-permute-start | bytes 1572872 | tf_op jit(solution)/shard_map/ppermute | solution.py:381
  87.4 15.1 %collective-permute-start.5 = (bf16[3,256,512]{2,1,0:T(8,128)(2,1)}, bf16[3,256,512]{2,1,0:T(8,128)(2,1)}, u32[]{:S(2)}, u32[]{:S(2)}) collective-permute-start(bf16[3,256,512]{2,1,0:T(8,128)(2,1)} %collective-permute-done.4), channel_id=1, source_target_pairs={{0,4},{4,0},{8,12},{12,8},{16,20},{20,16},{24,28},{28,24},{1,5},{5... | collective-permute-start | bytes 2359304 | tf_op jit(solution)/shard_map/ppermute | solution.py:381
  87.9 17.0 %collective-permute-start.2 = (bf16[512,512]{1,0:T(8,128)(2,1)}, bf16[512,512]{1,0:T(8,128)(2,1)}, u32[]{:S(2)}, u32[]{:S(2)}) collective-permute-start(bf16[512,512]{1,0:T(8,128)(2,1)} %mixed_0.1.m_ref), channel_id=1, source_target_pairs={{1,2},{2,1},{5,6},{6,5},{9,10},{10,9},{13,14},{14,13},{17,18},{18,... | collective-permute-start | bytes 1572872 | tf_op jit(solution)/shard_map/ppermute | solution.py:381
  99.0 5.9 %collective-permute-start.3 = (bf16[512,512]{1,0:T(8,128)(2,1)}, bf16[512,512]{1,0:T(8,128)(2,1)}, u32[]{:S(2)}, u32[]{:S(2)}) collective-permute-start(bf16[512,512]{1,0:T(8,128)(2,1)} %collective-permute-done.1.x_ref), channel_id=1, source_target_pairs={{1,2},{2,1},{5,6},{6,5},{9,10},{10,9},{13,14},{14,13},{17,18},{18,... | collective-permute-start | bytes 1572872 | tf_op jit(solution)/shard_map/ppermute | solution.py:381
  101.6 18.8 %collective-permute-start.16 = (bf16[3,256,512]{2,1,0:T(8,128)(2,1)}, bf16[3,256,512]{2,1,0:T(8,128)(2,1)}, u32[]{:S(2)}, u32[]{:S(2)}) collective-permute-start(bf16[3,256,512]{2,1,0:T(8,128)(2,1)} %add_convert_fusion.2), channel_id=1, source_target_pairs={{0,8},{4,20},{8,0},{12,28},{16,24},{20,4},{24,16},{28,12},{1,9},{5... | collective-permute-start | bytes 2359304 | tf_op jit(solution)/shard_map/ppermute | solution.py:381
  108.9 22.8 %collective-permute-start.11 = (bf16[512,512]{1,0:T(8,128)(2,1)S(1)}, bf16[512,512]{1,0:T(8,128)(2,1)}, u32[]{:S(2)}, u32[]{:S(2)}) collective-permute-start(bf16[512,512]{1,0:T(8,128)(2,1)S(1)} %broadcast_select_fusion), channel_id=1, source_target_pairs={{0,1},{1,0},{2,3},{3,2},{4,5},{5,4},{6,7},{7,6},{8,9},{9,8},{10,11... | collective-permute-start | bytes 1572872 | tf_op jit(solution)/shard_map/ppermute | solution.py:381
  122.9 18.9 %collective-permute-start.17 = (bf16[3,256,512]{2,1,0:T(8,128)(2,1)}, bf16[3,256,512]{2,1,0:T(8,128)(2,1)}, u32[]{:S(2)}, u32[]{:S(2)}) collective-permute-start(bf16[3,256,512]{2,1,0:T(8,128)(2,1)} %add_convert_fusion.1), channel_id=1, source_target_pairs={{0,16},{4,12},{8,24},{12,4},{16,0},{20,28},{24,8},{28,20},{1,17},{... | collective-permute-start | bytes 2359304 | tf_op jit(solution)/shard_map/ppermute | solution.py:381
  123.5 14.1 %collective-permute-start.12 = (bf16[512,512]{1,0:T(8,128)(2,1)}, bf16[512,512]{1,0:T(8,128)(2,1)}, u32[]{:S(2)}, u32[]{:S(2)}) collective-permute-start(bf16[512,512]{1,0:T(8,128)(2,1)} %get-tuple-element.14.m_ref), channel_id=1, source_target_pairs={{1,2},{2,1},{5,6},{6,5},{9,10},{10,9},{13,14},{14,13},{17,18},{18,... | collective-permute-start | bytes 1572872 | tf_op jit(solution)/shard_map/ppermute | solution.py:381
  131.7 5.9 %collective-permute-start.13 = (bf16[512,512]{1,0:T(8,128)(2,1)}, bf16[512,512]{1,0:T(8,128)(2,1)}, u32[]{:S(2)}, u32[]{:S(2)}) collective-permute-start(bf16[512,512]{1,0:T(8,128)(2,1)} %collective-permute-done.11.x_ref), channel_id=1, source_target_pairs={{1,2},{2,1},{5,6},{6,5},{9,10},{10,9},{13,14},{14,13},{17,18},{18,... | collective-permute-start | bytes 1572872 | tf_op jit(solution)/shard_map/ppermute | solution.py:381
  133.1 1.2 copy-start.5
  140.5 23.5 %collective-permute-start.14 = (bf16[512,512]{1,0:T(8,128)(2,1)S(1)}, bf16[512,512]{1,0:T(8,128)(2,1)S(1)}, u32[]{:S(2)}, u32[]{:S(2)}) collective-permute-start(bf16[512,512]{1,0:T(8,128)(2,1)S(1)} %edge_1.1), channel_id=1, source_target_pairs={{1,0},{2,3},{5,4},{6,7},{9,8},{10,11},{13,12},{14,15},{17,16},{18,... | collective-permute-start | bytes 1572872 | tf_op jit(solution)/shard_map/ppermute | solution.py:381
  143.4 1.4 copy-start.6
  143.4 21.8 %collective-permute-start.18 = (bf16[3,256,512]{2,1,0:T(8,128)(2,1)S(1)}, bf16[3,256,512]{2,1,0:T(8,128)(2,1)S(1)}, u32[]{:S(2)}, u32[]{:S(2)}) collective-permute-start(bf16[3,256,512]{2,1,0:T(8,128)(2,1)S(1)} %add_convert_fusion.mine_ref), channel_id=1, source_target_pairs={{0,4},{4,0},{8,12},{12,8},{16,20},{20,16},{24,28},{28,24},{1,5},{5... | collective-permute-start | bytes 2359304 | tf_op jit(solution)/shard_map/ppermute | solution.py:381

commit v2 on v1

--- a/solution.py
+++ b/solution.py
@@ -43,24 +43,34 @@
     return pl.BlockSpec(shape, lambda *_: zeros)
 
 
-def call(kernel, name, scalars, inputs, specs, outs, scratch=(), grid=(1,), flops=0, nbytes=0):
+def call(kernel, name, scalars, inputs, specs, outs, earlier=(), scratch=(), grid=(1,), out_specs=None, aliases=None):
     single = not isinstance(outs, (list, tuple))
     outs_list = [outs] if single else list(outs)
+    first = 1 + len(inputs)
+
+    def ordered(*refs):
+        kernel(*refs[:first], *refs[first + len(earlier) :])
+
     got = pl.pallas_call(
-        kernel,
+        ordered,
         out_shape=outs_list,
         grid_spec=pltpu.PrefetchScalarGridSpec(
             num_scalar_prefetch=1,
             grid=grid,
-            in_specs=specs,
-            out_specs=[whole_out(o.shape) for o in outs_list],
+            in_specs=[*specs, *[pl.BlockSpec(memory_space=pl.ANY) for _ in earlier]],
+            out_specs=out_specs or [whole_out(o.shape) for o in outs_list],
             scratch_shapes=list(scratch),
         ),
+        input_output_aliases={k + 1: v for k, v in (aliases or {}).items()},
         compiler_params=pltpu.CompilerParams(vmem_limit_bytes=LIMIT),
-        cost_estimate=pl.CostEstimate(flops=flops, bytes_accessed=nbytes, transcendentals=0),
+        cost_estimate=pl.CostEstimate(flops=20 * 10**9, bytes_accessed=1, transcendentals=0),
         name=name,
-    )(scalars, *inputs)
+    )(scalars, *inputs, *earlier)
     return got[0] if single else got
+
+
+def like(array, dtype=None):
+    return jax.ShapeDtypeStruct(array.shape, dtype or array.dtype)
 
 
 def grads_kernel(block, step_scale, sc, k_ref, v_ref, lr_ref, w1_ref, w3_ref, w2_ref, keep_ref, send_ref, acc):
@@ -99,7 +109,7 @@
         send_ref[...] = acc[:, pl.ds(other, half), :].astype(BF)
 
 
-def block_grads(block, scalars, projected, learn_rates, weights, step_scale, weight_specs):
+def block_grads(block, scalars, projected, learn_rates, weights, step_scale, weight_specs, earlier=()):
     _, _, rows, feats = projected.shape
     half = feats // 2
     shape = jax.ShapeDtypeStruct((3, half, feats), BF)
@@ -118,8 +128,7 @@
         [shape, shape],
         scratch=[pltpu.VMEM((3, feats, feats), F32)],
         grid=(rows // tile,),
-        flops=12 * rows * feats * feats,
-        nbytes=4 * feats * feats * 2,
+        earlier=earlier,
     )
 
 
@@ -206,7 +215,7 @@
     ]
 
 
-def attention_only(block, scalars, projected, halo):
+def attention_only(block, scalars, projected, halo, earlier=()):
     _, _, rows, feats = projected.shape
     return call(
         functools.partial(attend_kernel, block),
@@ -215,12 +224,11 @@
         (projected, projected, projected, halo),
         [*qkv_specs(block, projected), whole(halo)],
         jax.ShapeDtypeStruct((rows, feats), BF),
-        flops=8 * rows * WIN * feats,
-        nbytes=6 * rows * feats * 2,
-    )
-
-
-def mixed_first(block, scalars, projected, halo, weights, weight_specs):
+        earlier=earlier,
+    )
+
+
+def mixed_first(block, scalars, projected, halo, weights, weight_specs, earlier=()):
     _, _, rows, feats = projected.shape
     return call(
         functools.partial(mixed_kernel, block),
@@ -230,8 +238,7 @@
         [*qkv_specs(block, projected), whole(halo), *weight_specs],
         jax.ShapeDtypeStruct((rows, feats), BF),
         scratch=[pltpu.VMEM((rows, feats), BF)],
-        flops=8 * rows * WIN * feats + 6 * rows * feats * feats,
-        nbytes=8 * rows * feats * 2,
+        earlier=earlier,
     )
 
 
@@ -267,7 +274,7 @@
         mix_ref[at, :] = (att_ref[at, :].astype(F32) + fast).astype(BF)
 
 
-def update_and_mix(block, scalars, mine, theirs, state, projected, attended):
+def update_and_mix(block, scalars, mine, theirs, state, projected, attended, earlier=()):
     _, _, rows, feats = projected.shape
     first = block == 1
     return call(
@@ -288,8 +295,7 @@
             jax.ShapeDtypeStruct((3, feats, feats), F32),
             jax.ShapeDtypeStruct((3, feats, feats), BF),
         ],
-        flops=6 * rows * feats * feats,
-        nbytes=9 * feats * feats * 2,
+        earlier=earlier,
     )
 
 
@@ -304,7 +310,7 @@
     down_out[0] = moved[2]
 
 
-def final_update(first, scalars, mine, theirs, state):
+def final_update(first, scalars, mine, theirs, state, earlier=()):
     feats = mine.shape[2]
     return call(
         functools.partial(final_kernel, first),
@@ -314,8 +320,100 @@
         [whole(mine), whole(theirs), whole(state[0]), whole(state[1])],
         [jax.ShapeDtypeStruct((2, 1, feats, feats), F32), jax.ShapeDtypeStruct((1, feats, feats), F32)],
         scratch=[pltpu.VMEM((3, feats, feats), F32)],
-        flops=10 * feats * feats,
-        nbytes=9 * feats * feats * 2,
+        earlier=earlier,
+    )
+
+
+def pick_kernel(sc, w_ref, out_ref):
+    half = out_ref.shape[1]
+    feats = 2 * half
+    for i in range(3):
+        start = (sc[2] ^ (i + 1)) * feats + sc[0] * half
+        out_ref[i] = w_ref[pl.ds(pl.multiple_of(start, half), half), :]
+
+
+def pick_parts(scalars, w_out, earlier=()):
+    feats = w_out.shape[1]
+    return call(
+        pick_kernel,
+        "pick_parts",
+        scalars,
+        (w_out,),
+        [whole(w_out)],
+        jax.ShapeDtypeStruct((3, feats // 2, feats), BF),
+        earlier=earlier,
+    )
+
+
+def join_kernel(sc, mine_ref, theirs_ref, x_ref, out_ref, x_out_ref):
+    half = mine_ref.shape[1]
+    out_ref[:, pl.ds(pl.multiple_of(sc[0] * half, half), half), :] = mine_ref[...]
+    out_ref[:, pl.ds(pl.multiple_of((1 - sc[0]) * half, half), half), :] = theirs_ref[...]
+
+
+def join_halves(scalars, mine, theirs, x, earlier=()):
+    count, half, feats = mine.shape
+    return call(
+        join_kernel,
+        "join_halves",
+        scalars,
+        (mine, theirs, x),
+        [whole(mine), whole(theirs), pl.BlockSpec(memory_space=pl.ANY)],
+        [jax.ShapeDtypeStruct((count, 2 * half, feats), BF), like(x)],
+        out_specs=[whole_out((count, 2 * half, feats)), pl.BlockSpec(memory_space=pl.ANY)],
+        aliases={2: 1},
+        earlier=earlier,
+    )
+
+
+def gate_kernel(sc, x_ref, x_out_ref):
+    pass
+
+
+def gate(scalars, x, earlier):
+    return call(
+        gate_kernel,
+        "gate",
+        scalars,
+        (x,),
+        [pl.BlockSpec(memory_space=pl.ANY)],
+        like(x),
+        out_specs=[pl.BlockSpec(memory_space=pl.ANY)],
+        aliases={0: 0},
+        earlier=earlier,
+    )
+
+
+def add_kernel(sc, a_ref, b_ref, out_ref):
+    out_ref[...] = (a_ref[...].astype(F32) + b_ref[...].astype(F32)).astype(BF)
+
+
+def add(scalars, a, b, earlier=()):
+    return call(add_kernel, "add", scalars, (a, b), [whole(a), whole(b)], like(a, BF), earlier=earlier)
+
+
+def pack_kernel(sc, k_ref, v_ref, out_ref):
+    out_ref[0] = k_ref[...]
+    out_ref[1] = v_ref[...]
+
+
+def pack_halo(block, scalars, projected, last, earlier=()):
+    _, _, rows, feats = projected.shape
+
+    def which(s):
+        return block if block == 0 else jnp.where(s[1] == last, block - 1, block)
+
+    return call(
+        pack_kernel,
+        f"pack_{block}",
+        scalars,
+        (projected, projected),
+        [
+            pl.BlockSpec((None, None, WIN, feats), lambda i, s: (1, which(s), rows // WIN - 1, 0)),
+            pl.BlockSpec((None, None, WIN, feats), lambda i, s: (2, which(s), rows // WIN - 1, 0)),
+        ],
+        jax.ShapeDtypeStruct((2, WIN, feats), BF),
+        earlier=earlier,
     )
 
 
@@ -323,7 +421,7 @@
     out_ref[...] = (mm(m_ref[...], v_ref[0]) + mm(ya_ref[...], v_ref[1]) + mm(yb_ref[...], v_ref[2])).astype(BF)
 
 
-def edge_part(block, scalars, m, ya, yb, v):
+def edge_part(block, scalars, m, ya, yb, v, earlier=()):
     rows, feats = m.shape
     return call(
         edge_kernel,
@@ -332,8 +430,7 @@
         (m, ya, yb, v),
         [whole(m), whole(ya), whole(yb), whole(v)],
         jax.ShapeDtypeStruct((rows, feats), BF),
-        flops=6 * rows * feats * feats,
-        nbytes=7 * rows * feats * 2,
+        earlier=earlier,
     )
 
 
@@ -356,7 +453,7 @@
         )
 
 
-def own_part(block, scalars, m, x, ya, yb, w_out, hidden_in):
+def own_part(block, scalars, m, x, ya, yb, w_out, hidden_in, earlier=()):
     rows, feats = m.shape
     return call(
         own_kernel,
@@ -372,8 +469,26 @@
             pl.BlockSpec((None, rows, feats), lambda i, s: (block, 0, 0)),
         ],
         jax.ShapeDtypeStruct((rows, feats), F32),
-        flops=8 * rows * feats * feats,
-        nbytes=10 * rows * feats * 2,
+        earlier=earlier,
+    )
+
+
+def finish_kernel(sc, acc_ref, c_ref, *refs):
+    refs[-1][...] = (acc_ref[...] + c_ref[...].astype(F32)).astype(BF)
+
+
+def finish(block, blocks, scalars, acc, c, so_far, earlier=()):
+    rows, feats = acc.shape
+    return call(
+        finish_kernel,
+        f"finish_{block}",
+        scalars,
+        (acc, c, *so_far),
+        [whole(acc), whole(c), *[pl.BlockSpec(memory_space=pl.ANY) for _ in so_far]],
+        jax.ShapeDtypeStruct((blocks, rows, feats), BF),
+        out_specs=[pl.BlockSpec((None, rows, feats), lambda i, s: (block, 0, 0))],
+        aliases={2: 0} if so_far else None,
+        earlier=earlier,
     )
 
 
@@ -386,21 +501,9 @@
     return move(x, "ctx", [(i, i ^ (1 << bit)) for i in range(count)])
 
 
-def add(a, b):
-    return (a.astype(F32) + b.astype(F32)).astype(BF)
-
-
-def sum_over_ctx(keep, send):
-    count = lax.axis_size("ctx")
+def partners(count, step):
     bits = list(range(1, count.bit_length() - 1))
-    total = add(keep, flip(send, 0))
-    for step in range(len(bits)):
-        pairs = []
-        for i in range(count):
-            order = bits if i % 2 == 0 else bits[::-1]
-            pairs.append((i, i ^ (1 << order[step])))
-        total = add(total, move(total, "ctx", pairs))
-    return total, flip(total, 0)
+    return [(i, i ^ (1 << (bits if i % 2 == 0 else bits[::-1])[step])) for i in range(count)]
 
 
 def body(hidden_in, projected, w_out, fast_up, fast_down, learn_rates):
@@ -408,39 +511,15 @@
     ctx = lax.axis_index("ctx")
     head = lax.axis_index("head")
     ctx_count = lax.axis_size("ctx")
+    steps = ctx_count.bit_length() - 2
     parity = ctx % 2
     inner = ((head == 1) | (head == 2)).astype(jnp.int32)
     scalars = jnp.stack([parity, ctx, head, inner]).astype(jnp.int32)
     step_scale = 1.0 / math.sqrt(rows * ctx_count)
-
-    kv = projected[1:3, :, rows - WIN :, :]
     forward = [(i, i + 1) for i in range(ctx_count - 1)]
-    halos = []
-    for block in range(blocks):
-        if block == 0:
-            halos.append(move(kv[:, 0], "ctx", forward))
-        else:
-            source = jnp.where(ctx == ctx_count - 1, kv[:, block - 1], kv[:, block])
-            halos.append(move(source, "ctx", forward + [(ctx_count - 1, 0)]))
-
+    around = forward + [(ctx_count - 1, 0)]
     edge_in = [(0, 1), (3, 2)]
     middle = [(1, 2), (2, 1)]
-    w_parts = w_out.reshape(4, feats, w_out.shape[1])
-    half = feats // 2
-    v_send = jnp.stack(
-        [
-            lax.dynamic_slice(w_parts, (head ^ k, parity * half, 0), (1, half, w_out.shape[1]))[0]
-            for k in (1, 2, 3)
-        ]
-    )
-    v_mine = move(v_send, "head", edge_in)
-    v_other = flip(v_mine, 0)
-    v = jnp.where(
-        parity == 0,
-        jnp.concatenate([v_mine, v_other], axis=1),
-        jnp.concatenate([v_other, v_mine], axis=1),
-    )
-
     up_spec = [
         pl.BlockSpec((None, None, feats, feats), lambda *_: (0, 0, 0, 0)),
         pl.BlockSpec((None, None, feats, feats), lambda *_: (1, 0, 0, 0)),
@@ -449,38 +528,72 @@
     bf_spec = [
         pl.BlockSpec((None, feats, feats), functools.partial(lambda k, *_: (k, 0, 0), k)) for k in range(3)
     ]
+
     weights, specs = (fast_up, fast_up, fast_down), up_spec
     state = (fast_up, fast_down)
-    mine = theirs = None
-    c_before = None
-    accs, edges = [], []
-    for block in range(blocks):
-        if block == 0:
-            mixed = mixed_first(block, scalars, projected, halos[block], weights, specs)
+    edge_out = [(1, 0), (2, 3)]
+
+    kv_now = pack_halo(0, scalars, projected, ctx_count - 1)
+    halo = move(kv_now, "ctx", forward)
+    keep, send = block_grads(0, scalars, projected, learn_rates, weights, step_scale, specs, earlier=(kv_now,))
+    v_send = pick_parts(scalars, w_out, earlier=(send,))
+    total = add(scalars, keep, flip(send, 0), earlier=(v_send,))
+    received = move(total, "ctx", partners(ctx_count, 0))
+    v_send = gate(scalars, v_send, earlier=(total,))
+    v_mine = move(v_send, "head", edge_in)
+    v_other = flip(v_mine, 0)
+    mixed = mixed_first(0, scalars, projected, halo, weights, specs, earlier=(v_send,))
+    x = move(mixed, "head", edge_in)
+    ya = move(mixed, "head", middle)
+    last = mixed
+    so_far = ()
+    for block in range(1, blocks):
+        for step in range(steps):
+            total = last = add(scalars, total, received, earlier=(last,))
+            if step + 1 < steps:
+                received = move(total, "ctx", partners(ctx_count, step + 1))
+            if step == 0:
+                kv_now = last = pack_halo(block, scalars, projected, ctx_count - 1, earlier=(last,))
+                halo = move(kv_now, "ctx", around)
+        theirs = flip(total, 0)
+        if block == 1:
+            v, x = join_halves(scalars, v_mine, v_other, x, earlier=(last, ya))
+            last = v
         else:
-            attended = attention_only(block, scalars, projected, halos[block])
-            mixed, new, new_bf = update_and_mix(block, scalars, mine, theirs, state, projected, attended)
-            weights, specs = (new_bf, new_bf, new_bf), bf_spec
-            state = (new, new_bf)
-        keep, send = block_grads(block, scalars, projected, learn_rates, weights, step_scale, specs)
-        mine, theirs = sum_over_ctx(keep, send)
-        if block == 0:
-            x = move(mixed, "head", edge_in)
-        else:
-            x = move(
-                jnp.where(inner == 1, c_before, mixed), "head", [(0, 1), (1, 0), (2, 3), (3, 2)]
-            )
-            edges.append(x)
-        ya = move(mixed, "head", middle)
+            x = last = gate(scalars, x, earlier=(last, ya))
         yb = move(x, "head", middle)
-        c_before = edge_part(block, scalars, mixed, ya, yb, v)
-        accs.append(own_part(block, scalars, mixed, x, ya, yb, w_out, hidden_in))
-    edges.append(move(c_before, "head", [(1, 0), (2, 3)]))
-    up_final, down_final = final_update(blocks == 1, scalars, mine, theirs, state)
-    is_edge = (inner == 0).astype(F32)
-    layer_out = jnp.stack(
-        [(acc + is_edge * edge.astype(F32)).astype(BF) for acc, edge in zip(accs, edges)]
-    )
+        attended = attention_only(block, scalars, projected, halo, earlier=(last,))
+        mixed_next, new, new_bf = update_and_mix(block, scalars, total, theirs, state, projected, attended)
+        weights, specs = (new_bf, new_bf, new_bf), bf_spec
+        state = (new, new_bf)
+        x_next = move(mixed_next, "head", edge_in)
+        ya_next = move(mixed_next, "head", middle)
+        keep, send = block_grads(
+            block, scalars, projected, learn_rates, weights, step_scale, specs, earlier=(mixed_next,)
+        )
+        c = edge_part(block - 1, scalars, mixed, ya, yb, v, earlier=(send,))
+        c_there = move(c, "head", edge_out)
+        total = add(scalars, keep, flip(send, 0), earlier=(c,))
+        received = move(total, "ctx", partners(ctx_count, 0))
+        acc = last = own_part(block - 1, scalars, mixed, x, ya, yb, w_out, hidden_in, earlier=(total,))
+        if block < blocks - 1:
+            so_far = (finish(block - 1, blocks, scalars, acc, c_there, so_far),)
+            last = so_far[0]
+        mixed, x, ya = mixed_next, x_next, ya_next
+    x = last = gate(scalars, x, earlier=(last, ya))
+    yb = move(x, "head", middle)
+    for step in range(steps):
+        total = last = add(scalars, total, received, earlier=(last,))
+        if step + 1 < steps:
+            received = move(total, "ctx", partners(ctx_count, step + 1))
+        if step == 0:
+            c = last = edge_part(blocks - 1, scalars, mixed, ya, yb, v, earlier=(last,))
+            c_last = move(c, "head", edge_out)
+    theirs = flip(total, 0)
+    acc_last = own_part(blocks - 1, scalars, mixed, x, ya, yb, w_out, hidden_in, earlier=(last,))
+    up_final, down_final = final_update(blocks == 1, scalars, total, theirs, state, earlier=(acc_last,))
+    out = finish(blocks - 2, blocks, scalars, acc, c_there, so_far, earlier=(up_final,))
+    layer_out = finish(blocks - 1, blocks, scalars, acc_last, c_last, (out,))
     return layer_out, up_final, down_final
 
 

time: 172 us -> 130 us (0.76)
  waiting for transfers between devices: 64.7 us -> 38.7 us
  other arithmetic: 16.3 us -> 0.08 us
  Pallas kernels: 45.7 us -> 52.5 us
  starting transfers between devices: 36.8 us -> 31.9 us
  local copies, waits for them, and re-layouts: 6.4 us -> 3.94 us
    ppermute x19 -> x20, waiting for transfers between devices: 64.7 us -> 38.7 us  [move(): return lax.ppermute(x, axis, pairs)]
    convert_element_type x6 -> x0, other arithmetic: 8.98 us -> none  [add(): return (a.astype(F32) + b.astype(F32)).astype(BF)]
    pallas_call x10 -> x24, Pallas kernels: 45.7 us -> 52.5 us  [call(): pl.pallas_call(ordered, out_shape=outs_list, grid_spec=pltpu.PrefetchScal...]
    ppermute x19 -> x20, starting transfers between devices: 36.8 us -> 31.9 us  [move(): return lax.ppermute(x, axis, pairs)]
    select_n x3 -> x0, other arithmetic: 4.57 us -> none  [the longest x1 2.38 us: body(): jnp.where(parity == 0, jnp.concatenate([v_mine, v_other], axis=1), jnp.co...]
    another operation x4 -> x0, other arithmetic: 2.64 us -> none  [the longest x3 2.55 us: body(): jnp.stack([(acc + is_edge * edge.astype(F32)).astype(BF) for acc, edge in...]
    unnamed x18 -> x22, local copies, waits for them, and re-layouts: 4.21 us -> 3.94 us
  transfers between devices with their start and end apart: 19 -> 20, of which waited for: 6 -> 7; matrix products, arithmetic and copies ran while one was open for 10% -> 0% of each run, Pallas kernels for 21% -> 39%
where the time goes in v2:
time: 130 us; the launch traced here: 128 us
  Pallas kernels  52.5 us (40%)
  waiting for transfers between devices  38.7 us (30%)
  starting transfers between devices  31.9 us (25%)
  local copies, waits for them, and re-layouts  3.94 us (3%)
    pallas_call x24, Pallas kernels, call(): pl.pallas_call(ordered, out_shape=outs_list, grid_spec=pltpu.PrefetchScal...  52.5 us
    ppermute x20, waiting for transfers between devices, move(): return lax.ppermute(x, axis, pairs)  38.7 us
    ppermute x20, starting transfers between devices, move(): return lax.ppermute(x, axis, pairs)  31.9 us
    unnamed x22, local copies, waits for them, and re-layouts  3.94 us
  transfers between devices with their start and end apart: 20, of which 7 were waited for; matrix products, arithmetic and copies ran while one was open for 0% of the time, Pallas kernels for 39%

profile of v2, /device:TPU:0, one launch (start us, length us, event | category | flops | bytes accessed | tf_op | source)
XLA Modules:
  0.0 128.2 jit_solution(13871546915807750283)
XLA Ops:
  0.7 1.9 %copy-done = bf16[3,2,512,512]{3,2,1,0:T(8,128)(2,1)S(1)} copy-done((bf16[3,2,512,512]{3,2,1,0:T(8,128)(2,1)S(1)}, bf16[3,2,512,512]{3,2,1,0:T(8,128)(2,1)}, u32[]{:S(2)}) %copy-start) | copy-done | bytes 3145752
  3.2 2.6 %collective-permute-start.2 = (bf16[2,512,512]{2,1,0:T(8,128)(2,1)S(1)}, bf16[2,512,512]{2,1,0:T(8,128)(2,1)S(1)}, u32[]{:S(2)}, u32[]{:S(2)}) collective-permute-start(bf16[2,512,512]{2,1,0:T(8,128)(2,1)S(1)} %pack_0.1.refs_7_), channel_id=1, source_target_pairs={{0,4},{4,8},{8,12},{12,16},{16,20},{20,24},{24,28},{1,5},{5,9},{9,... | collective-permute-start | bytes 3145736 | tf_op jit(solution)/shard_map/ppermute | solution.py:496
  5.8 4.7 %grads_0.1 = (bf16[3,256,512]{2,1,0:T(8,128)(2,1)S(1)}, bf16[3,256,512]{2,1,0:T(8,128)(2,1)S(1)}) custom-call(s32[4]{0:T(128)S(1)} %pad_add_fusion.refs_0_, bf16[3,2,512,512]{3,2,1,0:T(8,128)(2,1)} %refs_2_.11, bf16[3,2,512,512]{3,2,1,0:T(8,128)(2,1)} %refs_2_.11, f32[1,2,512]{2,1,0:T(2,128)S(1)} %copy-done.6, bf16[2,1,512,512]{3,2,1,0:T(8,128)(2,1)S(1)} %copy-done.3, ...), custom_call_target="tpu_custom_call" | custom-call | flops 20000000000 | bytes 1 | tf_op jit(solution)/shard_map/grads_0/pallas_call | solution.py:54
  10.6 2.6 %collective-permute-start = (bf16[3,256,512]{2,1,0:T(8,128)(2,1)S(1)}, bf16[3,256,512]{2,1,0:T(8,128)(2,1)S(1)}, u32[]{:S(2)}, u32[]{:S(2)}) collective-permute-start(bf16[3,256,512]{2,1,0:T(8,128)(2,1)S(1)} %get-tuple-element.15.refs_2_), channel_id=1, source_target_pairs={{0,4},{4,0},{8,12},{12,8},{16,20},{20,16},{24,28},{28,24},{1,5},{5... | collective-permute-start | bytes 2359304 | tf_op jit(solution)/shard_map/ppermute | solution.py:496
  13.8 1.3 %collective-permute-done.refs_2_ = bf16[3,256,512]{2,1,0:T(8,128)(2,1)S(1)} collective-permute-done((bf16[3,256,512]{2,1,0:T(8,128)(2,1)S(1)}, bf16[3,256,512]{2,1,0:T(8,128)(2,1)S(1)}, u32[]{:S(2)}, u32[]{:S(2)}) %collective-permute-start) | collective-permute-done | bytes 786464 | tf_op jit(solution)/shard_map/ppermute | solution.py:496
  15.8 1.6 %collective-permute-start.1 = (bf16[3,256,512]{2,1,0:T(8,128)(2,1)S(1)}, bf16[3,256,512]{2,1,0:T(8,128)(2,1)S(1)}, u32[]{:S(2)}, u32[]{:S(2)}) collective-permute-start(bf16[3,256,512]{2,1,0:T(8,128)(2,1)S(1)} %add.17.refs_2_.refs_1_), channel_id=1, source_target_pairs={{0,8},{4,20},{8,0},{12,28},{16,24},{20,4},{24,16},{28,12},{1,9},{5... | collective-permute-start | bytes 2359304 | tf_op jit(solution)/shard_map/ppermute | solution.py:496
  17.9 3.5 %collective-permute-start.6 = (bf16[3,256,512]{2,1,0:T(8,128)(2,1)S(1)}, bf16[3,256,512]{2,1,0:T(8,128)(2,1)S(1)}, u32[]{:S(2)}, u32[]{:S(2)}) collective-permute-start(bf16[3,256,512]{2,1,0:T(8,128)(2,1)S(1)} %gate.2.refs_8_), channel_id=1, source_target_pairs={{0,1},{3,2},{4,5},{7,6},{8,9},{11,10},{12,13},{15,14},{16,17},{19,... | collective-permute-start | bytes 2359304 | tf_op jit(solution)/shard_map/ppermute | solution.py:496
  21.5 6.3 %mixed_0.1.refs_3_.refs_1_ = bf16[512,512]{1,0:T(8,128)(2,1)S(1)} custom-call(s32[4]{0:T(128)S(1)} %pad_add_fusion.refs_0_, bf16[3,2,512,512]{3,2,1,0:T(8,128)(2,1)} %refs_2_.11, bf16[3,2,512,512]{3,2,1,0:T(8,128)(2,1)} %refs_2_.11, bf16[3,2,512,512]{3,2,1,0:T(8,128)(2,1)} %refs_2_.11, bf16[2,512,512]{2,1,0:T(8,128)(2,1)S(1)} %collective-permute-done.2.refs_4_, ...), custom_call_target="tpu_custom_call" | custom-call | flops 20000000000 | bytes 1 | tf_op jit(solution)/shard_map/mixed_0/pallas_call | solution.py:54
  27.8 1.7 %collective-permute-start.8 = (bf16[512,512]{1,0:T(8,128)(2,1)S(1)}, bf16[512,512]{1,0:T(8,128)(2,1)S(1)}, u32[]{:S(2)}, u32[]{:S(2)}) collective-permute-start(bf16[512,512]{1,0:T(8,128)(2,1)S(1)} %mixed_0.1.refs_3_.refs_1_), channel_id=1, source_target_pairs={{0,1},{3,2},{4,5},{7,6},{8,9},{11,10},{12,13},{15,14},{16,17},{19,... | collective-permute-start | bytes 1572872 | tf_op jit(solution)/shard_map/ppermute | solution.py:496
  31.1 6.3 %collective-permute-start.3 = (bf16[3,256,512]{2,1,0:T(8,128)(2,1)S(1)}, bf16[3,256,512]{2,1,0:T(8,128)(2,1)S(1)}, u32[]{:S(2)}, u32[]{:S(2)}) collective-permute-start(bf16[3,256,512]{2,1,0:T(8,128)(2,1)S(1)} %add.18.refs_3_.refs_1_), channel_id=1, source_target_pairs={{0,16},{4,12},{8,24},{12,4},{16,0},{20,28},{24,8},{28,20},{1,17},{... | collective-permute-start | bytes 2359304 | tf_op jit(solution)/shard_map/ppermute | solution.py:496
  38.0 1.3 %collective-permute-done.6.refs_1_ = bf16[3,256,512]{2,1,0:T(8,128)(2,1)S(1)} collective-permute-done((bf16[3,256,512]{2,1,0:T(8,128)(2,1)S(1)}, bf16[3,256,512]{2,1,0:T(8,128)(2,1)S(1)}, u32[]{:S(2)}, u32[]{:S(2)}) %collective-permute-start.6) | collective-permute-done | bytes 786464 | tf_op jit(solution)/shard_map/ppermute | solution.py:496
  39.3 19.2 %collective-permute-done.3.refs_2_ = bf16[3,256,512]{2,1,0:T(8,128)(2,1)S(1)} collective-permute-done((bf16[3,256,512]{2,1,0:T(8,128)(2,1)S(1)}, bf16[3,256,512]{2,1,0:T(8,128)(2,1)S(1)}, u32[]{:S(2)}, u32[]{:S(2)}) %collective-permute-start.3) | collective-permute-done | bytes 786464 | tf_op jit(solution)/shard_map/ppermute | solution.py:496
  60.0 0.9 collective-permute-start.11
  60.9 5.3 %attend_1.1.refs_6_ = bf16[512,512]{1,0:T(8,128)(2,1)S(1)} custom-call(s32[4]{0:T(128)S(1)} %pad_add_fusion.refs_0_, bf16[3,2,512,512]{3,2,1,0:T(8,128)(2,1)} %refs_2_.11, bf16[3,2,512,512]{3,2,1,0:T(8,128)(2,1)} %refs_2_.11, bf16[3,2,512,512]{3,2,1,0:T(8,128)(2,1)} %refs_2_.11, bf16[2,512,512]{2,1,0:T(8,128)(2,1)S(1)} %collective-permute-done.5.refs_4_, ...), custom_call_target="tpu_custom_call" | custom-call | flops 20000000000 | bytes 1 | tf_op jit(solution)/shard_map/attend_1/pallas_call | solution.py:54
  66.3 5.1 %update_1.1 = (bf16[512,512]{1,0:T(8,128)(2,1)S(1)}, f32[3,512,512]{2,1,0:T(8,128)}, bf16[3,512,512]{2,1,0:T(8,128)(2,1)S(1)}) custom-call(s32[4]{0:T(128)S(1)} %pad_add_fusion.refs_0_, bf16[3,256,512]{2,1,0:T(8,128)(2,1)S(1)} %add.19.refs_4_.refs_1_, bf16[3,256,512]{2,1,0:T(8,128)(2,1)S(1)} %collective-permute-done.4.refs_2_, ...), custom_call_target="tpu_custom_call" | custom-call | flops 20000000000 | bytes 1 | tf_op jit(solution)/shard_map/update_1/pallas_call | solution.py:54
  71.4 5.7 %collective-permute-start.10 = (bf16[512,512]{1,0:T(8,128)(2,1)S(1)}, bf16[512,512]{1,0:T(8,128)(2,1)S(1)}, u32[]{:S(2)}, u32[]{:S(2)}) collective-permute-start(bf16[512,512]{1,0:T(8,128)(2,1)S(1)} %get-tuple-element.17.refs_7_.refs_1_), channel_id=1, source_target_pairs={{0,1},{3,2},{4,5},{7,6},{8,9},{11,10},{12,13},{15,14},{16,17},{19,... | collective-permute-start | bytes 1572872 | tf_op jit(solution)/shard_map/ppermute | solution.py:496
  77.8 4.7 %grads_1.1 = (bf16[3,256,512]{2,1,0:T(8,128)(2,1)S(1)}, bf16[3,256,512]{2,1,0:T(8,128)(2,1)S(1)}) custom-call(s32[4]{0:T(128)S(1)} %pad_add_fusion.refs_0_, bf16[3,2,512,512]{3,2,1,0:T(8,128)(2,1)} %refs_2_.11, bf16[3,2,512,512]{3,2,1,0:T(8,128)(2,1)} %refs_2_.11, f32[1,2,512]{2,1,0:T(2,128)S(1)} %copy-done.7, ...), custom_call_target="tpu_custom_call" | custom-call | flops 20000000000 | bytes 1 | tf_op jit(solution)/shard_map/grads_1/pallas_call | solution.py:54
  82.7 2.3 %edge_0.1.refs_3_ = bf16[512,512]{1,0:T(8,128)(2,1)} custom-call(s32[4]{0:T(128)S(1)} %pad_add_fusion.refs_0_, bf16[512,512]{1,0:T(8,128)(2,1)S(1)} %mixed_0.1.refs_3_.refs_1_, bf16[512,512]{1,0:T(8,128)(2,1)S(1)} %collective-permute-done.9.refs_5_.refs_2_.refs_3_, bf16[512,512]{1,0:T(8,128)(2,1)S(1)} %collective-permute-done.11.refs_3_.refs_4_, ...), custom_call_target="tpu_custom_call" | custom-call | flops 20000000000 | bytes 1 | tf_op jit(solution)/shard_map/edge_0/pallas_call | solution.py:54
  85.0 1.3 collective-permute-start.18
  86.3 0.7 add.20.refs_7_.refs_1_
  87.5 2.6 %own_0.1.refs_2_.refs_1_ = f32[512,512]{1,0:T(8,128)S(1)} custom-call(s32[4]{0:T(128)S(1)} %pad_add_fusion.refs_0_, bf16[512,512]{1,0:T(8,128)(2,1)S(1)} %mixed_0.1.refs_3_.refs_1_, bf16[512,512]{1,0:T(8,128)(2,1)S(1)} %get-tuple-element.18.refs_2_, bf16[512,512]{1,0:T(8,128)(2,1)S(1)} %collective-permute-done.9.refs_5_.refs_2_.refs_3_, ...), custom_call_target="tpu_custom_call" | custom-call | flops 20000000000 | bytes 1 | tf_op jit(solution)/shard_map/own_0/pallas_call | solution.py:54
  91.3 7.7 %collective-permute-done.15.refs_2_ = bf16[3,256,512]{2,1,0:T(8,128)(2,1)S(1)} collective-permute-done((bf16[3,256,512]{2,1,0:T(8,128)(2,1)S(1)}, bf16[3,256,512]{2,1,0:T(8,128)(2,1)S(1)}, u32[]{:S(2)}, u32[]{:S(2)}) %collective-permute-start.15) | collective-permute-done | bytes 786464 | tf_op jit(solution)/shard_map/ppermute | solution.py:496
  99.8 2.1 %collective-permute-start.16 = (bf16[3,256,512]{2,1,0:T(8,128)(2,1)S(1)}, bf16[3,256,512]{2,1,0:T(8,128)(2,1)S(1)}, u32[]{:S(2)}, u32[]{:S(2)}) collective-permute-start(bf16[3,256,512]{2,1,0:T(8,128)(2,1)S(1)} %add.21.refs_5_.refs_1_), channel_id=1, source_target_pairs={{0,16},{4,12},{8,24},{12,4},{16,0},{20,28},{24,8},{28,20},{1,17},{... | collective-permute-start | bytes 2359304 | tf_op jit(solution)/shard_map/ppermute | solution.py:496
  101.9 1.5 %edge_1.1.refs_3_ = bf16[512,512]{1,0:T(8,128)(2,1)S(1)} custom-call(s32[4]{0:T(128)S(1)} %pad_add_fusion.refs_0_, bf16[512,512]{1,0:T(8,128)(2,1)S(1)} %get-tuple-element.17.refs_7_.refs_1_, bf16[512,512]{1,0:T(8,128)(2,1)S(1)} %collective-permute-done.13.refs_3_.refs_2_, bf16[512,512]{1,0:T(8,128)(2,1)S(1)} %collective-permute-done.14.refs_3_.refs_4_, ...), custom_call_target="tpu_custom_call" | custom-call | flops 20000000000 | bytes 1 | tf_op jit(solution)/shard_map/edge_1/pallas_call | solution.py:54
  103.4 1.3 %collective-permute-start.17 = (bf16[512,512]{1,0:T(8,128)(2,1)S(1)}, bf16[512,512]{1,0:T(8,128)(2,1)S(1)}, u32[]{:S(2)}, u32[]{:S(2)}) collective-permute-start(bf16[512,512]{1,0:T(8,128)(2,1)S(1)} %edge_1.1.refs_3_), channel_id=1, source_target_pairs={{1,0},{2,3},{5,4},{6,7},{9,8},{10,11},{13,12},{14,15},{17,16},{18,... | collective-permute-start | bytes 1572872 | tf_op jit(solution)/shard_map/ppermute | solution.py:496
  104.7 7.1 %collective-permute-done.16.refs_2_ = bf16[3,256,512]{2,1,0:T(8,128)(2,1)S(1)} collective-permute-done((bf16[3,256,512]{2,1,0:T(8,128)(2,1)S(1)}, bf16[3,256,512]{2,1,0:T(8,128)(2,1)S(1)}, u32[]{:S(2)}, u32[]{:S(2)}) %collective-permute-start.16) | collective-permute-done | bytes 786464 | tf_op jit(solution)/shard_map/ppermute | solution.py:496
  112.7 2.6 %own_1.1.refs_5_.refs_1_ = f32[512,512]{1,0:T(8,128)S(1)} custom-call(s32[4]{0:T(128)S(1)} %pad_add_fusion.refs_0_, bf16[512,512]{1,0:T(8,128)(2,1)S(1)} %get-tuple-element.17.refs_7_.refs_1_, bf16[512,512]{1,0:T(8,128)(2,1)S(1)} %gate.3.refs_3_.refs_2_, bf16[512,512]{1,0:T(8,128)(2,1)S(1)} %collective-permute-done.13.refs_3_.refs_2_, ...), custom_call_target="tpu_custom_call" | custom-call | flops 20000000000 | bytes 1 | tf_op jit(solution)/shard_map/own_1/pallas_call | solution.py:54
  115.3 5.5 %final_update.1 = (f32[2,1,512,512]{3,2,1,0:T(8,128)}, f32[1,512,512]{2,1,0:T(8,128)}) custom-call(s32[4]{0:T(128)S(1)} %pad_add_fusion.refs_0_, bf16[3,256,512]{2,1,0:T(8,128)(2,1)S(1)} %add.22.refs_7_.refs_1_, bf16[3,256,512]{2,1,0:T(8,128)(2,1)S(1)} %collective-permute-done.19.refs_2_, f32[3,512,512]{2,1,0:T(8,128)} %get-tuple-element.22.refs_3_, ...), custom_call_target="tpu_custom_call" | custom-call | flops 20000000000 | bytes 1 | tf_op jit(solution)/shard_map/final_update/pallas_call | solution.py:54
  120.8 1.6 %copy-done.8 = f32[2,1,512,512]{3,2,1,0:T(8,128)S(1)} copy-done((f32[2,1,512,512]{3,2,1,0:T(8,128)S(1)}, f32[2,1,512,512]{3,2,1,0:T(8,128)}, u32[]{:S(2)}) %copy-start.8) | copy-done | bytes 2097176
  122.4 2.5 %finish_0.1.refs_3_ = bf16[2,512,512]{2,1,0:T(8,128)(2,1)} custom-call(s32[4]{0:T(128)S(1)} %pad_add_fusion.refs_0_, f32[512,512]{1,0:T(8,128)S(1)} %own_0.1.refs_2_.refs_1_, bf16[512,512]{1,0:T(8,128)(2,1)} %collective-permute-done.18.refs_2_, f32[2,1,512,512]{3,2,1,0:T(8,128)S(1)} %copy-done.8), custom_call_target="tpu_custom_call" | custom-call | flops 20000000000 | bytes 1 | tf_op jit(solution)/shard_map/finish_0/pallas_call | solution.py:54
  124.9 1.8 %collective-permute-done.17.refs_2_ = bf16[512,512]{1,0:T(8,128)(2,1)S(1)} collective-permute-done((bf16[512,512]{1,0:T(8,128)(2,1)S(1)}, bf16[512,512]{1,0:T(8,128)(2,1)S(1)}, u32[]{:S(2)}, u32[]{:S(2)}) %collective-permute-start.17) | collective-permute-done | bytes 524320 | tf_op jit(solution)/shard_map/ppermute | solution.py:496
  126.7 1.5 %finish_1.1 = bf16[2,512,512]{2,1,0:T(8,128)(2,1)} custom-call(s32[4]{0:T(128)S(1)} %pad_add_fusion.refs_0_, f32[512,512]{1,0:T(8,128)S(1)} %own_1.1.refs_5_.refs_1_, bf16[512,512]{1,0:T(8,128)(2,1)S(1)} %collective-permute-done.17.refs_2_, bf16[2,512,512]{2,1,0:T(8,128)(2,1)} %finish_0.1.refs_3_), custom_call_target="tpu_custom_call", output_to_operand_aliasing={{}: (3, {})} | custom-call | flops 20000000000 | bytes 1 | tf_op jit(solution)/shard_map/finish_1/pallas_call | solution.py:54
  (55 shorter events, 10.3 us)
Async XLA Ops:
  0.7 1.9 %copy-start = (bf16[3,2,512,512]{3,2,1,0:T(8,128)(2,1)S(1)}, bf16[3,2,512,512]{3,2,1,0:T(8,128)(2,1)}, u32[]{:S(2)}) copy-start(bf16[3,2,512,512]{3,2,1,0:T(8,128)(2,1)} %refs_2_.11) | copy-start | bytes 9437188
  2.6 3.2 %copy-start.3 = (bf16[2,1,512,512]{3,2,1,0:T(8,128)(2,1)S(1)}, bf16[2,1,512,512]{3,2,1,0:T(8,128)(2,1)}, u32[]{:S(2)}) copy-start(bf16[2,1,512,512]{3,2,1,0:T(8,128)(2,1)} %refs_3_.8) | copy-start | bytes 3145732
  2.6 3.2 %copy-start.5 = (bf16[1,512,512]{2,1,0:T(8,128)(2,1)S(1)}, bf16[1,512,512]{2,1,0:T(8,128)(2,1)}, u32[]{:S(2)}) copy-start(bf16[1,512,512]{2,1,0:T(8,128)(2,1)} %refs_4_.3) | copy-start | bytes 1572868
  2.6 3.2 %copy-start.6 = (f32[1,2,512]{2,1,0:T(2,128)S(1)}, f32[1,2,512]{2,1,0:T(2,128)}, u32[]{:S(2)}) copy-start(f32[1,2,512]{2,1,0:T(2,128)} %refs_3_.9) | copy-start | bytes 12292
  3.2 10.0 %copy-start.2 = (bf16[2048,512]{1,0:T(8,128)(2,1)S(1)}, bf16[2048,512]{1,0:T(8,128)(2,1)}, u32[]{:S(2)}) copy-start(bf16[2048,512]{1,0:T(8,128)(2,1)} %refs_5_.9) | copy-start | bytes 6291460
  3.2 18.2 %collective-permute-start.2 = (bf16[2,512,512]{2,1,0:T(8,128)(2,1)S(1)}, bf16[2,512,512]{2,1,0:T(8,128)(2,1)S(1)}, u32[]{:S(2)}, u32[]{:S(2)}) collective-permute-start(bf16[2,512,512]{2,1,0:T(8,128)(2,1)S(1)} %pack_0.1.refs_7_), channel_id=1, source_target_pairs={{0,4},{4,8},{8,12},{12,16},{16,20},{20,24},{24,28},{1,5},{5,9},{9,... | collective-permute-start | bytes 3145736 | tf_op jit(solution)/shard_map/ppermute | solution.py:496
  10.6 4.5 %collective-permute-start = (bf16[3,256,512]{2,1,0:T(8,128)(2,1)S(1)}, bf16[3,256,512]{2,1,0:T(8,128)(2,1)S(1)}, u32[]{:S(2)}, u32[]{:S(2)}) collective-permute-start(bf16[3,256,512]{2,1,0:T(8,128)(2,1)S(1)} %get-tuple-element.15.refs_2_), channel_id=1, source_target_pairs={{0,4},{4,0},{8,12},{12,8},{16,20},{20,16},{24,28},{28,24},{1,5},{5... | collective-permute-start | bytes 2359304 | tf_op jit(solution)/shard_map/ppermute | solution.py:496
  15.8 14.5 %collective-permute-start.1 = (bf16[3,256,512]{2,1,0:T(8,128)(2,1)S(1)}, bf16[3,256,512]{2,1,0:T(8,128)(2,1)S(1)}, u32[]{:S(2)}, u32[]{:S(2)}) collective-permute-start(bf16[3,256,512]{2,1,0:T(8,128)(2,1)S(1)} %add.17.refs_2_.refs_1_), channel_id=1, source_target_pairs={{0,8},{4,20},{8,0},{12,28},{16,24},{20,4},{24,16},{28,12},{1,9},{5... | collective-permute-start | bytes 2359304 | tf_op jit(solution)/shard_map/ppermute | solution.py:496
  17.9 21.4 %collective-permute-start.6 = (bf16[3,256,512]{2,1,0:T(8,128)(2,1)S(1)}, bf16[3,256,512]{2,1,0:T(8,128)(2,1)S(1)}, u32[]{:S(2)}, u32[]{:S(2)}) collective-permute-start(bf16[3,256,512]{2,1,0:T(8,128)(2,1)S(1)} %gate.2.refs_8_), channel_id=1, source_target_pairs={{0,1},{3,2},{4,5},{7,6},{8,9},{11,10},{12,13},{15,14},{16,17},{19,... | collective-permute-start | bytes 2359304 | tf_op jit(solution)/shard_map/ppermute | solution.py:496
  27.8 9.6 %copy-start.1 = (bf16[3,2,512,512]{3,2,1,0:T(8,128)(2,1)S(1)}, bf16[3,2,512,512]{3,2,1,0:T(8,128)(2,1)}, u32[]{:S(2)}) copy-start(bf16[3,2,512,512]{3,2,1,0:T(8,128)(2,1)} %refs_2_.11) | copy-start | bytes 9437188
  27.8 31.6 %collective-permute-start.8 = (bf16[512,512]{1,0:T(8,128)(2,1)S(1)}, bf16[512,512]{1,0:T(8,128)(2,1)S(1)}, u32[]{:S(2)}, u32[]{:S(2)}) collective-permute-start(bf16[512,512]{1,0:T(8,128)(2,1)S(1)} %mixed_0.1.refs_3_.refs_1_), channel_id=1, source_target_pairs={{0,1},{3,2},{4,5},{7,6},{8,9},{11,10},{12,13},{15,14},{16,17},{19,... | collective-permute-start | bytes 1572872 | tf_op jit(solution)/shard_map/ppermute | solution.py:496
  29.5 29.9 %collective-permute-start.9 = (bf16[512,512]{1,0:T(8,128)(2,1)S(1)}, bf16[512,512]{1,0:T(8,128)(2,1)S(1)}, u32[]{:S(2)}, u32[]{:S(2)}) collective-permute-start(bf16[512,512]{1,0:T(8,128)(2,1)S(1)} %mixed_0.1.refs_3_.refs_1_), channel_id=1, source_target_pairs={{1,2},{2,1},{5,6},{6,5},{9,10},{10,9},{13,14},{14,13},{17,18},{18,... | collective-permute-start | bytes 1572872 | tf_op jit(solution)/shard_map/ppermute | solution.py:496
  31.1 27.5 %collective-permute-start.3 = (bf16[3,256,512]{2,1,0:T(8,128)(2,1)S(1)}, bf16[3,256,512]{2,1,0:T(8,128)(2,1)S(1)}, u32[]{:S(2)}, u32[]{:S(2)}) collective-permute-start(bf16[3,256,512]{2,1,0:T(8,128)(2,1)S(1)} %add.18.refs_3_.refs_1_), channel_id=1, source_target_pairs={{0,16},{4,12},{8,24},{12,4},{16,0},{20,28},{24,8},{28,20},{1,17},{... | collective-permute-start | bytes 2359304 | tf_op jit(solution)/shard_map/ppermute | solution.py:496
  38.0 23.0 %collective-permute-start.5 = (bf16[2,512,512]{2,1,0:T(8,128)(2,1)S(1)}, bf16[2,512,512]{2,1,0:T(8,128)(2,1)S(1)}, u32[]{:S(2)}, u32[]{:S(2)}) collective-permute-start(bf16[2,512,512]{2,1,0:T(8,128)(2,1)S(1)} %pack_1.1.refs_3_), channel_id=1, source_target_pairs={{0,4},{4,8},{8,12},{12,16},{16,20},{20,24},{24,28},{28,0},{1,5},{5... | collective-permute-start | bytes 3145736 | tf_op jit(solution)/shard_map/ppermute | solution.py:496
  39.3 20.1 %collective-permute-start.7 = (bf16[3,256,512]{2,1,0:T(8,128)(2,1)S(1)}, bf16[3,256,512]{2,1,0:T(8,128)(2,1)S(1)}, u32[]{:S(2)}, u32[]{:S(2)}) collective-permute-start(bf16[3,256,512]{2,1,0:T(8,128)(2,1)S(1)} %collective-permute-done.6.refs_1_), channel_id=1, source_target_pairs={{0,4},{4,0},{8,12},{12,8},{16,20},{20,16},{24,28},{28,24},{1,5},{5... | collective-permute-start | bytes 2359304 | tf_op jit(solution)/shard_map/ppermute | solution.py:496
  59.3 7.0 %collective-permute-start.4 = (bf16[3,256,512]{2,1,0:T(8,128)(2,1)S(1)}, bf16[3,256,512]{2,1,0:T(8,128)(2,1)S(1)}, u32[]{:S(2)}, u32[]{:S(2)}) collective-permute-start(bf16[3,256,512]{2,1,0:T(8,128)(2,1)S(1)} %add.19.refs_4_.refs_1_), channel_id=1, source_target_pairs={{0,4},{4,0},{8,12},{12,8},{16,20},{20,16},{24,28},{28,24},{1,5},{5... | collective-permute-start | bytes 2359304 | tf_op jit(solution)/shard_map/ppermute | solution.py:496
  60.0 22.6 %collective-permute-start.11 = (bf16[512,512]{1,0:T(8,128)(2,1)S(1)}, bf16[512,512]{1,0:T(8,128)(2,1)S(1)}, u32[]{:S(2)}, u32[]{:S(2)}) collective-permute-start(bf16[512,512]{1,0:T(8,128)(2,1)S(1)} %get-tuple-element.18.refs_2_), channel_id=1, source_target_pairs={{1,2},{2,1},{5,6},{6,5},{9,10},{10,9},{13,14},{14,13},{17,18},{18,... | collective-permute-start | bytes 1572872 | tf_op jit(solution)/shard_map/ppermute | solution.py:496
  66.3 11.6 %copy-start.7 = (f32[1,2,512]{2,1,0:T(2,128)S(1)}, f32[1,2,512]{2,1,0:T(2,128)}, u32[]{:S(2)}) copy-start(f32[1,2,512]{2,1,0:T(2,128)} %refs_3_.9) | copy-start | bytes 12292
  71.4 11.2 %copy-start.9 = (bf16[3,512,512]{2,1,0:T(8,128)(2,1)}, bf16[3,512,512]{2,1,0:T(8,128)(2,1)S(1)}, u32[]{:S(2)}) copy-start(bf16[3,512,512]{2,1,0:T(8,128)(2,1)S(1)} %get-tuple-element.19.refs_4_.refs_5_.refs_6_) | copy-start | bytes 4718596
  71.4 18.7 %collective-permute-start.10 = (bf16[512,512]{1,0:T(8,128)(2,1)S(1)}, bf16[512,512]{1,0:T(8,128)(2,1)S(1)}, u32[]{:S(2)}, u32[]{:S(2)}) collective-permute-start(bf16[512,512]{1,0:T(8,128)(2,1)S(1)} %get-tuple-element.17.refs_7_.refs_1_), channel_id=1, source_target_pairs={{0,1},{3,2},{4,5},{7,6},{8,9},{11,10},{12,13},{15,14},{16,17},{19,... | collective-permute-start | bytes 1572872 | tf_op jit(solution)/shard_map/ppermute | solution.py:496
  77.1 13.0 %collective-permute-start.13 = (bf16[512,512]{1,0:T(8,128)(2,1)S(1)}, bf16[512,512]{1,0:T(8,128)(2,1)S(1)}, u32[]{:S(2)}, u32[]{:S(2)}) collective-permute-start(bf16[512,512]{1,0:T(8,128)(2,1)S(1)} %get-tuple-element.17.refs_7_.refs_1_), channel_id=1, source_target_pairs={{1,2},{2,1},{5,6},{6,5},{9,10},{10,9},{13,14},{14,13},{17,18},{18,... | collective-permute-start | bytes 1572872 | tf_op jit(solution)/shard_map/ppermute | solution.py:496
  82.6 3.7 %collective-permute-start.12 = (bf16[3,256,512]{2,1,0:T(8,128)(2,1)S(1)}, bf16[3,256,512]{2,1,0:T(8,128)(2,1)S(1)}, u32[]{:S(2)}, u32[]{:S(2)}) collective-permute-start(bf16[3,256,512]{2,1,0:T(8,128)(2,1)S(1)} %get-tuple-element.21.refs_5_), channel_id=1, source_target_pairs={{0,4},{4,0},{8,12},{12,8},{16,20},{20,16},{24,28},{28,24},{1,5},{5... | collective-permute-start | bytes 2359304 | tf_op jit(solution)/shard_map/ppermute | solution.py:496
  85.0 35.8 %collective-permute-start.18 = (bf16[512,512]{1,0:T(8,128)(2,1)}, bf16[512,512]{1,0:T(8,128)(2,1)}, u32[]{:S(2)}, u32[]{:S(2)}) collective-permute-start(bf16[512,512]{1,0:T(8,128)(2,1)} %edge_0.1.refs_3_), channel_id=1, source_target_pairs={{1,0},{2,3},{5,4},{6,7},{9,8},{10,11},{13,12},{14,15},{17,16},{18,... | collective-permute-start | bytes 1572872 | tf_op jit(solution)/shard_map/ppermute | solution.py:496
  86.3 1.2 copy-start.4
  87.0 12.1 %collective-permute-start.15 = (bf16[3,256,512]{2,1,0:T(8,128)(2,1)S(1)}, bf16[3,256,512]{2,1,0:T(8,128)(2,1)S(1)}, u32[]{:S(2)}, u32[]{:S(2)}) collective-permute-start(bf16[3,256,512]{2,1,0:T(8,128)(2,1)S(1)} %add.20.refs_7_.refs_1_), channel_id=1, source_target_pairs={{0,8},{4,20},{8,0},{12,28},{16,24},{20,4},{24,16},{28,12},{1,9},{5... | collective-permute-start | bytes 2359304 | tf_op jit(solution)/shard_map/ppermute | solution.py:496
  90.6 11.2 %collective-permute-start.14 = (bf16[512,512]{1,0:T(8,128)(2,1)S(1)}, bf16[512,512]{1,0:T(8,128)(2,1)S(1)}, u32[]{:S(2)}, u32[]{:S(2)}) collective-permute-start(bf16[512,512]{1,0:T(8,128)(2,1)S(1)} %gate.3.refs_3_.refs_2_), channel_id=1, source_target_pairs={{1,2},{2,1},{5,6},{6,5},{9,10},{10,9},{13,14},{14,13},{17,18},{18,... | collective-permute-start | bytes 1572872 | tf_op jit(solution)/shard_map/ppermute | solution.py:496
  99.8 12.1 %collective-permute-start.16 = (bf16[3,256,512]{2,1,0:T(8,128)(2,1)S(1)}, bf16[3,256,512]{2,1,0:T(8,128)(2,1)S(1)}, u32[]{:S(2)}, u32[]{:S(2)}) collective-permute-start(bf16[3,256,512]{2,1,0:T(8,128)(2,1)S(1)} %add.21.refs_5_.refs_1_), channel_id=1, source_target_pairs={{0,16},{4,12},{8,24},{12,4},{16,0},{20,28},{24,8},{28,20},{1,17},{... | collective-permute-start | bytes 2359304 | tf_op jit(solution)/shard_map/ppermute | solution.py:496
  103.4 23.3 %collective-permute-start.17 = (bf16[512,512]{1,0:T(8,128)(2,1)S(1)}, bf16[512,512]{1,0:T(8,128)(2,1)S(1)}, u32[]{:S(2)}, u32[]{:S(2)}) collective-permute-start(bf16[512,512]{1,0:T(8,128)(2,1)S(1)} %edge_1.1.refs_3_), channel_id=1, source_target_pairs={{1,0},{2,3},{5,4},{6,7},{9,8},{10,11},{13,12},{14,15},{17,16},{18,... | collective-permute-start | bytes 1572872 | tf_op jit(solution)/shard_map/ppermute | solution.py:496
  112.6 2.7 %copy-start.10 = (bf16[3,512,512]{2,1,0:T(8,128)(2,1)S(1)}, bf16[3,512,512]{2,1,0:T(8,128)(2,1)}, u32[]{:S(2)}) copy-start(bf16[3,512,512]{2,1,0:T(8,128)(2,1)} %copy-done.9) | copy-start | bytes 4718596
  112.6 2.7 %collective-permute-start.19 = (bf16[3,256,512]{2,1,0:T(8,128)(2,1)S(1)}, bf16[3,256,512]{2,1,0:T(8,128)(2,1)S(1)}, u32[]{:S(2)}, u32[]{:S(2)}) collective-permute-start(bf16[3,256,512]{2,1,0:T(8,128)(2,1)S(1)} %add.22.refs_7_.refs_1_), channel_id=1, source_target_pairs={{0,4},{4,0},{8,12},{12,8},{16,20},{20,16},{24,28},{28,24},{1,5},{5... | collective-permute-start | bytes 2359304 | tf_op jit(solution)/shard_map/ppermute | solution.py:496
  120.8 1.6 %copy-start.8 = (f32[2,1,512,512]{3,2,1,0:T(8,128)S(1)}, f32[2,1,512,512]{3,2,1,0:T(8,128)}, u32[]{:S(2)}) copy-start(f32[2,1,512,512]{3,2,1,0:T(8,128)} %get-tuple-element.12.refs_3_) | copy-start | bytes 6291460

commit v3 on v2

--- a/solution.py
+++ b/solution.py
@@ -14,6 +14,7 @@
 MASKED = -1e30
 BF = jnp.bfloat16
 F32 = jnp.float32
+PARTS = 1
 LIMIT = 48 * 1024 * 1024
 
 
@@ -43,7 +44,7 @@
     return pl.BlockSpec(shape, lambda *_: zeros)
 
 
-def call(kernel, name, scalars, inputs, specs, outs, earlier=(), scratch=(), grid=(1,), out_specs=None, aliases=None):
+def call(kernel, name, scalars, inputs, specs, outs, earlier=(), scratch=(), grid=(1,), out_specs=None, aliases=None, limit=LIMIT):
     single = not isinstance(outs, (list, tuple))
     outs_list = [outs] if single else list(outs)
     first = 1 + len(inputs)
@@ -62,7 +63,7 @@
             scratch_shapes=list(scratch),
         ),
         input_output_aliases={k + 1: v for k, v in (aliases or {}).items()},
-        compiler_params=pltpu.CompilerParams(vmem_limit_bytes=LIMIT),
+        compiler_params=pltpu.CompilerParams(vmem_limit_bytes=limit),
         cost_estimate=pl.CostEstimate(flops=20 * 10**9, bytes_accessed=1, transcendentals=0),
         name=name,
     )(scalars, *inputs, *earlier)
@@ -105,7 +106,7 @@
         half = keep_ref.shape[1]
         own = pl.multiple_of(sc[0] * half, half)
         other = pl.multiple_of((1 - sc[0]) * half, half)
-        keep_ref[...] = acc[:, pl.ds(own, half), :].astype(BF)
+        keep_ref[...] = acc[:, pl.ds(own, half), :]
         send_ref[...] = acc[:, pl.ds(other, half), :].astype(BF)
 
 
@@ -125,7 +126,7 @@
             pl.BlockSpec((1, learn_rates.shape[1], tile), lambda i, s: (0, 0, i)),
             *weight_specs,
         ],
-        [shape, shape],
+        [jax.ShapeDtypeStruct(shape.shape, F32), shape],
         scratch=[pltpu.VMEM((3, feats, feats), F32)],
         grid=(rows // tile,),
         earlier=earlier,
@@ -242,84 +243,131 @@
     )
 
 
-def renorm_into(sc, old, mine_ref, theirs_ref, moved):
-    half = mine_ref.shape[1]
-    own = pl.multiple_of(sc[0] * half, half)
-    other = pl.multiple_of((1 - sc[0]) * half, half)
+def halves(parity, mine, theirs):
+    half = mine.shape[0]
+    own = pl.multiple_of(parity * half, half)
+    other = pl.multiple_of((1 - parity) * half, half)
+    return ((pl.ds(own, half), mine), (pl.ds(other, half), theirs))
+
+
+def renorm_one(old, mine, theirs, parity, put):
+    before = jnp.zeros((), F32)
+    after = jnp.zeros((), F32)
+    moved = []
+    for rows, part in halves(parity, mine, theirs):
+        w = old(rows).astype(F32)
+        new = w - part.astype(F32)
+        moved.append((rows, new))
+        before += jnp.sum(w * w)
+        after += jnp.sum(new * new)
+    ratio = jnp.sqrt(before) / jnp.sqrt(after + 1e-06)
+    for rows, new in moved:
+        put(rows, new * ratio)
+    return ratio
+
+
+def old_of(refs, i, rows):
+    if len(refs) == 1:
+        return refs[0][i, rows, :]
+    return refs[0][i, 0, rows, :] if i < 2 else refs[1][0, rows, :]
+
+
+def update_kernel(states, keep_state, parts, sc, mine_ref, theirs_ref, *refs):
+    old, (q_ref, att_ref, mix_ref, new_bf_ref), rest = refs[:states], refs[states : states + 4], refs[states + 4 :]
+    piece_refs, ratio_ref = rest[:parts], rest[parts]
     for i in range(3):
-        before = jnp.zeros((), F32)
-        after = jnp.zeros((), F32)
-        for start, part in ((own, mine_ref), (other, theirs_ref)):
-            w = old(i, pl.ds(start, half)).astype(F32)
-            new = w - part[i].astype(F32)
-            moved[i, pl.ds(start, half), :] = new
-            before += jnp.sum(w * w)
-            after += jnp.sum(new * new)
-        ratio = jnp.sqrt(before) / jnp.sqrt(after + 1e-06)
-        moved[i] = moved[i] * ratio
-
-
-def update_kernel(first, sc, mine_ref, theirs_ref, up_ref, down_ref, q_ref, att_ref, mix_ref, new_ref, new_bf_ref):
-    if first:
-        old = lambda i, rows: up_ref[i, 0, rows, :] if i < 2 else down_ref[0, rows, :]
-    else:
-        old = lambda i, rows: up_ref[i, rows, :]
-    renorm_into(sc, old, mine_ref, theirs_ref, new_ref)
-    new_bf_ref[...] = new_ref[...].astype(BF)
+
+        def put(rows, value, i=i):
+            new_bf_ref[i, rows, :] = value.astype(BF)
+            if keep_state:
+                rest[parts + 1][i, rows, :] = value
+
+        ratio = renorm_one(lambda rows, i=i: old_of(old, i, rows), mine_ref[i], theirs_ref[i], sc[0], put)
+        ratio_ref[i] = jnp.full(ratio_ref.shape[1:], ratio, F32)
     rows = q_ref.shape[0]
     tile = min(TILE, rows)
     for start in range(0, rows, tile):
         at = slice(start, start + tile)
         fast = fast_rows(q_ref[at, :], new_bf_ref[0], new_bf_ref[1], new_bf_ref[2])
         mix_ref[at, :] = (att_ref[at, :].astype(F32) + fast).astype(BF)
-
-
-def update_and_mix(block, scalars, mine, theirs, state, projected, attended, earlier=()):
+    for i, piece_ref in enumerate(piece_refs):
+        size = piece_ref.shape[0]
+        piece_ref[...] = mix_ref[i * size : (i + 1) * size, :]
+
+
+def update_and_mix(block, scalars, mine, theirs, state, keep_state, projected, attended, parts, earlier=()):
     _, _, rows, feats = projected.shape
-    first = block == 1
-    return call(
-        functools.partial(update_kernel, first),
+    pieces = parts if parts > 1 else 0
+    got = call(
+        functools.partial(update_kernel, len(state), keep_state, pieces),
         f"update_{block}",
         scalars,
-        (mine, theirs, state[0], state[1], projected, attended),
+        (mine, theirs, *state, projected, attended),
         [
             whole(mine),
             whole(theirs),
-            whole(state[0]),
-            whole(state[1]),
+            *[whole(a) for a in state],
             pl.BlockSpec((None, None, rows, feats), lambda i, s: (0, block, 0, 0)),
             whole(attended),
         ],
         [
             jax.ShapeDtypeStruct((rows, feats), BF),
-            jax.ShapeDtypeStruct((3, feats, feats), F32),
             jax.ShapeDtypeStruct((3, feats, feats), BF),
-        ],
-        earlier=earlier,
-    )
-
-
-def final_kernel(first, sc, mine_ref, theirs_ref, up_ref, down_ref, up_out, down_out, moved):
-    if first:
-        old = lambda i, rows: up_ref[i, 0, rows, :] if i < 2 else down_ref[0, rows, :]
-    else:
-        old = lambda i, rows: up_ref[i, rows, :]
-    renorm_into(sc, old, mine_ref, theirs_ref, moved)
-    up_out[0, 0] = moved[0]
-    up_out[1, 0] = moved[1]
-    down_out[0] = moved[2]
-
-
-def final_update(first, scalars, mine, theirs, state, earlier=()):
-    feats = mine.shape[2]
-    return call(
-        functools.partial(final_kernel, first),
+            *[jax.ShapeDtypeStruct((rows // parts, feats), BF) for _ in range(pieces)],
+            jax.ShapeDtypeStruct((3, 8, HD), F32),
+            *([jax.ShapeDtypeStruct((3, feats, feats), F32)] if keep_state else []),
+        ],
+        earlier=earlier,
+    )
+    new_state = got[-1] if keep_state else None
+    ratio = got[-2] if keep_state else got[-1]
+    return got[0], got[1], got[2 : 2 + pieces] or [got[0]], ratio, new_state
+
+
+def final_kernel(states, sc, mine_ref, theirs_ref, mine_before, theirs_before, ratio_ref, *refs):
+    old = refs[:states]
+    up_out, down_out, token, now = refs[states:]
+    token[...] = jnp.zeros_like(token)
+    step = pl.program_id(0)
+
+    def run(i, out):
+        ratio = ratio_ref[i, 0:1, 0:1]
+        for rows, part in halves(sc[0], mine_before[i], theirs_before[i]):
+            now[rows, :] = (old_of(old, i, rows).astype(F32) - part.astype(F32)) * ratio
+
+        def put(rows, value):
+            out[rows, :] = value
+
+        renorm_one(lambda rows: now[rows, :], mine_ref[...], theirs_ref[...], sc[0], put)
+
+    for i in range(3):
+        pl.when(step == i)(functools.partial(run, i, up_out if i < 2 else down_out))
+
+
+def final_update(scalars, mine, theirs, mine_before, theirs_before, ratio, state, earlier=()):
+    _, half, feats = mine.shape
+    return call(
+        functools.partial(final_kernel, len(state)),
         "final_update",
         scalars,
-        (mine, theirs, *state),
-        [whole(mine), whole(theirs), whole(state[0]), whole(state[1])],
-        [jax.ShapeDtypeStruct((2, 1, feats, feats), F32), jax.ShapeDtypeStruct((1, feats, feats), F32)],
-        scratch=[pltpu.VMEM((3, feats, feats), F32)],
+        (mine, theirs, mine_before, theirs_before, ratio, *state),
+        [
+            pl.BlockSpec((None, half, feats), lambda i, s: (i, 0, 0)),
+            pl.BlockSpec((None, half, feats), lambda i, s: (i, 0, 0)),
+            *[whole(a) for a in (mine_before, theirs_before, ratio, *state)],
+        ],
+        [
+            jax.ShapeDtypeStruct((2, 1, feats, feats), F32),
+            jax.ShapeDtypeStruct((1, feats, feats), F32),
+            jax.ShapeDtypeStruct((8, HD), F32),
+        ],
+        out_specs=[
+            pl.BlockSpec((None, None, feats, feats), lambda i, s: (jnp.minimum(i, 1), 0, 0, 0)),
+            pl.BlockSpec((None, feats, feats), lambda i, s: (0, 0, 0)),
+            pl.BlockSpec((8, HD), lambda i, s: (0, 0)),
+        ],
+        grid=(3,),
+        scratch=[pltpu.VMEM((feats, feats), F32)],
         earlier=earlier,
     )
 
@@ -345,27 +393,6 @@
     )
 
 
-def join_kernel(sc, mine_ref, theirs_ref, x_ref, out_ref, x_out_ref):
-    half = mine_ref.shape[1]
-    out_ref[:, pl.ds(pl.multiple_of(sc[0] * half, half), half), :] = mine_ref[...]
-    out_ref[:, pl.ds(pl.multiple_of((1 - sc[0]) * half, half), half), :] = theirs_ref[...]
-
-
-def join_halves(scalars, mine, theirs, x, earlier=()):
-    count, half, feats = mine.shape
-    return call(
-        join_kernel,
-        "join_halves",
-        scalars,
-        (mine, theirs, x),
-        [whole(mine), whole(theirs), pl.BlockSpec(memory_space=pl.ANY)],
-        [jax.ShapeDtypeStruct((count, 2 * half, feats), BF), like(x)],
-        out_specs=[whole_out((count, 2 * half, feats)), pl.BlockSpec(memory_space=pl.ANY)],
-        aliases={2: 1},
-        earlier=earlier,
-    )
-
-
 def gate_kernel(sc, x_ref, x_out_ref):
     pass
 
@@ -417,77 +444,130 @@
     )
 
 
-def edge_kernel(sc, m_ref, ya_ref, yb_ref, v_ref, out_ref):
-    out_ref[...] = (mm(m_ref[...], v_ref[0]) + mm(ya_ref[...], v_ref[1]) + mm(yb_ref[...], v_ref[2])).astype(BF)
-
-
-def edge_part(block, scalars, m, ya, yb, v, earlier=()):
-    rows, feats = m.shape
+def edge_kernel(sc, m_ref, ya_ref, yb_ref, mine_ref, theirs_ref, out_ref):
+    half = mine_ref.shape[1]
+    total = None
+    for part, parity in ((mine_ref, sc[0]), (theirs_ref, 1 - sc[0])):
+        cols = pl.ds(pl.multiple_of(parity * half, half), half)
+        for i, ref in enumerate((m_ref, ya_ref, yb_ref)):
+            term = mm(ref[:, cols], part[i])
+            total = term if total is None else total + term
+    out_ref[...] = total.astype(BF)
+
+
+def part_spec(rows, feats, part):
+    return pl.BlockSpec((rows, feats), lambda i, s: (part, 0))
+
+
+def edge_part(name, scalars, part, m, ya, yb, v_mine, v_other, earlier=()):
+    rows, feats = yb.shape
     return call(
         edge_kernel,
-        f"edge_{block}",
-        scalars,
-        (m, ya, yb, v),
-        [whole(m), whole(ya), whole(yb), whole(v)],
+        f"edge_{name}",
+        scalars,
+        (m, ya, yb, v_mine, v_other),
+        [part_spec(rows, feats, part), part_spec(rows, feats, part), whole(yb), whole(v_mine), whole(v_other)],
         jax.ShapeDtypeStruct((rows, feats), BF),
         earlier=earlier,
     )
 
 
-def own_kernel(sc, m_ref, x_ref, ya_ref, yb_ref, w_ref, hid_ref, out_ref):
-    feats = m_ref.shape[1]
+def own_rows(sc, m, x, ya, yb, w_ref, hid, put, get):
+    feats = w_ref.shape[1]
     head = sc[2]
 
     def weight(which):
         return w_ref[pl.ds(pl.multiple_of(which * feats, feats), feats), :]
 
-    out_ref[...] = hid_ref[...].astype(F32) + mm(m_ref[...], weight(head))
+    put(hid.astype(F32) + mm(m, weight(head)))
 
     @pl.when(sc[3] == 1)
     def _():
-        out_ref[...] = (
-            out_ref[...]
-            + mm(x_ref[...], weight(head ^ 1))
-            + mm(ya_ref[...], weight(head ^ 3))
-            + mm(yb_ref[...], weight(head ^ 2))
-        )
-
-
-def own_part(block, scalars, m, x, ya, yb, w_out, hidden_in, earlier=()):
+        put(get() + mm(x[...], weight(head ^ 1)) + mm(ya[...], weight(head ^ 3)) + mm(yb[...], weight(head ^ 2)))
+
+
+def own_kernel(sc, m_ref, x_ref, ya_ref, yb_ref, w_ref, hid_ref, c_ref, *refs):
+    out_ref, acc = refs[-2:]
+
+    def put(value):
+        acc[...] = value
+
+    own_rows(sc, m_ref[...], x_ref, ya_ref, yb_ref, w_ref, hid_ref[...], put, lambda: acc[...])
+    out_ref[...] = (acc[...] + c_ref[...].astype(F32)).astype(BF)
+
+
+def own_part(block, scalars, m, x, ya, yb, w_out, hidden_in, c, so_far, earlier=()):
     rows, feats = m.shape
     return call(
         own_kernel,
         f"own_{block}",
         scalars,
-        (m, x, ya, yb, w_out, hidden_in),
+        (m, x, ya, yb, w_out, hidden_in, c, *so_far),
         [
-            whole(m),
-            whole(x),
-            whole(ya),
-            whole(yb),
-            whole(w_out),
+            *[whole(a) for a in (m, x, ya, yb, w_out)],
             pl.BlockSpec((None, rows, feats), lambda i, s: (block, 0, 0)),
+            whole(c),
+            *[pl.BlockSpec(memory_space=pl.ANY) for _ in so_far],
+        ],
+        like(hidden_in),
+        out_specs=[pl.BlockSpec((None, rows, feats), lambda i, s: (block, 0, 0))],
+        aliases={7: 0} if so_far else None,
+        scratch=[pltpu.VMEM((rows, feats), F32)],
+        earlier=earlier,
+    )
+
+
+def last_kernel(parts, sc, *refs):
+    m_ref, ya_ref = refs[:2]
+    xs, ybs = refs[2 : 2 + parts], refs[2 + parts : 2 + 2 * parts]
+    w_ref, hid_ref, out_ref = refs[2 + 2 * parts :]
+    rows = m_ref.shape[0] // parts
+    for i in range(parts):
+        at = pl.ds(i * rows, rows)
+
+        def put(value, at=at):
+            out_ref[at, :] = value
+
+        own_rows(
+            sc, m_ref[at, :], xs[i], ya_ref.at[at, :], ybs[i], w_ref, hid_ref[at, :], put, lambda at=at: out_ref[at, :]
+        )
+
+
+def own_last(block, scalars, m, xs, ya, ybs, w_out, hidden_in, earlier=()):
+    rows, feats = m.shape
+    return call(
+        functools.partial(last_kernel, len(xs)),
+        f"own_{block}",
+        scalars,
+        (m, ya, *xs, *ybs, w_out, hidden_in),
+        [
+            *[whole(a) for a in (m, ya, *xs, *ybs, w_out)],
+            pl.BlockSpec((None, rows, feats), lambda i, s: (block, 0, 0)),
         ],
         jax.ShapeDtypeStruct((rows, feats), F32),
         earlier=earlier,
     )
 
 
-def finish_kernel(sc, acc_ref, c_ref, *refs):
-    refs[-1][...] = (acc_ref[...] + c_ref[...].astype(F32)).astype(BF)
-
-
-def finish(block, blocks, scalars, acc, c, so_far, earlier=()):
+def finish_kernel(parts, sc, acc_ref, *refs):
+    out_ref = refs[-1]
+    rows = acc_ref.shape[0] // parts
+    for i in range(parts):
+        at = pl.ds(i * rows, rows)
+        out_ref[at, :] = (acc_ref[at, :] + refs[i][...].astype(F32)).astype(BF)
+
+
+def finish(block, scalars, acc, cs, so_far, earlier=()):
     rows, feats = acc.shape
     return call(
-        finish_kernel,
-        f"finish_{block}",
-        scalars,
-        (acc, c, *so_far),
-        [whole(acc), whole(c), *[pl.BlockSpec(memory_space=pl.ANY) for _ in so_far]],
-        jax.ShapeDtypeStruct((blocks, rows, feats), BF),
+        functools.partial(finish_kernel, len(cs)),
+        "finish",
+        scalars,
+        (acc, *cs, *so_far),
+        [whole(acc), *[whole(c) for c in cs], *[pl.BlockSpec(memory_space=pl.ANY) for _ in so_far]],
+        like(so_far[0]) if so_far else None,
         out_specs=[pl.BlockSpec((None, rows, feats), lambda i, s: (block, 0, 0))],
-        aliases={2: 0} if so_far else None,
+        aliases={1 + len(cs): 0},
         earlier=earlier,
     )
 
@@ -537,64 +617,79 @@
     halo = move(kv_now, "ctx", forward)
     keep, send = block_grads(0, scalars, projected, learn_rates, weights, step_scale, specs, earlier=(kv_now,))
     v_send = pick_parts(scalars, w_out, earlier=(send,))
+    v_mine = move(v_send, "head", edge_in)
     total = add(scalars, keep, flip(send, 0), earlier=(v_send,))
     received = move(total, "ctx", partners(ctx_count, 0))
-    v_send = gate(scalars, v_send, earlier=(total,))
-    v_mine = move(v_send, "head", edge_in)
-    v_other = flip(v_mine, 0)
-    mixed = mixed_first(0, scalars, projected, halo, weights, specs, earlier=(v_send,))
-    x = move(mixed, "head", edge_in)
+    kv_now = pack_halo(1, scalars, projected, ctx_count - 1, earlier=(total,))
+    halo_next = move(kv_now, "ctx", around)
+    mixed = last = mixed_first(0, scalars, projected, halo, weights, specs, earlier=(kv_now,))
+    xs = [move(mixed, "head", edge_in)]
     ya = move(mixed, "head", middle)
-    last = mixed
     so_far = ()
     for block in range(1, blocks):
+        at_end = block == blocks - 1
+        parts = PARTS if at_end else 1
         for step in range(steps):
             total = last = add(scalars, total, received, earlier=(last,))
             if step + 1 < steps:
                 received = move(total, "ctx", partners(ctx_count, step + 1))
             if step == 0:
-                kv_now = last = pack_halo(block, scalars, projected, ctx_count - 1, earlier=(last,))
-                halo = move(kv_now, "ctx", around)
+                attended = last = attention_only(block, scalars, projected, halo_next, earlier=(last,))
+                if block == 1:
+                    v_mine = last = gate(scalars, v_mine, earlier=(attended,))
+                    v_other = flip(v_mine, 0)
         theirs = flip(total, 0)
-        if block == 1:
-            v, x = join_halves(scalars, v_mine, v_other, x, earlier=(last, ya))
-            last = v
-        else:
-            x = last = gate(scalars, x, earlier=(last, ya))
-        yb = move(x, "head", middle)
-        attended = attention_only(block, scalars, projected, halo, earlier=(last,))
-        mixed_next, new, new_bf = update_and_mix(block, scalars, total, theirs, state, projected, attended)
+        xs[0] = last = gate(scalars, xs[0], earlier=(total, last, ya))
+        yb = move(xs[0], "head", middle)
+        mixed_next, new_bf, pieces, ratio, new_state = update_and_mix(
+            block, scalars, total, theirs, state, not at_end, projected, attended, parts, earlier=(last,)
+        )
+        xs_next = [move(pieces[0], "head", edge_in)]
+        ya_next = move(mixed_next, "head", middle)
+        xs_next += [move(piece, "head", edge_in) for piece in pieces[1:]]
         weights, specs = (new_bf, new_bf, new_bf), bf_spec
-        state = (new, new_bf)
-        x_next = move(mixed_next, "head", edge_in)
-        ya_next = move(mixed_next, "head", middle)
         keep, send = block_grads(
             block, scalars, projected, learn_rates, weights, step_scale, specs, earlier=(mixed_next,)
         )
-        c = edge_part(block - 1, scalars, mixed, ya, yb, v, earlier=(send,))
+        c = last = edge_part(block - 1, scalars, 0, mixed, ya, yb, v_mine, v_other, earlier=(send,))
         c_there = move(c, "head", edge_out)
-        total = add(scalars, keep, flip(send, 0), earlier=(c,))
+        total_before, theirs_before = total, theirs
+        total = last = add(scalars, keep, flip(send, 0), earlier=(last,))
         received = move(total, "ctx", partners(ctx_count, 0))
-        acc = last = own_part(block - 1, scalars, mixed, x, ya, yb, w_out, hidden_in, earlier=(total,))
-        if block < blocks - 1:
-            so_far = (finish(block - 1, blocks, scalars, acc, c_there, so_far),)
-            last = so_far[0]
-        mixed, x, ya = mixed_next, x_next, ya_next
-    x = last = gate(scalars, x, earlier=(last, ya))
-    yb = move(x, "head", middle)
+        if not at_end:
+            kv_now = last = pack_halo(block + 1, scalars, projected, ctx_count - 1, earlier=(last,))
+            halo_next = move(kv_now, "ctx", around)
+            out = last = own_part(
+                block - 1, scalars, mixed, xs[0], ya, yb, w_out, hidden_in, c_there, so_far, earlier=(last,)
+            )
+            so_far = (out,)
+            state = (new_state,)
+            mixed, xs, ya = mixed_next, xs_next, ya_next
+    ybs = []
+    for i in range(parts):
+        xs_next[i] = last = gate(scalars, xs_next[i], earlier=(last,))
+        ybs.append(move(xs_next[i], "head", middle))
     for step in range(steps):
         total = last = add(scalars, total, received, earlier=(last,))
         if step + 1 < steps:
             received = move(total, "ctx", partners(ctx_count, step + 1))
         if step == 0:
-            c = last = edge_part(blocks - 1, scalars, mixed, ya, yb, v, earlier=(last,))
-            c_last = move(c, "head", edge_out)
+            c_last = []
+            for i in range(parts):
+                c = last = edge_part(
+                    f"{blocks - 1}_{i}", scalars, i, mixed_next, ya_next, ybs[i], v_mine, v_other, earlier=(last,)
+                )
+                c_last.append(move(c, "head", edge_out))
+            out = last = own_part(
+                blocks - 2, scalars, mixed, xs[0], ya, yb, w_out, hidden_in, c_there, so_far, earlier=(last,)
+            )
     theirs = flip(total, 0)
-    acc_last = own_part(blocks - 1, scalars, mixed, x, ya, yb, w_out, hidden_in, earlier=(last,))
-    up_final, down_final = final_update(blocks == 1, scalars, total, theirs, state, earlier=(acc_last,))
-    out = finish(blocks - 2, blocks, scalars, acc, c_there, so_far, earlier=(up_final,))
-    layer_out = finish(blocks - 1, blocks, scalars, acc_last, c_last, (out,))
-    return layer_out, up_final, down_final
+    acc = own_last(blocks - 1, scalars, mixed_next, xs_next, ya_next, ybs, w_out, hidden_in, earlier=(total,))
+    up_final, down_final, token = final_update(
+        scalars, total, theirs, total_before, theirs_before, ratio, state, earlier=(acc,)
+    )
+    out = finish(blocks - 1, scalars, acc, c_last, (out,), earlier=(token,))
+    return out, up_final, down_final
 
 
 def solution(mesh):

time: 130 us -> 112 us (0.86)
  waiting for transfers between devices: 38.7 us -> 30.3 us
  Pallas kernels: 52.5 us -> 46.8 us
  starting transfers between devices: 31.9 us -> 26.8 us
  local copies, waits for them, and re-layouts: 3.94 us -> 5.72 us
    ppermute x20, waiting for transfers between devices: 38.7 us -> 30.3 us  [move(): return lax.ppermute(x, axis, pairs)]
    pallas_call x24 -> x23, Pallas kernels: 52.5 us -> 46.8 us  [call(): pl.pallas_call(ordered, out_shape=outs_list, grid_spec=pltpu.PrefetchScal...]
    ppermute x20, starting transfers between devices: 31.9 us -> 26.8 us  [move(): return lax.ppermute(x, axis, pairs)]
    unnamed x22 -> x34, local copies, waits for them, and re-layouts: 3.94 us -> 5.72 us
  transfers between devices with their start and end apart: 20 -> 20, of which waited for: 7 -> 7; matrix products, arithmetic and copies ran while one was open for 0% -> 0% of each run, Pallas kernels for 39% -> 40%
where the time goes in v3:
time: 112 us; the launch traced here: 111 us
  Pallas kernels  46.8 us (42%)
  waiting for transfers between devices  30.3 us (27%)
  starting transfers between devices  26.8 us (24%)
  local copies, waits for them, and re-layouts  5.72 us (5%)
  between operations  1.13 us (1%)
    pallas_call x23, Pallas kernels, call(): pl.pallas_call(ordered, out_shape=outs_list, grid_spec=pltpu.PrefetchScal...  46.8 us
    ppermute x20, waiting for transfers between devices, move(): return lax.ppermute(x, axis, pairs)  30.3 us
    ppermute x20, starting transfers between devices, move(): return lax.ppermute(x, axis, pairs)  26.8 us
    unnamed x34, local copies, waits for them, and re-layouts  5.72 us
  transfers between devices with their start and end apart: 20, of which 7 were waited for; matrix products, arithmetic and copies ran while one was open for 0% of the time, Pallas kernels for 40%

profile of v3, /device:TPU:0, one launch (start us, length us, event | category | flops | bytes accessed | tf_op | source)
XLA Modules:
  0.0 110.9 jit_solution(678559089063107455)
XLA Ops:
  0.7 1.9 %copy-done = bf16[3,2,512,512]{3,2,1,0:T(8,128)(2,1)S(1)} copy-done((bf16[3,2,512,512]{3,2,1,0:T(8,128)(2,1)S(1)}, bf16[3,2,512,512]{3,2,1,0:T(8,128)(2,1)}, u32[]{:S(2)}) %copy-start) | copy-done | bytes 3145752
  3.2 2.6 %collective-permute-start.2 = (bf16[2,512,512]{2,1,0:T(8,128)(2,1)S(1)}, bf16[2,512,512]{2,1,0:T(8,128)(2,1)S(1)}, u32[]{:S(2)}, u32[]{:S(2)}) collective-permute-start(bf16[2,512,512]{2,1,0:T(8,128)(2,1)S(1)} %pack_0.1.refs_7_), channel_id=1, source_target_pairs={{0,4},{4,8},{8,12},{12,16},{16,20},{20,24},{24,28},{1,5},{5,9},{9,... | collective-permute-start | bytes 3145736 | tf_op jit(solution)/shard_map/ppermute | solution.py:576
  5.8 4.8 %grads_0.1 = (f32[3,256,512]{2,1,0:T(8,128)S(1)}, bf16[3,256,512]{2,1,0:T(8,128)(2,1)S(1)}) custom-call(s32[4]{0:T(128)S(1)} %pad_add_fusion.refs_0_, bf16[3,2,512,512]{3,2,1,0:T(8,128)(2,1)} %refs_2_.11, bf16[3,2,512,512]{3,2,1,0:T(8,128)(2,1)} %refs_2_.11, f32[1,2,512]{2,1,0:T(2,128)S(1)} %copy-done.11, bf16[2,1,512,512]{3,2,1,0:T(8,128)(2,1)S(1)} %copy-done.5, ...), custom_call_target="tpu_custom_call" | custom-call | flops 20000000000 | bytes 1 | tf_op jit(solution)/shard_map/grads_0/pallas_call | solution.py:55
  10.6 2.6 %collective-permute-start = (bf16[3,256,512]{2,1,0:T(8,128)(2,1)S(1)}, bf16[3,256,512]{2,1,0:T(8,128)(2,1)S(1)}, u32[]{:S(2)}, u32[]{:S(2)}) collective-permute-start(bf16[3,256,512]{2,1,0:T(8,128)(2,1)S(1)} %get-tuple-element.14.refs_2_), channel_id=1, source_target_pairs={{0,4},{4,0},{8,12},{12,8},{16,20},{20,16},{24,28},{28,24},{1,5},{5... | collective-permute-start | bytes 2359304 | tf_op jit(solution)/shard_map/ppermute | solution.py:576
  13.8 3.5 %collective-permute-start.4 = (bf16[3,256,512]{2,1,0:T(8,128)(2,1)S(1)}, bf16[3,256,512]{2,1,0:T(8,128)(2,1)S(1)}, u32[]{:S(2)}, u32[]{:S(2)}) collective-permute-start(bf16[3,256,512]{2,1,0:T(8,128)(2,1)S(1)} %pick_parts.1.refs_3_), channel_id=1, source_target_pairs={{0,1},{3,2},{4,5},{7,6},{8,9},{11,10},{12,13},{15,14},{16,17},{19,... | collective-permute-start | bytes 2359304 | tf_op jit(solution)/shard_map/ppermute | solution.py:576
  18.1 1.6 %collective-permute-start.1 = (bf16[3,256,512]{2,1,0:T(8,128)(2,1)S(1)}, bf16[3,256,512]{2,1,0:T(8,128)(2,1)S(1)}, u32[]{:S(2)}, u32[]{:S(2)}) collective-permute-start(bf16[3,256,512]{2,1,0:T(8,128)(2,1)S(1)} %add.17.refs_3_.refs_1_), channel_id=1, source_target_pairs={{0,8},{4,20},{8,0},{12,28},{16,24},{20,4},{24,16},{28,12},{1,9},{5... | collective-permute-start | bytes 2359304 | tf_op jit(solution)/shard_map/ppermute | solution.py:576
  20.4 6.3 %mixed_0.1.refs_3_.refs_1_ = bf16[512,512]{1,0:T(8,128)(2,1)S(1)} custom-call(s32[4]{0:T(128)S(1)} %pad_add_fusion.refs_0_, bf16[3,2,512,512]{3,2,1,0:T(8,128)(2,1)} %refs_2_.11, bf16[3,2,512,512]{3,2,1,0:T(8,128)(2,1)} %refs_2_.11, bf16[3,2,512,512]{3,2,1,0:T(8,128)(2,1)} %refs_2_.11, bf16[2,512,512]{2,1,0:T(8,128)(2,1)S(1)} %collective-permute-done.2.refs_4_, ...), custom_call_target="tpu_custom_call" | custom-call | flops 20000000000 | bytes 1 | tf_op jit(solution)/shard_map/mixed_0/pallas_call | solution.py:55
  26.7 1.6 %collective-permute-start.7 = (bf16[512,512]{1,0:T(8,128)(2,1)S(1)}, bf16[512,512]{1,0:T(8,128)(2,1)S(1)}, u32[]{:S(2)}, u32[]{:S(2)}) collective-permute-start(bf16[512,512]{1,0:T(8,128)(2,1)S(1)} %mixed_0.1.refs_3_.refs_1_), channel_id=1, source_target_pairs={{0,1},{3,2},{4,5},{7,6},{8,9},{11,10},{12,13},{15,14},{16,17},{19,... | collective-permute-start | bytes 1572872 | tf_op jit(solution)/shard_map/ppermute | solution.py:576
  29.1 7.7 %collective-permute-done.1.refs_2_ = bf16[3,256,512]{2,1,0:T(8,128)(2,1)S(1)} collective-permute-done((bf16[3,256,512]{2,1,0:T(8,128)(2,1)S(1)}, bf16[3,256,512]{2,1,0:T(8,128)(2,1)S(1)}, u32[]{:S(2)}, u32[]{:S(2)}) %collective-permute-start.1) | collective-permute-done | bytes 786464 | tf_op jit(solution)/shard_map/ppermute | solution.py:576
  37.4 1.9 %collective-permute-start.3 = (bf16[3,256,512]{2,1,0:T(8,128)(2,1)S(1)}, bf16[3,256,512]{2,1,0:T(8,128)(2,1)S(1)}, u32[]{:S(2)}, u32[]{:S(2)}) collective-permute-start(bf16[3,256,512]{2,1,0:T(8,128)(2,1)S(1)} %add.18.refs_5_.refs_1_), channel_id=1, source_target_pairs={{0,16},{4,12},{8,24},{12,4},{16,0},{20,28},{24,8},{28,20},{1,17},{... | collective-permute-start | bytes 2359304 | tf_op jit(solution)/shard_map/ppermute | solution.py:576
  39.3 3.2 %collective-permute-done.5.refs_4_ = bf16[2,512,512]{2,1,0:T(8,128)(2,1)S(1)} collective-permute-done((bf16[2,512,512]{2,1,0:T(8,128)(2,1)S(1)}, bf16[2,512,512]{2,1,0:T(8,128)(2,1)S(1)}, u32[]{:S(2)}, u32[]{:S(2)}) %collective-permute-start.5) | collective-permute-done | bytes 1048608 | tf_op jit(solution)/shard_map/ppermute | solution.py:576
  42.5 4.0 %attend_1.1.refs_2_.refs_6_ = bf16[512,512]{1,0:T(8,128)(2,1)S(1)} custom-call(s32[4]{0:T(128)S(1)} %pad_add_fusion.refs_0_, bf16[3,2,512,512]{3,2,1,0:T(8,128)(2,1)S(1)} %copy-done.2, bf16[3,2,512,512]{3,2,1,0:T(8,128)(2,1)S(1)} %copy-done.2, bf16[3,2,512,512]{3,2,1,0:T(8,128)(2,1)S(1)} %copy-done.2, ...), custom_call_target="tpu_custom_call" | custom-call | flops 20000000000 | bytes 1 | tf_op jit(solution)/shard_map/attend_1/pallas_call | solution.py:55
  47.1 3.7 %collective-permute-done.3.refs_2_ = bf16[3,256,512]{2,1,0:T(8,128)(2,1)S(1)} collective-permute-done((bf16[3,256,512]{2,1,0:T(8,128)(2,1)S(1)}, bf16[3,256,512]{2,1,0:T(8,128)(2,1)S(1)}, u32[]{:S(2)}, u32[]{:S(2)}) %collective-permute-start.3) | collective-permute-done | bytes 786464 | tf_op jit(solution)/shard_map/ppermute | solution.py:576
  53.9 4.1 %update_1.1 = (bf16[512,512]{1,0:T(8,128)(2,1)S(1)}, bf16[3,512,512]{2,1,0:T(8,128)(2,1)}, f32[3,8,128]{2,1,0:T(8,128)S(1)}) custom-call(s32[4]{0:T(128)S(1)} %pad_add_fusion.refs_0_, bf16[3,256,512]{2,1,0:T(8,128)(2,1)S(1)} %add.19.refs_2_.refs_3_.refs_1_, bf16[3,256,512]{2,1,0:T(8,128)(2,1)S(1)} %collective-permute-done.6.refs_2_.refs_4_, ...), custom_call_target="tpu_custom_call" | custom-call | flops 20000000000 | bytes 1 | tf_op jit(solution)/shard_map/update_1/pallas_call | solution.py:55
  58.0 4.5 %collective-permute-start.10 = (bf16[512,512]{1,0:T(8,128)(2,1)S(1)}, bf16[512,512]{1,0:T(8,128)(2,1)S(1)}, u32[]{:S(2)}, u32[]{:S(2)}) collective-permute-start(bf16[512,512]{1,0:T(8,128)(2,1)S(1)} %get-tuple-element.15.refs_7_.refs_1_), channel_id=1, source_target_pairs={{0,1},{3,2},{4,5},{7,6},{8,9},{11,10},{12,13},{15,14},{16,17},{19,... | collective-permute-start | bytes 1572872 | tf_op jit(solution)/shard_map/ppermute | solution.py:576
  63.2 1.4 %copy-done.16 = bf16[3,512,512]{2,1,0:T(8,128)(2,1)S(1)} copy-done((bf16[3,512,512]{2,1,0:T(8,128)(2,1)S(1)}, bf16[3,512,512]{2,1,0:T(8,128)(2,1)}, u32[]{:S(2)}) %copy-start.16) | copy-done | bytes 1572888
  64.6 4.8 %grads_1.1 = (f32[3,256,512]{2,1,0:T(8,128)S(1)}, bf16[3,256,512]{2,1,0:T(8,128)(2,1)S(1)}) custom-call(s32[4]{0:T(128)S(1)} %pad_add_fusion.refs_0_, bf16[3,2,512,512]{3,2,1,0:T(8,128)(2,1)} %refs_2_.11, bf16[3,2,512,512]{3,2,1,0:T(8,128)(2,1)} %refs_2_.11, f32[1,2,512]{2,1,0:T(2,128)S(1)} %copy-done.12, bf16[3,512,512]{2,1,0:T(8,128)(2,1)S(1)} %copy-done.16, ...), custom_call_target="tpu_custom_call" | custom-call | flops 20000000000 | bytes 1 | tf_op jit(solution)/shard_map/grads_1/pallas_call | solution.py:55
  69.4 1.1 %copy-done.14 = f32[3,256,512]{2,1,0:T(8,128)} copy-done((f32[3,256,512]{2,1,0:T(8,128)}, f32[3,256,512]{2,1,0:T(8,128)S(1)}, u32[]{:S(2)}) %copy-start.14) | copy-done | bytes 1572888
  70.6 1.5 %edge_0.1.refs_3_ = bf16[512,512]{1,0:T(8,128)(2,1)S(1)} custom-call(s32[4]{0:T(128)S(1)} %pad_add_fusion.refs_0_, bf16[512,512]{1,0:T(8,128)(2,1)S(1)} %mixed_0.1.refs_3_.refs_1_, bf16[512,512]{1,0:T(8,128)(2,1)S(1)} %collective-permute-done.8.refs_4_.refs_2_.refs_3_, bf16[512,512]{1,0:T(8,128)(2,1)S(1)} %collective-permute-done.12.refs_3_.refs_4_, ...), custom_call_target="tpu_custom_call" | custom-call | flops 20000000000 | bytes 1 | tf_op jit(solution)/shard_map/edge_0/pallas_call | solution.py:55
  72.1 1.3 %collective-permute-start.17 = (bf16[512,512]{1,0:T(8,128)(2,1)S(1)}, bf16[512,512]{1,0:T(8,128)(2,1)S(1)}, u32[]{:S(2)}, u32[]{:S(2)}) collective-permute-start(bf16[512,512]{1,0:T(8,128)(2,1)S(1)} %edge_0.1.refs_3_), channel_id=1, source_target_pairs={{1,0},{2,3},{5,4},{6,7},{9,8},{10,11},{13,12},{14,15},{17,16},{18,... | collective-permute-start | bytes 1572872 | tf_op jit(solution)/shard_map/ppermute | solution.py:576
  74.2 1.0 collective-permute-start.15
  76.4 9.8 %collective-permute-done.15.refs_2_ = bf16[3,256,512]{2,1,0:T(8,128)(2,1)S(1)} collective-permute-done((bf16[3,256,512]{2,1,0:T(8,128)(2,1)S(1)}, bf16[3,256,512]{2,1,0:T(8,128)(2,1)S(1)}, u32[]{:S(2)}, u32[]{:S(2)}) %collective-permute-start.15) | collective-permute-done | bytes 786464 | tf_op jit(solution)/shard_map/ppermute | solution.py:576
  87.0 1.7 %collective-permute-start.16 = (bf16[3,256,512]{2,1,0:T(8,128)(2,1)S(1)}, bf16[3,256,512]{2,1,0:T(8,128)(2,1)S(1)}, u32[]{:S(2)}, u32[]{:S(2)}) collective-permute-start(bf16[3,256,512]{2,1,0:T(8,128)(2,1)S(1)} %add.21.refs_6_.refs_1_), channel_id=1, source_target_pairs={{0,16},{4,12},{8,24},{12,4},{16,0},{20,28},{24,8},{28,20},{1,17},{... | collective-permute-start | bytes 2359304 | tf_op jit(solution)/shard_map/ppermute | solution.py:576
  88.7 1.5 %edge_1_0.1.refs_8_ = bf16[512,512]{1,0:T(8,128)(2,1)S(1)} custom-call(s32[4]{0:T(128)S(1)} %pad_add_fusion.refs_0_, bf16[512,512]{1,0:T(8,128)(2,1)S(1)} %get-tuple-element.15.refs_7_.refs_1_, bf16[512,512]{1,0:T(8,128)(2,1)S(1)} %collective-permute-done.9.refs_2_, bf16[512,512]{1,0:T(8,128)(2,1)S(1)} %collective-permute-done.14.refs_3_.refs_4_, ...), custom_call_target="tpu_custom_call" | custom-call | flops 20000000000 | bytes 1 | tf_op jit(solution)/shard_map/edge_1_0/pallas_call | solution.py:55
  90.2 1.3 %collective-permute-start.18 = (bf16[512,512]{1,0:T(8,128)(2,1)S(1)}, bf16[512,512]{1,0:T(8,128)(2,1)S(1)}, u32[]{:S(2)}, u32[]{:S(2)}) collective-permute-start(bf16[512,512]{1,0:T(8,128)(2,1)S(1)} %edge_1_0.1.refs_8_), channel_id=1, source_target_pairs={{1,0},{2,3},{5,4},{6,7},{9,8},{10,11},{13,12},{14,15},{17,16},{18,... | collective-permute-start | bytes 1572872 | tf_op jit(solution)/shard_map/ppermute | solution.py:576
  91.5 3.5 %own_0.1.refs_3_ = bf16[2,512,512]{2,1,0:T(8,128)(2,1)} custom-call(s32[4]{0:T(128)S(1)} %pad_add_fusion.refs_0_, bf16[512,512]{1,0:T(8,128)(2,1)S(1)} %mixed_0.1.refs_3_.refs_1_, bf16[512,512]{1,0:T(8,128)(2,1)S(1)} %gate.4.refs_7_.refs_2_, bf16[512,512]{1,0:T(8,128)(2,1)S(1)} %collective-permute-done.8.refs_4_.refs_2_.refs_3_, ...), custom_call_target="tpu_custom_call" | custom-call | flops 20000000000 | bytes 1 | tf_op jit(solution)/shard_map/own_0/pallas_call | solution.py:55
  95.0 4.0 %collective-permute-done.16.refs_2_ = bf16[3,256,512]{2,1,0:T(8,128)(2,1)S(1)} collective-permute-done((bf16[3,256,512]{2,1,0:T(8,128)(2,1)S(1)}, bf16[3,256,512]{2,1,0:T(8,128)(2,1)S(1)}, u32[]{:S(2)}, u32[]{:S(2)}) %collective-permute-start.16) | collective-permute-done | bytes 786464 | tf_op jit(solution)/shard_map/ppermute | solution.py:576
  99.0 1.2 %copy-done.13 = bf16[2,512,512]{2,1,0:T(8,128)(2,1)S(1)} copy-done((bf16[2,512,512]{2,1,0:T(8,128)(2,1)S(1)}, bf16[2,512,512]{2,1,0:T(8,128)(2,1)}, u32[]{:S(2)}) %copy-start.13) | copy-done | bytes 1048600
  101.1 2.6 %own_1.1.refs_8_.refs_1_ = f32[512,512]{1,0:T(8,128)S(1)} custom-call(s32[4]{0:T(128)S(1)} %pad_add_fusion.refs_0_, bf16[512,512]{1,0:T(8,128)(2,1)S(1)} %get-tuple-element.15.refs_7_.refs_1_, bf16[512,512]{1,0:T(8,128)(2,1)S(1)} %collective-permute-done.9.refs_2_, bf16[512,512]{1,0:T(8,128)(2,1)S(1)} %gate.5.refs_3_, ...), custom_call_target="tpu_custom_call" | custom-call | flops 20000000000 | bytes 1 | tf_op jit(solution)/shard_map/own_1/pallas_call | solution.py:55
  103.7 4.6 %final_update.1 = (f32[2,1,512,512]{3,2,1,0:T(8,128)}, f32[1,512,512]{2,1,0:T(8,128)}, f32[8,128]{1,0:T(8,128)S(1)}) custom-call(s32[4]{0:T(128)S(1)} %pad_add_fusion.refs_0_, bf16[3,256,512]{2,1,0:T(8,128)(2,1)S(1)} %add.22.refs_7_.refs_1_, bf16[3,256,512]{2,1,0:T(8,128)(2,1)S(1)} %collective-permute-done.19.refs_2_, bf16[3,256,512]{2,1,0:T(8,128)(2,1)S(1)} %copy-done.7, ...), custom_call_target="tpu_custom_call" | custom-call | flops 20000000000 | bytes 1 | tf_op jit(solution)/shard_map/final_update/pallas_call | solution.py:55
  108.2 1.2 %collective-permute-done.18.refs_2_ = bf16[512,512]{1,0:T(8,128)(2,1)S(1)} collective-permute-done((bf16[512,512]{1,0:T(8,128)(2,1)S(1)}, bf16[512,512]{1,0:T(8,128)(2,1)S(1)}, u32[]{:S(2)}, u32[]{:S(2)}) %collective-permute-start.18) | collective-permute-done | bytes 524320 | tf_op jit(solution)/shard_map/ppermute | solution.py:576
  109.5 1.4 %finish.1 = bf16[2,512,512]{2,1,0:T(8,128)(2,1)} custom-call(s32[4]{0:T(128)S(1)} %pad_add_fusion.refs_0_, f32[512,512]{1,0:T(8,128)S(1)} %own_1.1.refs_8_.refs_1_, bf16[512,512]{1,0:T(8,128)(2,1)S(1)} %collective-permute-done.18.refs_2_, bf16[2,512,512]{2,1,0:T(8,128)(2,1)} %own_0.1.refs_3_, ...), custom_call_target="tpu_custom_call", output_to_operand_aliasing={{}: (3, {})} | custom-call | flops 20000000000 | bytes 1 | tf_op jit(solution)/shard_map/finish/pallas_call | solution.py:55
  (66 shorter events, 12.1 us)
Async XLA Ops:
  2.6 3.2 %copy-start.5 = (bf16[2,1,512,512]{3,2,1,0:T(8,128)(2,1)S(1)}, bf16[2,1,512,512]{3,2,1,0:T(8,128)(2,1)}, u32[]{:S(2)}) copy-start(bf16[2,1,512,512]{3,2,1,0:T(8,128)(2,1)} %refs_6_.9) | copy-start | bytes 3145732
  2.6 3.2 %copy-start.10 = (bf16[1,512,512]{2,1,0:T(8,128)(2,1)S(1)}, bf16[1,512,512]{2,1,0:T(8,128)(2,1)}, u32[]{:S(2)}) copy-start(bf16[1,512,512]{2,1,0:T(8,128)(2,1)} %refs_7_.3) | copy-start | bytes 1572868
  2.6 3.2 %copy-start.11 = (f32[1,2,512]{2,1,0:T(2,128)S(1)}, f32[1,2,512]{2,1,0:T(2,128)}, u32[]{:S(2)}) copy-start(f32[1,2,512]{2,1,0:T(2,128)} %refs_3_.9) | copy-start | bytes 12292
  3.2 10.0 %copy-start.3 = (bf16[2048,512]{1,0:T(8,128)(2,1)S(1)}, bf16[2048,512]{1,0:T(8,128)(2,1)}, u32[]{:S(2)}) copy-start(bf16[2048,512]{1,0:T(8,128)(2,1)} %refs_5_.9) | copy-start | bytes 6291460
  3.2 17.1 %collective-permute-start.2 = (bf16[2,512,512]{2,1,0:T(8,128)(2,1)S(1)}, bf16[2,512,512]{2,1,0:T(8,128)(2,1)S(1)}, u32[]{:S(2)}, u32[]{:S(2)}) collective-permute-start(bf16[2,512,512]{2,1,0:T(8,128)(2,1)S(1)} %pack_0.1.refs_7_), channel_id=1, source_target_pairs={{0,4},{4,8},{8,12},{12,16},{16,20},{20,24},{24,28},{1,5},{5,9},{9,... | collective-permute-start | bytes 3145736 | tf_op jit(solution)/shard_map/ppermute | solution.py:576
  10.6 6.7 %collective-permute-start = (bf16[3,256,512]{2,1,0:T(8,128)(2,1)S(1)}, bf16[3,256,512]{2,1,0:T(8,128)(2,1)S(1)}, u32[]{:S(2)}, u32[]{:S(2)}) collective-permute-start(bf16[3,256,512]{2,1,0:T(8,128)(2,1)S(1)} %get-tuple-element.14.refs_2_), channel_id=1, source_target_pairs={{0,4},{4,0},{8,12},{12,8},{16,20},{20,16},{24,28},{28,24},{1,5},{5... | collective-permute-start | bytes 2359304 | tf_op jit(solution)/shard_map/ppermute | solution.py:576
  13.8 32.6 %collective-permute-start.4 = (bf16[3,256,512]{2,1,0:T(8,128)(2,1)S(1)}, bf16[3,256,512]{2,1,0:T(8,128)(2,1)S(1)}, u32[]{:S(2)}, u32[]{:S(2)}) collective-permute-start(bf16[3,256,512]{2,1,0:T(8,128)(2,1)S(1)} %pick_parts.1.refs_3_), channel_id=1, source_target_pairs={{0,1},{3,2},{4,5},{7,6},{8,9},{11,10},{12,13},{15,14},{16,17},{19,... | collective-permute-start | bytes 2359304 | tf_op jit(solution)/shard_map/ppermute | solution.py:576
  18.1 18.6 %collective-permute-start.1 = (bf16[3,256,512]{2,1,0:T(8,128)(2,1)S(1)}, bf16[3,256,512]{2,1,0:T(8,128)(2,1)S(1)}, u32[]{:S(2)}, u32[]{:S(2)}) collective-permute-start(bf16[3,256,512]{2,1,0:T(8,128)(2,1)S(1)} %add.17.refs_3_.refs_1_), channel_id=1, source_target_pairs={{0,8},{4,20},{8,0},{12,28},{16,24},{20,4},{24,16},{28,12},{1,9},{5... | collective-permute-start | bytes 2359304 | tf_op jit(solution)/shard_map/ppermute | solution.py:576
  20.3 22.2 %collective-permute-start.5 = (bf16[2,512,512]{2,1,0:T(8,128)(2,1)S(1)}, bf16[2,512,512]{2,1,0:T(8,128)(2,1)S(1)}, u32[]{:S(2)}, u32[]{:S(2)}) collective-permute-start(bf16[2,512,512]{2,1,0:T(8,128)(2,1)S(1)} %pack_1.1.refs_8_), channel_id=1, source_target_pairs={{0,4},{4,8},{8,12},{12,16},{16,20},{20,24},{24,28},{28,0},{1,5},{5... | collective-permute-start | bytes 3145736 | tf_op jit(solution)/shard_map/ppermute | solution.py:576
  26.7 15.8 %copy-start.2 = (bf16[3,2,512,512]{3,2,1,0:T(8,128)(2,1)S(1)}, bf16[3,2,512,512]{3,2,1,0:T(8,128)(2,1)}, u32[]{:S(2)}) copy-start(bf16[3,2,512,512]{3,2,1,0:T(8,128)(2,1)} %refs_2_.11) | copy-start | bytes 9437188
  26.7 24.9 %collective-permute-start.7 = (bf16[512,512]{1,0:T(8,128)(2,1)S(1)}, bf16[512,512]{1,0:T(8,128)(2,1)S(1)}, u32[]{:S(2)}, u32[]{:S(2)}) collective-permute-start(bf16[512,512]{1,0:T(8,128)(2,1)S(1)} %mixed_0.1.refs_3_.refs_1_), channel_id=1, source_target_pairs={{0,1},{3,2},{4,5},{7,6},{8,9},{11,10},{12,13},{15,14},{16,17},{19,... | collective-permute-start | bytes 1572872 | tf_op jit(solution)/shard_map/ppermute | solution.py:576
  28.3 23.3 %collective-permute-start.8 = (bf16[512,512]{1,0:T(8,128)(2,1)S(1)}, bf16[512,512]{1,0:T(8,128)(2,1)S(1)}, u32[]{:S(2)}, u32[]{:S(2)}) collective-permute-start(bf16[512,512]{1,0:T(8,128)(2,1)S(1)} %mixed_0.1.refs_3_.refs_1_), channel_id=1, source_target_pairs={{1,2},{2,1},{5,6},{6,5},{9,10},{10,9},{13,14},{14,13},{17,18},{18,... | collective-permute-start | bytes 1572872 | tf_op jit(solution)/shard_map/ppermute | solution.py:576
  37.4 13.4 %collective-permute-start.3 = (bf16[3,256,512]{2,1,0:T(8,128)(2,1)S(1)}, bf16[3,256,512]{2,1,0:T(8,128)(2,1)S(1)}, u32[]{:S(2)}, u32[]{:S(2)}) collective-permute-start(bf16[3,256,512]{2,1,0:T(8,128)(2,1)S(1)} %add.18.refs_5_.refs_1_), channel_id=1, source_target_pairs={{0,16},{4,12},{8,24},{12,4},{16,0},{20,28},{24,8},{28,20},{1,17},{... | collective-permute-start | bytes 2359304 | tf_op jit(solution)/shard_map/ppermute | solution.py:576
  47.0 23.5 %collective-permute-start.13 = (bf16[3,256,512]{2,1,0:T(8,128)(2,1)S(1)}, bf16[3,256,512]{2,1,0:T(8,128)(2,1)S(1)}, u32[]{:S(2)}, u32[]{:S(2)}) collective-permute-start(bf16[3,256,512]{2,1,0:T(8,128)(2,1)S(1)} %gate.3.refs_3_.refs_4_), channel_id=1, source_target_pairs={{0,4},{4,0},{8,12},{12,8},{16,20},{20,16},{24,28},{28,24},{1,5},{5... | collective-permute-start | bytes 2359304 | tf_op jit(solution)/shard_map/ppermute | solution.py:576
  51.5 2.4 %copy-start.6 = (bf16[3,256,512]{2,1,0:T(8,128)(2,1)}, bf16[3,256,512]{2,1,0:T(8,128)(2,1)S(1)}, u32[]{:S(2)}) copy-start(bf16[3,256,512]{2,1,0:T(8,128)(2,1)S(1)} %add.19.refs_2_.refs_3_.refs_1_) | copy-start | bytes 2359300
  51.6 2.4 %collective-permute-start.6 = (bf16[3,256,512]{2,1,0:T(8,128)(2,1)S(1)}, bf16[3,256,512]{2,1,0:T(8,128)(2,1)S(1)}, u32[]{:S(2)}, u32[]{:S(2)}) collective-permute-start(bf16[3,256,512]{2,1,0:T(8,128)(2,1)S(1)} %add.19.refs_2_.refs_3_.refs_1_), channel_id=1, source_target_pairs={{0,4},{4,0},{8,12},{12,8},{16,20},{20,16},{24,28},{28,24},{1,5},{5... | collective-permute-start | bytes 2359304 | tf_op jit(solution)/shard_map/ppermute | solution.py:576
  52.2 11.0 %copy-start.12 = (f32[1,2,512]{2,1,0:T(2,128)S(1)}, f32[1,2,512]{2,1,0:T(2,128)}, u32[]{:S(2)}) copy-start(f32[1,2,512]{2,1,0:T(2,128)} %refs_3_.9) | copy-start | bytes 12292
  52.2 18.3 %collective-permute-start.12 = (bf16[512,512]{1,0:T(8,128)(2,1)S(1)}, bf16[512,512]{1,0:T(8,128)(2,1)S(1)}, u32[]{:S(2)}, u32[]{:S(2)}) collective-permute-start(bf16[512,512]{1,0:T(8,128)(2,1)S(1)} %gate.4.refs_7_.refs_2_), channel_id=1, source_target_pairs={{1,2},{2,1},{5,6},{6,5},{9,10},{10,9},{13,14},{14,13},{17,18},{18,... | collective-permute-start | bytes 1572872 | tf_op jit(solution)/shard_map/ppermute | solution.py:576
  53.9 4.1 %copy-start.8 = (bf16[3,256,512]{2,1,0:T(8,128)(2,1)}, bf16[3,256,512]{2,1,0:T(8,128)(2,1)S(1)}, u32[]{:S(2)}) copy-start(bf16[3,256,512]{2,1,0:T(8,128)(2,1)S(1)} %collective-permute-done.6.refs_2_.refs_4_) | copy-start | bytes 2359300
  58.0 17.2 %collective-permute-start.10 = (bf16[512,512]{1,0:T(8,128)(2,1)S(1)}, bf16[512,512]{1,0:T(8,128)(2,1)S(1)}, u32[]{:S(2)}, u32[]{:S(2)}) collective-permute-start(bf16[512,512]{1,0:T(8,128)(2,1)S(1)} %get-tuple-element.15.refs_7_.refs_1_), channel_id=1, source_target_pairs={{0,1},{3,2},{4,5},{7,6},{8,9},{11,10},{12,13},{15,14},{16,17},{19,... | collective-permute-start | bytes 1572872 | tf_op jit(solution)/shard_map/ppermute | solution.py:576
  62.5 26.2 %collective-permute-start.9 = (bf16[512,512]{1,0:T(8,128)(2,1)S(1)}, bf16[512,512]{1,0:T(8,128)(2,1)S(1)}, u32[]{:S(2)}, u32[]{:S(2)}) collective-permute-start(bf16[512,512]{1,0:T(8,128)(2,1)S(1)} %get-tuple-element.15.refs_7_.refs_1_), channel_id=1, source_target_pairs={{1,2},{2,1},{5,6},{6,5},{9,10},{10,9},{13,14},{14,13},{17,18},{18,... | collective-permute-start | bytes 1572872 | tf_op jit(solution)/shard_map/ppermute | solution.py:576
  70.5 2.9 %copy-start.15 = (f32[3,256,512]{2,1,0:T(8,128)S(1)}, f32[3,256,512]{2,1,0:T(8,128)}, u32[]{:S(2)}) copy-start(f32[3,256,512]{2,1,0:T(8,128)} %copy-done.14) | copy-start | bytes 4718596
  70.5 2.8 %collective-permute-start.11 = (bf16[3,256,512]{2,1,0:T(8,128)(2,1)S(1)}, bf16[3,256,512]{2,1,0:T(8,128)(2,1)S(1)}, u32[]{:S(2)}, u32[]{:S(2)}) collective-permute-start(bf16[3,256,512]{2,1,0:T(8,128)(2,1)S(1)} %get-tuple-element.18.refs_6_), channel_id=1, source_target_pairs={{0,4},{4,0},{8,12},{12,8},{16,20},{20,16},{24,28},{28,24},{1,5},{5... | collective-permute-start | bytes 2359304 | tf_op jit(solution)/shard_map/ppermute | solution.py:576
  72.1 19.4 %collective-permute-start.17 = (bf16[512,512]{1,0:T(8,128)(2,1)S(1)}, bf16[512,512]{1,0:T(8,128)(2,1)S(1)}, u32[]{:S(2)}, u32[]{:S(2)}) collective-permute-start(bf16[512,512]{1,0:T(8,128)(2,1)S(1)} %edge_0.1.refs_3_), channel_id=1, source_target_pairs={{1,0},{2,3},{5,4},{6,7},{9,8},{10,11},{13,12},{14,15},{17,16},{18,... | collective-permute-start | bytes 1572872 | tf_op jit(solution)/shard_map/ppermute | solution.py:576
  74.2 12.1 %collective-permute-start.15 = (bf16[3,256,512]{2,1,0:T(8,128)(2,1)S(1)}, bf16[3,256,512]{2,1,0:T(8,128)(2,1)S(1)}, u32[]{:S(2)}, u32[]{:S(2)}) collective-permute-start(bf16[3,256,512]{2,1,0:T(8,128)(2,1)S(1)} %add.20.refs_2_.refs_1_), channel_id=1, source_target_pairs={{0,8},{4,20},{8,0},{12,28},{16,24},{20,4},{24,16},{28,12},{1,9},{5... | collective-permute-start | bytes 2359304 | tf_op jit(solution)/shard_map/ppermute | solution.py:576
  75.7 13.0 %collective-permute-start.14 = (bf16[512,512]{1,0:T(8,128)(2,1)S(1)}, bf16[512,512]{1,0:T(8,128)(2,1)S(1)}, u32[]{:S(2)}, u32[]{:S(2)}) collective-permute-start(bf16[512,512]{1,0:T(8,128)(2,1)S(1)} %gate.5.refs_3_), channel_id=1, source_target_pairs={{1,2},{2,1},{5,6},{6,5},{9,10},{10,9},{13,14},{14,13},{17,18},{18,... | collective-permute-start | bytes 1572872 | tf_op jit(solution)/shard_map/ppermute | solution.py:576
  86.9 4.6 %copy-start.4 = (bf16[2,512,512]{2,1,0:T(8,128)(2,1)S(1)}, bf16[2,512,512]{2,1,0:T(8,128)(2,1)}, u32[]{:S(2)}) copy-start(bf16[2,512,512]{2,1,0:T(8,128)(2,1)} %refs_6_.8) | copy-start | bytes 3145732
  87.0 12.1 %collective-permute-start.16 = (bf16[3,256,512]{2,1,0:T(8,128)(2,1)S(1)}, bf16[3,256,512]{2,1,0:T(8,128)(2,1)S(1)}, u32[]{:S(2)}, u32[]{:S(2)}) collective-permute-start(bf16[3,256,512]{2,1,0:T(8,128)(2,1)S(1)} %add.21.refs_6_.refs_1_), channel_id=1, source_target_pairs={{0,16},{4,12},{8,24},{12,4},{16,0},{20,28},{24,8},{28,20},{1,17},{... | collective-permute-start | bytes 2359304 | tf_op jit(solution)/shard_map/ppermute | solution.py:576
  90.2 19.2 %collective-permute-start.18 = (bf16[512,512]{1,0:T(8,128)(2,1)S(1)}, bf16[512,512]{1,0:T(8,128)(2,1)S(1)}, u32[]{:S(2)}, u32[]{:S(2)}) collective-permute-start(bf16[512,512]{1,0:T(8,128)(2,1)S(1)} %edge_1_0.1.refs_8_), channel_id=1, source_target_pairs={{1,0},{2,3},{5,4},{6,7},{9,8},{10,11},{13,12},{14,15},{17,16},{18,... | collective-permute-start | bytes 1572872 | tf_op jit(solution)/shard_map/ppermute | solution.py:576
  101.0 2.7 %copy-start.7 = (bf16[3,256,512]{2,1,0:T(8,128)(2,1)S(1)}, bf16[3,256,512]{2,1,0:T(8,128)(2,1)}, u32[]{:S(2)}) copy-start(bf16[3,256,512]{2,1,0:T(8,128)(2,1)} %copy-done.6) | copy-start | bytes 2359300
  101.0 2.7 %copy-start.9 = (bf16[3,256,512]{2,1,0:T(8,128)(2,1)S(1)}, bf16[3,256,512]{2,1,0:T(8,128)(2,1)}, u32[]{:S(2)}) copy-start(bf16[3,256,512]{2,1,0:T(8,128)(2,1)} %copy-done.8) | copy-start | bytes 2359300
  101.0 2.7 %collective-permute-start.19 = (bf16[3,256,512]{2,1,0:T(8,128)(2,1)S(1)}, bf16[3,256,512]{2,1,0:T(8,128)(2,1)S(1)}, u32[]{:S(2)}, u32[]{:S(2)}) collective-permute-start(bf16[3,256,512]{2,1,0:T(8,128)(2,1)S(1)} %add.22.refs_7_.refs_1_), channel_id=1, source_target_pairs={{0,4},{4,0},{8,12},{12,8},{16,20},{20,16},{24,28},{28,24},{1,5},{5... | collective-permute-start | bytes 2359304 | tf_op jit(solution)/shard_map/ppermute | solution.py:576
  (5 other events, 8.0 us)

commit v4 on v3

--- a/solution.py
+++ b/solution.py
@@ -14,8 +14,8 @@
 MASKED = -1e30
 BF = jnp.bfloat16
 F32 = jnp.float32
-PARTS = 1
-LIMIT = 48 * 1024 * 1024
+PARTS = 2
+LIMIT = 36 * 1024 * 1024
 
 
 def mm(a, b):
@@ -44,29 +44,34 @@
     return pl.BlockSpec(shape, lambda *_: zeros)
 
 
-def call(kernel, name, scalars, inputs, specs, outs, earlier=(), scratch=(), grid=(1,), out_specs=None, aliases=None, limit=LIMIT):
-    single = not isinstance(outs, (list, tuple))
-    outs_list = [outs] if single else list(outs)
+def call(
+    kernel, name, scalars, inputs, specs, outs, earlier=(), passing=(), scratch=(), grid=(1,), out_specs=None, aliases=None
+):
+    single = not isinstance(outs, (list, tuple)) and not passing
+    outs_list = list(outs) if isinstance(outs, (list, tuple)) else [outs]
+    any_spec = pl.BlockSpec(memory_space=pl.ANY)
     first = 1 + len(inputs)
+    past = first + len(earlier) + len(passing)
 
     def ordered(*refs):
-        kernel(*refs[:first], *refs[first + len(earlier) :])
-
+        kernel(*refs[:first], *refs[past : past + len(outs_list)], *refs[past + len(outs_list) + len(passing) :])
+
+    pass_at = {first + len(earlier) + i: len(outs_list) + i for i in range(len(passing))}
     got = pl.pallas_call(
         ordered,
-        out_shape=outs_list,
+        out_shape=[*outs_list, *[like(x) for x in passing]],
         grid_spec=pltpu.PrefetchScalarGridSpec(
             num_scalar_prefetch=1,
             grid=grid,
-            in_specs=[*specs, *[pl.BlockSpec(memory_space=pl.ANY) for _ in earlier]],
-            out_specs=out_specs or [whole_out(o.shape) for o in outs_list],
+            in_specs=[*specs, *[any_spec for _ in (*earlier, *passing)]],
+            out_specs=[*(out_specs or [whole_out(o.shape) for o in outs_list]), *[any_spec for _ in passing]],
             scratch_shapes=list(scratch),
         ),
-        input_output_aliases={k + 1: v for k, v in (aliases or {}).items()},
-        compiler_params=pltpu.CompilerParams(vmem_limit_bytes=limit),
+        input_output_aliases={**{k + 1: v for k, v in (aliases or {}).items()}, **pass_at},
+        compiler_params=pltpu.CompilerParams(vmem_limit_bytes=LIMIT),
         cost_estimate=pl.CostEstimate(flops=20 * 10**9, bytes_accessed=1, transcendentals=0),
         name=name,
-    )(scalars, *inputs, *earlier)
+    )(scalars, *inputs, *earlier, *passing)
     return got[0] if single else got
 
 
@@ -216,7 +221,7 @@
     ]
 
 
-def attention_only(block, scalars, projected, halo, earlier=()):
+def attention_only(block, scalars, projected, halo, earlier=(), passing=()):
     _, _, rows, feats = projected.shape
     return call(
         functools.partial(attend_kernel, block),
@@ -226,6 +231,7 @@
         [*qkv_specs(block, projected), whole(halo)],
         jax.ShapeDtypeStruct((rows, feats), BF),
         earlier=earlier,
+        passing=passing,
     )
 
 
@@ -250,20 +256,20 @@
     return ((pl.ds(own, half), mine), (pl.ds(other, half), theirs))
 
 
-def renorm_one(old, mine, theirs, parity, put):
-    before = jnp.zeros((), F32)
+def renorm_one(old, mine, theirs, parity, put, known=None):
+    before = jnp.zeros((), F32) if known is None else known
     after = jnp.zeros((), F32)
     moved = []
     for rows, part in halves(parity, mine, theirs):
         w = old(rows).astype(F32)
         new = w - part.astype(F32)
         moved.append((rows, new))
-        before += jnp.sum(w * w)
+        if known is None:
+            before += jnp.sum(w * w)
         after += jnp.sum(new * new)
     ratio = jnp.sqrt(before) / jnp.sqrt(after + 1e-06)
     for rows, new in moved:
         put(rows, new * ratio)
-    return ratio
 
 
 def old_of(refs, i, rows):
@@ -272,18 +278,14 @@
     return refs[0][i, 0, rows, :] if i < 2 else refs[1][0, rows, :]
 
 
-def update_kernel(states, keep_state, parts, sc, mine_ref, theirs_ref, *refs):
-    old, (q_ref, att_ref, mix_ref, new_bf_ref), rest = refs[:states], refs[states : states + 4], refs[states + 4 :]
-    piece_refs, ratio_ref = rest[:parts], rest[parts]
+def update_kernel(states, pieces, sc, mine_ref, theirs_ref, *refs):
+    old, (q_ref, att_ref, mix_ref, new_bf_ref), piece_refs = refs[:states], refs[states : states + 4], refs[states + 4 :]
     for i in range(3):
 
         def put(rows, value, i=i):
             new_bf_ref[i, rows, :] = value.astype(BF)
-            if keep_state:
-                rest[parts + 1][i, rows, :] = value
-
-        ratio = renorm_one(lambda rows, i=i: old_of(old, i, rows), mine_ref[i], theirs_ref[i], sc[0], put)
-        ratio_ref[i] = jnp.full(ratio_ref.shape[1:], ratio, F32)
+
+        renorm_one(lambda rows, i=i: old_of(old, i, rows), mine_ref[i], theirs_ref[i], sc[0], put)
     rows = q_ref.shape[0]
     tile = min(TILE, rows)
     for start in range(0, rows, tile):
@@ -295,11 +297,11 @@
         piece_ref[...] = mix_ref[i * size : (i + 1) * size, :]
 
 
-def update_and_mix(block, scalars, mine, theirs, state, keep_state, projected, attended, parts, earlier=()):
+def update_and_mix(block, scalars, mine, theirs, state, projected, attended, parts, earlier=()):
     _, _, rows, feats = projected.shape
     pieces = parts if parts > 1 else 0
     got = call(
-        functools.partial(update_kernel, len(state), keep_state, pieces),
+        functools.partial(update_kernel, len(state), pieces),
         f"update_{block}",
         scalars,
         (mine, theirs, *state, projected, attended),
@@ -314,47 +316,62 @@
             jax.ShapeDtypeStruct((rows, feats), BF),
             jax.ShapeDtypeStruct((3, feats, feats), BF),
             *[jax.ShapeDtypeStruct((rows // parts, feats), BF) for _ in range(pieces)],
-            jax.ShapeDtypeStruct((3, 8, HD), F32),
-            *([jax.ShapeDtypeStruct((3, feats, feats), F32)] if keep_state else []),
-        ],
-        earlier=earlier,
-    )
-    new_state = got[-1] if keep_state else None
-    ratio = got[-2] if keep_state else got[-1]
-    return got[0], got[1], got[2 : 2 + pieces] or [got[0]], ratio, new_state
-
-
-def final_kernel(states, sc, mine_ref, theirs_ref, mine_before, theirs_before, ratio_ref, *refs):
-    old = refs[:states]
-    up_out, down_out, token, now = refs[states:]
+        ],
+        earlier=earlier,
+    )
+    return got[0], got[1], got[2:] or [got[0]]
+
+
+def state_kernel(states, sc, mine_ref, theirs_ref, *refs):
+    old, (new_ref, norm_ref) = refs[:states], refs[states:]
+    for i in range(3):
+
+        def put(rows, value, i=i):
+            new_ref[i, rows, :] = value
+
+        renorm_one(lambda rows, i=i: old_of(old, i, rows), mine_ref[i], theirs_ref[i], sc[0], put)
+        norm_ref[i] = jnp.full(norm_ref.shape[1:], jnp.sum(new_ref[i] * new_ref[i]), F32)
+
+
+def float_state(block, scalars, mine, theirs, state, earlier=()):
+    feats = mine.shape[2]
+    return call(
+        functools.partial(state_kernel, len(state)),
+        f"state_{block}",
+        scalars,
+        (mine, theirs, *state),
+        [whole(mine), whole(theirs), *[whole(a) for a in state]],
+        [jax.ShapeDtypeStruct((3, feats, feats), F32), jax.ShapeDtypeStruct((3, 8, HD), F32)],
+        earlier=earlier,
+    )
+
+
+def final_kernel(sc, mine_ref, theirs_ref, old_ref, norm_ref, up_out, down_out, token):
     token[...] = jnp.zeros_like(token)
     step = pl.program_id(0)
 
-    def run(i, out):
-        ratio = ratio_ref[i, 0:1, 0:1]
-        for rows, part in halves(sc[0], mine_before[i], theirs_before[i]):
-            now[rows, :] = (old_of(old, i, rows).astype(F32) - part.astype(F32)) * ratio
-
+    def run(out):
         def put(rows, value):
             out[rows, :] = value
 
-        renorm_one(lambda rows: now[rows, :], mine_ref[...], theirs_ref[...], sc[0], put)
-
-    for i in range(3):
-        pl.when(step == i)(functools.partial(run, i, up_out if i < 2 else down_out))
-
-
-def final_update(scalars, mine, theirs, mine_before, theirs_before, ratio, state, earlier=()):
+        renorm_one(lambda rows: old_ref[rows, :], mine_ref[...], theirs_ref[...], sc[0], put, norm_ref[0:1, 0:1])
+
+    pl.when(step < 2)(lambda: run(up_out))
+    pl.when(step == 2)(lambda: run(down_out))
+
+
+def final_update(scalars, mine, theirs, state, norms, earlier=()):
     _, half, feats = mine.shape
     return call(
-        functools.partial(final_kernel, len(state)),
+        final_kernel,
         "final_update",
         scalars,
-        (mine, theirs, mine_before, theirs_before, ratio, *state),
+        (mine, theirs, state, norms),
         [
             pl.BlockSpec((None, half, feats), lambda i, s: (i, 0, 0)),
             pl.BlockSpec((None, half, feats), lambda i, s: (i, 0, 0)),
-            *[whole(a) for a in (mine_before, theirs_before, ratio, *state)],
+            pl.BlockSpec((None, feats, feats), lambda i, s: (i, 0, 0)),
+            pl.BlockSpec((None, 8, HD), lambda i, s: (i, 0, 0)),
         ],
         [
             jax.ShapeDtypeStruct((2, 1, feats, feats), F32),
@@ -367,7 +384,6 @@
             pl.BlockSpec((8, HD), lambda i, s: (0, 0)),
         ],
         grid=(3,),
-        scratch=[pltpu.VMEM((feats, feats), F32)],
         earlier=earlier,
     )
 
@@ -411,12 +427,24 @@
     )
 
 
+def split_kernel(sc, x_ref, *piece_refs):
+    size = piece_refs[0].shape[0]
+    for i, piece_ref in enumerate(piece_refs):
+        piece_ref[...] = x_ref[i * size : (i + 1) * size, :]
+
+
+def split(scalars, x, parts, earlier):
+    rows, feats = x.shape
+    piece = jax.ShapeDtypeStruct((rows // parts, feats), BF)
+    return call(split_kernel, "split", scalars, (x,), [whole(x)], [piece] * parts, earlier=earlier)
+
+
 def add_kernel(sc, a_ref, b_ref, out_ref):
     out_ref[...] = (a_ref[...].astype(F32) + b_ref[...].astype(F32)).astype(BF)
 
 
-def add(scalars, a, b, earlier=()):
-    return call(add_kernel, "add", scalars, (a, b), [whole(a), whole(b)], like(a, BF), earlier=earlier)
+def add(scalars, a, b, earlier=(), passing=()):
+    return call(add_kernel, "add", scalars, (a, b), [whole(a), whole(b)], like(a, BF), earlier=earlier, passing=passing)
 
 
 def pack_kernel(sc, k_ref, v_ref, out_ref):
@@ -459,7 +487,7 @@
     return pl.BlockSpec((rows, feats), lambda i, s: (part, 0))
 
 
-def edge_part(name, scalars, part, m, ya, yb, v_mine, v_other, earlier=()):
+def edge_part(name, scalars, part, m, ya, yb, v_mine, v_other, earlier=(), passing=()):
     rows, feats = yb.shape
     return call(
         edge_kernel,
@@ -469,6 +497,7 @@
         [part_spec(rows, feats, part), part_spec(rows, feats, part), whole(yb), whole(v_mine), whole(v_other)],
         jax.ShapeDtypeStruct((rows, feats), BF),
         earlier=earlier,
+        passing=passing,
     )
 
 
@@ -487,7 +516,8 @@
 
 
 def own_kernel(sc, m_ref, x_ref, ya_ref, yb_ref, w_ref, hid_ref, c_ref, *refs):
-    out_ref, acc = refs[-2:]
+    out_ref, token, acc = refs[-3:]
+    token[...] = jnp.zeros_like(token)
 
     def put(value):
         acc[...] = value
@@ -509,8 +539,8 @@
             whole(c),
             *[pl.BlockSpec(memory_space=pl.ANY) for _ in so_far],
         ],
-        like(hidden_in),
-        out_specs=[pl.BlockSpec((None, rows, feats), lambda i, s: (block, 0, 0))],
+        [like(hidden_in), jax.ShapeDtypeStruct((8, HD), F32)],
+        out_specs=[pl.BlockSpec((None, rows, feats), lambda i, s: (block, 0, 0)), whole_out((8, HD))],
         aliases={7: 0} if so_far else None,
         scratch=[pltpu.VMEM((rows, feats), F32)],
         earlier=earlier,
@@ -616,78 +646,81 @@
     kv_now = pack_halo(0, scalars, projected, ctx_count - 1)
     halo = move(kv_now, "ctx", forward)
     keep, send = block_grads(0, scalars, projected, learn_rates, weights, step_scale, specs, earlier=(kv_now,))
-    v_send = pick_parts(scalars, w_out, earlier=(send,))
-    v_mine = move(v_send, "head", edge_in)
-    total = add(scalars, keep, flip(send, 0), earlier=(v_send,))
+    keep = gate(scalars, keep, earlier=(send,))
+    total = add(scalars, keep, flip(send, 0))
     received = move(total, "ctx", partners(ctx_count, 0))
     kv_now = pack_halo(1, scalars, projected, ctx_count - 1, earlier=(total,))
     halo_next = move(kv_now, "ctx", around)
-    mixed = last = mixed_first(0, scalars, projected, halo, weights, specs, earlier=(kv_now,))
-    xs = [move(mixed, "head", edge_in)]
+    mixed = mixed_first(0, scalars, projected, halo, weights, specs, earlier=(kv_now,))
+    x = move(mixed, "head", edge_in)
     ya = move(mixed, "head", middle)
+    v_send = last = pick_parts(scalars, w_out, earlier=(mixed,))
+    v_mine = move(v_send, "head", edge_in)
     so_far = ()
     for block in range(1, blocks):
-        at_end = block == blocks - 1
-        parts = PARTS if at_end else 1
         for step in range(steps):
             total = last = add(scalars, total, received, earlier=(last,))
             if step + 1 < steps:
                 received = move(total, "ctx", partners(ctx_count, step + 1))
             if step == 0:
                 attended = last = attention_only(block, scalars, projected, halo_next, earlier=(last,))
-                if block == 1:
-                    v_mine = last = gate(scalars, v_mine, earlier=(attended,))
-                    v_other = flip(v_mine, 0)
+                x = last = gate(scalars, x, earlier=(last,))
+                yb = move(x, "head", middle)
         theirs = flip(total, 0)
-        xs[0] = last = gate(scalars, xs[0], earlier=(total, last, ya))
-        yb = move(xs[0], "head", middle)
-        mixed_next, new_bf, pieces, ratio, new_state = update_and_mix(
-            block, scalars, total, theirs, state, not at_end, projected, attended, parts, earlier=(last,)
-        )
-        xs_next = [move(pieces[0], "head", edge_in)]
+        ya = last = gate(scalars, ya, earlier=(total,))
+        mixed_next, new_bf = update_and_mix(
+            block, scalars, total, theirs, state, projected, attended, 1, earlier=(last,)
+        )[:2]
+        x_next = move(mixed_next, "head", edge_in)
         ya_next = move(mixed_next, "head", middle)
-        xs_next += [move(piece, "head", edge_in) for piece in pieces[1:]]
         weights, specs = (new_bf, new_bf, new_bf), bf_spec
         keep, send = block_grads(
             block, scalars, projected, learn_rates, weights, step_scale, specs, earlier=(mixed_next,)
         )
-        c = last = edge_part(block - 1, scalars, 0, mixed, ya, yb, v_mine, v_other, earlier=(send,))
+        if block == 1:
+            v_mine = last = gate(scalars, v_mine, earlier=(send,))
+            v_other = flip(v_mine, 0)
+        else:
+            keep = last = gate(scalars, keep, earlier=(send,))
+        summed = add(scalars, keep, flip(send, 0), earlier=(last,))
+        received = move(summed, "ctx", partners(ctx_count, 0))
+        c = last = edge_part(block - 1, scalars, 0, mixed, ya, yb, v_mine, v_other, earlier=(summed,))
         c_there = move(c, "head", edge_out)
-        total_before, theirs_before = total, theirs
-        total = last = add(scalars, keep, flip(send, 0), earlier=(last,))
-        received = move(total, "ctx", partners(ctx_count, 0))
-        if not at_end:
-            kv_now = last = pack_halo(block + 1, scalars, projected, ctx_count - 1, earlier=(last,))
+        if block < blocks - 1:
+            now, norms = float_state(block, scalars, total, theirs, state, earlier=(last,))
+            kv_now = last = pack_halo(block + 1, scalars, projected, ctx_count - 1, earlier=(norms,))
             halo_next = move(kv_now, "ctx", around)
-            out = last = own_part(
-                block - 1, scalars, mixed, xs[0], ya, yb, w_out, hidden_in, c_there, so_far, earlier=(last,)
+            out, last = own_part(
+                block - 1, scalars, mixed, x, ya, yb, w_out, hidden_in, c_there, so_far, earlier=(last,)
             )
             so_far = (out,)
-            state = (new_state,)
-            mixed, xs, ya = mixed_next, xs_next, ya_next
-    ybs = []
-    for i in range(parts):
-        xs_next[i] = last = gate(scalars, xs_next[i], earlier=(last,))
-        ybs.append(move(xs_next[i], "head", middle))
+            state, total = (now,), summed
+            mixed, x, ya = mixed_next, x_next, ya_next
+    xs = split(scalars, x_next, PARTS, (last,))
+    ybs = [move(piece, "head", middle) for piece in xs]
+    now, norms = float_state(blocks - 1, scalars, total, theirs, state, earlier=(xs[0],))
+    total, last = summed, norms
     for step in range(steps):
         total = last = add(scalars, total, received, earlier=(last,))
         if step + 1 < steps:
             received = move(total, "ctx", partners(ctx_count, step + 1))
         if step == 0:
             c_last = []
-            for i in range(parts):
+            for i in range(PARTS):
                 c = last = edge_part(
                     f"{blocks - 1}_{i}", scalars, i, mixed_next, ya_next, ybs[i], v_mine, v_other, earlier=(last,)
                 )
                 c_last.append(move(c, "head", edge_out))
-            out = last = own_part(
-                blocks - 2, scalars, mixed, xs[0], ya, yb, w_out, hidden_in, c_there, so_far, earlier=(last,)
+                if i == 0:
+                    out, last = own_part(
+                        blocks - 2, scalars, mixed, x, ya, yb, w_out, hidden_in, c_there, so_far, earlier=(last,)
+                    )
+            acc = last = own_last(
+                blocks - 1, scalars, mixed_next, xs, ya_next, ybs, w_out, hidden_in, earlier=(last,)
             )
     theirs = flip(total, 0)
-    acc = own_last(blocks - 1, scalars, mixed_next, xs_next, ya_next, ybs, w_out, hidden_in, earlier=(total,))
-    up_final, down_final, token = final_update(
-        scalars, total, theirs, total_before, theirs_before, ratio, state, earlier=(acc,)
-    )
+    acc = gate(scalars, acc, earlier=(total,))
+    up_final, down_final, token = final_update(scalars, total, theirs, now, norms, earlier=(acc,))
     out = finish(blocks - 1, scalars, acc, c_last, (out,), earlier=(token,))
     return out, up_final, down_final
 

time: 112 us -> 103 us (0.920)
  waiting for transfers between devices: 30.3 us -> 20.9 us
  starting transfers between devices: 26.8 us -> 33.9 us
  local copies, waits for them, and re-layouts: 5.72 us -> 1.93 us
  Pallas kernels: 46.8 us -> 43.7 us
    ppermute x20 -> x22, waiting for transfers between devices: 30.3 us -> 20.9 us  [move(): return lax.ppermute(x, axis, pairs)]
    ppermute x20 -> x22, starting transfers between devices: 26.8 us -> 33.9 us  [move(): return lax.ppermute(x, axis, pairs)]
    unnamed x34 -> x18, local copies, waits for them, and re-layouts: 5.72 us -> 1.93 us
    pallas_call x23 -> x28, Pallas kernels: 46.8 us -> 43.7 us  [call(): pl.pallas_call(ordered, out_shape=[*outs_list, *[like(x) for x in passing...]
  transfers between devices with their start and end apart: 20 -> 22, of which waited for: 7 -> 11; matrix products, arithmetic and copies ran while one was open for 0% -> 0% of each run, Pallas kernels for 40% -> 41%
where the time goes in v4:
time: 103 us; the launch traced here: 102 us
  Pallas kernels  43.7 us (42%)
  starting transfers between devices  33.9 us (33%)
  waiting for transfers between devices  20.9 us (20%)
  local copies, waits for them, and re-layouts  1.93 us (2%)
  between operations  1.05 us (1%)
    pallas_call x28, Pallas kernels, call(): pl.pallas_call(ordered, out_shape=[*outs_list, *[like(x) for x in passing...  43.7 us
    ppermute x22, starting transfers between devices, move(): return lax.ppermute(x, axis, pairs)  33.9 us
    ppermute x22, waiting for transfers between devices, move(): return lax.ppermute(x, axis, pairs)  20.9 us
  transfers between devices with their start and end apart: 22, of which 11 were waited for; matrix products, arithmetic and copies ran while one was open for 0% of the time, Pallas kernels for 41%

profile of v4, /device:TPU:0, one launch (start us, length us, event | category | flops | bytes accessed | tf_op | source)
XLA Modules:
  0.0 101.6 jit_solution(15251130194714502017)
XLA Ops:
  0.7 1.9 %copy-done = bf16[3,2,512,512]{3,2,1,0:T(8,128)(2,1)S(1)} copy-done((bf16[3,2,512,512]{3,2,1,0:T(8,128)(2,1)S(1)}, bf16[3,2,512,512]{3,2,1,0:T(8,128)(2,1)}, u32[]{:S(2)}) %copy-start) | copy-done | bytes 3145752
  3.2 2.4 %collective-permute-start.2 = (bf16[2,512,512]{2,1,0:T(8,128)(2,1)S(1)}, bf16[2,512,512]{2,1,0:T(8,128)(2,1)S(1)}, u32[]{:S(2)}, u32[]{:S(2)}) collective-permute-start(bf16[2,512,512]{2,1,0:T(8,128)(2,1)S(1)} %pack_0.1.refs_7_), channel_id=1, source_target_pairs={{0,4},{4,8},{8,12},{12,16},{16,20},{20,24},{24,28},{1,5},{5,9},{9,... | collective-permute-start | bytes 3145736 | tf_op jit(solution)/shard_map/ppermute | solution.py:606
  5.7 3.7 %grads_0.1 = (f32[3,256,512]{2,1,0:T(8,128)S(1)}, bf16[3,256,512]{2,1,0:T(8,128)(2,1)S(1)}) custom-call(s32[4]{0:T(128)S(1)} %pad_add_fusion.refs_0_, bf16[3,2,512,512]{3,2,1,0:T(8,128)(2,1)S(1)} %copy-done, bf16[3,2,512,512]{3,2,1,0:T(8,128)(2,1)S(1)} %copy-done, f32[1,2,512]{2,1,0:T(2,128)S(1)} %copy-done.7, bf16[2,1,512,512]{3,2,1,0:T(8,128)(2,1)S(1)} %copy-done.4, ...), custom_call_target="tpu_custom_call" | custom-call | flops 20000000000 | bytes 1 | tf_op jit(solution)/shard_map/grads_0/pallas_call | solution.py:60
  9.4 2.6 %collective-permute-start = (bf16[3,256,512]{2,1,0:T(8,128)(2,1)S(1)}, bf16[3,256,512]{2,1,0:T(8,128)(2,1)S(1)}, u32[]{:S(2)}, u32[]{:S(2)}) collective-permute-start(bf16[3,256,512]{2,1,0:T(8,128)(2,1)S(1)} %get-tuple-element.19.refs_2_), channel_id=1, source_target_pairs={{0,4},{4,0},{8,12},{12,8},{16,20},{20,16},{24,28},{28,24},{1,5},{5... | collective-permute-start | bytes 2359304 | tf_op jit(solution)/shard_map/ppermute | solution.py:606
  12.6 1.4 %collective-permute-done.refs_2_ = bf16[3,256,512]{2,1,0:T(8,128)(2,1)S(1)} collective-permute-done((bf16[3,256,512]{2,1,0:T(8,128)(2,1)S(1)}, bf16[3,256,512]{2,1,0:T(8,128)(2,1)S(1)}, u32[]{:S(2)}, u32[]{:S(2)}) %collective-permute-start) | collective-permute-done | bytes 786464 | tf_op jit(solution)/shard_map/ppermute | solution.py:606
  14.7 1.6 %collective-permute-start.1 = (bf16[3,256,512]{2,1,0:T(8,128)(2,1)S(1)}, bf16[3,256,512]{2,1,0:T(8,128)(2,1)S(1)}, u32[]{:S(2)}, u32[]{:S(2)}) collective-permute-start(bf16[3,256,512]{2,1,0:T(8,128)(2,1)S(1)} %add.17.refs_3_.refs_1_), channel_id=1, source_target_pairs={{0,8},{4,20},{8,0},{12,28},{16,24},{20,4},{24,16},{28,12},{1,9},{5... | collective-permute-start | bytes 2359304 | tf_op jit(solution)/shard_map/ppermute | solution.py:606
  17.0 4.9 %mixed_0.1.refs_2_.refs_1_ = bf16[512,512]{1,0:T(8,128)(2,1)S(1)} custom-call(s32[4]{0:T(128)S(1)} %pad_add_fusion.refs_0_, bf16[3,2,512,512]{3,2,1,0:T(8,128)(2,1)S(1)} %copy-done.1, bf16[3,2,512,512]{3,2,1,0:T(8,128)(2,1)S(1)} %copy-done.1, bf16[3,2,512,512]{3,2,1,0:T(8,128)(2,1)S(1)} %copy-done.1, ...), custom_call_target="tpu_custom_call" | custom-call | flops 20000000000 | bytes 1 | tf_op jit(solution)/shard_map/mixed_0/pallas_call | solution.py:60
  22.0 3.5 %collective-permute-start.4 = (bf16[512,512]{1,0:T(8,128)(2,1)S(1)}, bf16[512,512]{1,0:T(8,128)(2,1)S(1)}, u32[]{:S(2)}, u32[]{:S(2)}) collective-permute-start(bf16[512,512]{1,0:T(8,128)(2,1)S(1)} %mixed_0.1.refs_2_.refs_1_), channel_id=1, source_target_pairs={{0,1},{3,2},{4,5},{7,6},{8,9},{11,10},{12,13},{15,14},{16,17},{19,... | collective-permute-start | bytes 1572872 | tf_op jit(solution)/shard_map/ppermute | solution.py:606
  26.8 4.1 %collective-permute-start.11 = (bf16[3,256,512]{2,1,0:T(8,128)(2,1)S(1)}, bf16[3,256,512]{2,1,0:T(8,128)(2,1)S(1)}, u32[]{:S(2)}, u32[]{:S(2)}) collective-permute-start(bf16[3,256,512]{2,1,0:T(8,128)(2,1)S(1)} %pick_parts.1.refs_3_), channel_id=1, source_target_pairs={{0,1},{3,2},{4,5},{7,6},{8,9},{11,10},{12,13},{15,14},{16,17},{19,... | collective-permute-start | bytes 2359304 | tf_op jit(solution)/shard_map/ppermute | solution.py:606
  30.9 4.3 %collective-permute-done.1.refs_2_ = bf16[3,256,512]{2,1,0:T(8,128)(2,1)S(1)} collective-permute-done((bf16[3,256,512]{2,1,0:T(8,128)(2,1)S(1)}, bf16[3,256,512]{2,1,0:T(8,128)(2,1)S(1)}, u32[]{:S(2)}, u32[]{:S(2)}) %collective-permute-start.1) | collective-permute-done | bytes 786464 | tf_op jit(solution)/shard_map/ppermute | solution.py:606
  35.9 5.4 %collective-permute-start.3 = (bf16[3,256,512]{2,1,0:T(8,128)(2,1)S(1)}, bf16[3,256,512]{2,1,0:T(8,128)(2,1)S(1)}, u32[]{:S(2)}, u32[]{:S(2)}) collective-permute-start(bf16[3,256,512]{2,1,0:T(8,128)(2,1)S(1)} %add.18.refs_5_.refs_1_), channel_id=1, source_target_pairs={{0,16},{4,12},{8,24},{12,4},{16,0},{20,28},{24,8},{28,20},{1,17},{... | collective-permute-start | bytes 2359304 | tf_op jit(solution)/shard_map/ppermute | solution.py:606
  41.3 4.0 %attend_1.1.refs_2_.refs_6_ = bf16[512,512]{1,0:T(8,128)(2,1)S(1)} custom-call(s32[4]{0:T(128)S(1)} %pad_add_fusion.refs_0_, bf16[3,2,512,512]{3,2,1,0:T(8,128)(2,1)S(1)} %copy-done.1, bf16[3,2,512,512]{3,2,1,0:T(8,128)(2,1)S(1)} %copy-done.1, bf16[3,2,512,512]{3,2,1,0:T(8,128)(2,1)S(1)} %copy-done.1, ...), custom_call_target="tpu_custom_call" | custom-call | flops 20000000000 | bytes 1 | tf_op jit(solution)/shard_map/attend_1/pallas_call | solution.py:60
  46.7 4.6 %collective-permute-done.3.refs_2_ = bf16[3,256,512]{2,1,0:T(8,128)(2,1)S(1)} collective-permute-done((bf16[3,256,512]{2,1,0:T(8,128)(2,1)S(1)}, bf16[3,256,512]{2,1,0:T(8,128)(2,1)S(1)}, u32[]{:S(2)}, u32[]{:S(2)}) %collective-permute-start.3) | collective-permute-done | bytes 786464 | tf_op jit(solution)/shard_map/ppermute | solution.py:606
  52.7 1.7 %collective-permute-done.6.refs_2_ = bf16[3,256,512]{2,1,0:T(8,128)(2,1)S(1)} collective-permute-done((bf16[3,256,512]{2,1,0:T(8,128)(2,1)S(1)}, bf16[3,256,512]{2,1,0:T(8,128)(2,1)S(1)}, u32[]{:S(2)}, u32[]{:S(2)}) %collective-permute-start.6) | collective-permute-done | bytes 786464 | tf_op jit(solution)/shard_map/ppermute | solution.py:606
  54.4 3.1 %update_1.1 = (bf16[512,512]{1,0:T(8,128)(2,1)S(1)}, bf16[3,512,512]{2,1,0:T(8,128)(2,1)S(1)}) custom-call(s32[4]{0:T(128)S(1)} %pad_add_fusion.refs_0_, bf16[3,256,512]{2,1,0:T(8,128)(2,1)S(1)} %add.19.refs_2_.refs_1_, bf16[3,256,512]{2,1,0:T(8,128)(2,1)S(1)} %collective-permute-done.6.refs_2_, bf16[2,1,512,512]{3,2,1,0:T(8,128)(2,1)S(1)} %copy-done.4, ...), custom_call_target="tpu_custom_call" | custom-call | flops 20000000000 | bytes 1 | tf_op jit(solution)/shard_map/update_1/pallas_call | solution.py:60
  57.5 1.8 %collective-permute-start.9 = (bf16[512,512]{1,0:T(8,128)(2,1)S(1)}, bf16[512,512]{1,0:T(8,128)(2,1)S(1)}, u32[]{:S(2)}, u32[]{:S(2)}) collective-permute-start(bf16[512,512]{1,0:T(8,128)(2,1)S(1)} %get-tuple-element.20.refs_7_.refs_1_), channel_id=1, source_target_pairs={{0,1},{3,2},{4,5},{7,6},{8,9},{11,10},{12,13},{15,14},{16,17},{19,... | collective-permute-start | bytes 1572872 | tf_op jit(solution)/shard_map/ppermute | solution.py:606
  60.0 3.8 %grads_1.1 = (f32[3,256,512]{2,1,0:T(8,128)S(1)}, bf16[3,256,512]{2,1,0:T(8,128)(2,1)S(1)}) custom-call(s32[4]{0:T(128)S(1)} %pad_add_fusion.refs_0_, bf16[3,2,512,512]{3,2,1,0:T(8,128)(2,1)S(1)} %copy-done.1, bf16[3,2,512,512]{3,2,1,0:T(8,128)(2,1)S(1)} %copy-done.1, f32[1,2,512]{2,1,0:T(2,128)S(1)} %copy-done.8, ...), custom_call_target="tpu_custom_call" | custom-call | flops 20000000000 | bytes 1 | tf_op jit(solution)/shard_map/grads_1/pallas_call | solution.py:60
  65.0 1.2 %collective-permute-done.13.refs_2_ = bf16[3,256,512]{2,1,0:T(8,128)(2,1)S(1)} collective-permute-done((bf16[3,256,512]{2,1,0:T(8,128)(2,1)S(1)}, bf16[3,256,512]{2,1,0:T(8,128)(2,1)S(1)}, u32[]{:S(2)}, u32[]{:S(2)}) %collective-permute-start.13) | collective-permute-done | bytes 786464 | tf_op jit(solution)/shard_map/ppermute | solution.py:606
  67.9 1.5 %edge_0.1.refs_2_ = bf16[512,512]{1,0:T(8,128)(2,1)S(1)} custom-call(s32[4]{0:T(128)S(1)} %pad_add_fusion.refs_0_, bf16[512,512]{1,0:T(8,128)(2,1)S(1)} %mixed_0.1.refs_2_.refs_1_, bf16[512,512]{1,0:T(8,128)(2,1)S(1)} %gate.7.refs_7_.refs_2_.refs_3_, bf16[512,512]{1,0:T(8,128)(2,1)S(1)} %collective-permute-done.10.refs_3_.refs_4_, ...), custom_call_target="tpu_custom_call" | custom-call | flops 20000000000 | bytes 1 | tf_op jit(solution)/shard_map/edge_0/pallas_call | solution.py:60
  69.4 1.3 %collective-permute-start.16 = (bf16[512,512]{1,0:T(8,128)(2,1)S(1)}, bf16[512,512]{1,0:T(8,128)(2,1)S(1)}, u32[]{:S(2)}, u32[]{:S(2)}) collective-permute-start(bf16[512,512]{1,0:T(8,128)(2,1)S(1)} %edge_0.1.refs_2_), channel_id=1, source_target_pairs={{1,0},{2,3},{5,4},{6,7},{9,8},{10,11},{13,12},{14,15},{17,16},{18,... | collective-permute-start | bytes 1572872 | tf_op jit(solution)/shard_map/ppermute | solution.py:606
  72.9 2.8 %state_1.1 = (f32[3,512,512]{2,1,0:T(8,128)S(1)}, f32[3,8,128]{2,1,0:T(8,128)S(1)}) custom-call(s32[4]{0:T(128)S(1)} %pad_add_fusion.refs_0_, bf16[3,256,512]{2,1,0:T(8,128)(2,1)S(1)} %add.19.refs_2_.refs_1_, bf16[3,256,512]{2,1,0:T(8,128)(2,1)S(1)} %collective-permute-done.6.refs_2_, bf16[2,1,512,512]{3,2,1,0:T(8,128)(2,1)S(1)} %copy-done.4, ...), custom_call_target="tpu_custom_call" | custom-call | flops 20000000000 | bytes 1 | tf_op jit(solution)/shard_map/state_1/pallas_call | solution.py:60
  75.8 3.2 %collective-permute-done.17.refs_2_ = bf16[3,256,512]{2,1,0:T(8,128)(2,1)S(1)} collective-permute-done((bf16[3,256,512]{2,1,0:T(8,128)(2,1)S(1)}, bf16[3,256,512]{2,1,0:T(8,128)(2,1)S(1)}, u32[]{:S(2)}, u32[]{:S(2)}) %collective-permute-start.17) | collective-permute-done | bytes 786464 | tf_op jit(solution)/shard_map/ppermute | solution.py:606
  79.7 3.0 %collective-permute-start.18 = (bf16[3,256,512]{2,1,0:T(8,128)(2,1)S(1)}, bf16[3,256,512]{2,1,0:T(8,128)(2,1)S(1)}, u32[]{:S(2)}, u32[]{:S(2)}) collective-permute-start(bf16[3,256,512]{2,1,0:T(8,128)(2,1)S(1)} %add.21.refs_6_.refs_1_), channel_id=1, source_target_pairs={{0,16},{4,12},{8,24},{12,4},{16,0},{20,28},{24,8},{28,20},{1,17},{... | collective-permute-start | bytes 2359304 | tf_op jit(solution)/shard_map/ppermute | solution.py:606
  82.7 1.1 %edge_1_0.1.refs_8_ = bf16[256,512]{1,0:T(8,128)(2,1)S(1)} custom-call(s32[4]{0:T(128)S(1)} %pad_add_fusion.refs_0_, bf16[512,512]{1,0:T(8,128)(2,1)S(1)} %get-tuple-element.20.refs_7_.refs_1_, bf16[512,512]{1,0:T(8,128)(2,1)S(1)} %collective-permute-done.8.refs_2_, bf16[256,512]{1,0:T(8,128)(2,1)S(1)} %collective-permute-done.14.refs_3_.refs_5_, ...), custom_call_target="tpu_custom_call" | custom-call | flops 20000000000 | bytes 1 | tf_op jit(solution)/shard_map/edge_1_0/pallas_call | solution.py:60
  83.8 1.3 %collective-permute-start.19 = (bf16[256,512]{1,0:T(8,128)(2,1)S(1)}, bf16[256,512]{1,0:T(8,128)(2,1)S(1)}, u32[]{:S(2)}, u32[]{:S(2)}) collective-permute-start(bf16[256,512]{1,0:T(8,128)(2,1)S(1)} %edge_1_0.1.refs_8_), channel_id=1, source_target_pairs={{1,0},{2,3},{5,4},{6,7},{9,8},{10,11},{13,12},{14,15},{17,16},{18,... | collective-permute-start | bytes 786440 | tf_op jit(solution)/shard_map/ppermute | solution.py:606
  85.3 1.9 %own_0.1 = (bf16[2,512,512]{2,1,0:T(8,128)(2,1)}, f32[8,128]{1,0:T(8,128)S(1)}) custom-call(s32[4]{0:T(128)S(1)} %pad_add_fusion.refs_0_, bf16[512,512]{1,0:T(8,128)(2,1)S(1)} %mixed_0.1.refs_2_.refs_1_, bf16[512,512]{1,0:T(8,128)(2,1)S(1)} %gate.6.refs_3_.refs_2_, bf16[512,512]{1,0:T(8,128)(2,1)S(1)} %gate.7.refs_7_.refs_2_.refs_3_, ...), custom_call_target="tpu_custom_call" | custom-call | flops 20000000000 | bytes 1 | tf_op jit(solution)/shard_map/own_0/pallas_call | solution.py:60
  88.3 1.3 %collective-permute-start.20 = (bf16[256,512]{1,0:T(8,128)(2,1)S(1)}, bf16[256,512]{1,0:T(8,128)(2,1)S(1)}, u32[]{:S(2)}, u32[]{:S(2)}) collective-permute-start(bf16[256,512]{1,0:T(8,128)(2,1)S(1)} %edge_1_1.1.refs_9_), channel_id=1, source_target_pairs={{1,0},{2,3},{5,4},{6,7},{9,8},{10,11},{13,12},{14,15},{17,16},{18,... | collective-permute-start | bytes 786440 | tf_op jit(solution)/shard_map/ppermute | solution.py:606
  89.6 1.2 %own_1.1.refs_3_.refs_1_ = f32[512,512]{1,0:T(8,128)S(1)} custom-call(s32[4]{0:T(128)S(1)} %pad_add_fusion.refs_0_, bf16[512,512]{1,0:T(8,128)(2,1)S(1)} %get-tuple-element.20.refs_7_.refs_1_, bf16[512,512]{1,0:T(8,128)(2,1)S(1)} %collective-permute-done.8.refs_2_, bf16[256,512]{1,0:T(8,128)(2,1)S(1)} %get-tuple-element.24.refs_5_.refs_3_, ...), custom_call_target="tpu_custom_call" | custom-call | flops 20000000000 | bytes 1 | tf_op jit(solution)/shard_map/own_1/pallas_call | solution.py:60
  90.7 1.9 %collective-permute-done.18.refs_2_ = bf16[3,256,512]{2,1,0:T(8,128)(2,1)S(1)} collective-permute-done((bf16[3,256,512]{2,1,0:T(8,128)(2,1)S(1)}, bf16[3,256,512]{2,1,0:T(8,128)(2,1)S(1)}, u32[]{:S(2)}, u32[]{:S(2)}) %collective-permute-start.18) | collective-permute-done | bytes 786464 | tf_op jit(solution)/shard_map/ppermute | solution.py:606
  94.0 1.7 %collective-permute-done.21.refs_2_ = bf16[3,256,512]{2,1,0:T(8,128)(2,1)S(1)} collective-permute-done((bf16[3,256,512]{2,1,0:T(8,128)(2,1)S(1)}, bf16[3,256,512]{2,1,0:T(8,128)(2,1)S(1)}, u32[]{:S(2)}, u32[]{:S(2)}) %collective-permute-start.21) | collective-permute-done | bytes 786464 | tf_op jit(solution)/shard_map/ppermute | solution.py:606
  95.7 3.8 %final_update.1 = (f32[2,1,512,512]{3,2,1,0:T(8,128)}, f32[1,512,512]{2,1,0:T(8,128)}, f32[8,128]{1,0:T(8,128)S(1)}) custom-call(s32[4]{0:T(128)S(1)} %pad_add_fusion.refs_0_, bf16[3,256,512]{2,1,0:T(8,128)(2,1)S(1)} %add.22.refs_2_.refs_1_, bf16[3,256,512]{2,1,0:T(8,128)(2,1)S(1)} %collective-permute-done.21.refs_2_, ...), custom_call_target="tpu_custom_call" | custom-call | flops 20000000000 | bytes 1 | tf_op jit(solution)/shard_map/final_update/pallas_call | solution.py:60
  100.2 1.4 %finish.1 = bf16[2,512,512]{2,1,0:T(8,128)(2,1)} custom-call(s32[4]{0:T(128)S(1)} %pad_add_fusion.refs_0_, f32[512,512]{1,0:T(8,128)S(1)} %gate.9.refs_5_.refs_1_, bf16[256,512]{1,0:T(8,128)(2,1)S(1)} %collective-permute-done.19.refs_2_, bf16[256,512]{1,0:T(8,128)(2,1)S(1)} %collective-permute-done.20.refs_3_, ...), custom_call_target="tpu_custom_call", output_to_operand_aliasing={{}: (4, {})} | custom-call | flops 20000000000 | bytes 1 | tf_op jit(solution)/shard_map/finish/pallas_call | solution.py:60
  (59 shorter events, 17.3 us)
Async XLA Ops:
  0.7 1.9 %copy-start = (bf16[3,2,512,512]{3,2,1,0:T(8,128)(2,1)S(1)}, bf16[3,2,512,512]{3,2,1,0:T(8,128)(2,1)}, u32[]{:S(2)}) copy-start(bf16[3,2,512,512]{3,2,1,0:T(8,128)(2,1)} %refs_2_.11) | copy-start | bytes 9437188
  2.6 3.1 %copy-start.4 = (bf16[2,1,512,512]{3,2,1,0:T(8,128)(2,1)S(1)}, bf16[2,1,512,512]{3,2,1,0:T(8,128)(2,1)}, u32[]{:S(2)}) copy-start(bf16[2,1,512,512]{3,2,1,0:T(8,128)(2,1)} %refs_3_.11) | copy-start | bytes 3145732
  2.6 3.1 %copy-start.6 = (bf16[1,512,512]{2,1,0:T(8,128)(2,1)S(1)}, bf16[1,512,512]{2,1,0:T(8,128)(2,1)}, u32[]{:S(2)}) copy-start(bf16[1,512,512]{2,1,0:T(8,128)(2,1)} %refs_4_.5) | copy-start | bytes 1572868
  2.6 3.1 %copy-start.7 = (f32[1,2,512]{2,1,0:T(2,128)S(1)}, f32[1,2,512]{2,1,0:T(2,128)}, u32[]{:S(2)}) copy-start(f32[1,2,512]{2,1,0:T(2,128)} %refs_3_.10) | copy-start | bytes 12292
  3.2 13.8 %collective-permute-start.2 = (bf16[2,512,512]{2,1,0:T(8,128)(2,1)S(1)}, bf16[2,512,512]{2,1,0:T(8,128)(2,1)S(1)}, u32[]{:S(2)}, u32[]{:S(2)}) collective-permute-start(bf16[2,512,512]{2,1,0:T(8,128)(2,1)S(1)} %pack_0.1.refs_7_), channel_id=1, source_target_pairs={{0,4},{4,8},{8,12},{12,16},{16,20},{20,24},{24,28},{1,5},{5,9},{9,... | collective-permute-start | bytes 3145736 | tf_op jit(solution)/shard_map/ppermute | solution.py:606
  9.4 4.5 %collective-permute-start = (bf16[3,256,512]{2,1,0:T(8,128)(2,1)S(1)}, bf16[3,256,512]{2,1,0:T(8,128)(2,1)S(1)}, u32[]{:S(2)}, u32[]{:S(2)}) collective-permute-start(bf16[3,256,512]{2,1,0:T(8,128)(2,1)S(1)} %get-tuple-element.19.refs_2_), channel_id=1, source_target_pairs={{0,4},{4,0},{8,12},{12,8},{16,20},{20,16},{24,28},{28,24},{1,5},{5... | collective-permute-start | bytes 2359304 | tf_op jit(solution)/shard_map/ppermute | solution.py:606
  12.6 3.6 %copy-start.1 = (bf16[3,2,512,512]{3,2,1,0:T(8,128)(2,1)S(1)}, bf16[3,2,512,512]{3,2,1,0:T(8,128)(2,1)}, u32[]{:S(2)}) copy-start(bf16[3,2,512,512]{3,2,1,0:T(8,128)(2,1)} %refs_2_.11) | copy-start | bytes 9437188
  14.7 20.5 %collective-permute-start.1 = (bf16[3,256,512]{2,1,0:T(8,128)(2,1)S(1)}, bf16[3,256,512]{2,1,0:T(8,128)(2,1)S(1)}, u32[]{:S(2)}, u32[]{:S(2)}) collective-permute-start(bf16[3,256,512]{2,1,0:T(8,128)(2,1)S(1)} %add.17.refs_3_.refs_1_), channel_id=1, source_target_pairs={{0,8},{4,20},{8,0},{12,28},{16,24},{20,4},{24,16},{28,12},{1,9},{5... | collective-permute-start | bytes 2359304 | tf_op jit(solution)/shard_map/ppermute | solution.py:606
  16.8 9.3 %copy-start.2 = (bf16[2048,512]{1,0:T(8,128)(2,1)S(1)}, bf16[2048,512]{1,0:T(8,128)(2,1)}, u32[]{:S(2)}) copy-start(bf16[2048,512]{1,0:T(8,128)(2,1)} %refs_7_.3) | copy-start | bytes 6291460
  16.8 24.5 %collective-permute-start.5 = (bf16[2,512,512]{2,1,0:T(8,128)(2,1)S(1)}, bf16[2,512,512]{2,1,0:T(8,128)(2,1)S(1)}, u32[]{:S(2)}, u32[]{:S(2)}) collective-permute-start(bf16[2,512,512]{2,1,0:T(8,128)(2,1)S(1)} %pack_1.1.refs_8_), channel_id=1, source_target_pairs={{0,4},{4,8},{8,12},{12,16},{16,20},{20,24},{24,28},{28,0},{1,5},{5... | collective-permute-start | bytes 3145736 | tf_op jit(solution)/shard_map/ppermute | solution.py:606
  22.0 23.3 %collective-permute-start.4 = (bf16[512,512]{1,0:T(8,128)(2,1)S(1)}, bf16[512,512]{1,0:T(8,128)(2,1)S(1)}, u32[]{:S(2)}, u32[]{:S(2)}) collective-permute-start(bf16[512,512]{1,0:T(8,128)(2,1)S(1)} %mixed_0.1.refs_2_.refs_1_), channel_id=1, source_target_pairs={{0,1},{3,2},{4,5},{7,6},{8,9},{11,10},{12,13},{15,14},{16,17},{19,... | collective-permute-start | bytes 1572872 | tf_op jit(solution)/shard_map/ppermute | solution.py:606
  25.5 26.6 %collective-permute-start.7 = (bf16[512,512]{1,0:T(8,128)(2,1)S(1)}, bf16[512,512]{1,0:T(8,128)(2,1)S(1)}, u32[]{:S(2)}, u32[]{:S(2)}) collective-permute-start(bf16[512,512]{1,0:T(8,128)(2,1)S(1)} %mixed_0.1.refs_2_.refs_1_), channel_id=1, source_target_pairs={{1,2},{2,1},{5,6},{6,5},{9,10},{10,9},{13,14},{14,13},{17,18},{18,... | collective-permute-start | bytes 1572872 | tf_op jit(solution)/shard_map/ppermute | solution.py:606
  26.8 37.2 %collective-permute-start.11 = (bf16[3,256,512]{2,1,0:T(8,128)(2,1)S(1)}, bf16[3,256,512]{2,1,0:T(8,128)(2,1)S(1)}, u32[]{:S(2)}, u32[]{:S(2)}) collective-permute-start(bf16[3,256,512]{2,1,0:T(8,128)(2,1)S(1)} %pick_parts.1.refs_3_), channel_id=1, source_target_pairs={{0,1},{3,2},{4,5},{7,6},{8,9},{11,10},{12,13},{15,14},{16,17},{19,... | collective-permute-start | bytes 2359304 | tf_op jit(solution)/shard_map/ppermute | solution.py:606
  35.9 15.4 %collective-permute-start.3 = (bf16[3,256,512]{2,1,0:T(8,128)(2,1)S(1)}, bf16[3,256,512]{2,1,0:T(8,128)(2,1)S(1)}, u32[]{:S(2)}, u32[]{:S(2)}) collective-permute-start(bf16[3,256,512]{2,1,0:T(8,128)(2,1)S(1)} %add.18.refs_5_.refs_1_), channel_id=1, source_target_pairs={{0,16},{4,12},{8,24},{12,4},{16,0},{20,28},{24,8},{28,20},{1,17},{... | collective-permute-start | bytes 2359304 | tf_op jit(solution)/shard_map/ppermute | solution.py:606
  45.8 22.1 %collective-permute-start.10 = (bf16[512,512]{1,0:T(8,128)(2,1)S(1)}, bf16[512,512]{1,0:T(8,128)(2,1)S(1)}, u32[]{:S(2)}, u32[]{:S(2)}) collective-permute-start(bf16[512,512]{1,0:T(8,128)(2,1)S(1)} %gate.6.refs_3_.refs_2_), channel_id=1, source_target_pairs={{1,2},{2,1},{5,6},{6,5},{9,10},{10,9},{13,14},{14,13},{17,18},{18,... | collective-permute-start | bytes 1572872 | tf_op jit(solution)/shard_map/ppermute | solution.py:606
  52.0 2.4 %collective-permute-start.6 = (bf16[3,256,512]{2,1,0:T(8,128)(2,1)S(1)}, bf16[3,256,512]{2,1,0:T(8,128)(2,1)S(1)}, u32[]{:S(2)}, u32[]{:S(2)}) collective-permute-start(bf16[3,256,512]{2,1,0:T(8,128)(2,1)S(1)} %add.19.refs_2_.refs_1_), channel_id=1, source_target_pairs={{0,4},{4,0},{8,12},{12,8},{16,20},{20,16},{24,28},{28,24},{1,5},{5... | collective-permute-start | bytes 2359304 | tf_op jit(solution)/shard_map/ppermute | solution.py:606
  52.6 7.4 %copy-start.8 = (f32[1,2,512]{2,1,0:T(2,128)S(1)}, f32[1,2,512]{2,1,0:T(2,128)}, u32[]{:S(2)}) copy-start(f32[1,2,512]{2,1,0:T(2,128)} %refs_3_.10) | copy-start | bytes 12292
  57.5 13.5 %collective-permute-start.9 = (bf16[512,512]{1,0:T(8,128)(2,1)S(1)}, bf16[512,512]{1,0:T(8,128)(2,1)S(1)}, u32[]{:S(2)}, u32[]{:S(2)}) collective-permute-start(bf16[512,512]{1,0:T(8,128)(2,1)S(1)} %get-tuple-element.20.refs_7_.refs_1_), channel_id=1, source_target_pairs={{0,1},{3,2},{4,5},{7,6},{8,9},{11,10},{12,13},{15,14},{16,17},{19,... | collective-permute-start | bytes 1572872 | tf_op jit(solution)/shard_map/ppermute | solution.py:606
  59.3 23.4 %collective-permute-start.8 = (bf16[512,512]{1,0:T(8,128)(2,1)S(1)}, bf16[512,512]{1,0:T(8,128)(2,1)S(1)}, u32[]{:S(2)}, u32[]{:S(2)}) collective-permute-start(bf16[512,512]{1,0:T(8,128)(2,1)S(1)} %get-tuple-element.20.refs_7_.refs_1_), channel_id=1, source_target_pairs={{1,2},{2,1},{5,6},{6,5},{9,10},{10,9},{13,14},{14,13},{17,18},{18,... | collective-permute-start | bytes 1572872 | tf_op jit(solution)/shard_map/ppermute | solution.py:606
  63.8 2.4 %collective-permute-start.13 = (bf16[3,256,512]{2,1,0:T(8,128)(2,1)S(1)}, bf16[3,256,512]{2,1,0:T(8,128)(2,1)S(1)}, u32[]{:S(2)}, u32[]{:S(2)}) collective-permute-start(bf16[3,256,512]{2,1,0:T(8,128)(2,1)S(1)} %get-tuple-element.22.refs_2_), channel_id=1, source_target_pairs={{0,4},{4,0},{8,12},{12,8},{16,20},{20,16},{24,28},{28,24},{1,5},{5... | collective-permute-start | bytes 2359304 | tf_op jit(solution)/shard_map/ppermute | solution.py:606
  64.5 3.4 %collective-permute-start.12 = (bf16[3,256,512]{2,1,0:T(8,128)(2,1)S(1)}, bf16[3,256,512]{2,1,0:T(8,128)(2,1)S(1)}, u32[]{:S(2)}, u32[]{:S(2)}) collective-permute-start(bf16[3,256,512]{2,1,0:T(8,128)(2,1)S(1)} %gate.8.refs_3_.refs_4_), channel_id=1, source_target_pairs={{0,4},{4,0},{8,12},{12,8},{16,20},{20,16},{24,28},{28,24},{1,5},{5... | collective-permute-start | bytes 2359304 | tf_op jit(solution)/shard_map/ppermute | solution.py:606
  66.9 12.1 %collective-permute-start.17 = (bf16[3,256,512]{2,1,0:T(8,128)(2,1)S(1)}, bf16[3,256,512]{2,1,0:T(8,128)(2,1)S(1)}, u32[]{:S(2)}, u32[]{:S(2)}) collective-permute-start(bf16[3,256,512]{2,1,0:T(8,128)(2,1)S(1)} %add.20.refs_6_.refs_1_), channel_id=1, source_target_pairs={{0,8},{4,20},{8,0},{12,28},{16,24},{20,4},{24,16},{28,12},{1,9},{5... | collective-permute-start | bytes 2359304 | tf_op jit(solution)/shard_map/ppermute | solution.py:606
  69.4 15.8 %collective-permute-start.16 = (bf16[512,512]{1,0:T(8,128)(2,1)S(1)}, bf16[512,512]{1,0:T(8,128)(2,1)S(1)}, u32[]{:S(2)}, u32[]{:S(2)}) collective-permute-start(bf16[512,512]{1,0:T(8,128)(2,1)S(1)} %edge_0.1.refs_2_), channel_id=1, source_target_pairs={{1,0},{2,3},{5,4},{6,7},{9,8},{10,11},{13,12},{14,15},{17,16},{18,... | collective-permute-start | bytes 1572872 | tf_op jit(solution)/shard_map/ppermute | solution.py:606
  71.5 11.2 %collective-permute-start.14 = (bf16[256,512]{1,0:T(8,128)(2,1)S(1)}, bf16[256,512]{1,0:T(8,128)(2,1)S(1)}, u32[]{:S(2)}, u32[]{:S(2)}) collective-permute-start(bf16[256,512]{1,0:T(8,128)(2,1)S(1)} %get-tuple-element.24.refs_5_.refs_3_), channel_id=1, source_target_pairs={{1,2},{2,1},{5,6},{6,5},{9,10},{10,9},{13,14},{14,13},{17,18},{18,... | collective-permute-start | bytes 786440 | tf_op jit(solution)/shard_map/ppermute | solution.py:606
  72.2 14.9 %collective-permute-start.15 = (bf16[256,512]{1,0:T(8,128)(2,1)S(1)}, bf16[256,512]{1,0:T(8,128)(2,1)S(1)}, u32[]{:S(2)}, u32[]{:S(2)}) collective-permute-start(bf16[256,512]{1,0:T(8,128)(2,1)S(1)} %get-tuple-element.25.refs_4_), channel_id=1, source_target_pairs={{1,2},{2,1},{5,6},{6,5},{9,10},{10,9},{13,14},{14,13},{17,18},{18,... | collective-permute-start | bytes 786440 | tf_op jit(solution)/shard_map/ppermute | solution.py:606
  79.6 5.6 %copy-start.3 = (bf16[2048,512]{1,0:T(8,128)(2,1)S(1)}, bf16[2048,512]{1,0:T(8,128)(2,1)}, u32[]{:S(2)}) copy-start(bf16[2048,512]{1,0:T(8,128)(2,1)} %refs_7_.3) | copy-start | bytes 6291460
  79.7 5.6 %copy-start.5 = (bf16[2,512,512]{2,1,0:T(8,128)(2,1)S(1)}, bf16[2,512,512]{2,1,0:T(8,128)(2,1)}, u32[]{:S(2)}) copy-start(bf16[2,512,512]{2,1,0:T(8,128)(2,1)} %refs_8_.1) | copy-start | bytes 3145732
  79.7 13.0 %collective-permute-start.18 = (bf16[3,256,512]{2,1,0:T(8,128)(2,1)S(1)}, bf16[3,256,512]{2,1,0:T(8,128)(2,1)S(1)}, u32[]{:S(2)}, u32[]{:S(2)}) collective-permute-start(bf16[3,256,512]{2,1,0:T(8,128)(2,1)S(1)} %add.21.refs_6_.refs_1_), channel_id=1, source_target_pairs={{0,16},{4,12},{8,24},{12,4},{16,0},{20,28},{24,8},{28,20},{1,17},{... | collective-permute-start | bytes 2359304 | tf_op jit(solution)/shard_map/ppermute | solution.py:606
  83.8 16.4 %collective-permute-start.19 = (bf16[256,512]{1,0:T(8,128)(2,1)S(1)}, bf16[256,512]{1,0:T(8,128)(2,1)S(1)}, u32[]{:S(2)}, u32[]{:S(2)}) collective-permute-start(bf16[256,512]{1,0:T(8,128)(2,1)S(1)} %edge_1_0.1.refs_8_), channel_id=1, source_target_pairs={{1,0},{2,3},{5,4},{6,7},{9,8},{10,11},{13,12},{14,15},{17,16},{18,... | collective-permute-start | bytes 786440 | tf_op jit(solution)/shard_map/ppermute | solution.py:606
  88.3 11.9 %collective-permute-start.20 = (bf16[256,512]{1,0:T(8,128)(2,1)S(1)}, bf16[256,512]{1,0:T(8,128)(2,1)S(1)}, u32[]{:S(2)}, u32[]{:S(2)}) collective-permute-start(bf16[256,512]{1,0:T(8,128)(2,1)S(1)} %edge_1_1.1.refs_9_), channel_id=1, source_target_pairs={{1,0},{2,3},{5,4},{6,7},{9,8},{10,11},{13,12},{14,15},{17,16},{18,... | collective-permute-start | bytes 786440 | tf_op jit(solution)/shard_map/ppermute | solution.py:606
  93.4 2.4 %collective-permute-start.21 = (bf16[3,256,512]{2,1,0:T(8,128)(2,1)S(1)}, bf16[3,256,512]{2,1,0:T(8,128)(2,1)S(1)}, u32[]{:S(2)}, u32[]{:S(2)}) collective-permute-start(bf16[3,256,512]{2,1,0:T(8,128)(2,1)S(1)} %add.22.refs_2_.refs_1_), channel_id=1, source_target_pairs={{0,4},{4,0},{8,12},{12,8},{16,20},{20,16},{24,28},{28,24},{1,5},{5... | collective-permute-start | bytes 2359304 | tf_op jit(solution)/shard_map/ppermute | solution.py:606

commit v5 on v4

--- a/solution.py
+++ b/solution.py
@@ -15,6 +15,9 @@
 BF = jnp.bfloat16
 F32 = jnp.float32
 PARTS = 2
+AHEAD = 1
+FAST_TILE = 256
+EDGES = [(0, 1), (1, 0), (2, 3), (3, 2)]
 LIMIT = 36 * 1024 * 1024
 
 
@@ -35,13 +38,11 @@
 
 
 def whole(array):
-    zeros = (0,) * array.ndim
-    return pl.BlockSpec(array.shape, lambda *_: zeros)
+    return pl.BlockSpec(memory_space=pltpu.VMEM)
 
 
 def whole_out(shape):
-    zeros = (0,) * len(shape)
-    return pl.BlockSpec(shape, lambda *_: zeros)
+    return pl.BlockSpec(memory_space=pltpu.VMEM)
 
 
 def call(
@@ -119,7 +120,7 @@
     _, _, rows, feats = projected.shape
     half = feats // 2
     shape = jax.ShapeDtypeStruct((3, half, feats), BF)
-    tile = min(TILE, rows)
+    tile = rows
     return call(
         functools.partial(grads_kernel, block, step_scale),
         f"grads_{block}",
@@ -138,47 +139,58 @@
     )
 
 
-def attend_rows(q, keys, values, usable):
+def window_scores(q, keys, usable):
     rows = q.shape[0]
     row_ids = lax.broadcasted_iota(jnp.int32, (rows, rows), 0)
     col_ids = lax.broadcasted_iota(jnp.int32, (rows, rows), 1)
-    scale = math.log2(math.e) / math.sqrt(HD)
     scores = []
     last = len(keys) - 1
     for i, (key, before) in enumerate(keys):
         s = mm_nt(q, key)
-        if before:
+        if before and usable is not None:
             s = s + usable
         if i == 0:
             s = jnp.where(col_ids > row_ids, s, MASKED)
         if i == last:
             s = jnp.where(col_ids <= row_ids, s, MASKED)
         scores.append(s)
-    top = functools.reduce(jnp.maximum, scores)
-    peak = jnp.max(top, axis=-1, keepdims=True) * scale
-    total = None
+    return scores
+
+
+def weigh(scores, values):
+    scale = math.log2(math.e) / math.sqrt(HD)
+    peak = jnp.max(functools.reduce(jnp.maximum, scores), axis=-1, keepdims=True) * scale
     result = None
     for s, value in zip(scores, values):
-        lifted = jnp.exp2(s * scale - peak)
-        total = lifted if total is None else total + lifted
-        part = mm(lifted.astype(BF), value)
+        lifted = jnp.exp2(s * scale - peak).astype(BF)
+        part = mm(lifted, jnp.concatenate([value, jnp.ones_like(value)], axis=1))
         result = part if result is None else result + part
-    return (result / jnp.sum(total, axis=-1, keepdims=True)).astype(BF)
+    return (result[:, :HD] / result[:, HD:]).astype(BF)
 
 
 def attend(q_ref, k_ref, v_ref, halo_ref, usable, store):
     rows, feats = q_ref.shape
     tile = min(TILE, rows)
-    for start in range(0, rows, tile):
-        for head in range(feats // HD):
-            cols = slice(head * HD, (head + 1) * HD)
-            keys, values = [], []
-            for at in range(start - WIN, start + tile, tile):
-                before = at < 0
-                where = slice(at + WIN, at + WIN + tile) if before else slice(at, at + tile)
-                keys.append(((halo_ref[0, where, cols] if before else k_ref[where, cols]), before))
-                values.append(halo_ref[1, where, cols] if before else v_ref[where, cols])
-            store(slice(start, start + tile), cols, attend_rows(q_ref[start : start + tile, cols], keys, values, usable))
+
+    def pieces(start, cols, which, own_ref):
+        for at in range(start - WIN, start + tile, tile):
+            before = at < 0
+            where = slice(at + WIN, at + WIN + tile) if before else slice(at, at + tile)
+            yield (halo_ref[which, where, cols] if before else own_ref[where, cols]), before
+
+    work = [
+        (start, slice(head * HD, (head + 1) * HD)) for start in range(0, rows, tile) for head in range(feats // HD)
+    ]
+    scored = []
+    for start, cols in work:
+        scored.append(window_scores(q_ref[start : start + tile, cols], list(pieces(start, cols, 0, k_ref)), usable))
+        if len(scored) > AHEAD:
+            at, there = work[len(scored) - 1 - AHEAD]
+            values = [value for value, _ in pieces(at, there, 1, v_ref)]
+            store(slice(at, at + tile), there, weigh(scored[len(scored) - 1 - AHEAD], values))
+    for (at, there), scores in zip(work[len(work) - AHEAD :], scored[len(work) - AHEAD :]):
+        values = [value for value, _ in pieces(at, there, 1, v_ref)]
+        store(slice(at, at + tile), there, weigh(scores, values))
 
 
 def fast_rows(q, w_one, w_three, w_two):
@@ -190,7 +202,9 @@
 
 
 def usable_bias(block, sc):
-    return jnp.where((sc[1] > 0) | (block > 0), 0.0, MASKED).astype(F32)
+    if block > 0:
+        return None
+    return jnp.where(sc[1] > 0, 0.0, MASKED).astype(F32)
 
 
 def mixed_kernel(block, sc, q_ref, k_ref, v_ref, halo_ref, w1_ref, w3_ref, w2_ref, out_ref, att):
@@ -256,20 +270,29 @@
     return ((pl.ds(own, half), mine), (pl.ds(other, half), theirs))
 
 
-def renorm_one(old, mine, theirs, parity, put, known=None):
-    before = jnp.zeros((), F32) if known is None else known
-    after = jnp.zeros((), F32)
-    moved = []
-    for rows, part in halves(parity, mine, theirs):
-        w = old(rows).astype(F32)
-        new = w - part.astype(F32)
-        moved.append((rows, new))
+def renorm_all(old, mine, theirs, parity, moved, put, known=None):
+    ratios = []
+    for i in range(3):
+        before = None if known is None else known[i, 0:1, 0:1]
+        after = None
+        for rows, part in halves(parity, mine[i], theirs[i]):
+            w = old(i, rows).astype(F32)
+            new = w - part.astype(F32)
+            moved[i, rows, :] = new
+            squares = jnp.sum(new * new, axis=0, keepdims=True)
+            after = squares if after is None else after + squares
+            if known is None:
+                squares = jnp.sum(w * w, axis=0, keepdims=True)
+                before = squares if before is None else before + squares
+        after = jnp.sum(after, axis=1, keepdims=True)
         if known is None:
-            before += jnp.sum(w * w)
-        after += jnp.sum(new * new)
-    ratio = jnp.sqrt(before) / jnp.sqrt(after + 1e-06)
-    for rows, new in moved:
-        put(rows, new * ratio)
+            before = jnp.sum(before, axis=1, keepdims=True)
+        ratios.append(jnp.sqrt(before) / jnp.sqrt(after + 1e-06))
+    for i in range(3):
+        half = mine.shape[1]
+        for start in (0, half):
+            rows = slice(start, start + half)
+            put(i, rows, moved[i, rows, :] * ratios[i])
 
 
 def old_of(refs, i, rows):
@@ -279,15 +302,15 @@
 
 
 def update_kernel(states, pieces, sc, mine_ref, theirs_ref, *refs):
+    *refs, moved = refs
     old, (q_ref, att_ref, mix_ref, new_bf_ref), piece_refs = refs[:states], refs[states : states + 4], refs[states + 4 :]
-    for i in range(3):
-
-        def put(rows, value, i=i):
-            new_bf_ref[i, rows, :] = value.astype(BF)
-
-        renorm_one(lambda rows, i=i: old_of(old, i, rows), mine_ref[i], theirs_ref[i], sc[0], put)
+
+    def put(i, rows, value):
+        new_bf_ref[i, rows, :] = value.astype(BF)
+
+    renorm_all(functools.partial(old_of, old), mine_ref, theirs_ref, sc[0], moved, put)
     rows = q_ref.shape[0]
-    tile = min(TILE, rows)
+    tile = min(FAST_TILE, rows)
     for start in range(0, rows, tile):
         at = slice(start, start + tile)
         fast = fast_rows(q_ref[at, :], new_bf_ref[0], new_bf_ref[1], new_bf_ref[2])
@@ -317,19 +340,20 @@
             jax.ShapeDtypeStruct((3, feats, feats), BF),
             *[jax.ShapeDtypeStruct((rows // parts, feats), BF) for _ in range(pieces)],
         ],
+        scratch=[pltpu.VMEM((3, *mine.shape[2:] * 2), F32)],
         earlier=earlier,
     )
     return got[0], got[1], got[2:] or [got[0]]
 
 
 def state_kernel(states, sc, mine_ref, theirs_ref, *refs):
-    old, (new_ref, norm_ref) = refs[:states], refs[states:]
+    old, (new_ref, norm_ref, moved) = refs[:states], refs[states:]
+
+    def put(i, rows, value):
+        new_ref[i, rows, :] = value
+
+    renorm_all(functools.partial(old_of, old), mine_ref, theirs_ref, sc[0], moved, put)
     for i in range(3):
-
-        def put(rows, value, i=i):
-            new_ref[i, rows, :] = value
-
-        renorm_one(lambda rows, i=i: old_of(old, i, rows), mine_ref[i], theirs_ref[i], sc[0], put)
         norm_ref[i] = jnp.full(norm_ref.shape[1:], jnp.sum(new_ref[i] * new_ref[i]), F32)
 
 
@@ -342,48 +366,49 @@
         (mine, theirs, *state),
         [whole(mine), whole(theirs), *[whole(a) for a in state]],
         [jax.ShapeDtypeStruct((3, feats, feats), F32), jax.ShapeDtypeStruct((3, 8, HD), F32)],
-        earlier=earlier,
-    )
-
-
-def final_kernel(sc, mine_ref, theirs_ref, old_ref, norm_ref, up_out, down_out, token):
+        scratch=[pltpu.VMEM((3, feats, feats), F32)],
+        earlier=earlier,
+    )
+
+
+def final_kernel(sc, mine_ref, theirs_ref, old_ref, norm_ref, up_out, down_out, token, moved, done, sems):
     token[...] = jnp.zeros_like(token)
-    step = pl.program_id(0)
-
-    def run(out):
-        def put(rows, value):
-            out[rows, :] = value
-
-        renorm_one(lambda rows: old_ref[rows, :], mine_ref[...], theirs_ref[...], sc[0], put, norm_ref[0:1, 0:1])
-
-    pl.when(step < 2)(lambda: run(up_out))
-    pl.when(step == 2)(lambda: run(down_out))
+    half = mine_ref.shape[1]
+    outs = (up_out.at[0, 0], up_out.at[1, 0], down_out.at[0])
+    copies = []
+
+    def put(i, rows, value):
+        done[i, rows, :] = value
+        part = rows.start // half
+        copy = pltpu.make_async_copy(done.at[i, rows, :], outs[i].at[rows, :], sems.at[i, part])
+        copy.start()
+        copies.append(copy)
+
+    renorm_all(lambda i, rows: old_ref[i, rows, :], mine_ref, theirs_ref, sc[0], moved, put, norm_ref)
+    for copy in copies:
+        copy.wait()
 
 
 def final_update(scalars, mine, theirs, state, norms, earlier=()):
     _, half, feats = mine.shape
+    any_spec = pl.BlockSpec(memory_space=pl.ANY)
     return call(
         final_kernel,
         "final_update",
         scalars,
         (mine, theirs, state, norms),
-        [
-            pl.BlockSpec((None, half, feats), lambda i, s: (i, 0, 0)),
-            pl.BlockSpec((None, half, feats), lambda i, s: (i, 0, 0)),
-            pl.BlockSpec((None, feats, feats), lambda i, s: (i, 0, 0)),
-            pl.BlockSpec((None, 8, HD), lambda i, s: (i, 0, 0)),
-        ],
+        [whole(mine), whole(theirs), whole(state), whole(norms)],
         [
             jax.ShapeDtypeStruct((2, 1, feats, feats), F32),
             jax.ShapeDtypeStruct((1, feats, feats), F32),
             jax.ShapeDtypeStruct((8, HD), F32),
         ],
-        out_specs=[
-            pl.BlockSpec((None, None, feats, feats), lambda i, s: (jnp.minimum(i, 1), 0, 0, 0)),
-            pl.BlockSpec((None, feats, feats), lambda i, s: (0, 0, 0)),
-            pl.BlockSpec((8, HD), lambda i, s: (0, 0)),
+        out_specs=[any_spec, any_spec, whole_out((8, HD))],
+        scratch=[
+            pltpu.VMEM((3, feats, feats), F32),
+            pltpu.VMEM((3, feats, feats), F32),
+            pltpu.SemaphoreType.DMA((3, 2)),
         ],
-        grid=(3,),
         earlier=earlier,
     )
 
@@ -501,6 +526,10 @@
     )
 
 
+def for_edge(sc, c):
+    return jnp.where(sc[3] == 0, c.astype(F32), 0.0)
+
+
 def own_rows(sc, m, x, ya, yb, w_ref, hid, put, get):
     feats = w_ref.shape[1]
     head = sc[2]
@@ -523,7 +552,7 @@
         acc[...] = value
 
     own_rows(sc, m_ref[...], x_ref, ya_ref, yb_ref, w_ref, hid_ref[...], put, lambda: acc[...])
-    out_ref[...] = (acc[...] + c_ref[...].astype(F32)).astype(BF)
+    out_ref[...] = (acc[...] + for_edge(sc, c_ref[...])).astype(BF)
 
 
 def own_part(block, scalars, m, x, ya, yb, w_out, hidden_in, c, so_far, earlier=()):
@@ -579,31 +608,47 @@
     )
 
 
-def finish_kernel(parts, sc, acc_ref, *refs):
-    out_ref = refs[-1]
+def finish_kernel(block, parts, sc, acc_ref, *refs):
+    out_ref, done, sems = refs[-3:]
     rows = acc_ref.shape[0] // parts
+    copies = []
     for i in range(parts):
-        at = pl.ds(i * rows, rows)
-        out_ref[at, :] = (acc_ref[at, :] + refs[i][...].astype(F32)).astype(BF)
+        at = slice(i * rows, (i + 1) * rows)
+        done[at, :] = (acc_ref[at, :] + for_edge(sc, refs[i][...])).astype(BF)
+        copies.append(pltpu.make_async_copy(done.at[at, :], out_ref.at[block, at, :], sems.at[i]))
+        copies[-1].start()
+    for copy in copies:
+        copy.wait()
 
 
 def finish(block, scalars, acc, cs, so_far, earlier=()):
-    rows, feats = acc.shape
-    return call(
-        functools.partial(finish_kernel, len(cs)),
+    any_spec = pl.BlockSpec(memory_space=pl.ANY)
+    return call(
+        functools.partial(finish_kernel, block, len(cs)),
         "finish",
         scalars,
-        (acc, *cs, *so_far),
-        [whole(acc), *[whole(c) for c in cs], *[pl.BlockSpec(memory_space=pl.ANY) for _ in so_far]],
-        like(so_far[0]) if so_far else None,
-        out_specs=[pl.BlockSpec((None, rows, feats), lambda i, s: (block, 0, 0))],
+        (acc, *cs, so_far),
+        [whole(acc), *[whole(c) for c in cs], any_spec],
+        like(so_far),
+        out_specs=[any_spec],
         aliases={1 + len(cs): 0},
+        scratch=[pltpu.VMEM(acc.shape, BF), pltpu.SemaphoreType.DMA((len(cs),))],
         earlier=earlier,
     )
 
 
 def move(x, axis, pairs):
     return lax.ppermute(x, axis, pairs)
+
+
+def between_inner(x):
+    count = lax.axis_size("ctx")
+    planes = lax.axis_size("head")
+    pairs = []
+    for i in range(count):
+        pairs += [(i * planes + 1, i * planes + 2), (i * planes + 2, i * planes + 1)]
+        pairs += [(i * planes + j, (i ^ 1) * planes + j) for j in (0, 3)]
+    return move(x, ("ctx", "head"), pairs)
 
 
 def flip(x, bit):
@@ -626,10 +671,8 @@
     inner = ((head == 1) | (head == 2)).astype(jnp.int32)
     scalars = jnp.stack([parity, ctx, head, inner]).astype(jnp.int32)
     step_scale = 1.0 / math.sqrt(rows * ctx_count)
-    forward = [(i, i + 1) for i in range(ctx_count - 1)]
-    around = forward + [(ctx_count - 1, 0)]
-    edge_in = [(0, 1), (3, 2)]
-    middle = [(1, 2), (2, 1)]
+    around = [(i, (i + 1) % ctx_count) for i in range(ctx_count)]
+
     up_spec = [
         pl.BlockSpec((None, None, feats, feats), lambda *_: (0, 0, 0, 0)),
         pl.BlockSpec((None, None, feats, feats), lambda *_: (1, 0, 0, 0)),
@@ -641,10 +684,9 @@
 
     weights, specs = (fast_up, fast_up, fast_down), up_spec
     state = (fast_up, fast_down)
-    edge_out = [(1, 0), (2, 3)]
 
     kv_now = pack_halo(0, scalars, projected, ctx_count - 1)
-    halo = move(kv_now, "ctx", forward)
+    halo = move(kv_now, "ctx", around)
     keep, send = block_grads(0, scalars, projected, learn_rates, weights, step_scale, specs, earlier=(kv_now,))
     keep = gate(scalars, keep, earlier=(send,))
     total = add(scalars, keep, flip(send, 0))
@@ -652,10 +694,10 @@
     kv_now = pack_halo(1, scalars, projected, ctx_count - 1, earlier=(total,))
     halo_next = move(kv_now, "ctx", around)
     mixed = mixed_first(0, scalars, projected, halo, weights, specs, earlier=(kv_now,))
-    x = move(mixed, "head", edge_in)
-    ya = move(mixed, "head", middle)
+    x = move(mixed, "head", EDGES)
+    ya = between_inner(mixed)
     v_send = last = pick_parts(scalars, w_out, earlier=(mixed,))
-    v_mine = move(v_send, "head", edge_in)
+    v_mine = move(v_send, "head", EDGES)
     so_far = ()
     for block in range(1, blocks):
         for step in range(steps):
@@ -665,14 +707,14 @@
             if step == 0:
                 attended = last = attention_only(block, scalars, projected, halo_next, earlier=(last,))
                 x = last = gate(scalars, x, earlier=(last,))
-                yb = move(x, "head", middle)
+                yb = between_inner(x)
         theirs = flip(total, 0)
         ya = last = gate(scalars, ya, earlier=(total,))
         mixed_next, new_bf = update_and_mix(
             block, scalars, total, theirs, state, projected, attended, 1, earlier=(last,)
         )[:2]
-        x_next = move(mixed_next, "head", edge_in)
-        ya_next = move(mixed_next, "head", middle)
+        x_next = move(mixed_next, "head", EDGES)
+        ya_next = between_inner(mixed_next)
         weights, specs = (new_bf, new_bf, new_bf), bf_spec
         keep, send = block_grads(
             block, scalars, projected, learn_rates, weights, step_scale, specs, earlier=(mixed_next,)
@@ -685,7 +727,7 @@
         summed = add(scalars, keep, flip(send, 0), earlier=(last,))
         received = move(summed, "ctx", partners(ctx_count, 0))
         c = last = edge_part(block - 1, scalars, 0, mixed, ya, yb, v_mine, v_other, earlier=(summed,))
-        c_there = move(c, "head", edge_out)
+        c_there = move(c, "head", EDGES)
         if block < blocks - 1:
             now, norms = float_state(block, scalars, total, theirs, state, earlier=(last,))
             kv_now = last = pack_halo(block + 1, scalars, projected, ctx_count - 1, earlier=(norms,))
@@ -696,10 +738,10 @@
             so_far = (out,)
             state, total = (now,), summed
             mixed, x, ya = mixed_next, x_next, ya_next
-    xs = split(scalars, x_next, PARTS, (last,))
-    ybs = [move(piece, "head", middle) for piece in xs]
-    now, norms = float_state(blocks - 1, scalars, total, theirs, state, earlier=(xs[0],))
-    total, last = summed, norms
+    now, norms = float_state(blocks - 1, scalars, total, theirs, state, earlier=(last,))
+    xs = split(scalars, x_next, PARTS, (norms,))
+    ybs = [between_inner(piece) for piece in xs]
+    total, last = summed, xs[0]
     for step in range(steps):
         total = last = add(scalars, total, received, earlier=(last,))
         if step + 1 < steps:
@@ -710,18 +752,14 @@
                 c = last = edge_part(
                     f"{blocks - 1}_{i}", scalars, i, mixed_next, ya_next, ybs[i], v_mine, v_other, earlier=(last,)
                 )
-                c_last.append(move(c, "head", edge_out))
-                if i == 0:
-                    out, last = own_part(
-                        blocks - 2, scalars, mixed, x, ya, yb, w_out, hidden_in, c_there, so_far, earlier=(last,)
-                    )
-            acc = last = own_last(
-                blocks - 1, scalars, mixed_next, xs, ya_next, ybs, w_out, hidden_in, earlier=(last,)
+                c_last.append(move(c, "head", EDGES))
+            out, last = own_part(
+                blocks - 2, scalars, mixed, x, ya, yb, w_out, hidden_in, c_there, so_far, earlier=(last,)
             )
     theirs = flip(total, 0)
-    acc = gate(scalars, acc, earlier=(total,))
+    acc = own_last(blocks - 1, scalars, mixed_next, xs, ya_next, ybs, w_out, hidden_in, earlier=(total,))
     up_final, down_final, token = final_update(scalars, total, theirs, now, norms, earlier=(acc,))
-    out = finish(blocks - 1, scalars, acc, c_last, (out,), earlier=(token,))
+    out = finish(blocks - 1, scalars, acc, c_last, out, earlier=(token,))
     return out, up_final, down_final
 
 

time: 103 us -> 95.1 us (0.923); the launches traced: 102 us -> 94.9 us
  Pallas kernels: 43.7 us -> 37.1 us
  starting transfers between devices: 33.9 us -> 30.7 us
  waiting for transfers between devices: 20.9 us -> 23.8 us
    pallas_call x28 -> x27, Pallas kernels: 43.7 us -> 37.1 us  [call(): pl.pallas_call(ordered, out_shape=[*outs_list, *[like(x) for x in passing...]
    ppermute x22, starting transfers between devices: 33.9 us -> 30.7 us  [move(): return lax.ppermute(x, axis, pairs)]
    ppermute x22, waiting for transfers between devices: 20.9 us -> 23.8 us  [move(): return lax.ppermute(x, axis, pairs)]
  transfers between devices with their start and end apart: 22 -> 22, of which waited for: 11 -> 8; matrix products, arithmetic and copies ran while one was open for 0% -> 0% of each run, Pallas kernels for 41% -> 37%
where the time goes in v5:
time: 95.1 us; the launch traced here: 94.9 us
  Pallas kernels  37.1 us (39%)
  starting transfers between devices  30.7 us (32%)
  waiting for transfers between devices  23.8 us (25%)
  local copies, waits for them, and re-layouts  2.16 us (2%)
  between operations  1.13 us (1%)
    pallas_call x27, Pallas kernels, call(): pl.pallas_call(ordered, out_shape=[*outs_list, *[like(x) for x in passing...  37.1 us
    ppermute x22, starting transfers between devices, move(): return lax.ppermute(x, axis, pairs)  30.7 us
    ppermute x22, waiting for transfers between devices, move(): return lax.ppermute(x, axis, pairs)  23.8 us
    unnamed x18, local copies, waits for them, and re-layouts  2.16 us
  transfers between devices with their start and end apart: 22, of which 8 were waited for; matrix products, arithmetic and copies ran while one was open for 0% of the time, Pallas kernels for 37%

profile of v5, /device:TPU:0, one launch (start us, length us, event | category | flops | bytes accessed | tf_op | source)
XLA Modules:
  0.0 94.9 jit_solution(2971136563070979500)
XLA Ops:
  0.7 1.9 %copy-done = bf16[3,2,512,512]{3,2,1,0:T(8,128)(2,1)S(1)} copy-done((bf16[3,2,512,512]{3,2,1,0:T(8,128)(2,1)S(1)}, bf16[3,2,512,512]{3,2,1,0:T(8,128)(2,1)}, u32[]{:S(2)}) %copy-start) | copy-done | bytes 3145752
  4.0 2.8 %grads_0.1 = (f32[3,256,512]{2,1,0:T(8,128)S(1)}, bf16[3,256,512]{2,1,0:T(8,128)(2,1)S(1)}) custom-call(s32[4]{0:T(128)S(1)} %pad_add_fusion.refs_0_, bf16[3,2,512,512]{3,2,1,0:T(8,128)(2,1)S(1)} %copy-done, bf16[3,2,512,512]{3,2,1,0:T(8,128)(2,1)S(1)} %copy-done, f32[1,2,512]{2,1,0:T(2,128)S(1)} %copy-done.7, bf16[2,1,512,512]{3,2,1,0:T(8,128)(2,1)S(1)} %copy-done.4, ...), custom_call_target="tpu_custom_call" | custom-call | flops 20000000000 | bytes 1 | tf_op jit(solution)/shard_map/grads_0/pallas_call | solution.py:61
  6.8 2.4 %collective-permute-start = (bf16[3,256,512]{2,1,0:T(8,128)(2,1)S(1)}, bf16[3,256,512]{2,1,0:T(8,128)(2,1)S(1)}, u32[]{:S(2)}, u32[]{:S(2)}) collective-permute-start(bf16[3,256,512]{2,1,0:T(8,128)(2,1)S(1)} %get-tuple-element.19.refs_2_), channel_id=1, source_target_pairs={{0,4},{4,0},{8,12},{12,8},{16,20},{20,16},{24,28},{28,24},{1,5},{5... | collective-permute-start | bytes 2359304 | tf_op jit(solution)/shard_map/ppermute | solution.py:641
  9.8 1.4 %collective-permute-done.refs_2_ = bf16[3,256,512]{2,1,0:T(8,128)(2,1)S(1)} collective-permute-done((bf16[3,256,512]{2,1,0:T(8,128)(2,1)S(1)}, bf16[3,256,512]{2,1,0:T(8,128)(2,1)S(1)}, u32[]{:S(2)}, u32[]{:S(2)}) %collective-permute-start) | collective-permute-done | bytes 786464 | tf_op jit(solution)/shard_map/ppermute | solution.py:641
  11.8 1.5 %collective-permute-start.1 = (bf16[3,256,512]{2,1,0:T(8,128)(2,1)S(1)}, bf16[3,256,512]{2,1,0:T(8,128)(2,1)S(1)}, u32[]{:S(2)}, u32[]{:S(2)}) collective-permute-start(bf16[3,256,512]{2,1,0:T(8,128)(2,1)S(1)} %add.17.refs_3_.refs_1_), channel_id=1, source_target_pairs={{0,8},{4,20},{8,0},{12,28},{16,24},{20,4},{24,16},{28,12},{1,9},{5... | collective-permute-start | bytes 2359304 | tf_op jit(solution)/shard_map/ppermute | solution.py:641
  14.4 7.4 %collective-permute-done.2.refs_4_ = bf16[2,512,512]{2,1,0:T(8,128)(2,1)S(1)} collective-permute-done((bf16[2,512,512]{2,1,0:T(8,128)(2,1)S(1)}, bf16[2,512,512]{2,1,0:T(8,128)(2,1)S(1)}, u32[]{:S(2)}, u32[]{:S(2)}) %collective-permute-start.2) | collective-permute-done | bytes 1048608 | tf_op jit(solution)/shard_map/ppermute | solution.py:641
  21.7 3.7 %mixed_0.1.refs_2_.refs_1_ = bf16[512,512]{1,0:T(8,128)(2,1)S(1)} custom-call(s32[4]{0:T(128)S(1)} %pad_add_fusion.refs_0_, bf16[3,2,512,512]{3,2,1,0:T(8,128)(2,1)S(1)} %copy-done.1, bf16[3,2,512,512]{3,2,1,0:T(8,128)(2,1)S(1)} %copy-done.1, bf16[3,2,512,512]{3,2,1,0:T(8,128)(2,1)S(1)} %copy-done.1, ...), custom_call_target="tpu_custom_call" | custom-call | flops 20000000000 | bytes 1 | tf_op jit(solution)/shard_map/mixed_0/pallas_call | solution.py:61
  25.5 3.1 %collective-permute-start.4 = (bf16[512,512]{1,0:T(8,128)(2,1)S(1)}, bf16[512,512]{1,0:T(8,128)(2,1)S(1)}, u32[]{:S(2)}, u32[]{:S(2)}) collective-permute-start(bf16[512,512]{1,0:T(8,128)(2,1)S(1)} %mixed_0.1.refs_2_.refs_1_), channel_id=1, source_target_pairs={{0,1},{1,0},{2,3},{3,2},{4,5},{5,4},{6,7},{7,6},{8,9},{9,8},{10,11... | collective-permute-start | bytes 1572872 | tf_op jit(solution)/shard_map/ppermute | solution.py:641
  29.2 3.2 %collective-permute-start.11 = (bf16[3,256,512]{2,1,0:T(8,128)(2,1)S(1)}, bf16[3,256,512]{2,1,0:T(8,128)(2,1)S(1)}, u32[]{:S(2)}, u32[]{:S(2)}) collective-permute-start(bf16[3,256,512]{2,1,0:T(8,128)(2,1)S(1)} %pick_parts.1.refs_3_), channel_id=1, source_target_pairs={{0,1},{1,0},{2,3},{3,2},{4,5},{5,4},{6,7},{7,6},{8,9},{9,8},{10,11... | collective-permute-start | bytes 2359304 | tf_op jit(solution)/shard_map/ppermute | solution.py:641
  33.2 2.6 %collective-permute-start.3 = (bf16[3,256,512]{2,1,0:T(8,128)(2,1)S(1)}, bf16[3,256,512]{2,1,0:T(8,128)(2,1)S(1)}, u32[]{:S(2)}, u32[]{:S(2)}) collective-permute-start(bf16[3,256,512]{2,1,0:T(8,128)(2,1)S(1)} %add.18.refs_5_.refs_1_), channel_id=1, source_target_pairs={{0,16},{4,12},{8,24},{12,4},{16,0},{20,28},{24,8},{28,20},{1,17},{... | collective-permute-start | bytes 2359304 | tf_op jit(solution)/shard_map/ppermute | solution.py:641
  35.8 3.1 %collective-permute-done.5.refs_4_ = bf16[2,512,512]{2,1,0:T(8,128)(2,1)S(1)} collective-permute-done((bf16[2,512,512]{2,1,0:T(8,128)(2,1)S(1)}, bf16[2,512,512]{2,1,0:T(8,128)(2,1)S(1)}, u32[]{:S(2)}, u32[]{:S(2)}) %collective-permute-start.5) | collective-permute-done | bytes 1048608 | tf_op jit(solution)/shard_map/ppermute | solution.py:641
  38.8 2.9 %attend_1.1.refs_2_.refs_6_ = bf16[512,512]{1,0:T(8,128)(2,1)S(1)} custom-call(s32[4]{0:T(128)S(1)} %pad_add_fusion.refs_0_, bf16[3,2,512,512]{3,2,1,0:T(8,128)(2,1)S(1)} %copy-done.1, bf16[3,2,512,512]{3,2,1,0:T(8,128)(2,1)S(1)} %copy-done.1, bf16[3,2,512,512]{3,2,1,0:T(8,128)(2,1)S(1)} %copy-done.1, ...), custom_call_target="tpu_custom_call" | custom-call | flops 20000000000 | bytes 1 | tf_op jit(solution)/shard_map/attend_1/pallas_call | solution.py:61
  42.4 4.9 %collective-permute-done.3.refs_2_ = bf16[3,256,512]{2,1,0:T(8,128)(2,1)S(1)} collective-permute-done((bf16[3,256,512]{2,1,0:T(8,128)(2,1)S(1)}, bf16[3,256,512]{2,1,0:T(8,128)(2,1)S(1)}, u32[]{:S(2)}, u32[]{:S(2)}) %collective-permute-start.3) | collective-permute-done | bytes 786464 | tf_op jit(solution)/shard_map/ppermute | solution.py:641
  49.5 1.3 %collective-permute-done.6.refs_2_ = bf16[3,256,512]{2,1,0:T(8,128)(2,1)S(1)} collective-permute-done((bf16[3,256,512]{2,1,0:T(8,128)(2,1)S(1)}, bf16[3,256,512]{2,1,0:T(8,128)(2,1)S(1)}, u32[]{:S(2)}, u32[]{:S(2)}) %collective-permute-start.6) | collective-permute-done | bytes 786464 | tf_op jit(solution)/shard_map/ppermute | solution.py:641
  50.8 2.5 %update_1.1 = (bf16[512,512]{1,0:T(8,128)(2,1)S(1)}, bf16[3,512,512]{2,1,0:T(8,128)(2,1)S(1)}) custom-call(s32[4]{0:T(128)S(1)} %pad_add_fusion.refs_0_, bf16[3,256,512]{2,1,0:T(8,128)(2,1)S(1)} %add.19.refs_2_.refs_1_, bf16[3,256,512]{2,1,0:T(8,128)(2,1)S(1)} %collective-permute-done.6.refs_2_, bf16[2,1,512,512]{3,2,1,0:T(8,128)(2,1)S(1)} %copy-done.4, ...), custom_call_target="tpu_custom_call" | custom-call | flops 20000000000 | bytes 1 | tf_op jit(solution)/shard_map/update_1/pallas_call | solution.py:61
  53.4 1.9 %collective-permute-start.9 = (bf16[512,512]{1,0:T(8,128)(2,1)S(1)}, bf16[512,512]{1,0:T(8,128)(2,1)S(1)}, u32[]{:S(2)}, u32[]{:S(2)}) collective-permute-start(bf16[512,512]{1,0:T(8,128)(2,1)S(1)} %get-tuple-element.20.refs_7_.refs_1_), channel_id=1, source_target_pairs={{0,1},{1,0},{2,3},{3,2},{4,5},{5,4},{6,7},{7,6},{8,9},{9,8},{10,11... | collective-permute-start | bytes 1572872 | tf_op jit(solution)/shard_map/ppermute | solution.py:641
  55.2 2.8 %grads_1.1 = (f32[3,256,512]{2,1,0:T(8,128)S(1)}, bf16[3,256,512]{2,1,0:T(8,128)(2,1)S(1)}) custom-call(s32[4]{0:T(128)S(1)} %pad_add_fusion.refs_0_, bf16[3,2,512,512]{3,2,1,0:T(8,128)(2,1)S(1)} %copy-done.1, bf16[3,2,512,512]{3,2,1,0:T(8,128)(2,1)S(1)} %copy-done.1, f32[1,2,512]{2,1,0:T(2,128)S(1)} %copy-done.8, ...), custom_call_target="tpu_custom_call" | custom-call | flops 20000000000 | bytes 1 | tf_op jit(solution)/shard_map/grads_1/pallas_call | solution.py:61
  59.3 1.3 %collective-permute-done.13.refs_2_ = bf16[3,256,512]{2,1,0:T(8,128)(2,1)S(1)} collective-permute-done((bf16[3,256,512]{2,1,0:T(8,128)(2,1)S(1)}, bf16[3,256,512]{2,1,0:T(8,128)(2,1)S(1)}, u32[]{:S(2)}, u32[]{:S(2)}) %collective-permute-start.13) | collective-permute-done | bytes 786464 | tf_op jit(solution)/shard_map/ppermute | solution.py:641
  61.7 1.5 %edge_0.1.refs_5_ = bf16[512,512]{1,0:T(8,128)(2,1)S(1)} custom-call(s32[4]{0:T(128)S(1)} %pad_add_fusion.refs_0_, bf16[512,512]{1,0:T(8,128)(2,1)S(1)} %mixed_0.1.refs_2_.refs_1_, bf16[512,512]{1,0:T(8,128)(2,1)S(1)} %gate.6.refs_7_.refs_2_.refs_3_, bf16[512,512]{1,0:T(8,128)(2,1)S(1)} %collective-permute-done.10.refs_3_.refs_4_, ...), custom_call_target="tpu_custom_call" | custom-call | flops 20000000000 | bytes 1 | tf_op jit(solution)/shard_map/edge_0/pallas_call | solution.py:61
  63.2 3.1 %collective-permute-start.18 = (bf16[512,512]{1,0:T(8,128)(2,1)S(1)}, bf16[512,512]{1,0:T(8,128)(2,1)S(1)}, u32[]{:S(2)}, u32[]{:S(2)}) collective-permute-start(bf16[512,512]{1,0:T(8,128)(2,1)S(1)} %edge_0.1.refs_5_), channel_id=1, source_target_pairs={{0,1},{1,0},{2,3},{3,2},{4,5},{5,4},{6,7},{7,6},{8,9},{9,8},{10,11... | collective-permute-start | bytes 1572872 | tf_op jit(solution)/shard_map/ppermute | solution.py:641
  66.3 2.2 %state_1.1 = (f32[3,512,512]{2,1,0:T(8,128)S(1)}, f32[3,8,128]{2,1,0:T(8,128)S(1)}) custom-call(s32[4]{0:T(128)S(1)} %pad_add_fusion.refs_0_, bf16[3,256,512]{2,1,0:T(8,128)(2,1)S(1)} %add.19.refs_2_.refs_1_, bf16[3,256,512]{2,1,0:T(8,128)(2,1)S(1)} %collective-permute-done.6.refs_2_, bf16[2,1,512,512]{3,2,1,0:T(8,128)(2,1)S(1)} %copy-done.4, ...), custom_call_target="tpu_custom_call" | custom-call | flops 20000000000 | bytes 1 | tf_op jit(solution)/shard_map/state_1/pallas_call | solution.py:61
  69.9 3.4 %collective-permute-done.16.refs_2_ = bf16[3,256,512]{2,1,0:T(8,128)(2,1)S(1)} collective-permute-done((bf16[3,256,512]{2,1,0:T(8,128)(2,1)S(1)}, bf16[3,256,512]{2,1,0:T(8,128)(2,1)S(1)}, u32[]{:S(2)}, u32[]{:S(2)}) %collective-permute-start.16) | collective-permute-done | bytes 786464 | tf_op jit(solution)/shard_map/ppermute | solution.py:641
  74.0 1.6 %collective-permute-start.17 = (bf16[3,256,512]{2,1,0:T(8,128)(2,1)S(1)}, bf16[3,256,512]{2,1,0:T(8,128)(2,1)S(1)}, u32[]{:S(2)}, u32[]{:S(2)}) collective-permute-start(bf16[3,256,512]{2,1,0:T(8,128)(2,1)S(1)} %add.21.refs_6_.refs_1_), channel_id=1, source_target_pairs={{0,16},{4,12},{8,24},{12,4},{16,0},{20,28},{24,8},{28,20},{1,17},{... | collective-permute-start | bytes 2359304 | tf_op jit(solution)/shard_map/ppermute | solution.py:641
  75.6 1.1 %edge_1_0.1.refs_6_ = bf16[256,512]{1,0:T(8,128)(2,1)S(1)} custom-call(s32[4]{0:T(128)S(1)} %pad_add_fusion.refs_0_, bf16[512,512]{1,0:T(8,128)(2,1)S(1)} %get-tuple-element.20.refs_7_.refs_1_, bf16[512,512]{1,0:T(8,128)(2,1)S(1)} %collective-permute-done.8.refs_2_, bf16[256,512]{1,0:T(8,128)(2,1)S(1)} %collective-permute-done.14.refs_3_.refs_5_, ...), custom_call_target="tpu_custom_call" | custom-call | flops 20000000000 | bytes 1 | tf_op jit(solution)/shard_map/edge_1_0/pallas_call | solution.py:61
  76.7 3.9 %collective-permute-start.19 = (bf16[256,512]{1,0:T(8,128)(2,1)S(1)}, bf16[256,512]{1,0:T(8,128)(2,1)S(1)}, u32[]{:S(2)}, u32[]{:S(2)}) collective-permute-start(bf16[256,512]{1,0:T(8,128)(2,1)S(1)} %edge_1_0.1.refs_6_), channel_id=1, source_target_pairs={{0,1},{1,0},{2,3},{3,2},{4,5},{5,4},{6,7},{7,6},{8,9},{9,8},{10,11... | collective-permute-start | bytes 786440 | tf_op jit(solution)/shard_map/ppermute | solution.py:641
  80.6 1.1 %edge_1_1.1.refs_8_ = bf16[256,512]{1,0:T(8,128)(2,1)S(1)} custom-call(s32[4]{0:T(128)S(1)} %pad_add_fusion.refs_0_, bf16[512,512]{1,0:T(8,128)(2,1)S(1)} %get-tuple-element.20.refs_7_.refs_1_, bf16[512,512]{1,0:T(8,128)(2,1)S(1)} %collective-permute-done.8.refs_2_, bf16[256,512]{1,0:T(8,128)(2,1)S(1)} %collective-permute-done.15.refs_3_.refs_6_, ...), custom_call_target="tpu_custom_call" | custom-call | flops 20000000000 | bytes 1 | tf_op jit(solution)/shard_map/edge_1_1/pallas_call | solution.py:61
  81.7 3.5 %collective-permute-start.20 = (bf16[256,512]{1,0:T(8,128)(2,1)S(1)}, bf16[256,512]{1,0:T(8,128)(2,1)S(1)}, u32[]{:S(2)}, u32[]{:S(2)}) collective-permute-start(bf16[256,512]{1,0:T(8,128)(2,1)S(1)} %edge_1_1.1.refs_8_), channel_id=1, source_target_pairs={{0,1},{1,0},{2,3},{3,2},{4,5},{5,4},{6,7},{7,6},{8,9},{9,8},{10,11... | collective-permute-start | bytes 786440 | tf_op jit(solution)/shard_map/ppermute | solution.py:641
  85.2 1.9 %own_0.1 = (bf16[2,512,512]{2,1,0:T(8,128)(2,1)}, f32[8,128]{1,0:T(8,128)S(1)}) custom-call(s32[4]{0:T(128)S(1)} %pad_add_fusion.refs_0_, bf16[512,512]{1,0:T(8,128)(2,1)S(1)} %mixed_0.1.refs_2_.refs_1_, bf16[512,512]{1,0:T(8,128)(2,1)S(1)} %gate.5.refs_3_.refs_2_, bf16[512,512]{1,0:T(8,128)(2,1)S(1)} %gate.6.refs_7_.refs_2_.refs_3_, ...), custom_call_target="tpu_custom_call" | custom-call | flops 20000000000 | bytes 1 | tf_op jit(solution)/shard_map/own_0/pallas_call | solution.py:61
  87.9 1.2 %own_1.1.refs_5_.refs_1_ = f32[512,512]{1,0:T(8,128)S(1)} custom-call(s32[4]{0:T(128)S(1)} %pad_add_fusion.refs_0_, bf16[512,512]{1,0:T(8,128)(2,1)S(1)} %get-tuple-element.20.refs_7_.refs_1_, bf16[512,512]{1,0:T(8,128)(2,1)S(1)} %collective-permute-done.8.refs_2_, bf16[256,512]{1,0:T(8,128)(2,1)S(1)} %get-tuple-element.25.refs_3_, ...), custom_call_target="tpu_custom_call" | custom-call | flops 20000000000 | bytes 1 | tf_op jit(solution)/shard_map/own_1/pallas_call | solution.py:61
  89.1 1.1 %collective-permute-done.21.refs_2_ = bf16[3,256,512]{2,1,0:T(8,128)(2,1)S(1)} collective-permute-done((bf16[3,256,512]{2,1,0:T(8,128)(2,1)S(1)}, bf16[3,256,512]{2,1,0:T(8,128)(2,1)S(1)}, u32[]{:S(2)}, u32[]{:S(2)}) %collective-permute-start.21) | collective-permute-done | bytes 786464 | tf_op jit(solution)/shard_map/ppermute | solution.py:641
  90.2 3.1 %final_update.1 = (f32[2,1,512,512]{3,2,1,0:T(8,128)}, f32[1,512,512]{2,1,0:T(8,128)}, f32[8,128]{1,0:T(8,128)S(1)}) custom-call(s32[4]{0:T(128)S(1)} %pad_add_fusion.refs_0_, bf16[3,256,512]{2,1,0:T(8,128)(2,1)S(1)} %add.22.refs_9_.refs_1_, bf16[3,256,512]{2,1,0:T(8,128)(2,1)S(1)} %collective-permute-done.21.refs_2_, ...), custom_call_target="tpu_custom_call" | custom-call | flops 20000000000 | bytes 1 | tf_op jit(solution)/shard_map/final_update/pallas_call | solution.py:61
  93.3 1.4 %finish.1 = bf16[2,512,512]{2,1,0:T(8,128)(2,1)} custom-call(s32[4]{0:T(128)S(1)} %pad_add_fusion.refs_0_, f32[512,512]{1,0:T(8,128)S(1)} %own_1.1.refs_5_.refs_1_, bf16[256,512]{1,0:T(8,128)(2,1)S(1)} %collective-permute-done.19.refs_2_, bf16[256,512]{1,0:T(8,128)(2,1)S(1)} %collective-permute-done.20.refs_3_, ...), custom_call_target="tpu_custom_call", output_to_operand_aliasing={{}: (4, {})} | custom-call | flops 20000000000 | bytes 1 | tf_op jit(solution)/shard_map/finish/pallas_call | solution.py:61
  (58 shorter events, 13.1 us)
Async XLA Ops:
  0.7 1.9 %copy-start = (bf16[3,2,512,512]{3,2,1,0:T(8,128)(2,1)S(1)}, bf16[3,2,512,512]{3,2,1,0:T(8,128)(2,1)}, u32[]{:S(2)}) copy-start(bf16[3,2,512,512]{3,2,1,0:T(8,128)(2,1)} %refs_2_.11) | copy-start | bytes 9437188
  2.6 1.2 %copy-start.4 = (bf16[2,1,512,512]{3,2,1,0:T(8,128)(2,1)S(1)}, bf16[2,1,512,512]{3,2,1,0:T(8,128)(2,1)}, u32[]{:S(2)}) copy-start(bf16[2,1,512,512]{3,2,1,0:T(8,128)(2,1)} %refs_3_.11) | copy-start | bytes 3145732
  2.6 1.4 %copy-start.6 = (bf16[1,512,512]{2,1,0:T(8,128)(2,1)S(1)}, bf16[1,512,512]{2,1,0:T(8,128)(2,1)}, u32[]{:S(2)}) copy-start(bf16[1,512,512]{2,1,0:T(8,128)(2,1)} %refs_4_.5) | copy-start | bytes 1572868
  2.6 1.4 %copy-start.7 = (f32[1,2,512]{2,1,0:T(2,128)S(1)}, f32[1,2,512]{2,1,0:T(2,128)}, u32[]{:S(2)}) copy-start(f32[1,2,512]{2,1,0:T(2,128)} %refs_3_.10) | copy-start | bytes 12292
  3.2 18.5 %collective-permute-start.2 = (bf16[2,512,512]{2,1,0:T(8,128)(2,1)S(1)}, bf16[2,512,512]{2,1,0:T(8,128)(2,1)S(1)}, u32[]{:S(2)}, u32[]{:S(2)}) collective-permute-start(bf16[2,512,512]{2,1,0:T(8,128)(2,1)S(1)} %pack_0.1.refs_7_), channel_id=1, source_target_pairs={{0,4},{4,8},{8,12},{12,16},{16,20},{20,24},{24,28},{28,0},{1,5},{5... | collective-permute-start | bytes 3145736 | tf_op jit(solution)/shard_map/ppermute | solution.py:641
  6.8 4.4 %collective-permute-start = (bf16[3,256,512]{2,1,0:T(8,128)(2,1)S(1)}, bf16[3,256,512]{2,1,0:T(8,128)(2,1)S(1)}, u32[]{:S(2)}, u32[]{:S(2)}) collective-permute-start(bf16[3,256,512]{2,1,0:T(8,128)(2,1)S(1)} %get-tuple-element.19.refs_2_), channel_id=1, source_target_pairs={{0,4},{4,0},{8,12},{12,8},{16,20},{20,16},{24,28},{28,24},{1,5},{5... | collective-permute-start | bytes 2359304 | tf_op jit(solution)/shard_map/ppermute | solution.py:641
  9.8 3.6 %copy-start.1 = (bf16[3,2,512,512]{3,2,1,0:T(8,128)(2,1)S(1)}, bf16[3,2,512,512]{3,2,1,0:T(8,128)(2,1)}, u32[]{:S(2)}) copy-start(bf16[3,2,512,512]{3,2,1,0:T(8,128)(2,1)} %refs_2_.11) | copy-start | bytes 9437188
  11.8 20.6 %collective-permute-start.1 = (bf16[3,256,512]{2,1,0:T(8,128)(2,1)S(1)}, bf16[3,256,512]{2,1,0:T(8,128)(2,1)S(1)}, u32[]{:S(2)}, u32[]{:S(2)}) collective-permute-start(bf16[3,256,512]{2,1,0:T(8,128)(2,1)S(1)} %add.17.refs_3_.refs_1_), channel_id=1, source_target_pairs={{0,8},{4,20},{8,0},{12,28},{16,24},{20,4},{24,16},{28,12},{1,9},{5... | collective-permute-start | bytes 2359304 | tf_op jit(solution)/shard_map/ppermute | solution.py:641
  14.0 14.6 %copy-start.2 = (bf16[2048,512]{1,0:T(8,128)(2,1)S(1)}, bf16[2048,512]{1,0:T(8,128)(2,1)}, u32[]{:S(2)}) copy-start(bf16[2048,512]{1,0:T(8,128)(2,1)} %refs_7_.3) | copy-start | bytes 6291460
  14.0 24.8 %collective-permute-start.5 = (bf16[2,512,512]{2,1,0:T(8,128)(2,1)S(1)}, bf16[2,512,512]{2,1,0:T(8,128)(2,1)S(1)}, u32[]{:S(2)}, u32[]{:S(2)}) collective-permute-start(bf16[2,512,512]{2,1,0:T(8,128)(2,1)S(1)} %pack_1.1.refs_8_), channel_id=1, source_target_pairs={{0,4},{4,8},{8,12},{12,16},{16,20},{20,24},{24,28},{28,0},{1,5},{5... | collective-permute-start | bytes 3145736 | tf_op jit(solution)/shard_map/ppermute | solution.py:641
  25.5 16.2 %collective-permute-start.4 = (bf16[512,512]{1,0:T(8,128)(2,1)S(1)}, bf16[512,512]{1,0:T(8,128)(2,1)S(1)}, u32[]{:S(2)}, u32[]{:S(2)}) collective-permute-start(bf16[512,512]{1,0:T(8,128)(2,1)S(1)} %mixed_0.1.refs_2_.refs_1_), channel_id=1, source_target_pairs={{0,1},{1,0},{2,3},{3,2},{4,5},{5,4},{6,7},{7,6},{8,9},{9,8},{10,11... | collective-permute-start | bytes 1572872 | tf_op jit(solution)/shard_map/ppermute | solution.py:641
  28.6 20.3 %collective-permute-start.7 = (bf16[512,512]{1,0:T(8,128)(2,1)S(1)}, bf16[512,512]{1,0:T(8,128)(2,1)S(1)}, u32[]{:S(2)}, u32[]{:S(2)}) collective-permute-start(bf16[512,512]{1,0:T(8,128)(2,1)S(1)} %mixed_0.1.refs_2_.refs_1_), channel_id=1, source_target_pairs={{1,2},{2,1},{0,4},{3,7},{5,6},{6,5},{4,0},{7,3},{9,10},{10,9},{8,1... | collective-permute-start | bytes 1572872 | tf_op jit(solution)/shard_map/ppermute | solution.py:641
  29.2 29.4 %collective-permute-start.11 = (bf16[3,256,512]{2,1,0:T(8,128)(2,1)S(1)}, bf16[3,256,512]{2,1,0:T(8,128)(2,1)S(1)}, u32[]{:S(2)}, u32[]{:S(2)}) collective-permute-start(bf16[3,256,512]{2,1,0:T(8,128)(2,1)S(1)} %pick_parts.1.refs_3_), channel_id=1, source_target_pairs={{0,1},{1,0},{2,3},{3,2},{4,5},{5,4},{6,7},{7,6},{8,9},{9,8},{10,11... | collective-permute-start | bytes 2359304 | tf_op jit(solution)/shard_map/ppermute | solution.py:641
  33.2 14.0 %collective-permute-start.3 = (bf16[3,256,512]{2,1,0:T(8,128)(2,1)S(1)}, bf16[3,256,512]{2,1,0:T(8,128)(2,1)S(1)}, u32[]{:S(2)}, u32[]{:S(2)}) collective-permute-start(bf16[3,256,512]{2,1,0:T(8,128)(2,1)S(1)} %add.18.refs_5_.refs_1_), channel_id=1, source_target_pairs={{0,16},{4,12},{8,24},{12,4},{16,0},{20,28},{24,8},{28,20},{1,17},{... | collective-permute-start | bytes 2359304 | tf_op jit(solution)/shard_map/ppermute | solution.py:641
  42.3 19.4 %collective-permute-start.10 = (bf16[512,512]{1,0:T(8,128)(2,1)S(1)}, bf16[512,512]{1,0:T(8,128)(2,1)S(1)}, u32[]{:S(2)}, u32[]{:S(2)}) collective-permute-start(bf16[512,512]{1,0:T(8,128)(2,1)S(1)} %gate.5.refs_3_.refs_2_), channel_id=1, source_target_pairs={{1,2},{2,1},{0,4},{3,7},{5,6},{6,5},{4,0},{7,3},{9,10},{10,9},{8,1... | collective-permute-start | bytes 1572872 | tf_op jit(solution)/shard_map/ppermute | solution.py:641
  47.9 2.9 %collective-permute-start.6 = (bf16[3,256,512]{2,1,0:T(8,128)(2,1)S(1)}, bf16[3,256,512]{2,1,0:T(8,128)(2,1)S(1)}, u32[]{:S(2)}, u32[]{:S(2)}) collective-permute-start(bf16[3,256,512]{2,1,0:T(8,128)(2,1)S(1)} %add.19.refs_2_.refs_1_), channel_id=1, source_target_pairs={{0,4},{4,0},{8,12},{12,8},{16,20},{20,16},{24,28},{28,24},{1,5},{5... | collective-permute-start | bytes 2359304 | tf_op jit(solution)/shard_map/ppermute | solution.py:641
  49.5 5.8 %copy-start.8 = (f32[1,2,512]{2,1,0:T(2,128)S(1)}, f32[1,2,512]{2,1,0:T(2,128)}, u32[]{:S(2)}) copy-start(f32[1,2,512]{2,1,0:T(2,128)} %refs_3_.10) | copy-start | bytes 12292
  53.4 15.1 %collective-permute-start.9 = (bf16[512,512]{1,0:T(8,128)(2,1)S(1)}, bf16[512,512]{1,0:T(8,128)(2,1)S(1)}, u32[]{:S(2)}, u32[]{:S(2)}) collective-permute-start(bf16[512,512]{1,0:T(8,128)(2,1)S(1)} %get-tuple-element.20.refs_7_.refs_1_), channel_id=1, source_target_pairs={{0,1},{1,0},{2,3},{3,2},{4,5},{5,4},{6,7},{7,6},{8,9},{9,8},{10,11... | collective-permute-start | bytes 1572872 | tf_op jit(solution)/shard_map/ppermute | solution.py:641
  55.2 20.4 %collective-permute-start.8 = (bf16[512,512]{1,0:T(8,128)(2,1)S(1)}, bf16[512,512]{1,0:T(8,128)(2,1)S(1)}, u32[]{:S(2)}, u32[]{:S(2)}) collective-permute-start(bf16[512,512]{1,0:T(8,128)(2,1)S(1)} %get-tuple-element.20.refs_7_.refs_1_), channel_id=1, source_target_pairs={{1,2},{2,1},{0,4},{3,7},{5,6},{6,5},{4,0},{7,3},{9,10},{10,9},{8,1... | collective-permute-start | bytes 1572872 | tf_op jit(solution)/shard_map/ppermute | solution.py:641
  58.1 2.5 %collective-permute-start.13 = (bf16[3,256,512]{2,1,0:T(8,128)(2,1)S(1)}, bf16[3,256,512]{2,1,0:T(8,128)(2,1)S(1)}, u32[]{:S(2)}, u32[]{:S(2)}) collective-permute-start(bf16[3,256,512]{2,1,0:T(8,128)(2,1)S(1)} %get-tuple-element.22.refs_2_), channel_id=1, source_target_pairs={{0,4},{4,0},{8,12},{12,8},{16,20},{20,16},{24,28},{28,24},{1,5},{5... | collective-permute-start | bytes 2359304 | tf_op jit(solution)/shard_map/ppermute | solution.py:641
  59.2 2.5 %collective-permute-start.12 = (bf16[3,256,512]{2,1,0:T(8,128)(2,1)S(1)}, bf16[3,256,512]{2,1,0:T(8,128)(2,1)S(1)}, u32[]{:S(2)}, u32[]{:S(2)}) collective-permute-start(bf16[3,256,512]{2,1,0:T(8,128)(2,1)S(1)} %gate.7.refs_3_.refs_4_), channel_id=1, source_target_pairs={{0,4},{4,0},{8,12},{12,8},{16,20},{20,16},{24,28},{28,24},{1,5},{5... | collective-permute-start | bytes 2359304 | tf_op jit(solution)/shard_map/ppermute | solution.py:641
  61.2 12.1 %collective-permute-start.16 = (bf16[3,256,512]{2,1,0:T(8,128)(2,1)S(1)}, bf16[3,256,512]{2,1,0:T(8,128)(2,1)S(1)}, u32[]{:S(2)}, u32[]{:S(2)}) collective-permute-start(bf16[3,256,512]{2,1,0:T(8,128)(2,1)S(1)} %add.20.refs_6_.refs_1_), channel_id=1, source_target_pairs={{0,8},{4,20},{8,0},{12,28},{16,24},{20,4},{24,16},{28,12},{1,9},{5... | collective-permute-start | bytes 2359304 | tf_op jit(solution)/shard_map/ppermute | solution.py:641
  63.2 22.0 %collective-permute-start.18 = (bf16[512,512]{1,0:T(8,128)(2,1)S(1)}, bf16[512,512]{1,0:T(8,128)(2,1)S(1)}, u32[]{:S(2)}, u32[]{:S(2)}) collective-permute-start(bf16[512,512]{1,0:T(8,128)(2,1)S(1)} %edge_0.1.refs_5_), channel_id=1, source_target_pairs={{0,1},{1,0},{2,3},{3,2},{4,5},{5,4},{6,7},{7,6},{8,9},{9,8},{10,11... | collective-permute-start | bytes 1572872 | tf_op jit(solution)/shard_map/ppermute | solution.py:641
  69.1 6.5 %collective-permute-start.14 = (bf16[256,512]{1,0:T(8,128)(2,1)S(1)}, bf16[256,512]{1,0:T(8,128)(2,1)S(1)}, u32[]{:S(2)}, u32[]{:S(2)}) collective-permute-start(bf16[256,512]{1,0:T(8,128)(2,1)S(1)} %get-tuple-element.25.refs_3_), channel_id=1, source_target_pairs={{1,2},{2,1},{0,4},{3,7},{5,6},{6,5},{4,0},{7,3},{9,10},{10,9},{8,1... | collective-permute-start | bytes 786440 | tf_op jit(solution)/shard_map/ppermute | solution.py:641
  69.9 10.7 %collective-permute-start.15 = (bf16[256,512]{1,0:T(8,128)(2,1)S(1)}, bf16[256,512]{1,0:T(8,128)(2,1)S(1)}, u32[]{:S(2)}, u32[]{:S(2)}) collective-permute-start(bf16[256,512]{1,0:T(8,128)(2,1)S(1)} %get-tuple-element.26.refs_4_), channel_id=1, source_target_pairs={{1,2},{2,1},{0,4},{3,7},{5,6},{6,5},{4,0},{7,3},{9,10},{10,9},{8,1... | collective-permute-start | bytes 786440 | tf_op jit(solution)/shard_map/ppermute | solution.py:641
  74.0 13.1 %collective-permute-start.17 = (bf16[3,256,512]{2,1,0:T(8,128)(2,1)S(1)}, bf16[3,256,512]{2,1,0:T(8,128)(2,1)S(1)}, u32[]{:S(2)}, u32[]{:S(2)}) collective-permute-start(bf16[3,256,512]{2,1,0:T(8,128)(2,1)S(1)} %add.21.refs_6_.refs_1_), channel_id=1, source_target_pairs={{0,16},{4,12},{8,24},{12,4},{16,0},{20,28},{24,8},{28,20},{1,17},{... | collective-permute-start | bytes 2359304 | tf_op jit(solution)/shard_map/ppermute | solution.py:641
  76.7 8.5 %copy-start.3 = (bf16[2048,512]{1,0:T(8,128)(2,1)S(1)}, bf16[2048,512]{1,0:T(8,128)(2,1)}, u32[]{:S(2)}) copy-start(bf16[2048,512]{1,0:T(8,128)(2,1)} %refs_7_.3) | copy-start | bytes 6291460
  76.7 8.5 %copy-start.5 = (bf16[2,512,512]{2,1,0:T(8,128)(2,1)S(1)}, bf16[2,512,512]{2,1,0:T(8,128)(2,1)}, u32[]{:S(2)}) copy-start(bf16[2,512,512]{2,1,0:T(8,128)(2,1)} %refs_8_.1) | copy-start | bytes 3145732
  76.7 16.6 %collective-permute-start.19 = (bf16[256,512]{1,0:T(8,128)(2,1)S(1)}, bf16[256,512]{1,0:T(8,128)(2,1)S(1)}, u32[]{:S(2)}, u32[]{:S(2)}) collective-permute-start(bf16[256,512]{1,0:T(8,128)(2,1)S(1)} %edge_1_0.1.refs_6_), channel_id=1, source_target_pairs={{0,1},{1,0},{2,3},{3,2},{4,5},{5,4},{6,7},{7,6},{8,9},{9,8},{10,11... | collective-permute-start | bytes 786440 | tf_op jit(solution)/shard_map/ppermute | solution.py:641
  81.7 11.6 %collective-permute-start.20 = (bf16[256,512]{1,0:T(8,128)(2,1)S(1)}, bf16[256,512]{1,0:T(8,128)(2,1)S(1)}, u32[]{:S(2)}, u32[]{:S(2)}) collective-permute-start(bf16[256,512]{1,0:T(8,128)(2,1)S(1)} %edge_1_1.1.refs_8_), channel_id=1, source_target_pairs={{0,1},{1,0},{2,3},{3,2},{4,5},{5,4},{6,7},{7,6},{8,9},{9,8},{10,11... | collective-permute-start | bytes 786440 | tf_op jit(solution)/shard_map/ppermute | solution.py:641
  87.8 2.4 %collective-permute-start.21 = (bf16[3,256,512]{2,1,0:T(8,128)(2,1)S(1)}, bf16[3,256,512]{2,1,0:T(8,128)(2,1)S(1)}, u32[]{:S(2)}, u32[]{:S(2)}) collective-permute-start(bf16[3,256,512]{2,1,0:T(8,128)(2,1)S(1)} %add.22.refs_9_.refs_1_), channel_id=1, source_target_pairs={{0,4},{4,0},{8,12},{12,8},{16,20},{20,16},{24,28},{28,24},{1,5},{5... | collective-permute-start | bytes 2359304 | tf_op jit(solution)/shard_map/ppermute | solution.py:641

commit v6 on v5

--- a/solution.py
+++ b/solution.py
@@ -116,7 +116,7 @@
         send_ref[...] = acc[:, pl.ds(other, half), :].astype(BF)
 
 
-def block_grads(block, scalars, projected, learn_rates, weights, step_scale, weight_specs, earlier=()):
+def block_grads(block, scalars, projected, learn_rates, weights, step_scale, weight_specs, earlier=(), own=None):
     _, _, rows, feats = projected.shape
     half = feats // 2
     shape = jax.ShapeDtypeStruct((3, half, feats), BF)
@@ -125,10 +125,16 @@
         functools.partial(grads_kernel, block, step_scale),
         f"grads_{block}",
         scalars,
-        (projected, projected, learn_rates, *weights),
+        (*(own or (projected, projected)), learn_rates, *weights),
         [
-            pl.BlockSpec((None, None, tile, feats), lambda i, s: (1, block, i, 0)),
-            pl.BlockSpec((None, None, tile, feats), lambda i, s: (2, block, i, 0)),
+            *(
+                [whole(x) for x in own]
+                if own
+                else [
+                    pl.BlockSpec((None, None, tile, feats), lambda i, s: (1, block, i, 0)),
+                    pl.BlockSpec((None, None, tile, feats), lambda i, s: (2, block, i, 0)),
+                ]
+            ),
             pl.BlockSpec((1, learn_rates.shape[1], tile), lambda i, s: (0, 0, i)),
             *weight_specs,
         ],
@@ -168,7 +174,7 @@
     return (result[:, :HD] / result[:, HD:]).astype(BF)
 
 
-def attend(q_ref, k_ref, v_ref, halo_ref, usable, store):
+def attend(q_ref, k_ref, v_ref, halo, usable, store):
     rows, feats = q_ref.shape
     tile = min(TILE, rows)
 
@@ -176,7 +182,7 @@
         for at in range(start - WIN, start + tile, tile):
             before = at < 0
             where = slice(at + WIN, at + WIN + tile) if before else slice(at, at + tile)
-            yield (halo_ref[which, where, cols] if before else own_ref[where, cols]), before
+            yield (halo[which][where, cols] if before else own_ref[where, cols]), before
 
     work = [
         (start, slice(head * HD, (head + 1) * HD)) for start in range(0, rows, tile) for head in range(feats // HD)
@@ -207,11 +213,11 @@
     return jnp.where(sc[1] > 0, 0.0, MASKED).astype(F32)
 
 
-def mixed_kernel(block, sc, q_ref, k_ref, v_ref, halo_ref, w1_ref, w3_ref, w2_ref, out_ref, att):
+def mixed_kernel(block, sc, q_ref, k_ref, v_ref, k_halo, v_halo, w1_ref, w3_ref, w2_ref, out_ref, att):
     def store(rows, cols, value):
         att[rows, cols] = value
 
-    attend(q_ref, k_ref, v_ref, halo_ref, usable_bias(block, sc), store)
+    attend(q_ref, k_ref, v_ref, (k_halo, v_halo), usable_bias(block, sc), store)
     rows = q_ref.shape[0]
     tile = min(TILE, rows)
     for start in range(0, rows, tile):
@@ -224,7 +230,7 @@
     def store(rows, cols, value):
         out_ref[rows, cols] = value
 
-    attend(q_ref, k_ref, v_ref, halo_ref, usable_bias(block, sc), store)
+    attend(q_ref, k_ref, v_ref, (halo_ref.at[0], halo_ref.at[1]), usable_bias(block, sc), store)
 
 
 def qkv_specs(block, projected):
@@ -255,8 +261,8 @@
         functools.partial(mixed_kernel, block),
         f"mixed_{block}",
         scalars,
-        (projected, projected, projected, halo, *weights),
-        [*qkv_specs(block, projected), whole(halo), *weight_specs],
+        (projected, projected, projected, *halo, *weights),
+        [*qkv_specs(block, projected), *[whole(x) for x in halo], *weight_specs],
         jax.ShapeDtypeStruct((rows, feats), BF),
         scratch=[pltpu.VMEM((rows, feats), BF)],
         earlier=earlier,
@@ -477,6 +483,11 @@
     out_ref[1] = v_ref[...]
 
 
+def first_rows(projected, kind):
+    _, _, rows, feats = projected.shape
+    return lax.slice(projected, (kind, 0, 0, 0), (kind + 1, 1, rows, feats)).reshape(rows, feats)
+
+
 def pack_halo(block, scalars, projected, last, earlier=()):
     _, _, rows, feats = projected.shape
 
@@ -685,9 +696,9 @@
     weights, specs = (fast_up, fast_up, fast_down), up_spec
     state = (fast_up, fast_down)
 
-    kv_now = pack_halo(0, scalars, projected, ctx_count - 1)
-    halo = move(kv_now, "ctx", around)
-    keep, send = block_grads(0, scalars, projected, learn_rates, weights, step_scale, specs, earlier=(kv_now,))
+    kv_now = [first_rows(projected, kind) for kind in (1, 2)]
+    halo = [move(x[rows - WIN :], "ctx", around) for x in kv_now]
+    keep, send = block_grads(0, scalars, projected, learn_rates, weights, step_scale, specs, own=kv_now)
     keep = gate(scalars, keep, earlier=(send,))
     total = add(scalars, keep, flip(send, 0))
     received = move(total, "ctx", partners(ctx_count, 0))

time: 95.1 us -> 94 us (0.988)
    unnamed x18 -> x14, local copies, waits for them, and re-layouts: 2.16 us -> 0.04 us
    reshape x0 -> x1, local copies, waits for them, and re-layouts: none -> 1.39 us  [first_rows(): lax.slice(projected, (kind, 0, 0, 0), (kind + 1, 1, rows, feats))]
    ppermute x22 -> x23, starting transfers between devices: 30.7 us -> 29.8 us  [move(): return lax.ppermute(x, axis, pairs)]
    pallas_call x27 -> x26, Pallas kernels: 37.1 us -> 37.8 us  [call(): pl.pallas_call(ordered, out_shape=[*outs_list, *[like(x) for x in passing...]
    ppermute x22 -> x23, waiting for transfers between devices: 23.8 us -> 23.6 us  [move(): return lax.ppermute(x, axis, pairs)]
  transfers between devices with their start and end apart: 22 -> 23, of which waited for: 8 -> 9; matrix products, arithmetic and copies ran while one was open for 0% -> 0% of each run, Pallas kernels for 37% -> 39%
where the time goes in v6:
time: 94 us; the launch traced here: 93.8 us
  Pallas kernels  37.8 us (40%)
  starting transfers between devices  29.8 us (32%)
  waiting for transfers between devices  23.6 us (25%)
  local copies, waits for them, and re-layouts  1.42 us (2%)
  between operations  1.13 us (1%)
    pallas_call x26, Pallas kernels, call(): pl.pallas_call(ordered, out_shape=[*outs_list, *[like(x) for x in passing...  37.8 us
    ppermute x23, starting transfers between devices, move(): return lax.ppermute(x, axis, pairs)  29.8 us
    ppermute x23, waiting for transfers between devices, move(): return lax.ppermute(x, axis, pairs)  23.6 us
  transfers between devices with their start and end apart: 23, of which 9 were waited for; matrix products, arithmetic and copies ran while one was open for 0% of the time, Pallas kernels for 39%

profile of v6, /device:TPU:0, one launch (start us, length us, event | category | flops | bytes accessed | tf_op | source)
XLA Modules:
  0.0 93.8 jit_solution(3118258859559095948)
XLA Ops:
  0.7 1.4 %slice_bitcast_fusion = (bf16[512,512]{1,0:T(8,128)(2,1)S(1)}, bf16[512,512]{1,0:T(8,128)(2,1)S(1)}) fusion(bf16[3,2,512,512]{3,2,1,0:T(8,128)(2,1)} %refs_2_.7), kind=kLoop, calls=%fused_computation | loop fusion | bytes 2097152 | tf_op jit(solution)/shard_map/reshape | solution.py:488
  2.6 2.6 %collective-permute-start.3 = (bf16[512,512]{1,0:T(8,128)(2,1)S(1)}, bf16[512,512]{1,0:T(8,128)(2,1)}, u32[]{:S(2)}, u32[]{:S(2)}) collective-permute-start(bf16[512,512]{1,0:T(8,128)(2,1)S(1)} %get-tuple-element.33.refs_2_), channel_id=1, source_target_pairs={{0,4},{4,8},{8,12},{12,16},{16,20},{20,24},{24,28},{28,0},{1,5},{5... | collective-permute-start | bytes 1572872 | tf_op jit(solution)/shard_map/ppermute | solution.py:652
  5.2 2.8 %grads_0.1 = (f32[3,256,512]{2,1,0:T(8,128)S(1)}, bf16[3,256,512]{2,1,0:T(8,128)(2,1)S(1)}) custom-call(s32[4]{0:T(128)S(1)} %pad_add_fusion.refs_0_, bf16[512,512]{1,0:T(8,128)(2,1)S(1)} %get-tuple-element.34.refs_1_, bf16[512,512]{1,0:T(8,128)(2,1)S(1)} %get-tuple-element.33.refs_2_, f32[1,2,512]{2,1,0:T(2,128)S(1)} %copy-done.6, ...), custom_call_target="tpu_custom_call" | custom-call | flops 20000000000 | bytes 1 | tf_op jit(solution)/shard_map/grads_0/pallas_call | solution.py:61
  8.7 1.7 %collective-permute-done.refs_2_ = bf16[3,256,512]{2,1,0:T(8,128)(2,1)S(1)} collective-permute-done((bf16[3,256,512]{2,1,0:T(8,128)(2,1)S(1)}, bf16[3,256,512]{2,1,0:T(8,128)(2,1)S(1)}, u32[]{:S(2)}, u32[]{:S(2)}) %collective-permute-start) | collective-permute-done | bytes 786464 | tf_op jit(solution)/shard_map/ppermute | solution.py:652
  11.7 1.6 %collective-permute-start.1 = (bf16[3,256,512]{2,1,0:T(8,128)(2,1)S(1)}, bf16[3,256,512]{2,1,0:T(8,128)(2,1)S(1)}, u32[]{:S(2)}, u32[]{:S(2)}) collective-permute-start(bf16[3,256,512]{2,1,0:T(8,128)(2,1)S(1)} %add.17.refs_3_.refs_1_), channel_id=1, source_target_pairs={{0,8},{4,20},{8,0},{12,28},{16,24},{20,4},{24,16},{28,12},{1,9},{5... | collective-permute-start | bytes 2359304 | tf_op jit(solution)/shard_map/ppermute | solution.py:652
  13.3 6.3 %collective-permute-done.3.refs_5_ = bf16[512,512]{1,0:T(8,128)(2,1)} collective-permute-done((bf16[512,512]{1,0:T(8,128)(2,1)S(1)}, bf16[512,512]{1,0:T(8,128)(2,1)}, u32[]{:S(2)}, u32[]{:S(2)}) %collective-permute-start.3) | collective-permute-done | bytes 524320 | tf_op jit(solution)/shard_map/ppermute | solution.py:652
  19.6 4.9 %mixed_0.1.refs_2_.refs_1_ = bf16[512,512]{1,0:T(8,128)(2,1)S(1)} custom-call(s32[4]{0:T(128)S(1)} %pad_add_fusion.refs_0_, bf16[3,2,512,512]{3,2,1,0:T(8,128)(2,1)S(1)} %copy-done, bf16[3,2,512,512]{3,2,1,0:T(8,128)(2,1)S(1)} %copy-done, bf16[3,2,512,512]{3,2,1,0:T(8,128)(2,1)S(1)} %copy-done, bf16[512,512]{1,0:T(8,128)(2,1)S(1)} %collective-permute-done.2.refs_4_, ...), custom_call_target="tpu_custom_call" | custom-call | flops 20000000000 | bytes 1 | tf_op jit(solution)/shard_map/mixed_0/pallas_call | solution.py:61
  24.6 3.2 %collective-permute-start.5 = (bf16[512,512]{1,0:T(8,128)(2,1)S(1)}, bf16[512,512]{1,0:T(8,128)(2,1)S(1)}, u32[]{:S(2)}, u32[]{:S(2)}) collective-permute-start(bf16[512,512]{1,0:T(8,128)(2,1)S(1)} %mixed_0.1.refs_2_.refs_1_), channel_id=1, source_target_pairs={{0,1},{1,0},{2,3},{3,2},{4,5},{5,4},{6,7},{7,6},{8,9},{9,8},{10,11... | collective-permute-start | bytes 1572872 | tf_op jit(solution)/shard_map/ppermute | solution.py:652
  28.3 3.2 %collective-permute-start.12 = (bf16[3,256,512]{2,1,0:T(8,128)(2,1)S(1)}, bf16[3,256,512]{2,1,0:T(8,128)(2,1)S(1)}, u32[]{:S(2)}, u32[]{:S(2)}) collective-permute-start(bf16[3,256,512]{2,1,0:T(8,128)(2,1)S(1)} %pick_parts.1.refs_3_), channel_id=1, source_target_pairs={{0,1},{1,0},{2,3},{3,2},{4,5},{5,4},{6,7},{7,6},{8,9},{9,8},{10,11... | collective-permute-start | bytes 2359304 | tf_op jit(solution)/shard_map/ppermute | solution.py:652
  33.0 1.8 %collective-permute-start.4 = (bf16[3,256,512]{2,1,0:T(8,128)(2,1)S(1)}, bf16[3,256,512]{2,1,0:T(8,128)(2,1)S(1)}, u32[]{:S(2)}, u32[]{:S(2)}) collective-permute-start(bf16[3,256,512]{2,1,0:T(8,128)(2,1)S(1)} %add.18.refs_5_.refs_1_), channel_id=1, source_target_pairs={{0,16},{4,12},{8,24},{12,4},{16,0},{20,28},{24,8},{28,20},{1,17},{... | collective-permute-start | bytes 2359304 | tf_op jit(solution)/shard_map/ppermute | solution.py:652
  34.8 2.9 %collective-permute-done.6.refs_4_ = bf16[2,512,512]{2,1,0:T(8,128)(2,1)S(1)} collective-permute-done((bf16[2,512,512]{2,1,0:T(8,128)(2,1)S(1)}, bf16[2,512,512]{2,1,0:T(8,128)(2,1)S(1)}, u32[]{:S(2)}, u32[]{:S(2)}) %collective-permute-start.6) | collective-permute-done | bytes 1048608 | tf_op jit(solution)/shard_map/ppermute | solution.py:652
  37.7 2.9 %attend_1.1.refs_2_.refs_6_ = bf16[512,512]{1,0:T(8,128)(2,1)S(1)} custom-call(s32[4]{0:T(128)S(1)} %pad_add_fusion.refs_0_, bf16[3,2,512,512]{3,2,1,0:T(8,128)(2,1)S(1)} %copy-done, bf16[3,2,512,512]{3,2,1,0:T(8,128)(2,1)S(1)} %copy-done, bf16[3,2,512,512]{3,2,1,0:T(8,128)(2,1)S(1)} %copy-done, bf16[2,512,512]{2,1,0:T(8,128)(2,1)S(1)} %collective-permute-done.6.refs_4_, ...), custom_call_target="tpu_custom_call" | custom-call | flops 20000000000 | bytes 1 | tf_op jit(solution)/shard_map/attend_1/pallas_call | solution.py:61
  41.3 4.8 %collective-permute-done.4.refs_2_ = bf16[3,256,512]{2,1,0:T(8,128)(2,1)S(1)} collective-permute-done((bf16[3,256,512]{2,1,0:T(8,128)(2,1)S(1)}, bf16[3,256,512]{2,1,0:T(8,128)(2,1)S(1)}, u32[]{:S(2)}, u32[]{:S(2)}) %collective-permute-start.4) | collective-permute-done | bytes 786464 | tf_op jit(solution)/shard_map/ppermute | solution.py:652
  48.3 1.4 %collective-permute-done.7.refs_2_ = bf16[3,256,512]{2,1,0:T(8,128)(2,1)S(1)} collective-permute-done((bf16[3,256,512]{2,1,0:T(8,128)(2,1)S(1)}, bf16[3,256,512]{2,1,0:T(8,128)(2,1)S(1)}, u32[]{:S(2)}, u32[]{:S(2)}) %collective-permute-start.7) | collective-permute-done | bytes 786464 | tf_op jit(solution)/shard_map/ppermute | solution.py:652
  49.6 2.6 %update_1.1 = (bf16[512,512]{1,0:T(8,128)(2,1)S(1)}, bf16[3,512,512]{2,1,0:T(8,128)(2,1)S(1)}) custom-call(s32[4]{0:T(128)S(1)} %pad_add_fusion.refs_0_, bf16[3,256,512]{2,1,0:T(8,128)(2,1)S(1)} %add.19.refs_2_.refs_1_, bf16[3,256,512]{2,1,0:T(8,128)(2,1)S(1)} %collective-permute-done.7.refs_2_, bf16[2,1,512,512]{3,2,1,0:T(8,128)(2,1)S(1)} %copy-done.3, ...), custom_call_target="tpu_custom_call" | custom-call | flops 20000000000 | bytes 1 | tf_op jit(solution)/shard_map/update_1/pallas_call | solution.py:61
  52.2 1.9 %collective-permute-start.10 = (bf16[512,512]{1,0:T(8,128)(2,1)S(1)}, bf16[512,512]{1,0:T(8,128)(2,1)S(1)}, u32[]{:S(2)}, u32[]{:S(2)}) collective-permute-start(bf16[512,512]{1,0:T(8,128)(2,1)S(1)} %get-tuple-element.20.refs_7_.refs_1_), channel_id=1, source_target_pairs={{0,1},{1,0},{2,3},{3,2},{4,5},{5,4},{6,7},{7,6},{8,9},{9,8},{10,11... | collective-permute-start | bytes 1572872 | tf_op jit(solution)/shard_map/ppermute | solution.py:652
  54.1 2.8 %grads_1.1 = (f32[3,256,512]{2,1,0:T(8,128)S(1)}, bf16[3,256,512]{2,1,0:T(8,128)(2,1)S(1)}) custom-call(s32[4]{0:T(128)S(1)} %pad_add_fusion.refs_0_, bf16[3,2,512,512]{3,2,1,0:T(8,128)(2,1)S(1)} %copy-done, bf16[3,2,512,512]{3,2,1,0:T(8,128)(2,1)S(1)} %copy-done, f32[1,2,512]{2,1,0:T(2,128)S(1)} %copy-done.6, ...), custom_call_target="tpu_custom_call" | custom-call | flops 20000000000 | bytes 1 | tf_op jit(solution)/shard_map/grads_1/pallas_call | solution.py:61
  58.2 1.3 %collective-permute-done.14.refs_2_ = bf16[3,256,512]{2,1,0:T(8,128)(2,1)S(1)} collective-permute-done((bf16[3,256,512]{2,1,0:T(8,128)(2,1)S(1)}, bf16[3,256,512]{2,1,0:T(8,128)(2,1)S(1)}, u32[]{:S(2)}, u32[]{:S(2)}) %collective-permute-start.14) | collective-permute-done | bytes 786464 | tf_op jit(solution)/shard_map/ppermute | solution.py:652
  60.6 1.5 %edge_0.1.refs_5_ = bf16[512,512]{1,0:T(8,128)(2,1)S(1)} custom-call(s32[4]{0:T(128)S(1)} %pad_add_fusion.refs_0_, bf16[512,512]{1,0:T(8,128)(2,1)S(1)} %mixed_0.1.refs_2_.refs_1_, bf16[512,512]{1,0:T(8,128)(2,1)S(1)} %gate.6.refs_7_.refs_2_.refs_3_, bf16[512,512]{1,0:T(8,128)(2,1)S(1)} %collective-permute-done.11.refs_3_.refs_4_, ...), custom_call_target="tpu_custom_call" | custom-call | flops 20000000000 | bytes 1 | tf_op jit(solution)/shard_map/edge_0/pallas_call | solution.py:61
  62.1 3.1 %collective-permute-start.19 = (bf16[512,512]{1,0:T(8,128)(2,1)S(1)}, bf16[512,512]{1,0:T(8,128)(2,1)S(1)}, u32[]{:S(2)}, u32[]{:S(2)}) collective-permute-start(bf16[512,512]{1,0:T(8,128)(2,1)S(1)} %edge_0.1.refs_5_), channel_id=1, source_target_pairs={{0,1},{1,0},{2,3},{3,2},{4,5},{5,4},{6,7},{7,6},{8,9},{9,8},{10,11... | collective-permute-start | bytes 1572872 | tf_op jit(solution)/shard_map/ppermute | solution.py:652
  65.2 2.2 %state_1.1 = (f32[3,512,512]{2,1,0:T(8,128)S(1)}, f32[3,8,128]{2,1,0:T(8,128)S(1)}) custom-call(s32[4]{0:T(128)S(1)} %pad_add_fusion.refs_0_, bf16[3,256,512]{2,1,0:T(8,128)(2,1)S(1)} %add.19.refs_2_.refs_1_, bf16[3,256,512]{2,1,0:T(8,128)(2,1)S(1)} %collective-permute-done.7.refs_2_, bf16[2,1,512,512]{3,2,1,0:T(8,128)(2,1)S(1)} %copy-done.3, ...), custom_call_target="tpu_custom_call" | custom-call | flops 20000000000 | bytes 1 | tf_op jit(solution)/shard_map/state_1/pallas_call | solution.py:61
  68.9 3.4 %collective-permute-done.17.refs_2_ = bf16[3,256,512]{2,1,0:T(8,128)(2,1)S(1)} collective-permute-done((bf16[3,256,512]{2,1,0:T(8,128)(2,1)S(1)}, bf16[3,256,512]{2,1,0:T(8,128)(2,1)S(1)}, u32[]{:S(2)}, u32[]{:S(2)}) %collective-permute-start.17) | collective-permute-done | bytes 786464 | tf_op jit(solution)/shard_map/ppermute | solution.py:652
  72.9 1.6 %collective-permute-start.18 = (bf16[3,256,512]{2,1,0:T(8,128)(2,1)S(1)}, bf16[3,256,512]{2,1,0:T(8,128)(2,1)S(1)}, u32[]{:S(2)}, u32[]{:S(2)}) collective-permute-start(bf16[3,256,512]{2,1,0:T(8,128)(2,1)S(1)} %add.21.refs_6_.refs_1_), channel_id=1, source_target_pairs={{0,16},{4,12},{8,24},{12,4},{16,0},{20,28},{24,8},{28,20},{1,17},{... | collective-permute-start | bytes 2359304 | tf_op jit(solution)/shard_map/ppermute | solution.py:652
  74.5 1.1 %edge_1_0.1.refs_6_ = bf16[256,512]{1,0:T(8,128)(2,1)S(1)} custom-call(s32[4]{0:T(128)S(1)} %pad_add_fusion.refs_0_, bf16[512,512]{1,0:T(8,128)(2,1)S(1)} %get-tuple-element.20.refs_7_.refs_1_, bf16[512,512]{1,0:T(8,128)(2,1)S(1)} %collective-permute-done.9.refs_2_, bf16[256,512]{1,0:T(8,128)(2,1)S(1)} %collective-permute-done.15.refs_3_.refs_5_, ...), custom_call_target="tpu_custom_call" | custom-call | flops 20000000000 | bytes 1 | tf_op jit(solution)/shard_map/edge_1_0/pallas_call | solution.py:61
  75.6 3.8 %collective-permute-start.20 = (bf16[256,512]{1,0:T(8,128)(2,1)S(1)}, bf16[256,512]{1,0:T(8,128)(2,1)S(1)}, u32[]{:S(2)}, u32[]{:S(2)}) collective-permute-start(bf16[256,512]{1,0:T(8,128)(2,1)S(1)} %edge_1_0.1.refs_6_), channel_id=1, source_target_pairs={{0,1},{1,0},{2,3},{3,2},{4,5},{5,4},{6,7},{7,6},{8,9},{9,8},{10,11... | collective-permute-start | bytes 786440 | tf_op jit(solution)/shard_map/ppermute | solution.py:652
  79.5 1.1 %edge_1_1.1.refs_8_ = bf16[256,512]{1,0:T(8,128)(2,1)S(1)} custom-call(s32[4]{0:T(128)S(1)} %pad_add_fusion.refs_0_, bf16[512,512]{1,0:T(8,128)(2,1)S(1)} %get-tuple-element.20.refs_7_.refs_1_, bf16[512,512]{1,0:T(8,128)(2,1)S(1)} %collective-permute-done.9.refs_2_, bf16[256,512]{1,0:T(8,128)(2,1)S(1)} %collective-permute-done.16.refs_3_.refs_6_, ...), custom_call_target="tpu_custom_call" | custom-call | flops 20000000000 | bytes 1 | tf_op jit(solution)/shard_map/edge_1_1/pallas_call | solution.py:61
  80.6 3.5 %collective-permute-start.21 = (bf16[256,512]{1,0:T(8,128)(2,1)S(1)}, bf16[256,512]{1,0:T(8,128)(2,1)S(1)}, u32[]{:S(2)}, u32[]{:S(2)}) collective-permute-start(bf16[256,512]{1,0:T(8,128)(2,1)S(1)} %edge_1_1.1.refs_8_), channel_id=1, source_target_pairs={{0,1},{1,0},{2,3},{3,2},{4,5},{5,4},{6,7},{7,6},{8,9},{9,8},{10,11... | collective-permute-start | bytes 786440 | tf_op jit(solution)/shard_map/ppermute | solution.py:652
  84.1 1.9 %own_0.1 = (bf16[2,512,512]{2,1,0:T(8,128)(2,1)}, f32[8,128]{1,0:T(8,128)S(1)}) custom-call(s32[4]{0:T(128)S(1)} %pad_add_fusion.refs_0_, bf16[512,512]{1,0:T(8,128)(2,1)S(1)} %mixed_0.1.refs_2_.refs_1_, bf16[512,512]{1,0:T(8,128)(2,1)S(1)} %gate.5.refs_3_.refs_2_, bf16[512,512]{1,0:T(8,128)(2,1)S(1)} %gate.6.refs_7_.refs_2_.refs_3_, ...), custom_call_target="tpu_custom_call" | custom-call | flops 20000000000 | bytes 1 | tf_op jit(solution)/shard_map/own_0/pallas_call | solution.py:61
  86.8 1.2 %own_1.1.refs_5_.refs_1_ = f32[512,512]{1,0:T(8,128)S(1)} custom-call(s32[4]{0:T(128)S(1)} %pad_add_fusion.refs_0_, bf16[512,512]{1,0:T(8,128)(2,1)S(1)} %get-tuple-element.20.refs_7_.refs_1_, bf16[512,512]{1,0:T(8,128)(2,1)S(1)} %collective-permute-done.9.refs_2_, bf16[256,512]{1,0:T(8,128)(2,1)S(1)} %get-tuple-element.25.refs_3_, ...), custom_call_target="tpu_custom_call" | custom-call | flops 20000000000 | bytes 1 | tf_op jit(solution)/shard_map/own_1/pallas_call | solution.py:61
  88.0 1.1 %collective-permute-done.22.refs_2_ = bf16[3,256,512]{2,1,0:T(8,128)(2,1)S(1)} collective-permute-done((bf16[3,256,512]{2,1,0:T(8,128)(2,1)S(1)}, bf16[3,256,512]{2,1,0:T(8,128)(2,1)S(1)}, u32[]{:S(2)}, u32[]{:S(2)}) %collective-permute-start.22) | collective-permute-done | bytes 786464 | tf_op jit(solution)/shard_map/ppermute | solution.py:652
  89.1 3.1 %final_update.1 = (f32[2,1,512,512]{3,2,1,0:T(8,128)}, f32[1,512,512]{2,1,0:T(8,128)}, f32[8,128]{1,0:T(8,128)S(1)}) custom-call(s32[4]{0:T(128)S(1)} %pad_add_fusion.refs_0_, bf16[3,256,512]{2,1,0:T(8,128)(2,1)S(1)} %add.22.refs_9_.refs_1_, bf16[3,256,512]{2,1,0:T(8,128)(2,1)S(1)} %collective-permute-done.22.refs_2_, ...), custom_call_target="tpu_custom_call" | custom-call | flops 20000000000 | bytes 1 | tf_op jit(solution)/shard_map/final_update/pallas_call | solution.py:61
  92.2 1.4 %finish.1 = bf16[2,512,512]{2,1,0:T(8,128)(2,1)} custom-call(s32[4]{0:T(128)S(1)} %pad_add_fusion.refs_0_, f32[512,512]{1,0:T(8,128)S(1)} %own_1.1.refs_5_.refs_1_, bf16[256,512]{1,0:T(8,128)(2,1)S(1)} %collective-permute-done.20.refs_2_, bf16[256,512]{1,0:T(8,128)(2,1)S(1)} %collective-permute-done.21.refs_3_, ...), custom_call_target="tpu_custom_call", output_to_operand_aliasing={{}: (4, {})} | custom-call | flops 20000000000 | bytes 1 | tf_op jit(solution)/shard_map/finish/pallas_call | solution.py:61
  (56 shorter events, 12.8 us)
Async XLA Ops:
  0.6 4.6 %copy-start.5 = (bf16[1,512,512]{2,1,0:T(8,128)(2,1)S(1)}, bf16[1,512,512]{2,1,0:T(8,128)(2,1)}, u32[]{:S(2)}) copy-start(bf16[1,512,512]{2,1,0:T(8,128)(2,1)} %refs_4_.5) | copy-start | bytes 1572868
  0.6 4.6 %copy-start.6 = (f32[1,2,512]{2,1,0:T(2,128)S(1)}, f32[1,2,512]{2,1,0:T(2,128)}, u32[]{:S(2)}) copy-start(f32[1,2,512]{2,1,0:T(2,128)} %refs_3_.10) | copy-start | bytes 12292
  0.7 4.6 %copy-start.3 = (bf16[2,1,512,512]{3,2,1,0:T(8,128)(2,1)S(1)}, bf16[2,1,512,512]{3,2,1,0:T(8,128)(2,1)}, u32[]{:S(2)}) copy-start(bf16[2,1,512,512]{3,2,1,0:T(8,128)(2,1)} %refs_3_.11) | copy-start | bytes 3145732
  2.0 11.2 %collective-permute-start.2 = (bf16[512,512]{1,0:T(8,128)(2,1)S(1)}, bf16[512,512]{1,0:T(8,128)(2,1)S(1)}, u32[]{:S(2)}, u32[]{:S(2)}) collective-permute-start(bf16[512,512]{1,0:T(8,128)(2,1)S(1)} %get-tuple-element.34.refs_1_), channel_id=1, source_target_pairs={{0,4},{4,8},{8,12},{12,16},{16,20},{20,24},{24,28},{28,0},{1,5},{5... | collective-permute-start | bytes 1572872 | tf_op jit(solution)/shard_map/ppermute | solution.py:652
  2.6 17.1 %collective-permute-start.3 = (bf16[512,512]{1,0:T(8,128)(2,1)S(1)}, bf16[512,512]{1,0:T(8,128)(2,1)}, u32[]{:S(2)}, u32[]{:S(2)}) collective-permute-start(bf16[512,512]{1,0:T(8,128)(2,1)S(1)} %get-tuple-element.33.refs_2_), channel_id=1, source_target_pairs={{0,4},{4,8},{8,12},{12,16},{16,20},{20,24},{24,28},{28,0},{1,5},{5... | collective-permute-start | bytes 1572872 | tf_op jit(solution)/shard_map/ppermute | solution.py:652
  8.1 2.4 %collective-permute-start = (bf16[3,256,512]{2,1,0:T(8,128)(2,1)S(1)}, bf16[3,256,512]{2,1,0:T(8,128)(2,1)S(1)}, u32[]{:S(2)}, u32[]{:S(2)}) collective-permute-start(bf16[3,256,512]{2,1,0:T(8,128)(2,1)S(1)} %get-tuple-element.19.refs_2_), channel_id=1, source_target_pairs={{0,4},{4,0},{8,12},{12,8},{16,20},{20,16},{24,28},{28,24},{1,5},{5... | collective-permute-start | bytes 2359304 | tf_op jit(solution)/shard_map/ppermute | solution.py:652
  8.7 2.4 %copy-start = (bf16[3,2,512,512]{3,2,1,0:T(8,128)(2,1)S(1)}, bf16[3,2,512,512]{3,2,1,0:T(8,128)(2,1)}, u32[]{:S(2)}) copy-start(bf16[3,2,512,512]{3,2,1,0:T(8,128)(2,1)} %refs_2_.7) | copy-start | bytes 9437188
  11.7 16.0 %copy-start.1 = (bf16[2048,512]{1,0:T(8,128)(2,1)S(1)}, bf16[2048,512]{1,0:T(8,128)(2,1)}, u32[]{:S(2)}) copy-start(bf16[2048,512]{1,0:T(8,128)(2,1)} %refs_7_.3) | copy-start | bytes 6291460
  11.7 20.5 %collective-permute-start.1 = (bf16[3,256,512]{2,1,0:T(8,128)(2,1)S(1)}, bf16[3,256,512]{2,1,0:T(8,128)(2,1)S(1)}, u32[]{:S(2)}, u32[]{:S(2)}) collective-permute-start(bf16[3,256,512]{2,1,0:T(8,128)(2,1)S(1)} %add.17.refs_3_.refs_1_), channel_id=1, source_target_pairs={{0,8},{4,20},{8,0},{12,28},{16,24},{20,4},{24,16},{28,12},{1,9},{5... | collective-permute-start | bytes 2359304 | tf_op jit(solution)/shard_map/ppermute | solution.py:652
  13.3 24.4 %collective-permute-start.6 = (bf16[2,512,512]{2,1,0:T(8,128)(2,1)S(1)}, bf16[2,512,512]{2,1,0:T(8,128)(2,1)S(1)}, u32[]{:S(2)}, u32[]{:S(2)}) collective-permute-start(bf16[2,512,512]{2,1,0:T(8,128)(2,1)S(1)} %pack_1.1.refs_9_), channel_id=1, source_target_pairs={{0,4},{4,8},{8,12},{12,16},{16,20},{20,24},{24,28},{28,0},{1,5},{5... | collective-permute-start | bytes 3145736 | tf_op jit(solution)/shard_map/ppermute | solution.py:652
  24.6 16.1 %collective-permute-start.5 = (bf16[512,512]{1,0:T(8,128)(2,1)S(1)}, bf16[512,512]{1,0:T(8,128)(2,1)S(1)}, u32[]{:S(2)}, u32[]{:S(2)}) collective-permute-start(bf16[512,512]{1,0:T(8,128)(2,1)S(1)} %mixed_0.1.refs_2_.refs_1_), channel_id=1, source_target_pairs={{0,1},{1,0},{2,3},{3,2},{4,5},{5,4},{6,7},{7,6},{8,9},{9,8},{10,11... | collective-permute-start | bytes 1572872 | tf_op jit(solution)/shard_map/ppermute | solution.py:652
  27.7 20.0 %collective-permute-start.8 = (bf16[512,512]{1,0:T(8,128)(2,1)S(1)}, bf16[512,512]{1,0:T(8,128)(2,1)S(1)}, u32[]{:S(2)}, u32[]{:S(2)}) collective-permute-start(bf16[512,512]{1,0:T(8,128)(2,1)S(1)} %mixed_0.1.refs_2_.refs_1_), channel_id=1, source_target_pairs={{1,2},{2,1},{0,4},{3,7},{5,6},{6,5},{4,0},{7,3},{9,10},{10,9},{8,1... | collective-permute-start | bytes 1572872 | tf_op jit(solution)/shard_map/ppermute | solution.py:652
  28.3 29.2 %collective-permute-start.12 = (bf16[3,256,512]{2,1,0:T(8,128)(2,1)S(1)}, bf16[3,256,512]{2,1,0:T(8,128)(2,1)S(1)}, u32[]{:S(2)}, u32[]{:S(2)}) collective-permute-start(bf16[3,256,512]{2,1,0:T(8,128)(2,1)S(1)} %pick_parts.1.refs_3_), channel_id=1, source_target_pairs={{0,1},{1,0},{2,3},{3,2},{4,5},{5,4},{6,7},{7,6},{8,9},{9,8},{10,11... | collective-permute-start | bytes 2359304 | tf_op jit(solution)/shard_map/ppermute | solution.py:652
  33.0 13.0 %collective-permute-start.4 = (bf16[3,256,512]{2,1,0:T(8,128)(2,1)S(1)}, bf16[3,256,512]{2,1,0:T(8,128)(2,1)S(1)}, u32[]{:S(2)}, u32[]{:S(2)}) collective-permute-start(bf16[3,256,512]{2,1,0:T(8,128)(2,1)S(1)} %add.18.refs_5_.refs_1_), channel_id=1, source_target_pairs={{0,16},{4,12},{8,24},{12,4},{16,0},{20,28},{24,8},{28,20},{1,17},{... | collective-permute-start | bytes 2359304 | tf_op jit(solution)/shard_map/ppermute | solution.py:652
  41.2 19.4 %collective-permute-start.11 = (bf16[512,512]{1,0:T(8,128)(2,1)S(1)}, bf16[512,512]{1,0:T(8,128)(2,1)S(1)}, u32[]{:S(2)}, u32[]{:S(2)}) collective-permute-start(bf16[512,512]{1,0:T(8,128)(2,1)S(1)} %gate.5.refs_3_.refs_2_), channel_id=1, source_target_pairs={{1,2},{2,1},{0,4},{3,7},{5,6},{6,5},{4,0},{7,3},{9,10},{10,9},{8,1... | collective-permute-start | bytes 1572872 | tf_op jit(solution)/shard_map/ppermute | solution.py:652
  46.8 2.9 %collective-permute-start.7 = (bf16[3,256,512]{2,1,0:T(8,128)(2,1)S(1)}, bf16[3,256,512]{2,1,0:T(8,128)(2,1)S(1)}, u32[]{:S(2)}, u32[]{:S(2)}) collective-permute-start(bf16[3,256,512]{2,1,0:T(8,128)(2,1)S(1)} %add.19.refs_2_.refs_1_), channel_id=1, source_target_pairs={{0,4},{4,0},{8,12},{12,8},{16,20},{20,16},{24,28},{28,24},{1,5},{5... | collective-permute-start | bytes 2359304 | tf_op jit(solution)/shard_map/ppermute | solution.py:652
  52.2 15.2 %collective-permute-start.10 = (bf16[512,512]{1,0:T(8,128)(2,1)S(1)}, bf16[512,512]{1,0:T(8,128)(2,1)S(1)}, u32[]{:S(2)}, u32[]{:S(2)}) collective-permute-start(bf16[512,512]{1,0:T(8,128)(2,1)S(1)} %get-tuple-element.20.refs_7_.refs_1_), channel_id=1, source_target_pairs={{0,1},{1,0},{2,3},{3,2},{4,5},{5,4},{6,7},{7,6},{8,9},{9,8},{10,11... | collective-permute-start | bytes 1572872 | tf_op jit(solution)/shard_map/ppermute | solution.py:652
  54.1 20.4 %collective-permute-start.9 = (bf16[512,512]{1,0:T(8,128)(2,1)S(1)}, bf16[512,512]{1,0:T(8,128)(2,1)S(1)}, u32[]{:S(2)}, u32[]{:S(2)}) collective-permute-start(bf16[512,512]{1,0:T(8,128)(2,1)S(1)} %get-tuple-element.20.refs_7_.refs_1_), channel_id=1, source_target_pairs={{1,2},{2,1},{0,4},{3,7},{5,6},{6,5},{4,0},{7,3},{9,10},{10,9},{8,1... | collective-permute-start | bytes 1572872 | tf_op jit(solution)/shard_map/ppermute | solution.py:652
  57.0 2.5 %collective-permute-start.14 = (bf16[3,256,512]{2,1,0:T(8,128)(2,1)S(1)}, bf16[3,256,512]{2,1,0:T(8,128)(2,1)S(1)}, u32[]{:S(2)}, u32[]{:S(2)}) collective-permute-start(bf16[3,256,512]{2,1,0:T(8,128)(2,1)S(1)} %get-tuple-element.22.refs_2_), channel_id=1, source_target_pairs={{0,4},{4,0},{8,12},{12,8},{16,20},{20,16},{24,28},{28,24},{1,5},{5... | collective-permute-start | bytes 2359304 | tf_op jit(solution)/shard_map/ppermute | solution.py:652
  58.1 2.5 %collective-permute-start.13 = (bf16[3,256,512]{2,1,0:T(8,128)(2,1)S(1)}, bf16[3,256,512]{2,1,0:T(8,128)(2,1)S(1)}, u32[]{:S(2)}, u32[]{:S(2)}) collective-permute-start(bf16[3,256,512]{2,1,0:T(8,128)(2,1)S(1)} %gate.7.refs_3_.refs_4_), channel_id=1, source_target_pairs={{0,4},{4,0},{8,12},{12,8},{16,20},{20,16},{24,28},{28,24},{1,5},{5... | collective-permute-start | bytes 2359304 | tf_op jit(solution)/shard_map/ppermute | solution.py:652
  60.2 12.1 %collective-permute-start.17 = (bf16[3,256,512]{2,1,0:T(8,128)(2,1)S(1)}, bf16[3,256,512]{2,1,0:T(8,128)(2,1)S(1)}, u32[]{:S(2)}, u32[]{:S(2)}) collective-permute-start(bf16[3,256,512]{2,1,0:T(8,128)(2,1)S(1)} %add.20.refs_6_.refs_1_), channel_id=1, source_target_pairs={{0,8},{4,20},{8,0},{12,28},{16,24},{20,4},{24,16},{28,12},{1,9},{5... | collective-permute-start | bytes 2359304 | tf_op jit(solution)/shard_map/ppermute | solution.py:652
  62.1 22.0 %collective-permute-start.19 = (bf16[512,512]{1,0:T(8,128)(2,1)S(1)}, bf16[512,512]{1,0:T(8,128)(2,1)S(1)}, u32[]{:S(2)}, u32[]{:S(2)}) collective-permute-start(bf16[512,512]{1,0:T(8,128)(2,1)S(1)} %edge_0.1.refs_5_), channel_id=1, source_target_pairs={{0,1},{1,0},{2,3},{3,2},{4,5},{5,4},{6,7},{7,6},{8,9},{9,8},{10,11... | collective-permute-start | bytes 1572872 | tf_op jit(solution)/shard_map/ppermute | solution.py:652
  68.0 6.5 %collective-permute-start.15 = (bf16[256,512]{1,0:T(8,128)(2,1)S(1)}, bf16[256,512]{1,0:T(8,128)(2,1)S(1)}, u32[]{:S(2)}, u32[]{:S(2)}) collective-permute-start(bf16[256,512]{1,0:T(8,128)(2,1)S(1)} %get-tuple-element.25.refs_3_), channel_id=1, source_target_pairs={{1,2},{2,1},{0,4},{3,7},{5,6},{6,5},{4,0},{7,3},{9,10},{10,9},{8,1... | collective-permute-start | bytes 786440 | tf_op jit(solution)/shard_map/ppermute | solution.py:652
  68.8 10.7 %collective-permute-start.16 = (bf16[256,512]{1,0:T(8,128)(2,1)S(1)}, bf16[256,512]{1,0:T(8,128)(2,1)S(1)}, u32[]{:S(2)}, u32[]{:S(2)}) collective-permute-start(bf16[256,512]{1,0:T(8,128)(2,1)S(1)} %get-tuple-element.26.refs_4_), channel_id=1, source_target_pairs={{1,2},{2,1},{0,4},{3,7},{5,6},{6,5},{4,0},{7,3},{9,10},{10,9},{8,1... | collective-permute-start | bytes 786440 | tf_op jit(solution)/shard_map/ppermute | solution.py:652
  72.9 13.1 %collective-permute-start.18 = (bf16[3,256,512]{2,1,0:T(8,128)(2,1)S(1)}, bf16[3,256,512]{2,1,0:T(8,128)(2,1)S(1)}, u32[]{:S(2)}, u32[]{:S(2)}) collective-permute-start(bf16[3,256,512]{2,1,0:T(8,128)(2,1)S(1)} %add.21.refs_6_.refs_1_), channel_id=1, source_target_pairs={{0,16},{4,12},{8,24},{12,4},{16,0},{20,28},{24,8},{28,20},{1,17},{... | collective-permute-start | bytes 2359304 | tf_op jit(solution)/shard_map/ppermute | solution.py:652
  75.6 8.5 %copy-start.2 = (bf16[2048,512]{1,0:T(8,128)(2,1)S(1)}, bf16[2048,512]{1,0:T(8,128)(2,1)}, u32[]{:S(2)}) copy-start(bf16[2048,512]{1,0:T(8,128)(2,1)} %refs_7_.3) | copy-start | bytes 6291460
  75.6 8.5 %copy-start.4 = (bf16[2,512,512]{2,1,0:T(8,128)(2,1)S(1)}, bf16[2,512,512]{2,1,0:T(8,128)(2,1)}, u32[]{:S(2)}) copy-start(bf16[2,512,512]{2,1,0:T(8,128)(2,1)} %refs_8_.3) | copy-start | bytes 3145732
  75.6 16.5 %collective-permute-start.20 = (bf16[256,512]{1,0:T(8,128)(2,1)S(1)}, bf16[256,512]{1,0:T(8,128)(2,1)S(1)}, u32[]{:S(2)}, u32[]{:S(2)}) collective-permute-start(bf16[256,512]{1,0:T(8,128)(2,1)S(1)} %edge_1_0.1.refs_6_), channel_id=1, source_target_pairs={{0,1},{1,0},{2,3},{3,2},{4,5},{5,4},{6,7},{7,6},{8,9},{9,8},{10,11... | collective-permute-start | bytes 786440 | tf_op jit(solution)/shard_map/ppermute | solution.py:652
  80.6 11.6 %collective-permute-start.21 = (bf16[256,512]{1,0:T(8,128)(2,1)S(1)}, bf16[256,512]{1,0:T(8,128)(2,1)S(1)}, u32[]{:S(2)}, u32[]{:S(2)}) collective-permute-start(bf16[256,512]{1,0:T(8,128)(2,1)S(1)} %edge_1_1.1.refs_8_), channel_id=1, source_target_pairs={{0,1},{1,0},{2,3},{3,2},{4,5},{5,4},{6,7},{7,6},{8,9},{9,8},{10,11... | collective-permute-start | bytes 786440 | tf_op jit(solution)/shard_map/ppermute | solution.py:652
  86.7 2.4 %collective-permute-start.22 = (bf16[3,256,512]{2,1,0:T(8,128)(2,1)S(1)}, bf16[3,256,512]{2,1,0:T(8,128)(2,1)S(1)}, u32[]{:S(2)}, u32[]{:S(2)}) collective-permute-start(bf16[3,256,512]{2,1,0:T(8,128)(2,1)S(1)} %add.22.refs_9_.refs_1_), channel_id=1, source_target_pairs={{0,4},{4,0},{8,12},{12,8},{16,20},{20,16},{24,28},{28,24},{1,5},{5... | collective-permute-start | bytes 2359304 | tf_op jit(solution)/shard_map/ppermute | solution.py:652

commit v7 on v6

--- a/solution.py
+++ b/solution.py
@@ -764,9 +764,10 @@
                     f"{blocks - 1}_{i}", scalars, i, mixed_next, ya_next, ybs[i], v_mine, v_other, earlier=(last,)
                 )
                 c_last.append(move(c, "head", EDGES))
-            out, last = own_part(
-                blocks - 2, scalars, mixed, x, ya, yb, w_out, hidden_in, c_there, so_far, earlier=(last,)
-            )
+                if i == 0:
+                    out, last = own_part(
+                        blocks - 2, scalars, mixed, x, ya, yb, w_out, hidden_in, c_there, so_far, earlier=(last,)
+                    )
     theirs = flip(total, 0)
     acc = own_last(blocks - 1, scalars, mixed_next, xs, ya_next, ybs, w_out, hidden_in, earlier=(total,))
     up_final, down_final, token = final_update(scalars, total, theirs, now, norms, earlier=(acc,))

time: 94 us -> 93.7 us (level)
  starting transfers between devices: 29.8 us -> 27.9 us
    ppermute x23, starting transfers between devices: 29.8 us -> 27.9 us  [move(): return lax.ppermute(x, axis, pairs)]
  transfers between devices with their start and end apart: 23 -> 23, of which waited for: 9 -> 10; matrix products, arithmetic and copies ran while one was open for 0% -> 0% of each run, Pallas kernels for 39% -> 39%
where the time goes in v7:
time: 93.7 us; the launch traced here: 92.8 us
  Pallas kernels  37.8 us (40%)
  starting transfers between devices  27.9 us (30%)
  waiting for transfers between devices  24.5 us (26%)
  local copies, waits for them, and re-layouts  1.42 us (2%)
  between operations  1.13 us (1%)
    pallas_call x26, Pallas kernels, call(): pl.pallas_call(ordered, out_shape=[*outs_list, *[like(x) for x in passing...  37.8 us
    ppermute x23, starting transfers between devices, move(): return lax.ppermute(x, axis, pairs)  27.9 us
    ppermute x23, waiting for transfers between devices, move(): return lax.ppermute(x, axis, pairs)  24.5 us
  transfers between devices with their start and end apart: 23, of which 10 were waited for; matrix products, arithmetic and copies ran while one was open for 0% of the time, Pallas kernels for 39%

profile of v7, /device:TPU:0, one launch (start us, length us, event | category | flops | bytes accessed | tf_op | source)
XLA Modules:
  0.0 92.8 jit_solution(4852356151805706354)
XLA Ops:
  0.7 1.4 %slice_bitcast_fusion = (bf16[512,512]{1,0:T(8,128)(2,1)S(1)}, bf16[512,512]{1,0:T(8,128)(2,1)S(1)}) fusion(bf16[3,2,512,512]{3,2,1,0:T(8,128)(2,1)} %refs_2_.7), kind=kLoop, calls=%fused_computation | loop fusion | bytes 2097152 | tf_op jit(solution)/shard_map/reshape | solution.py:488
  2.6 2.6 %collective-permute-start.3 = (bf16[512,512]{1,0:T(8,128)(2,1)S(1)}, bf16[512,512]{1,0:T(8,128)(2,1)}, u32[]{:S(2)}, u32[]{:S(2)}) collective-permute-start(bf16[512,512]{1,0:T(8,128)(2,1)S(1)} %get-tuple-element.33.refs_2_), channel_id=1, source_target_pairs={{0,4},{4,8},{8,12},{12,16},{16,20},{20,24},{24,28},{28,0},{1,5},{5... | collective-permute-start | bytes 1572872 | tf_op jit(solution)/shard_map/ppermute | solution.py:652
  5.2 2.8 %grads_0.1 = (f32[3,256,512]{2,1,0:T(8,128)S(1)}, bf16[3,256,512]{2,1,0:T(8,128)(2,1)S(1)}) custom-call(s32[4]{0:T(128)S(1)} %pad_add_fusion.refs_0_, bf16[512,512]{1,0:T(8,128)(2,1)S(1)} %get-tuple-element.34.refs_1_, bf16[512,512]{1,0:T(8,128)(2,1)S(1)} %get-tuple-element.33.refs_2_, f32[1,2,512]{2,1,0:T(2,128)S(1)} %copy-done.6, ...), custom_call_target="tpu_custom_call" | custom-call | flops 20000000000 | bytes 1 | tf_op jit(solution)/shard_map/grads_0/pallas_call | solution.py:61
  8.7 1.7 %collective-permute-done.refs_2_ = bf16[3,256,512]{2,1,0:T(8,128)(2,1)S(1)} collective-permute-done((bf16[3,256,512]{2,1,0:T(8,128)(2,1)S(1)}, bf16[3,256,512]{2,1,0:T(8,128)(2,1)S(1)}, u32[]{:S(2)}, u32[]{:S(2)}) %collective-permute-start) | collective-permute-done | bytes 786464 | tf_op jit(solution)/shard_map/ppermute | solution.py:652
  11.7 1.6 %collective-permute-start.1 = (bf16[3,256,512]{2,1,0:T(8,128)(2,1)S(1)}, bf16[3,256,512]{2,1,0:T(8,128)(2,1)S(1)}, u32[]{:S(2)}, u32[]{:S(2)}) collective-permute-start(bf16[3,256,512]{2,1,0:T(8,128)(2,1)S(1)} %add.17.refs_3_.refs_1_), channel_id=1, source_target_pairs={{0,8},{4,20},{8,0},{12,28},{16,24},{20,4},{24,16},{28,12},{1,9},{5... | collective-permute-start | bytes 2359304 | tf_op jit(solution)/shard_map/ppermute | solution.py:652
  13.3 6.3 %collective-permute-done.3.refs_5_ = bf16[512,512]{1,0:T(8,128)(2,1)} collective-permute-done((bf16[512,512]{1,0:T(8,128)(2,1)S(1)}, bf16[512,512]{1,0:T(8,128)(2,1)}, u32[]{:S(2)}, u32[]{:S(2)}) %collective-permute-start.3) | collective-permute-done | bytes 524320 | tf_op jit(solution)/shard_map/ppermute | solution.py:652
  19.6 4.9 %mixed_0.1.refs_2_.refs_1_ = bf16[512,512]{1,0:T(8,128)(2,1)S(1)} custom-call(s32[4]{0:T(128)S(1)} %pad_add_fusion.refs_0_, bf16[3,2,512,512]{3,2,1,0:T(8,128)(2,1)S(1)} %copy-done, bf16[3,2,512,512]{3,2,1,0:T(8,128)(2,1)S(1)} %copy-done, bf16[3,2,512,512]{3,2,1,0:T(8,128)(2,1)S(1)} %copy-done, bf16[512,512]{1,0:T(8,128)(2,1)S(1)} %collective-permute-done.2.refs_4_, ...), custom_call_target="tpu_custom_call" | custom-call | flops 20000000000 | bytes 1 | tf_op jit(solution)/shard_map/mixed_0/pallas_call | solution.py:61
  24.6 3.2 %collective-permute-start.5 = (bf16[512,512]{1,0:T(8,128)(2,1)S(1)}, bf16[512,512]{1,0:T(8,128)(2,1)S(1)}, u32[]{:S(2)}, u32[]{:S(2)}) collective-permute-start(bf16[512,512]{1,0:T(8,128)(2,1)S(1)} %mixed_0.1.refs_2_.refs_1_), channel_id=1, source_target_pairs={{0,1},{1,0},{2,3},{3,2},{4,5},{5,4},{6,7},{7,6},{8,9},{9,8},{10,11... | collective-permute-start | bytes 1572872 | tf_op jit(solution)/shard_map/ppermute | solution.py:652
  28.3 3.2 %collective-permute-start.12 = (bf16[3,256,512]{2,1,0:T(8,128)(2,1)S(1)}, bf16[3,256,512]{2,1,0:T(8,128)(2,1)S(1)}, u32[]{:S(2)}, u32[]{:S(2)}) collective-permute-start(bf16[3,256,512]{2,1,0:T(8,128)(2,1)S(1)} %pick_parts.1.refs_3_), channel_id=1, source_target_pairs={{0,1},{1,0},{2,3},{3,2},{4,5},{5,4},{6,7},{7,6},{8,9},{9,8},{10,11... | collective-permute-start | bytes 2359304 | tf_op jit(solution)/shard_map/ppermute | solution.py:652
  33.0 1.8 %collective-permute-start.4 = (bf16[3,256,512]{2,1,0:T(8,128)(2,1)S(1)}, bf16[3,256,512]{2,1,0:T(8,128)(2,1)S(1)}, u32[]{:S(2)}, u32[]{:S(2)}) collective-permute-start(bf16[3,256,512]{2,1,0:T(8,128)(2,1)S(1)} %add.18.refs_5_.refs_1_), channel_id=1, source_target_pairs={{0,16},{4,12},{8,24},{12,4},{16,0},{20,28},{24,8},{28,20},{1,17},{... | collective-permute-start | bytes 2359304 | tf_op jit(solution)/shard_map/ppermute | solution.py:652
  34.8 2.9 %collective-permute-done.6.refs_4_ = bf16[2,512,512]{2,1,0:T(8,128)(2,1)S(1)} collective-permute-done((bf16[2,512,512]{2,1,0:T(8,128)(2,1)S(1)}, bf16[2,512,512]{2,1,0:T(8,128)(2,1)S(1)}, u32[]{:S(2)}, u32[]{:S(2)}) %collective-permute-start.6) | collective-permute-done | bytes 1048608 | tf_op jit(solution)/shard_map/ppermute | solution.py:652
  37.7 2.9 %attend_1.1.refs_2_.refs_6_ = bf16[512,512]{1,0:T(8,128)(2,1)S(1)} custom-call(s32[4]{0:T(128)S(1)} %pad_add_fusion.refs_0_, bf16[3,2,512,512]{3,2,1,0:T(8,128)(2,1)S(1)} %copy-done, bf16[3,2,512,512]{3,2,1,0:T(8,128)(2,1)S(1)} %copy-done, bf16[3,2,512,512]{3,2,1,0:T(8,128)(2,1)S(1)} %copy-done, bf16[2,512,512]{2,1,0:T(8,128)(2,1)S(1)} %collective-permute-done.6.refs_4_, ...), custom_call_target="tpu_custom_call" | custom-call | flops 20000000000 | bytes 1 | tf_op jit(solution)/shard_map/attend_1/pallas_call | solution.py:61
  41.3 4.8 %collective-permute-done.4.refs_2_ = bf16[3,256,512]{2,1,0:T(8,128)(2,1)S(1)} collective-permute-done((bf16[3,256,512]{2,1,0:T(8,128)(2,1)S(1)}, bf16[3,256,512]{2,1,0:T(8,128)(2,1)S(1)}, u32[]{:S(2)}, u32[]{:S(2)}) %collective-permute-start.4) | collective-permute-done | bytes 786464 | tf_op jit(solution)/shard_map/ppermute | solution.py:652
  48.3 1.4 %collective-permute-done.7.refs_2_ = bf16[3,256,512]{2,1,0:T(8,128)(2,1)S(1)} collective-permute-done((bf16[3,256,512]{2,1,0:T(8,128)(2,1)S(1)}, bf16[3,256,512]{2,1,0:T(8,128)(2,1)S(1)}, u32[]{:S(2)}, u32[]{:S(2)}) %collective-permute-start.7) | collective-permute-done | bytes 786464 | tf_op jit(solution)/shard_map/ppermute | solution.py:652
  49.6 2.6 %update_1.1 = (bf16[512,512]{1,0:T(8,128)(2,1)S(1)}, bf16[3,512,512]{2,1,0:T(8,128)(2,1)S(1)}) custom-call(s32[4]{0:T(128)S(1)} %pad_add_fusion.refs_0_, bf16[3,256,512]{2,1,0:T(8,128)(2,1)S(1)} %add.19.refs_2_.refs_1_, bf16[3,256,512]{2,1,0:T(8,128)(2,1)S(1)} %collective-permute-done.7.refs_2_, bf16[2,1,512,512]{3,2,1,0:T(8,128)(2,1)S(1)} %copy-done.3, ...), custom_call_target="tpu_custom_call" | custom-call | flops 20000000000 | bytes 1 | tf_op jit(solution)/shard_map/update_1/pallas_call | solution.py:61
  52.2 1.9 %collective-permute-start.10 = (bf16[512,512]{1,0:T(8,128)(2,1)S(1)}, bf16[512,512]{1,0:T(8,128)(2,1)S(1)}, u32[]{:S(2)}, u32[]{:S(2)}) collective-permute-start(bf16[512,512]{1,0:T(8,128)(2,1)S(1)} %get-tuple-element.20.refs_7_.refs_1_), channel_id=1, source_target_pairs={{0,1},{1,0},{2,3},{3,2},{4,5},{5,4},{6,7},{7,6},{8,9},{9,8},{10,11... | collective-permute-start | bytes 1572872 | tf_op jit(solution)/shard_map/ppermute | solution.py:652
  54.1 2.8 %grads_1.1 = (f32[3,256,512]{2,1,0:T(8,128)S(1)}, bf16[3,256,512]{2,1,0:T(8,128)(2,1)S(1)}) custom-call(s32[4]{0:T(128)S(1)} %pad_add_fusion.refs_0_, bf16[3,2,512,512]{3,2,1,0:T(8,128)(2,1)S(1)} %copy-done, bf16[3,2,512,512]{3,2,1,0:T(8,128)(2,1)S(1)} %copy-done, f32[1,2,512]{2,1,0:T(2,128)S(1)} %copy-done.6, ...), custom_call_target="tpu_custom_call" | custom-call | flops 20000000000 | bytes 1 | tf_op jit(solution)/shard_map/grads_1/pallas_call | solution.py:61
  58.2 1.3 %collective-permute-done.14.refs_2_ = bf16[3,256,512]{2,1,0:T(8,128)(2,1)S(1)} collective-permute-done((bf16[3,256,512]{2,1,0:T(8,128)(2,1)S(1)}, bf16[3,256,512]{2,1,0:T(8,128)(2,1)S(1)}, u32[]{:S(2)}, u32[]{:S(2)}) %collective-permute-start.14) | collective-permute-done | bytes 786464 | tf_op jit(solution)/shard_map/ppermute | solution.py:652
  60.6 1.5 %edge_0.1.refs_5_ = bf16[512,512]{1,0:T(8,128)(2,1)S(1)} custom-call(s32[4]{0:T(128)S(1)} %pad_add_fusion.refs_0_, bf16[512,512]{1,0:T(8,128)(2,1)S(1)} %mixed_0.1.refs_2_.refs_1_, bf16[512,512]{1,0:T(8,128)(2,1)S(1)} %gate.6.refs_7_.refs_2_.refs_3_, bf16[512,512]{1,0:T(8,128)(2,1)S(1)} %collective-permute-done.11.refs_3_.refs_4_, ...), custom_call_target="tpu_custom_call" | custom-call | flops 20000000000 | bytes 1 | tf_op jit(solution)/shard_map/edge_0/pallas_call | solution.py:61
  62.1 3.1 %collective-permute-start.19 = (bf16[512,512]{1,0:T(8,128)(2,1)S(1)}, bf16[512,512]{1,0:T(8,128)(2,1)S(1)}, u32[]{:S(2)}, u32[]{:S(2)}) collective-permute-start(bf16[512,512]{1,0:T(8,128)(2,1)S(1)} %edge_0.1.refs_5_), channel_id=1, source_target_pairs={{0,1},{1,0},{2,3},{3,2},{4,5},{5,4},{6,7},{7,6},{8,9},{9,8},{10,11... | collective-permute-start | bytes 1572872 | tf_op jit(solution)/shard_map/ppermute | solution.py:652
  65.2 2.2 %state_1.1 = (f32[3,512,512]{2,1,0:T(8,128)S(1)}, f32[3,8,128]{2,1,0:T(8,128)S(1)}) custom-call(s32[4]{0:T(128)S(1)} %pad_add_fusion.refs_0_, bf16[3,256,512]{2,1,0:T(8,128)(2,1)S(1)} %add.19.refs_2_.refs_1_, bf16[3,256,512]{2,1,0:T(8,128)(2,1)S(1)} %collective-permute-done.7.refs_2_, bf16[2,1,512,512]{3,2,1,0:T(8,128)(2,1)S(1)} %copy-done.3, ...), custom_call_target="tpu_custom_call" | custom-call | flops 20000000000 | bytes 1 | tf_op jit(solution)/shard_map/state_1/pallas_call | solution.py:61
  68.9 3.4 %collective-permute-done.17.refs_2_ = bf16[3,256,512]{2,1,0:T(8,128)(2,1)S(1)} collective-permute-done((bf16[3,256,512]{2,1,0:T(8,128)(2,1)S(1)}, bf16[3,256,512]{2,1,0:T(8,128)(2,1)S(1)}, u32[]{:S(2)}, u32[]{:S(2)}) %collective-permute-start.17) | collective-permute-done | bytes 786464 | tf_op jit(solution)/shard_map/ppermute | solution.py:652
  73.0 1.6 %collective-permute-start.18 = (bf16[3,256,512]{2,1,0:T(8,128)(2,1)S(1)}, bf16[3,256,512]{2,1,0:T(8,128)(2,1)S(1)}, u32[]{:S(2)}, u32[]{:S(2)}) collective-permute-start(bf16[3,256,512]{2,1,0:T(8,128)(2,1)S(1)} %add.21.refs_6_.refs_1_), channel_id=1, source_target_pairs={{0,16},{4,12},{8,24},{12,4},{16,0},{20,28},{24,8},{28,20},{1,17},{... | collective-permute-start | bytes 2359304 | tf_op jit(solution)/shard_map/ppermute | solution.py:652
  74.5 1.1 %edge_1_0.1.refs_8_ = bf16[256,512]{1,0:T(8,128)(2,1)S(1)} custom-call(s32[4]{0:T(128)S(1)} %pad_add_fusion.refs_0_, bf16[512,512]{1,0:T(8,128)(2,1)S(1)} %get-tuple-element.20.refs_7_.refs_1_, bf16[512,512]{1,0:T(8,128)(2,1)S(1)} %collective-permute-done.9.refs_2_, bf16[256,512]{1,0:T(8,128)(2,1)S(1)} %collective-permute-done.15.refs_3_.refs_5_, ...), custom_call_target="tpu_custom_call" | custom-call | flops 20000000000 | bytes 1 | tf_op jit(solution)/shard_map/edge_1_0/pallas_call | solution.py:61
  75.6 3.8 %collective-permute-start.20 = (bf16[256,512]{1,0:T(8,128)(2,1)S(1)}, bf16[256,512]{1,0:T(8,128)(2,1)S(1)}, u32[]{:S(2)}, u32[]{:S(2)}) collective-permute-start(bf16[256,512]{1,0:T(8,128)(2,1)S(1)} %edge_1_0.1.refs_8_), channel_id=1, source_target_pairs={{0,1},{1,0},{2,3},{3,2},{4,5},{5,4},{6,7},{7,6},{8,9},{9,8},{10,11... | collective-permute-start | bytes 786440 | tf_op jit(solution)/shard_map/ppermute | solution.py:652
  79.5 1.9 %own_0.1 = (bf16[2,512,512]{2,1,0:T(8,128)(2,1)}, f32[8,128]{1,0:T(8,128)S(1)}) custom-call(s32[4]{0:T(128)S(1)} %pad_add_fusion.refs_0_, bf16[512,512]{1,0:T(8,128)(2,1)S(1)} %mixed_0.1.refs_2_.refs_1_, bf16[512,512]{1,0:T(8,128)(2,1)S(1)} %gate.5.refs_3_.refs_2_, bf16[512,512]{1,0:T(8,128)(2,1)S(1)} %gate.6.refs_7_.refs_2_.refs_3_, ...), custom_call_target="tpu_custom_call" | custom-call | flops 20000000000 | bytes 1 | tf_op jit(solution)/shard_map/own_0/pallas_call | solution.py:61
  81.4 1.1 %edge_1_1.1.refs_3_ = bf16[256,512]{1,0:T(8,128)(2,1)S(1)} custom-call(s32[4]{0:T(128)S(1)} %pad_add_fusion.refs_0_, bf16[512,512]{1,0:T(8,128)(2,1)S(1)} %get-tuple-element.20.refs_7_.refs_1_, bf16[512,512]{1,0:T(8,128)(2,1)S(1)} %collective-permute-done.9.refs_2_, bf16[256,512]{1,0:T(8,128)(2,1)S(1)} %collective-permute-done.16.refs_3_.refs_6_, ...), custom_call_target="tpu_custom_call" | custom-call | flops 20000000000 | bytes 1 | tf_op jit(solution)/shard_map/edge_1_1/pallas_call | solution.py:61
  82.5 1.6 %collective-permute-start.21 = (bf16[256,512]{1,0:T(8,128)(2,1)S(1)}, bf16[256,512]{1,0:T(8,128)(2,1)S(1)}, u32[]{:S(2)}, u32[]{:S(2)}) collective-permute-start(bf16[256,512]{1,0:T(8,128)(2,1)S(1)} %edge_1_1.1.refs_3_), channel_id=1, source_target_pairs={{0,1},{1,0},{2,3},{3,2},{4,5},{5,4},{6,7},{7,6},{8,9},{9,8},{10,11... | collective-permute-start | bytes 786440 | tf_op jit(solution)/shard_map/ppermute | solution.py:652
  85.8 1.2 %own_1.1.refs_5_.refs_1_ = f32[512,512]{1,0:T(8,128)S(1)} custom-call(s32[4]{0:T(128)S(1)} %pad_add_fusion.refs_0_, bf16[512,512]{1,0:T(8,128)(2,1)S(1)} %get-tuple-element.20.refs_7_.refs_1_, bf16[512,512]{1,0:T(8,128)(2,1)S(1)} %collective-permute-done.9.refs_2_, bf16[256,512]{1,0:T(8,128)(2,1)S(1)} %get-tuple-element.25.refs_3_, ...), custom_call_target="tpu_custom_call" | custom-call | flops 20000000000 | bytes 1 | tf_op jit(solution)/shard_map/own_1/pallas_call | solution.py:61
  87.0 1.1 %collective-permute-done.22.refs_2_ = bf16[3,256,512]{2,1,0:T(8,128)(2,1)S(1)} collective-permute-done((bf16[3,256,512]{2,1,0:T(8,128)(2,1)S(1)}, bf16[3,256,512]{2,1,0:T(8,128)(2,1)S(1)}, u32[]{:S(2)}, u32[]{:S(2)}) %collective-permute-start.22) | collective-permute-done | bytes 786464 | tf_op jit(solution)/shard_map/ppermute | solution.py:652
  88.1 3.1 %final_update.1 = (f32[2,1,512,512]{3,2,1,0:T(8,128)}, f32[1,512,512]{2,1,0:T(8,128)}, f32[8,128]{1,0:T(8,128)S(1)}) custom-call(s32[4]{0:T(128)S(1)} %pad_add_fusion.refs_0_, bf16[3,256,512]{2,1,0:T(8,128)(2,1)S(1)} %add.22.refs_9_.refs_1_, bf16[3,256,512]{2,1,0:T(8,128)(2,1)S(1)} %collective-permute-done.22.refs_2_, ...), custom_call_target="tpu_custom_call" | custom-call | flops 20000000000 | bytes 1 | tf_op jit(solution)/shard_map/final_update/pallas_call | solution.py:61
  91.2 1.4 %finish.1 = bf16[2,512,512]{2,1,0:T(8,128)(2,1)} custom-call(s32[4]{0:T(128)S(1)} %pad_add_fusion.refs_0_, f32[512,512]{1,0:T(8,128)S(1)} %own_1.1.refs_5_.refs_1_, bf16[256,512]{1,0:T(8,128)(2,1)S(1)} %collective-permute-done.20.refs_2_, bf16[256,512]{1,0:T(8,128)(2,1)S(1)} %collective-permute-done.21.refs_3_, ...), custom_call_target="tpu_custom_call", output_to_operand_aliasing={{}: (4, {})} | custom-call | flops 20000000000 | bytes 1 | tf_op jit(solution)/shard_map/finish/pallas_call | solution.py:61
  (56 shorter events, 13.7 us)
Async XLA Ops:
  0.6 4.6 %copy-start.5 = (bf16[1,512,512]{2,1,0:T(8,128)(2,1)S(1)}, bf16[1,512,512]{2,1,0:T(8,128)(2,1)}, u32[]{:S(2)}) copy-start(bf16[1,512,512]{2,1,0:T(8,128)(2,1)} %refs_4_.5) | copy-start | bytes 1572868
  0.6 4.6 %copy-start.6 = (f32[1,2,512]{2,1,0:T(2,128)S(1)}, f32[1,2,512]{2,1,0:T(2,128)}, u32[]{:S(2)}) copy-start(f32[1,2,512]{2,1,0:T(2,128)} %refs_3_.10) | copy-start | bytes 12292
  0.7 4.6 %copy-start.3 = (bf16[2,1,512,512]{3,2,1,0:T(8,128)(2,1)S(1)}, bf16[2,1,512,512]{3,2,1,0:T(8,128)(2,1)}, u32[]{:S(2)}) copy-start(bf16[2,1,512,512]{3,2,1,0:T(8,128)(2,1)} %refs_3_.11) | copy-start | bytes 3145732
  2.0 11.2 %collective-permute-start.2 = (bf16[512,512]{1,0:T(8,128)(2,1)S(1)}, bf16[512,512]{1,0:T(8,128)(2,1)S(1)}, u32[]{:S(2)}, u32[]{:S(2)}) collective-permute-start(bf16[512,512]{1,0:T(8,128)(2,1)S(1)} %get-tuple-element.34.refs_1_), channel_id=1, source_target_pairs={{0,4},{4,8},{8,12},{12,16},{16,20},{20,24},{24,28},{28,0},{1,5},{5... | collective-permute-start | bytes 1572872 | tf_op jit(solution)/shard_map/ppermute | solution.py:652
  2.6 17.1 %collective-permute-start.3 = (bf16[512,512]{1,0:T(8,128)(2,1)S(1)}, bf16[512,512]{1,0:T(8,128)(2,1)}, u32[]{:S(2)}, u32[]{:S(2)}) collective-permute-start(bf16[512,512]{1,0:T(8,128)(2,1)S(1)} %get-tuple-element.33.refs_2_), channel_id=1, source_target_pairs={{0,4},{4,8},{8,12},{12,16},{16,20},{20,24},{24,28},{28,0},{1,5},{5... | collective-permute-start | bytes 1572872 | tf_op jit(solution)/shard_map/ppermute | solution.py:652
  8.1 2.4 %collective-permute-start = (bf16[3,256,512]{2,1,0:T(8,128)(2,1)S(1)}, bf16[3,256,512]{2,1,0:T(8,128)(2,1)S(1)}, u32[]{:S(2)}, u32[]{:S(2)}) collective-permute-start(bf16[3,256,512]{2,1,0:T(8,128)(2,1)S(1)} %get-tuple-element.19.refs_2_), channel_id=1, source_target_pairs={{0,4},{4,0},{8,12},{12,8},{16,20},{20,16},{24,28},{28,24},{1,5},{5... | collective-permute-start | bytes 2359304 | tf_op jit(solution)/shard_map/ppermute | solution.py:652
  8.7 2.4 %copy-start = (bf16[3,2,512,512]{3,2,1,0:T(8,128)(2,1)S(1)}, bf16[3,2,512,512]{3,2,1,0:T(8,128)(2,1)}, u32[]{:S(2)}) copy-start(bf16[3,2,512,512]{3,2,1,0:T(8,128)(2,1)} %refs_2_.7) | copy-start | bytes 9437188
  11.7 16.0 %copy-start.1 = (bf16[2048,512]{1,0:T(8,128)(2,1)S(1)}, bf16[2048,512]{1,0:T(8,128)(2,1)}, u32[]{:S(2)}) copy-start(bf16[2048,512]{1,0:T(8,128)(2,1)} %refs_7_.3) | copy-start | bytes 6291460
  11.7 20.5 %collective-permute-start.1 = (bf16[3,256,512]{2,1,0:T(8,128)(2,1)S(1)}, bf16[3,256,512]{2,1,0:T(8,128)(2,1)S(1)}, u32[]{:S(2)}, u32[]{:S(2)}) collective-permute-start(bf16[3,256,512]{2,1,0:T(8,128)(2,1)S(1)} %add.17.refs_3_.refs_1_), channel_id=1, source_target_pairs={{0,8},{4,20},{8,0},{12,28},{16,24},{20,4},{24,16},{28,12},{1,9},{5... | collective-permute-start | bytes 2359304 | tf_op jit(solution)/shard_map/ppermute | solution.py:652
  13.3 24.4 %collective-permute-start.6 = (bf16[2,512,512]{2,1,0:T(8,128)(2,1)S(1)}, bf16[2,512,512]{2,1,0:T(8,128)(2,1)S(1)}, u32[]{:S(2)}, u32[]{:S(2)}) collective-permute-start(bf16[2,512,512]{2,1,0:T(8,128)(2,1)S(1)} %pack_1.1.refs_9_), channel_id=1, source_target_pairs={{0,4},{4,8},{8,12},{12,16},{16,20},{20,24},{24,28},{28,0},{1,5},{5... | collective-permute-start | bytes 3145736 | tf_op jit(solution)/shard_map/ppermute | solution.py:652
  24.6 16.1 %collective-permute-start.5 = (bf16[512,512]{1,0:T(8,128)(2,1)S(1)}, bf16[512,512]{1,0:T(8,128)(2,1)S(1)}, u32[]{:S(2)}, u32[]{:S(2)}) collective-permute-start(bf16[512,512]{1,0:T(8,128)(2,1)S(1)} %mixed_0.1.refs_2_.refs_1_), channel_id=1, source_target_pairs={{0,1},{1,0},{2,3},{3,2},{4,5},{5,4},{6,7},{7,6},{8,9},{9,8},{10,11... | collective-permute-start | bytes 1572872 | tf_op jit(solution)/shard_map/ppermute | solution.py:652
  27.7 20.0 %collective-permute-start.8 = (bf16[512,512]{1,0:T(8,128)(2,1)S(1)}, bf16[512,512]{1,0:T(8,128)(2,1)S(1)}, u32[]{:S(2)}, u32[]{:S(2)}) collective-permute-start(bf16[512,512]{1,0:T(8,128)(2,1)S(1)} %mixed_0.1.refs_2_.refs_1_), channel_id=1, source_target_pairs={{1,2},{2,1},{0,4},{3,7},{5,6},{6,5},{4,0},{7,3},{9,10},{10,9},{8,1... | collective-permute-start | bytes 1572872 | tf_op jit(solution)/shard_map/ppermute | solution.py:652
  28.3 29.2 %collective-permute-start.12 = (bf16[3,256,512]{2,1,0:T(8,128)(2,1)S(1)}, bf16[3,256,512]{2,1,0:T(8,128)(2,1)S(1)}, u32[]{:S(2)}, u32[]{:S(2)}) collective-permute-start(bf16[3,256,512]{2,1,0:T(8,128)(2,1)S(1)} %pick_parts.1.refs_3_), channel_id=1, source_target_pairs={{0,1},{1,0},{2,3},{3,2},{4,5},{5,4},{6,7},{7,6},{8,9},{9,8},{10,11... | collective-permute-start | bytes 2359304 | tf_op jit(solution)/shard_map/ppermute | solution.py:652
  33.0 13.0 %collective-permute-start.4 = (bf16[3,256,512]{2,1,0:T(8,128)(2,1)S(1)}, bf16[3,256,512]{2,1,0:T(8,128)(2,1)S(1)}, u32[]{:S(2)}, u32[]{:S(2)}) collective-permute-start(bf16[3,256,512]{2,1,0:T(8,128)(2,1)S(1)} %add.18.refs_5_.refs_1_), channel_id=1, source_target_pairs={{0,16},{4,12},{8,24},{12,4},{16,0},{20,28},{24,8},{28,20},{1,17},{... | collective-permute-start | bytes 2359304 | tf_op jit(solution)/shard_map/ppermute | solution.py:652
  41.2 19.4 %collective-permute-start.11 = (bf16[512,512]{1,0:T(8,128)(2,1)S(1)}, bf16[512,512]{1,0:T(8,128)(2,1)S(1)}, u32[]{:S(2)}, u32[]{:S(2)}) collective-permute-start(bf16[512,512]{1,0:T(8,128)(2,1)S(1)} %gate.5.refs_3_.refs_2_), channel_id=1, source_target_pairs={{1,2},{2,1},{0,4},{3,7},{5,6},{6,5},{4,0},{7,3},{9,10},{10,9},{8,1... | collective-permute-start | bytes 1572872 | tf_op jit(solution)/shard_map/ppermute | solution.py:652
  46.8 2.9 %collective-permute-start.7 = (bf16[3,256,512]{2,1,0:T(8,128)(2,1)S(1)}, bf16[3,256,512]{2,1,0:T(8,128)(2,1)S(1)}, u32[]{:S(2)}, u32[]{:S(2)}) collective-permute-start(bf16[3,256,512]{2,1,0:T(8,128)(2,1)S(1)} %add.19.refs_2_.refs_1_), channel_id=1, source_target_pairs={{0,4},{4,0},{8,12},{12,8},{16,20},{20,16},{24,28},{28,24},{1,5},{5... | collective-permute-start | bytes 2359304 | tf_op jit(solution)/shard_map/ppermute | solution.py:652
  52.2 15.2 %collective-permute-start.10 = (bf16[512,512]{1,0:T(8,128)(2,1)S(1)}, bf16[512,512]{1,0:T(8,128)(2,1)S(1)}, u32[]{:S(2)}, u32[]{:S(2)}) collective-permute-start(bf16[512,512]{1,0:T(8,128)(2,1)S(1)} %get-tuple-element.20.refs_7_.refs_1_), channel_id=1, source_target_pairs={{0,1},{1,0},{2,3},{3,2},{4,5},{5,4},{6,7},{7,6},{8,9},{9,8},{10,11... | collective-permute-start | bytes 1572872 | tf_op jit(solution)/shard_map/ppermute | solution.py:652
  54.1 20.4 %collective-permute-start.9 = (bf16[512,512]{1,0:T(8,128)(2,1)S(1)}, bf16[512,512]{1,0:T(8,128)(2,1)S(1)}, u32[]{:S(2)}, u32[]{:S(2)}) collective-permute-start(bf16[512,512]{1,0:T(8,128)(2,1)S(1)} %get-tuple-element.20.refs_7_.refs_1_), channel_id=1, source_target_pairs={{1,2},{2,1},{0,4},{3,7},{5,6},{6,5},{4,0},{7,3},{9,10},{10,9},{8,1... | collective-permute-start | bytes 1572872 | tf_op jit(solution)/shard_map/ppermute | solution.py:652
  57.0 2.5 %collective-permute-start.14 = (bf16[3,256,512]{2,1,0:T(8,128)(2,1)S(1)}, bf16[3,256,512]{2,1,0:T(8,128)(2,1)S(1)}, u32[]{:S(2)}, u32[]{:S(2)}) collective-permute-start(bf16[3,256,512]{2,1,0:T(8,128)(2,1)S(1)} %get-tuple-element.22.refs_2_), channel_id=1, source_target_pairs={{0,4},{4,0},{8,12},{12,8},{16,20},{20,16},{24,28},{28,24},{1,5},{5... | collective-permute-start | bytes 2359304 | tf_op jit(solution)/shard_map/ppermute | solution.py:652
  58.1 2.5 %collective-permute-start.13 = (bf16[3,256,512]{2,1,0:T(8,128)(2,1)S(1)}, bf16[3,256,512]{2,1,0:T(8,128)(2,1)S(1)}, u32[]{:S(2)}, u32[]{:S(2)}) collective-permute-start(bf16[3,256,512]{2,1,0:T(8,128)(2,1)S(1)} %gate.7.refs_3_.refs_4_), channel_id=1, source_target_pairs={{0,4},{4,0},{8,12},{12,8},{16,20},{20,16},{24,28},{28,24},{1,5},{5... | collective-permute-start | bytes 2359304 | tf_op jit(solution)/shard_map/ppermute | solution.py:652
  60.2 12.1 %collective-permute-start.17 = (bf16[3,256,512]{2,1,0:T(8,128)(2,1)S(1)}, bf16[3,256,512]{2,1,0:T(8,128)(2,1)S(1)}, u32[]{:S(2)}, u32[]{:S(2)}) collective-permute-start(bf16[3,256,512]{2,1,0:T(8,128)(2,1)S(1)} %add.20.refs_6_.refs_1_), channel_id=1, source_target_pairs={{0,8},{4,20},{8,0},{12,28},{16,24},{20,4},{24,16},{28,12},{1,9},{5... | collective-permute-start | bytes 2359304 | tf_op jit(solution)/shard_map/ppermute | solution.py:652
  62.1 17.3 %collective-permute-start.19 = (bf16[512,512]{1,0:T(8,128)(2,1)S(1)}, bf16[512,512]{1,0:T(8,128)(2,1)S(1)}, u32[]{:S(2)}, u32[]{:S(2)}) collective-permute-start(bf16[512,512]{1,0:T(8,128)(2,1)S(1)} %edge_0.1.refs_5_), channel_id=1, source_target_pairs={{0,1},{1,0},{2,3},{3,2},{4,5},{5,4},{6,7},{7,6},{8,9},{9,8},{10,11... | collective-permute-start | bytes 1572872 | tf_op jit(solution)/shard_map/ppermute | solution.py:652
  68.0 6.5 %collective-permute-start.15 = (bf16[256,512]{1,0:T(8,128)(2,1)S(1)}, bf16[256,512]{1,0:T(8,128)(2,1)S(1)}, u32[]{:S(2)}, u32[]{:S(2)}) collective-permute-start(bf16[256,512]{1,0:T(8,128)(2,1)S(1)} %get-tuple-element.25.refs_3_), channel_id=1, source_target_pairs={{1,2},{2,1},{0,4},{3,7},{5,6},{6,5},{4,0},{7,3},{9,10},{10,9},{8,1... | collective-permute-start | bytes 786440 | tf_op jit(solution)/shard_map/ppermute | solution.py:652
  68.8 12.6 %collective-permute-start.16 = (bf16[256,512]{1,0:T(8,128)(2,1)S(1)}, bf16[256,512]{1,0:T(8,128)(2,1)S(1)}, u32[]{:S(2)}, u32[]{:S(2)}) collective-permute-start(bf16[256,512]{1,0:T(8,128)(2,1)S(1)} %get-tuple-element.26.refs_4_), channel_id=1, source_target_pairs={{1,2},{2,1},{0,4},{3,7},{5,6},{6,5},{4,0},{7,3},{9,10},{10,9},{8,1... | collective-permute-start | bytes 786440 | tf_op jit(solution)/shard_map/ppermute | solution.py:652
  72.9 6.5 %copy-start.2 = (bf16[2048,512]{1,0:T(8,128)(2,1)S(1)}, bf16[2048,512]{1,0:T(8,128)(2,1)}, u32[]{:S(2)}) copy-start(bf16[2048,512]{1,0:T(8,128)(2,1)} %refs_7_.3) | copy-start | bytes 6291460
  73.0 6.5 %copy-start.4 = (bf16[2,512,512]{2,1,0:T(8,128)(2,1)S(1)}, bf16[2,512,512]{2,1,0:T(8,128)(2,1)}, u32[]{:S(2)}) copy-start(bf16[2,512,512]{2,1,0:T(8,128)(2,1)} %refs_8_.3) | copy-start | bytes 3145732
  73.0 12.1 %collective-permute-start.18 = (bf16[3,256,512]{2,1,0:T(8,128)(2,1)S(1)}, bf16[3,256,512]{2,1,0:T(8,128)(2,1)S(1)}, u32[]{:S(2)}, u32[]{:S(2)}) collective-permute-start(bf16[3,256,512]{2,1,0:T(8,128)(2,1)S(1)} %add.21.refs_6_.refs_1_), channel_id=1, source_target_pairs={{0,16},{4,12},{8,24},{12,4},{16,0},{20,28},{24,8},{28,20},{1,17},{... | collective-permute-start | bytes 2359304 | tf_op jit(solution)/shard_map/ppermute | solution.py:652
  75.6 15.6 %collective-permute-start.20 = (bf16[256,512]{1,0:T(8,128)(2,1)S(1)}, bf16[256,512]{1,0:T(8,128)(2,1)S(1)}, u32[]{:S(2)}, u32[]{:S(2)}) collective-permute-start(bf16[256,512]{1,0:T(8,128)(2,1)S(1)} %edge_1_0.1.refs_8_), channel_id=1, source_target_pairs={{0,1},{1,0},{2,3},{3,2},{4,5},{5,4},{6,7},{7,6},{8,9},{9,8},{10,11... | collective-permute-start | bytes 786440 | tf_op jit(solution)/shard_map/ppermute | solution.py:652
  82.5 8.7 %collective-permute-start.21 = (bf16[256,512]{1,0:T(8,128)(2,1)S(1)}, bf16[256,512]{1,0:T(8,128)(2,1)S(1)}, u32[]{:S(2)}, u32[]{:S(2)}) collective-permute-start(bf16[256,512]{1,0:T(8,128)(2,1)S(1)} %edge_1_1.1.refs_3_), channel_id=1, source_target_pairs={{0,1},{1,0},{2,3},{3,2},{4,5},{5,4},{6,7},{7,6},{8,9},{9,8},{10,11... | collective-permute-start | bytes 786440 | tf_op jit(solution)/shard_map/ppermute | solution.py:652
  85.7 2.4 %collective-permute-start.22 = (bf16[3,256,512]{2,1,0:T(8,128)(2,1)S(1)}, bf16[3,256,512]{2,1,0:T(8,128)(2,1)S(1)}, u32[]{:S(2)}, u32[]{:S(2)}) collective-permute-start(bf16[3,256,512]{2,1,0:T(8,128)(2,1)S(1)} %add.22.refs_9_.refs_1_), channel_id=1, source_target_pairs={{0,4},{4,0},{8,12},{12,8},{16,20},{20,16},{24,28},{28,24},{1,5},{5... | collective-permute-start | bytes 2359304 | tf_op jit(solution)/shard_map/ppermute | solution.py:652

commit v8 on v7

--- a/solution.py
+++ b/solution.py
@@ -213,17 +213,32 @@
     return jnp.where(sc[1] > 0, 0.0, MASKED).astype(F32)
 
 
-def mixed_kernel(block, sc, q_ref, k_ref, v_ref, k_halo, v_halo, w1_ref, w3_ref, w2_ref, out_ref, att):
-    def store(rows, cols, value):
-        att[rows, cols] = value
-
-    attend(q_ref, k_ref, v_ref, (k_halo, v_halo), usable_bias(block, sc), store)
+def fast_kernel(sc, q_ref, w1_ref, w3_ref, w2_ref, out_ref):
     rows = q_ref.shape[0]
     tile = min(TILE, rows)
     for start in range(0, rows, tile):
         at = slice(start, start + tile)
-        fast = fast_rows(q_ref[at, :], w1_ref[...], w3_ref[...], w2_ref[...])
-        out_ref[at, :] = (att[at, :].astype(F32) + fast).astype(BF)
+        out_ref[at, :] = fast_rows(q_ref[at, :], w1_ref[...], w3_ref[...], w2_ref[...])
+
+
+def fast_first(scalars, projected, weights, weight_specs, earlier=()):
+    _, _, rows, feats = projected.shape
+    return call(
+        fast_kernel,
+        "fast_0",
+        scalars,
+        (projected, *weights),
+        [qkv_specs(0, projected)[0], *weight_specs],
+        jax.ShapeDtypeStruct((rows, feats), F32),
+        earlier=earlier,
+    )
+
+
+def mixed_kernel(block, sc, q_ref, k_ref, v_ref, k_halo, v_halo, fast_ref, out_ref):
+    def store(rows, cols, value):
+        out_ref[rows, cols] = (value.astype(F32) + fast_ref[rows, cols]).astype(BF)
+
+    attend(q_ref, k_ref, v_ref, (k_halo, v_halo), usable_bias(block, sc), store)
 
 
 def attend_kernel(block, sc, q_ref, k_ref, v_ref, halo_ref, out_ref):
@@ -255,16 +270,15 @@
     )
 
 
-def mixed_first(block, scalars, projected, halo, weights, weight_specs, earlier=()):
+def mixed_first(block, scalars, projected, halo, fast, earlier=()):
     _, _, rows, feats = projected.shape
     return call(
         functools.partial(mixed_kernel, block),
         f"mixed_{block}",
         scalars,
-        (projected, projected, projected, *halo, *weights),
-        [*qkv_specs(block, projected), *[whole(x) for x in halo], *weight_specs],
+        (projected, projected, projected, *halo, fast),
+        [*qkv_specs(block, projected), *[whole(x) for x in halo], whole(fast)],
         jax.ShapeDtypeStruct((rows, feats), BF),
-        scratch=[pltpu.VMEM((rows, feats), BF)],
         earlier=earlier,
     )
 
@@ -704,7 +718,8 @@
     received = move(total, "ctx", partners(ctx_count, 0))
     kv_now = pack_halo(1, scalars, projected, ctx_count - 1, earlier=(total,))
     halo_next = move(kv_now, "ctx", around)
-    mixed = mixed_first(0, scalars, projected, halo, weights, specs, earlier=(kv_now,))
+    fast = fast_first(scalars, projected, weights, specs, earlier=(kv_now,))
+    mixed = mixed_first(0, scalars, projected, halo, fast)
     x = move(mixed, "head", EDGES)
     ya = between_inner(mixed)
     v_send = last = pick_parts(scalars, w_out, earlier=(mixed,))

time: 93.7 us -> 93.9 us (level)
    pallas_call x26 -> x27, Pallas kernels: 37.8 us -> 38.5 us  [call(): pl.pallas_call(ordered, out_shape=[*outs_list, *[like(x) for x in passing...]
  transfers between devices with their start and end apart: 23 -> 23, of which waited for: 10 -> 10; matrix products, arithmetic and copies ran while one was open for 0% -> 0% of each run, Pallas kernels for 39% -> 40%
where the time goes in v8:
time: 93.9 us; the launch traced here: 93 us
  Pallas kernels  38.5 us (41%)
  starting transfers between devices  27.8 us (30%)
  waiting for transfers between devices  24 us (26%)
  local copies, waits for them, and re-layouts  1.42 us (2%)
  between operations  1.15 us (1%)
    pallas_call x27, Pallas kernels, call(): pl.pallas_call(ordered, out_shape=[*outs_list, *[like(x) for x in passing...  38.5 us
    ppermute x23, starting transfers between devices, move(): return lax.ppermute(x, axis, pairs)  27.8 us
    ppermute x23, waiting for transfers between devices, move(): return lax.ppermute(x, axis, pairs)  24 us
  transfers between devices with their start and end apart: 23, of which 10 were waited for; matrix products, arithmetic and copies ran while one was open for 0% of the time, Pallas kernels for 40%

profile of v8, /device:TPU:0, one launch (start us, length us, event | category | flops | bytes accessed | tf_op | source)
XLA Modules:
  0.0 93.0 jit_solution(15465124917502124366)
XLA Ops:
  0.7 1.4 %slice_bitcast_fusion = (bf16[512,512]{1,0:T(8,128)(2,1)S(1)}, bf16[512,512]{1,0:T(8,128)(2,1)S(1)}) fusion(bf16[3,2,512,512]{3,2,1,0:T(8,128)(2,1)} %refs_2_.9), kind=kLoop, calls=%fused_computation | loop fusion | bytes 2097152 | tf_op jit(solution)/shard_map/reshape | solution.py:502
  2.6 2.6 %collective-permute-start.3 = (bf16[512,512]{1,0:T(8,128)(2,1)S(1)}, bf16[512,512]{1,0:T(8,128)(2,1)}, u32[]{:S(2)}, u32[]{:S(2)}) collective-permute-start(bf16[512,512]{1,0:T(8,128)(2,1)S(1)} %get-tuple-element.33.refs_2_), channel_id=1, source_target_pairs={{0,4},{4,8},{8,12},{12,16},{16,20},{20,24},{24,28},{28,0},{1,5},{5... | collective-permute-start | bytes 1572872 | tf_op jit(solution)/shard_map/ppermute | solution.py:666
  5.2 2.8 %grads_0.1 = (f32[3,256,512]{2,1,0:T(8,128)S(1)}, bf16[3,256,512]{2,1,0:T(8,128)(2,1)S(1)}) custom-call(s32[4]{0:T(128)S(1)} %pad_add_fusion.refs_0_, bf16[512,512]{1,0:T(8,128)(2,1)S(1)} %get-tuple-element.34.refs_1_, bf16[512,512]{1,0:T(8,128)(2,1)S(1)} %get-tuple-element.33.refs_2_, f32[1,2,512]{2,1,0:T(2,128)S(1)} %copy-done.6, ...), custom_call_target="tpu_custom_call" | custom-call | flops 20000000000 | bytes 1 | tf_op jit(solution)/shard_map/grads_0/pallas_call | solution.py:61
  8.7 1.7 %collective-permute-done.refs_2_ = bf16[3,256,512]{2,1,0:T(8,128)(2,1)S(1)} collective-permute-done((bf16[3,256,512]{2,1,0:T(8,128)(2,1)S(1)}, bf16[3,256,512]{2,1,0:T(8,128)(2,1)S(1)}, u32[]{:S(2)}, u32[]{:S(2)}) %collective-permute-start) | collective-permute-done | bytes 786464 | tf_op jit(solution)/shard_map/ppermute | solution.py:666
  11.7 1.6 %collective-permute-start.1 = (bf16[3,256,512]{2,1,0:T(8,128)(2,1)S(1)}, bf16[3,256,512]{2,1,0:T(8,128)(2,1)S(1)}, u32[]{:S(2)}, u32[]{:S(2)}) collective-permute-start(bf16[3,256,512]{2,1,0:T(8,128)(2,1)S(1)} %add.17.refs_3_.refs_1_), channel_id=1, source_target_pairs={{0,8},{4,20},{8,0},{12,28},{16,24},{20,4},{24,16},{28,12},{1,9},{5... | collective-permute-start | bytes 2359304 | tf_op jit(solution)/shard_map/ppermute | solution.py:666
  13.3 1.8 %fast_0.1.refs_6_ = f32[512,512]{1,0:T(8,128)S(1)} custom-call(s32[4]{0:T(128)S(1)} %pad_add_fusion.refs_0_, bf16[3,2,512,512]{3,2,1,0:T(8,128)(2,1)S(1)} %copy-done, bf16[2,1,512,512]{3,2,1,0:T(8,128)(2,1)S(1)} %copy-done.3, bf16[2,1,512,512]{3,2,1,0:T(8,128)(2,1)S(1)} %copy-done.3, bf16[1,512,512]{2,1,0:T(8,128)(2,1)S(1)} %copy-done.5, ...), custom_call_target="tpu_custom_call" | custom-call | flops 20000000000 | bytes 1 | tf_op jit(solution)/shard_map/fast_0/pallas_call | solution.py:61
  15.4 4.3 %collective-permute-done.3.refs_5_ = bf16[512,512]{1,0:T(8,128)(2,1)} collective-permute-done((bf16[512,512]{1,0:T(8,128)(2,1)S(1)}, bf16[512,512]{1,0:T(8,128)(2,1)}, u32[]{:S(2)}, u32[]{:S(2)}) %collective-permute-start.3) | collective-permute-done | bytes 524320 | tf_op jit(solution)/shard_map/ppermute | solution.py:666
  19.6 4.0 %mixed_0.1.refs_2_.refs_1_ = bf16[512,512]{1,0:T(8,128)(2,1)S(1)} custom-call(s32[4]{0:T(128)S(1)} %pad_add_fusion.refs_0_, bf16[3,2,512,512]{3,2,1,0:T(8,128)(2,1)S(1)} %copy-done, bf16[3,2,512,512]{3,2,1,0:T(8,128)(2,1)S(1)} %copy-done, bf16[3,2,512,512]{3,2,1,0:T(8,128)(2,1)S(1)} %copy-done, bf16[512,512]{1,0:T(8,128)(2,1)S(1)} %collective-permute-done.2.refs_4_, ...), custom_call_target="tpu_custom_call" | custom-call | flops 20000000000 | bytes 1 | tf_op jit(solution)/shard_map/mixed_0/pallas_call | solution.py:61
  23.6 3.1 %collective-permute-start.5 = (bf16[512,512]{1,0:T(8,128)(2,1)S(1)}, bf16[512,512]{1,0:T(8,128)(2,1)S(1)}, u32[]{:S(2)}, u32[]{:S(2)}) collective-permute-start(bf16[512,512]{1,0:T(8,128)(2,1)S(1)} %mixed_0.1.refs_2_.refs_1_), channel_id=1, source_target_pairs={{0,1},{1,0},{2,3},{3,2},{4,5},{5,4},{6,7},{7,6},{8,9},{9,8},{10,11... | collective-permute-start | bytes 1572872 | tf_op jit(solution)/shard_map/ppermute | solution.py:666
  27.4 3.2 %collective-permute-start.12 = (bf16[3,256,512]{2,1,0:T(8,128)(2,1)S(1)}, bf16[3,256,512]{2,1,0:T(8,128)(2,1)S(1)}, u32[]{:S(2)}, u32[]{:S(2)}) collective-permute-start(bf16[3,256,512]{2,1,0:T(8,128)(2,1)S(1)} %pick_parts.1.refs_3_), channel_id=1, source_target_pairs={{0,1},{1,0},{2,3},{3,2},{4,5},{5,4},{6,7},{7,6},{8,9},{9,8},{10,11... | collective-permute-start | bytes 2359304 | tf_op jit(solution)/shard_map/ppermute | solution.py:666
  30.6 1.7 %collective-permute-done.1.refs_2_ = bf16[3,256,512]{2,1,0:T(8,128)(2,1)S(1)} collective-permute-done((bf16[3,256,512]{2,1,0:T(8,128)(2,1)S(1)}, bf16[3,256,512]{2,1,0:T(8,128)(2,1)S(1)}, u32[]{:S(2)}, u32[]{:S(2)}) %collective-permute-start.1) | collective-permute-done | bytes 786464 | tf_op jit(solution)/shard_map/ppermute | solution.py:666
  33.0 1.6 %collective-permute-start.4 = (bf16[3,256,512]{2,1,0:T(8,128)(2,1)S(1)}, bf16[3,256,512]{2,1,0:T(8,128)(2,1)S(1)}, u32[]{:S(2)}, u32[]{:S(2)}) collective-permute-start(bf16[3,256,512]{2,1,0:T(8,128)(2,1)S(1)} %add.18.refs_5_.refs_1_), channel_id=1, source_target_pairs={{0,16},{4,12},{8,24},{12,4},{16,0},{20,28},{24,8},{28,20},{1,17},{... | collective-permute-start | bytes 2359304 | tf_op jit(solution)/shard_map/ppermute | solution.py:666
  34.6 3.1 %collective-permute-done.6.refs_4_ = bf16[2,512,512]{2,1,0:T(8,128)(2,1)S(1)} collective-permute-done((bf16[2,512,512]{2,1,0:T(8,128)(2,1)S(1)}, bf16[2,512,512]{2,1,0:T(8,128)(2,1)S(1)}, u32[]{:S(2)}, u32[]{:S(2)}) %collective-permute-start.6) | collective-permute-done | bytes 1048608 | tf_op jit(solution)/shard_map/ppermute | solution.py:666
  37.7 3.0 %attend_1.1.refs_2_.refs_6_ = bf16[512,512]{1,0:T(8,128)(2,1)S(1)} custom-call(s32[4]{0:T(128)S(1)} %pad_add_fusion.refs_0_, bf16[3,2,512,512]{3,2,1,0:T(8,128)(2,1)S(1)} %copy-done, bf16[3,2,512,512]{3,2,1,0:T(8,128)(2,1)S(1)} %copy-done, bf16[3,2,512,512]{3,2,1,0:T(8,128)(2,1)S(1)} %copy-done, bf16[2,512,512]{2,1,0:T(8,128)(2,1)S(1)} %collective-permute-done.6.refs_4_, ...), custom_call_target="tpu_custom_call" | custom-call | flops 20000000000 | bytes 1 | tf_op jit(solution)/shard_map/attend_1/pallas_call | solution.py:61
  41.3 4.7 %collective-permute-done.4.refs_2_ = bf16[3,256,512]{2,1,0:T(8,128)(2,1)S(1)} collective-permute-done((bf16[3,256,512]{2,1,0:T(8,128)(2,1)S(1)}, bf16[3,256,512]{2,1,0:T(8,128)(2,1)S(1)}, u32[]{:S(2)}, u32[]{:S(2)}) %collective-permute-start.4) | collective-permute-done | bytes 786464 | tf_op jit(solution)/shard_map/ppermute | solution.py:666
  48.3 1.4 %collective-permute-done.7.refs_2_ = bf16[3,256,512]{2,1,0:T(8,128)(2,1)S(1)} collective-permute-done((bf16[3,256,512]{2,1,0:T(8,128)(2,1)S(1)}, bf16[3,256,512]{2,1,0:T(8,128)(2,1)S(1)}, u32[]{:S(2)}, u32[]{:S(2)}) %collective-permute-start.7) | collective-permute-done | bytes 786464 | tf_op jit(solution)/shard_map/ppermute | solution.py:666
  49.6 2.6 %update_1.1 = (bf16[512,512]{1,0:T(8,128)(2,1)S(1)}, bf16[3,512,512]{2,1,0:T(8,128)(2,1)S(1)}) custom-call(s32[4]{0:T(128)S(1)} %pad_add_fusion.refs_0_, bf16[3,256,512]{2,1,0:T(8,128)(2,1)S(1)} %add.19.refs_2_.refs_1_, bf16[3,256,512]{2,1,0:T(8,128)(2,1)S(1)} %collective-permute-done.7.refs_2_, bf16[2,1,512,512]{3,2,1,0:T(8,128)(2,1)S(1)} %copy-done.3, ...), custom_call_target="tpu_custom_call" | custom-call | flops 20000000000 | bytes 1 | tf_op jit(solution)/shard_map/update_1/pallas_call | solution.py:61
  52.2 1.9 %collective-permute-start.10 = (bf16[512,512]{1,0:T(8,128)(2,1)S(1)}, bf16[512,512]{1,0:T(8,128)(2,1)S(1)}, u32[]{:S(2)}, u32[]{:S(2)}) collective-permute-start(bf16[512,512]{1,0:T(8,128)(2,1)S(1)} %get-tuple-element.20.refs_7_.refs_1_), channel_id=1, source_target_pairs={{0,1},{1,0},{2,3},{3,2},{4,5},{5,4},{6,7},{7,6},{8,9},{9,8},{10,11... | collective-permute-start | bytes 1572872 | tf_op jit(solution)/shard_map/ppermute | solution.py:666
  54.1 2.9 %grads_1.1 = (f32[3,256,512]{2,1,0:T(8,128)S(1)}, bf16[3,256,512]{2,1,0:T(8,128)(2,1)S(1)}) custom-call(s32[4]{0:T(128)S(1)} %pad_add_fusion.refs_0_, bf16[3,2,512,512]{3,2,1,0:T(8,128)(2,1)S(1)} %copy-done, bf16[3,2,512,512]{3,2,1,0:T(8,128)(2,1)S(1)} %copy-done, f32[1,2,512]{2,1,0:T(2,128)S(1)} %copy-done.6, ...), custom_call_target="tpu_custom_call" | custom-call | flops 20000000000 | bytes 1 | tf_op jit(solution)/shard_map/grads_1/pallas_call | solution.py:61
  58.2 1.3 %collective-permute-done.14.refs_2_ = bf16[3,256,512]{2,1,0:T(8,128)(2,1)S(1)} collective-permute-done((bf16[3,256,512]{2,1,0:T(8,128)(2,1)S(1)}, bf16[3,256,512]{2,1,0:T(8,128)(2,1)S(1)}, u32[]{:S(2)}, u32[]{:S(2)}) %collective-permute-start.14) | collective-permute-done | bytes 786464 | tf_op jit(solution)/shard_map/ppermute | solution.py:666
  60.6 1.5 %edge_0.1.refs_5_ = bf16[512,512]{1,0:T(8,128)(2,1)S(1)} custom-call(s32[4]{0:T(128)S(1)} %pad_add_fusion.refs_0_, bf16[512,512]{1,0:T(8,128)(2,1)S(1)} %mixed_0.1.refs_2_.refs_1_, bf16[512,512]{1,0:T(8,128)(2,1)S(1)} %gate.6.refs_7_.refs_2_.refs_3_, bf16[512,512]{1,0:T(8,128)(2,1)S(1)} %collective-permute-done.11.refs_3_.refs_4_, ...), custom_call_target="tpu_custom_call" | custom-call | flops 20000000000 | bytes 1 | tf_op jit(solution)/shard_map/edge_0/pallas_call | solution.py:61
  62.1 3.1 %collective-permute-start.19 = (bf16[512,512]{1,0:T(8,128)(2,1)S(1)}, bf16[512,512]{1,0:T(8,128)(2,1)S(1)}, u32[]{:S(2)}, u32[]{:S(2)}) collective-permute-start(bf16[512,512]{1,0:T(8,128)(2,1)S(1)} %edge_0.1.refs_5_), channel_id=1, source_target_pairs={{0,1},{1,0},{2,3},{3,2},{4,5},{5,4},{6,7},{7,6},{8,9},{9,8},{10,11... | collective-permute-start | bytes 1572872 | tf_op jit(solution)/shard_map/ppermute | solution.py:666
  65.2 2.0 %state_1.1 = (f32[3,512,512]{2,1,0:T(8,128)S(1)}, f32[3,8,128]{2,1,0:T(8,128)S(1)}) custom-call(s32[4]{0:T(128)S(1)} %pad_add_fusion.refs_0_, bf16[3,256,512]{2,1,0:T(8,128)(2,1)S(1)} %add.19.refs_2_.refs_1_, bf16[3,256,512]{2,1,0:T(8,128)(2,1)S(1)} %collective-permute-done.7.refs_2_, bf16[2,1,512,512]{3,2,1,0:T(8,128)(2,1)S(1)} %copy-done.3, ...), custom_call_target="tpu_custom_call" | custom-call | flops 20000000000 | bytes 1 | tf_op jit(solution)/shard_map/state_1/pallas_call | solution.py:61
  68.6 3.6 %collective-permute-done.17.refs_2_ = bf16[3,256,512]{2,1,0:T(8,128)(2,1)S(1)} collective-permute-done((bf16[3,256,512]{2,1,0:T(8,128)(2,1)S(1)}, bf16[3,256,512]{2,1,0:T(8,128)(2,1)S(1)}, u32[]{:S(2)}, u32[]{:S(2)}) %collective-permute-start.17) | collective-permute-done | bytes 786464 | tf_op jit(solution)/shard_map/ppermute | solution.py:666
  73.0 1.8 %collective-permute-start.18 = (bf16[3,256,512]{2,1,0:T(8,128)(2,1)S(1)}, bf16[3,256,512]{2,1,0:T(8,128)(2,1)S(1)}, u32[]{:S(2)}, u32[]{:S(2)}) collective-permute-start(bf16[3,256,512]{2,1,0:T(8,128)(2,1)S(1)} %add.21.refs_6_.refs_1_), channel_id=1, source_target_pairs={{0,16},{4,12},{8,24},{12,4},{16,0},{20,28},{24,8},{28,20},{1,17},{... | collective-permute-start | bytes 2359304 | tf_op jit(solution)/shard_map/ppermute | solution.py:666
  75.8 3.6 %collective-permute-start.20 = (bf16[256,512]{1,0:T(8,128)(2,1)S(1)}, bf16[256,512]{1,0:T(8,128)(2,1)S(1)}, u32[]{:S(2)}, u32[]{:S(2)}) collective-permute-start(bf16[256,512]{1,0:T(8,128)(2,1)S(1)} %edge_1_0.1.refs_8_), channel_id=1, source_target_pairs={{0,1},{1,0},{2,3},{3,2},{4,5},{5,4},{6,7},{7,6},{8,9},{9,8},{10,11... | collective-permute-start | bytes 786440 | tf_op jit(solution)/shard_map/ppermute | solution.py:666
  79.5 1.9 %own_0.1 = (bf16[2,512,512]{2,1,0:T(8,128)(2,1)}, f32[8,128]{1,0:T(8,128)S(1)}) custom-call(s32[4]{0:T(128)S(1)} %pad_add_fusion.refs_0_, bf16[512,512]{1,0:T(8,128)(2,1)S(1)} %mixed_0.1.refs_2_.refs_1_, bf16[512,512]{1,0:T(8,128)(2,1)S(1)} %gate.5.refs_3_.refs_2_, bf16[512,512]{1,0:T(8,128)(2,1)S(1)} %gate.6.refs_7_.refs_2_.refs_3_, ...), custom_call_target="tpu_custom_call" | custom-call | flops 20000000000 | bytes 1 | tf_op jit(solution)/shard_map/own_0/pallas_call | solution.py:61
  82.5 1.5 %collective-permute-start.21 = (bf16[256,512]{1,0:T(8,128)(2,1)S(1)}, bf16[256,512]{1,0:T(8,128)(2,1)S(1)}, u32[]{:S(2)}, u32[]{:S(2)}) collective-permute-start(bf16[256,512]{1,0:T(8,128)(2,1)S(1)} %edge_1_1.1.refs_3_), channel_id=1, source_target_pairs={{0,1},{1,0},{2,3},{3,2},{4,5},{5,4},{6,7},{7,6},{8,9},{9,8},{10,11... | collective-permute-start | bytes 786440 | tf_op jit(solution)/shard_map/ppermute | solution.py:666
  84.0 1.2 %collective-permute-done.18.refs_2_ = bf16[3,256,512]{2,1,0:T(8,128)(2,1)S(1)} collective-permute-done((bf16[3,256,512]{2,1,0:T(8,128)(2,1)S(1)}, bf16[3,256,512]{2,1,0:T(8,128)(2,1)S(1)}, u32[]{:S(2)}, u32[]{:S(2)}) %collective-permute-start.18) | collective-permute-done | bytes 786464 | tf_op jit(solution)/shard_map/ppermute | solution.py:666
  86.0 1.2 %own_1.1.refs_5_.refs_1_ = f32[512,512]{1,0:T(8,128)S(1)} custom-call(s32[4]{0:T(128)S(1)} %pad_add_fusion.refs_0_, bf16[512,512]{1,0:T(8,128)(2,1)S(1)} %get-tuple-element.20.refs_7_.refs_1_, bf16[512,512]{1,0:T(8,128)(2,1)S(1)} %collective-permute-done.9.refs_2_, bf16[256,512]{1,0:T(8,128)(2,1)S(1)} %get-tuple-element.25.refs_3_, ...), custom_call_target="tpu_custom_call" | custom-call | flops 20000000000 | bytes 1 | tf_op jit(solution)/shard_map/own_1/pallas_call | solution.py:61
  88.3 3.1 %final_update.1 = (f32[2,1,512,512]{3,2,1,0:T(8,128)}, f32[1,512,512]{2,1,0:T(8,128)}, f32[8,128]{1,0:T(8,128)S(1)}) custom-call(s32[4]{0:T(128)S(1)} %pad_add_fusion.refs_0_, bf16[3,256,512]{2,1,0:T(8,128)(2,1)S(1)} %add.22.refs_9_.refs_1_, bf16[3,256,512]{2,1,0:T(8,128)(2,1)S(1)} %collective-permute-done.22.refs_2_, ...), custom_call_target="tpu_custom_call" | custom-call | flops 20000000000 | bytes 1 | tf_op jit(solution)/shard_map/final_update/pallas_call | solution.py:61
  91.4 1.4 %finish.1 = bf16[2,512,512]{2,1,0:T(8,128)(2,1)} custom-call(s32[4]{0:T(128)S(1)} %pad_add_fusion.refs_0_, f32[512,512]{1,0:T(8,128)S(1)} %own_1.1.refs_5_.refs_1_, bf16[256,512]{1,0:T(8,128)(2,1)S(1)} %collective-permute-done.20.refs_2_, bf16[256,512]{1,0:T(8,128)(2,1)S(1)} %collective-permute-done.21.refs_3_, ...), custom_call_target="tpu_custom_call", output_to_operand_aliasing={{}: (4, {})} | custom-call | flops 20000000000 | bytes 1 | tf_op jit(solution)/shard_map/finish/pallas_call | solution.py:61
  (57 shorter events, 15.6 us)
Async XLA Ops:
  0.6 4.6 %copy-start.5 = (bf16[1,512,512]{2,1,0:T(8,128)(2,1)S(1)}, bf16[1,512,512]{2,1,0:T(8,128)(2,1)}, u32[]{:S(2)}) copy-start(bf16[1,512,512]{2,1,0:T(8,128)(2,1)} %refs_4_.7) | copy-start | bytes 1572868
  0.6 4.6 %copy-start.6 = (f32[1,2,512]{2,1,0:T(2,128)S(1)}, f32[1,2,512]{2,1,0:T(2,128)}, u32[]{:S(2)}) copy-start(f32[1,2,512]{2,1,0:T(2,128)} %refs_3_.12) | copy-start | bytes 12292
  0.7 4.6 %copy-start.3 = (bf16[2,1,512,512]{3,2,1,0:T(8,128)(2,1)S(1)}, bf16[2,1,512,512]{3,2,1,0:T(8,128)(2,1)}, u32[]{:S(2)}) copy-start(bf16[2,1,512,512]{3,2,1,0:T(8,128)(2,1)} %refs_3_.13) | copy-start | bytes 3145732
  2.0 13.3 %collective-permute-start.2 = (bf16[512,512]{1,0:T(8,128)(2,1)S(1)}, bf16[512,512]{1,0:T(8,128)(2,1)S(1)}, u32[]{:S(2)}, u32[]{:S(2)}) collective-permute-start(bf16[512,512]{1,0:T(8,128)(2,1)S(1)} %get-tuple-element.34.refs_1_), channel_id=1, source_target_pairs={{0,4},{4,8},{8,12},{12,16},{16,20},{20,24},{24,28},{28,0},{1,5},{5... | collective-permute-start | bytes 1572872 | tf_op jit(solution)/shard_map/ppermute | solution.py:666
  2.6 17.1 %collective-permute-start.3 = (bf16[512,512]{1,0:T(8,128)(2,1)S(1)}, bf16[512,512]{1,0:T(8,128)(2,1)}, u32[]{:S(2)}, u32[]{:S(2)}) collective-permute-start(bf16[512,512]{1,0:T(8,128)(2,1)S(1)} %get-tuple-element.33.refs_2_), channel_id=1, source_target_pairs={{0,4},{4,8},{8,12},{12,16},{16,20},{20,24},{24,28},{28,0},{1,5},{5... | collective-permute-start | bytes 1572872 | tf_op jit(solution)/shard_map/ppermute | solution.py:666
  8.1 2.4 %collective-permute-start = (bf16[3,256,512]{2,1,0:T(8,128)(2,1)S(1)}, bf16[3,256,512]{2,1,0:T(8,128)(2,1)S(1)}, u32[]{:S(2)}, u32[]{:S(2)}) collective-permute-start(bf16[3,256,512]{2,1,0:T(8,128)(2,1)S(1)} %get-tuple-element.19.refs_2_), channel_id=1, source_target_pairs={{0,4},{4,0},{8,12},{12,8},{16,20},{20,16},{24,28},{28,24},{1,5},{5... | collective-permute-start | bytes 2359304 | tf_op jit(solution)/shard_map/ppermute | solution.py:666
  8.7 2.4 %copy-start = (bf16[3,2,512,512]{3,2,1,0:T(8,128)(2,1)S(1)}, bf16[3,2,512,512]{3,2,1,0:T(8,128)(2,1)}, u32[]{:S(2)}) copy-start(bf16[3,2,512,512]{3,2,1,0:T(8,128)(2,1)} %refs_2_.9) | copy-start | bytes 9437188
  11.7 20.5 %collective-permute-start.1 = (bf16[3,256,512]{2,1,0:T(8,128)(2,1)S(1)}, bf16[3,256,512]{2,1,0:T(8,128)(2,1)S(1)}, u32[]{:S(2)}, u32[]{:S(2)}) collective-permute-start(bf16[3,256,512]{2,1,0:T(8,128)(2,1)S(1)} %add.17.refs_3_.refs_1_), channel_id=1, source_target_pairs={{0,8},{4,20},{8,0},{12,28},{16,24},{20,4},{24,16},{28,12},{1,9},{5... | collective-permute-start | bytes 2359304 | tf_op jit(solution)/shard_map/ppermute | solution.py:666
  15.1 11.7 %copy-start.1 = (bf16[2048,512]{1,0:T(8,128)(2,1)S(1)}, bf16[2048,512]{1,0:T(8,128)(2,1)}, u32[]{:S(2)}) copy-start(bf16[2048,512]{1,0:T(8,128)(2,1)} %refs_7_.1) | copy-start | bytes 6291460
  15.1 22.6 %collective-permute-start.6 = (bf16[2,512,512]{2,1,0:T(8,128)(2,1)S(1)}, bf16[2,512,512]{2,1,0:T(8,128)(2,1)S(1)}, u32[]{:S(2)}, u32[]{:S(2)}) collective-permute-start(bf16[2,512,512]{2,1,0:T(8,128)(2,1)S(1)} %pack_1.1.refs_5_), channel_id=1, source_target_pairs={{0,4},{4,8},{8,12},{12,16},{16,20},{20,24},{24,28},{28,0},{1,5},{5... | collective-permute-start | bytes 3145736 | tf_op jit(solution)/shard_map/ppermute | solution.py:666
  23.6 17.0 %collective-permute-start.5 = (bf16[512,512]{1,0:T(8,128)(2,1)S(1)}, bf16[512,512]{1,0:T(8,128)(2,1)S(1)}, u32[]{:S(2)}, u32[]{:S(2)}) collective-permute-start(bf16[512,512]{1,0:T(8,128)(2,1)S(1)} %mixed_0.1.refs_2_.refs_1_), channel_id=1, source_target_pairs={{0,1},{1,0},{2,3},{3,2},{4,5},{5,4},{6,7},{7,6},{8,9},{9,8},{10,11... | collective-permute-start | bytes 1572872 | tf_op jit(solution)/shard_map/ppermute | solution.py:666
  26.8 20.9 %collective-permute-start.8 = (bf16[512,512]{1,0:T(8,128)(2,1)S(1)}, bf16[512,512]{1,0:T(8,128)(2,1)S(1)}, u32[]{:S(2)}, u32[]{:S(2)}) collective-permute-start(bf16[512,512]{1,0:T(8,128)(2,1)S(1)} %mixed_0.1.refs_2_.refs_1_), channel_id=1, source_target_pairs={{1,2},{2,1},{0,4},{3,7},{5,6},{6,5},{4,0},{7,3},{9,10},{10,9},{8,1... | collective-permute-start | bytes 1572872 | tf_op jit(solution)/shard_map/ppermute | solution.py:666
  27.4 30.1 %collective-permute-start.12 = (bf16[3,256,512]{2,1,0:T(8,128)(2,1)S(1)}, bf16[3,256,512]{2,1,0:T(8,128)(2,1)S(1)}, u32[]{:S(2)}, u32[]{:S(2)}) collective-permute-start(bf16[3,256,512]{2,1,0:T(8,128)(2,1)S(1)} %pick_parts.1.refs_3_), channel_id=1, source_target_pairs={{0,1},{1,0},{2,3},{3,2},{4,5},{5,4},{6,7},{7,6},{8,9},{9,8},{10,11... | collective-permute-start | bytes 2359304 | tf_op jit(solution)/shard_map/ppermute | solution.py:666
  33.0 13.0 %collective-permute-start.4 = (bf16[3,256,512]{2,1,0:T(8,128)(2,1)S(1)}, bf16[3,256,512]{2,1,0:T(8,128)(2,1)S(1)}, u32[]{:S(2)}, u32[]{:S(2)}) collective-permute-start(bf16[3,256,512]{2,1,0:T(8,128)(2,1)S(1)} %add.18.refs_5_.refs_1_), channel_id=1, source_target_pairs={{0,16},{4,12},{8,24},{12,4},{16,0},{20,28},{24,8},{28,20},{1,17},{... | collective-permute-start | bytes 2359304 | tf_op jit(solution)/shard_map/ppermute | solution.py:666
  41.2 19.3 %collective-permute-start.11 = (bf16[512,512]{1,0:T(8,128)(2,1)S(1)}, bf16[512,512]{1,0:T(8,128)(2,1)S(1)}, u32[]{:S(2)}, u32[]{:S(2)}) collective-permute-start(bf16[512,512]{1,0:T(8,128)(2,1)S(1)} %gate.5.refs_3_.refs_2_), channel_id=1, source_target_pairs={{1,2},{2,1},{0,4},{3,7},{5,6},{6,5},{4,0},{7,3},{9,10},{10,9},{8,1... | collective-permute-start | bytes 1572872 | tf_op jit(solution)/shard_map/ppermute | solution.py:666
  46.8 2.9 %collective-permute-start.7 = (bf16[3,256,512]{2,1,0:T(8,128)(2,1)S(1)}, bf16[3,256,512]{2,1,0:T(8,128)(2,1)S(1)}, u32[]{:S(2)}, u32[]{:S(2)}) collective-permute-start(bf16[3,256,512]{2,1,0:T(8,128)(2,1)S(1)} %add.19.refs_2_.refs_1_), channel_id=1, source_target_pairs={{0,4},{4,0},{8,12},{12,8},{16,20},{20,16},{24,28},{28,24},{1,5},{5... | collective-permute-start | bytes 2359304 | tf_op jit(solution)/shard_map/ppermute | solution.py:666
  52.2 15.0 %collective-permute-start.10 = (bf16[512,512]{1,0:T(8,128)(2,1)S(1)}, bf16[512,512]{1,0:T(8,128)(2,1)S(1)}, u32[]{:S(2)}, u32[]{:S(2)}) collective-permute-start(bf16[512,512]{1,0:T(8,128)(2,1)S(1)} %get-tuple-element.20.refs_7_.refs_1_), channel_id=1, source_target_pairs={{0,1},{1,0},{2,3},{3,2},{4,5},{5,4},{6,7},{7,6},{8,9},{9,8},{10,11... | collective-permute-start | bytes 1572872 | tf_op jit(solution)/shard_map/ppermute | solution.py:666
  54.1 20.6 %collective-permute-start.9 = (bf16[512,512]{1,0:T(8,128)(2,1)S(1)}, bf16[512,512]{1,0:T(8,128)(2,1)S(1)}, u32[]{:S(2)}, u32[]{:S(2)}) collective-permute-start(bf16[512,512]{1,0:T(8,128)(2,1)S(1)} %get-tuple-element.20.refs_7_.refs_1_), channel_id=1, source_target_pairs={{1,2},{2,1},{0,4},{3,7},{5,6},{6,5},{4,0},{7,3},{9,10},{10,9},{8,1... | collective-permute-start | bytes 1572872 | tf_op jit(solution)/shard_map/ppermute | solution.py:666
  57.0 2.5 %collective-permute-start.14 = (bf16[3,256,512]{2,1,0:T(8,128)(2,1)S(1)}, bf16[3,256,512]{2,1,0:T(8,128)(2,1)S(1)}, u32[]{:S(2)}, u32[]{:S(2)}) collective-permute-start(bf16[3,256,512]{2,1,0:T(8,128)(2,1)S(1)} %get-tuple-element.22.refs_2_), channel_id=1, source_target_pairs={{0,4},{4,0},{8,12},{12,8},{16,20},{20,16},{24,28},{28,24},{1,5},{5... | collective-permute-start | bytes 2359304 | tf_op jit(solution)/shard_map/ppermute | solution.py:666
  58.1 2.5 %collective-permute-start.13 = (bf16[3,256,512]{2,1,0:T(8,128)(2,1)S(1)}, bf16[3,256,512]{2,1,0:T(8,128)(2,1)S(1)}, u32[]{:S(2)}, u32[]{:S(2)}) collective-permute-start(bf16[3,256,512]{2,1,0:T(8,128)(2,1)S(1)} %gate.7.refs_3_.refs_4_), channel_id=1, source_target_pairs={{0,4},{4,0},{8,12},{12,8},{16,20},{20,16},{24,28},{28,24},{1,5},{5... | collective-permute-start | bytes 2359304 | tf_op jit(solution)/shard_map/ppermute | solution.py:666
  60.2 12.1 %collective-permute-start.17 = (bf16[3,256,512]{2,1,0:T(8,128)(2,1)S(1)}, bf16[3,256,512]{2,1,0:T(8,128)(2,1)S(1)}, u32[]{:S(2)}, u32[]{:S(2)}) collective-permute-start(bf16[3,256,512]{2,1,0:T(8,128)(2,1)S(1)} %add.20.refs_6_.refs_1_), channel_id=1, source_target_pairs={{0,8},{4,20},{8,0},{12,28},{16,24},{20,4},{24,16},{28,12},{1,9},{5... | collective-permute-start | bytes 2359304 | tf_op jit(solution)/shard_map/ppermute | solution.py:666
  62.1 17.4 %collective-permute-start.19 = (bf16[512,512]{1,0:T(8,128)(2,1)S(1)}, bf16[512,512]{1,0:T(8,128)(2,1)S(1)}, u32[]{:S(2)}, u32[]{:S(2)}) collective-permute-start(bf16[512,512]{1,0:T(8,128)(2,1)S(1)} %edge_0.1.refs_5_), channel_id=1, source_target_pairs={{0,1},{1,0},{2,3},{3,2},{4,5},{5,4},{6,7},{7,6},{8,9},{9,8},{10,11... | collective-permute-start | bytes 1572872 | tf_op jit(solution)/shard_map/ppermute | solution.py:666
  67.8 6.9 %collective-permute-start.15 = (bf16[256,512]{1,0:T(8,128)(2,1)S(1)}, bf16[256,512]{1,0:T(8,128)(2,1)S(1)}, u32[]{:S(2)}, u32[]{:S(2)}) collective-permute-start(bf16[256,512]{1,0:T(8,128)(2,1)S(1)} %get-tuple-element.25.refs_3_), channel_id=1, source_target_pairs={{1,2},{2,1},{0,4},{3,7},{5,6},{6,5},{4,0},{7,3},{9,10},{10,9},{8,1... | collective-permute-start | bytes 786440 | tf_op jit(solution)/shard_map/ppermute | solution.py:666
  68.5 12.8 %collective-permute-start.16 = (bf16[256,512]{1,0:T(8,128)(2,1)S(1)}, bf16[256,512]{1,0:T(8,128)(2,1)S(1)}, u32[]{:S(2)}, u32[]{:S(2)}) collective-permute-start(bf16[256,512]{1,0:T(8,128)(2,1)S(1)} %get-tuple-element.26.refs_4_), channel_id=1, source_target_pairs={{1,2},{2,1},{0,4},{3,7},{5,6},{6,5},{4,0},{7,3},{9,10},{10,9},{8,1... | collective-permute-start | bytes 786440 | tf_op jit(solution)/shard_map/ppermute | solution.py:666
  72.9 6.5 %copy-start.2 = (bf16[2048,512]{1,0:T(8,128)(2,1)S(1)}, bf16[2048,512]{1,0:T(8,128)(2,1)}, u32[]{:S(2)}) copy-start(bf16[2048,512]{1,0:T(8,128)(2,1)} %refs_7_.1) | copy-start | bytes 6291460
  72.9 6.5 %copy-start.4 = (bf16[2,512,512]{2,1,0:T(8,128)(2,1)S(1)}, bf16[2,512,512]{2,1,0:T(8,128)(2,1)}, u32[]{:S(2)}) copy-start(bf16[2,512,512]{2,1,0:T(8,128)(2,1)} %refs_8_.1) | copy-start | bytes 3145732
  73.0 12.3 %collective-permute-start.18 = (bf16[3,256,512]{2,1,0:T(8,128)(2,1)S(1)}, bf16[3,256,512]{2,1,0:T(8,128)(2,1)S(1)}, u32[]{:S(2)}, u32[]{:S(2)}) collective-permute-start(bf16[3,256,512]{2,1,0:T(8,128)(2,1)S(1)} %add.21.refs_6_.refs_1_), channel_id=1, source_target_pairs={{0,16},{4,12},{8,24},{12,4},{16,0},{20,28},{24,8},{28,20},{1,17},{... | collective-permute-start | bytes 2359304 | tf_op jit(solution)/shard_map/ppermute | solution.py:666
  75.8 15.6 %collective-permute-start.20 = (bf16[256,512]{1,0:T(8,128)(2,1)S(1)}, bf16[256,512]{1,0:T(8,128)(2,1)S(1)}, u32[]{:S(2)}, u32[]{:S(2)}) collective-permute-start(bf16[256,512]{1,0:T(8,128)(2,1)S(1)} %edge_1_0.1.refs_8_), channel_id=1, source_target_pairs={{0,1},{1,0},{2,3},{3,2},{4,5},{5,4},{6,7},{7,6},{8,9},{9,8},{10,11... | collective-permute-start | bytes 786440 | tf_op jit(solution)/shard_map/ppermute | solution.py:666
  82.5 8.9 %collective-permute-start.21 = (bf16[256,512]{1,0:T(8,128)(2,1)S(1)}, bf16[256,512]{1,0:T(8,128)(2,1)S(1)}, u32[]{:S(2)}, u32[]{:S(2)}) collective-permute-start(bf16[256,512]{1,0:T(8,128)(2,1)S(1)} %edge_1_1.1.refs_3_), channel_id=1, source_target_pairs={{0,1},{1,0},{2,3},{3,2},{4,5},{5,4},{6,7},{7,6},{8,9},{9,8},{10,11... | collective-permute-start | bytes 786440 | tf_op jit(solution)/shard_map/ppermute | solution.py:666
  86.0 2.4 %collective-permute-start.22 = (bf16[3,256,512]{2,1,0:T(8,128)(2,1)S(1)}, bf16[3,256,512]{2,1,0:T(8,128)(2,1)S(1)}, u32[]{:S(2)}, u32[]{:S(2)}) collective-permute-start(bf16[3,256,512]{2,1,0:T(8,128)(2,1)S(1)} %add.22.refs_9_.refs_1_), channel_id=1, source_target_pairs={{0,4},{4,0},{8,12},{12,8},{16,20},{20,16},{24,28},{28,24},{1,5},{5... | collective-permute-start | bytes 2359304 | tf_op jit(solution)/shard_map/ppermute | solution.py:666
